TPU v7x, 32 devices: a whole 2x2x4 slice. The times are simulated.
32 devices in a mesh: grp: 8 (over y, x, core), rep: 4 (over z).
Axes of the slice: x: 2, y: 2, z: 4, core: 2. Of those that a mesh axis runs over, the one named last changes fastest.
Arguments:
- layer_input: bfloat16 [4, 2048, 2048], P('rep', 'grp'), may hold values from -6 to 6
- cotangent: bfloat16 [4, 2048, 2048], P('rep', 'grp'), may hold values from -6 to 6
- cut_order: int32 [4, 16], P('rep'), may hold values from 0 to 15, each once within a row
- piece_ids: int32 [4, 2048], P('rep'), may hold values from 0 to 8, as said below
- w_query: bfloat16 [2048, 2048], P('grp'), may hold values from -0.1875 to 0.1875
- w_key: bfloat16 [2048, 1024], P('grp'), may hold values from -0.1875 to 0.1875
- w_value: bfloat16 [2048, 1024], P('grp'), may hold values from -0.125 to 0.125
- w_out: bfloat16 [2048, 2048], P('grp'), may hold values from -0.5 to 0.5
- w_gate: bfloat16 [2048, 8192], P('grp'), may hold values from -0.125 to 0.125
- w_up: bfloat16 [2048, 8192], P('grp'), may hold values from -0.125 to 0.125
- w_down: bfloat16 [8192, 2048], P('grp'), may hold values from -0.125 to 0.125
- gain_attn: float32 [2048], replicated, may hold values from 0.25 to 1.75
- gain_ffn: float32 [2048], replicated, may hold values from 0.25 to 1.75
Outputs:
- layer_output: bfloat16 [4, 2048, 2048], P('rep', 'grp')
- grad_x: bfloat16 [4, 2048, 2048], P('rep', 'grp')
- grad_w_query: float32 [2048, 2048], P('grp')
- grad_w_key: float32 [2048, 1024], P('grp')
- grad_w_value: float32 [2048, 1024], P('grp')
- grad_w_out: float32 [2048, 2048], P('grp')
- grad_w_gate: float32 [2048, 8192], P('grp')
- grad_w_up: float32 [2048, 8192], P('grp')
- grad_w_down: float32 [8192, 2048], P('grp')
- grad_gain_attn: float32 [2048], P('grp')
- grad_gain_ffn: float32 [2048], P('grp')
Inputs may be any that keep to these rules, and one draw needn't show every extreme that they name: `cut_order`: each row is a permutation of the 16 cut numbers. `piece_ids`: A sequence is cut into aligned runs of 256 positions; run k carries id k + 1 on all its positions if it is a picture, else 0; the last run of every sequence is a picture.
All inputs are finite; a program needn't handle non-finite values.
Results may differ from a plain program's by a relative error of at most 0.024.
Values may be sent and summed in bfloat16 or wider, within the bound.
A program may use at most 640 MiB of HBM per device.

v0:
```python
import jax
import jax.numpy as jnp
from jax import lax
from jax.sharding import PartitionSpec as P

HD = 128


EPS = 1e-05
ROPE_BASE = 1000000.0


def matmul_f32(first, second):
    return jnp.dot(first, second, preferred_element_type=jnp.float32)


def against_rows(first, second):
    return jnp.einsum("tc,rc->tr", first, second, preferred_element_type=jnp.float32)


def over_tokens(first, second):
    return jnp.einsum("tr,tc->rc", first, second, preferred_element_type=jnp.float32)


def turn_tables(places, head_size):
    half_size = head_size // 2
    inverse = ROPE_BASE ** (-(jnp.arange(half_size, dtype=jnp.float32) * 2.0) / head_size)
    angles = places.astype(jnp.float32)[..., None] * inverse
    cosine = jnp.concatenate([jnp.cos(angles), jnp.cos(angles)], -1)[:, :, None, :]
    sine_table = jnp.concatenate([jnp.sin(angles), jnp.sin(angles)], -1)[:, :, None, :]
    return (cosine, sine_table)


def rotate(features, cosine, sine_table):
    half_size = features.shape[-1] // 2
    turned = jnp.concatenate([-features[..., half_size:], features[..., :half_size]], -1)
    return features * cosine + turned * sine_table


def rotate_back(incoming, cosine, sine_table):
    half_size = incoming.shape[-1] // 2
    scaled = incoming * sine_table
    return incoming * cosine + jnp.concatenate(
        [scaled[..., half_size:], -scaled[..., :half_size]], -1
    )


def norm_back(upstream, grad_normed, unit_rows, inv_root, gain):
    scaled = grad_normed * gain
    center_term = jnp.mean(scaled * unit_rows, -1, keepdims=True)
    return (
        upstream + inv_root * (scaled - unit_rows * center_term),
        jnp.sum(grad_normed * unit_rows, 0),
    )


def seven_terms(
    normed_cols,
    attended_cols,
    second_cols,
    hidden_cols,
    grads,
    row_count,
    hidden_ratio,
    model_width,
):
    grad_query, grad_key, grad_value, grad_mid_low, grad_gate, grad_up, grad_out = grads
    return jnp.concatenate(
        [
            over_tokens(normed_cols, grad_query),
            over_tokens(normed_cols, grad_key),
            over_tokens(normed_cols, grad_value),
            over_tokens(attended_cols, grad_mid_low),
            over_tokens(second_cols, grad_gate),
            over_tokens(second_cols, grad_up),
            over_tokens(hidden_cols, grad_out).reshape(row_count, hidden_ratio * model_width),
        ],
        1,
    )


def on_device(
    layer_input,
    cotangent,
    cut_order,
    piece_ids,
    w_query,
    w_key,
    w_value,
    w_out,
    w_gate,
    w_up,
    w_down,
    gain_attn,
    gain_ffn,
):
    groups = lax.axis_size("grp")
    own_index = lax.axis_index("grp")
    seq_count, local_rows, model_width = layer_input.shape
    length = piece_ids.shape[1]
    cut_len = length // cut_order.shape[1]
    token_count = seq_count * local_rows
    q_width = w_query.shape[1]
    kv_width = w_key.shape[1]
    head_count = q_width // HD
    kv_heads = kv_width // HD
    group_size = head_count // kv_heads
    hidden_width = w_gate.shape[1]
    hidden_ratio = hidden_width // model_width
    score_scale = HD ** (-0.5)
    key_block = min(512, length)
    blocks = length // key_block
    rows_here = model_width // groups
    f32 = jnp.float32
    bf16 = jnp.bfloat16
    rows_all = jnp.arange(length, dtype=jnp.int32)
    slot_of_row = jnp.broadcast_to(rows_all // cut_len, (seq_count, length))
    key_places = jnp.take_along_axis(cut_order, slot_of_row, axis=1) * cut_len + rows_all % cut_len
    key_pieces = jnp.take_along_axis(piece_ids, key_places, axis=1)
    query_places = lax.dynamic_slice_in_dim(key_places, own_index * local_rows, local_rows, 1)
    query_pieces = lax.dynamic_slice_in_dim(key_pieces, own_index * local_rows, local_rows, 1)
    cosine, sine_table = turn_tables(query_places, HD)
    x_flat = layer_input.reshape(token_count, model_width).astype(f32)
    inv_one = lax.rsqrt(jnp.mean(x_flat * x_flat, -1, keepdims=True) + EPS)
    unit_one = x_flat * inv_one
    normed_one = (unit_one * gain_attn).astype(bf16)
    rows_query = lax.all_gather(w_query, "grp", axis=0, tiled=True)
    rows_key = lax.all_gather(w_key, "grp", axis=0, tiled=True)
    rows_value = lax.all_gather(w_value, "grp", axis=0, tiled=True)
    rows_out = lax.all_gather(w_out, "grp", axis=0, tiled=True)
    columns = normed_one
    query_lin = matmul_f32(columns, rows_query)
    key_lin = matmul_f32(columns, rows_key)
    value_lin = matmul_f32(columns, rows_value)
    out_full = rows_out
    query_turned = rotate(
        query_lin.reshape(seq_count, local_rows, head_count, HD), cosine, sine_table
    ).astype(bf16)
    key_turned = rotate(
        key_lin.reshape(seq_count, local_rows, kv_heads, HD), cosine, sine_table
    ).astype(bf16)
    value_local = value_lin.astype(bf16).reshape(seq_count, local_rows, kv_width)
    key_all, value_all = (
        lax.all_gather(
            key_turned.reshape(seq_count, local_rows, kv_width), "grp", axis=1, tiled=True
        ),
        lax.all_gather(value_local, "grp", axis=1, tiled=True),
    )
    query_grouped = query_turned.reshape(seq_count, local_rows, kv_heads, group_size, HD)

    def block_keys(step_index):
        first_row = step_index * key_block
        key_rows = lax.dynamic_slice_in_dim(key_all, first_row, key_block, 1).reshape(
            seq_count, key_block, kv_heads, HD
        )
        value_rows = lax.dynamic_slice_in_dim(value_all, first_row, key_block, 1).reshape(
            seq_count, key_block, kv_heads, HD
        )
        block_places = lax.dynamic_slice_in_dim(key_places, first_row, key_block, 1)
        block_pieces = lax.dynamic_slice_in_dim(key_pieces, first_row, key_block, 1)
        allowed = (block_places[:, None, :] <= query_places[:, :, None]) | (
            query_pieces[:, :, None] != 0
        ) & (block_pieces[:, None, :] == query_pieces[:, :, None])
        return (key_rows, value_rows, allowed)

    def scores_of(key_rows, allowed):
        raw_scores = (
            jnp.einsum("sqkgd,snkd->skgqn", query_grouped, key_rows, preferred_element_type=f32)
            * score_scale
        )
        return jnp.where(allowed[:, None, None], raw_scores, -1e30)

    stat_shape = (seq_count, kv_heads, group_size, local_rows)

    def extent(step_index, state_now):
        running_max, running_sum = state_now
        key_rows, value_rows, allowed = block_keys(step_index)
        scores = scores_of(key_rows, allowed)
        new_max = jnp.maximum(running_max, jnp.max(scores, -1))
        running_sum = running_sum * jnp.exp(running_max - new_max) + jnp.sum(
            jnp.exp(scores - new_max[..., None]), -1
        )
        return (new_max, running_sum)

    running_max, running_sum = lax.fori_loop(
        0, blocks, extent, (jnp.full(stat_shape, -1e30, f32), jnp.zeros(stat_shape, f32))
    )
    log_total = running_max + jnp.log(running_sum)

    def weigh(step_index, accum):
        key_rows, value_rows, allowed = block_keys(step_index)
        probabilities = jnp.exp(scores_of(key_rows, allowed) - log_total[..., None]).astype(bf16)
        return accum + jnp.einsum(
            "skgqn,snkd->sqkgd", probabilities, value_rows, preferred_element_type=f32
        )

    mixed_heads = lax.fori_loop(
        0, blocks, weigh, jnp.zeros((seq_count, local_rows, kv_heads, group_size, HD), f32)
    )
    attended = mixed_heads.reshape(token_count, q_width).astype(bf16)
    residual_mid = x_flat + matmul_f32(attended, out_full)
    inv_two = lax.rsqrt(jnp.mean(residual_mid * residual_mid, -1, keepdims=True) + EPS)
    unit_two = residual_mid * inv_two
    normed_two = (unit_two * gain_ffn).astype(bf16)
    rows_gate = lax.all_gather(w_gate, "grp", axis=0, tiled=True)
    rows_up = lax.all_gather(w_up, "grp", axis=0, tiled=True)
    columns = normed_two
    gate_proj = matmul_f32(columns, rows_gate)
    up_proj = matmul_f32(columns, rows_up)
    sigmoid_gate = jax.nn.sigmoid(gate_proj)
    swish = gate_proj * sigmoid_gate
    hidden = (swish * up_proj).astype(bf16)
    columns = hidden
    ffn_out = matmul_f32(columns, lax.all_gather(w_down, "grp", axis=0, tiled=True))
    result = (residual_mid + ffn_out).astype(bf16).reshape(seq_count, local_rows, model_width)
    grad_out = cotangent.reshape(token_count, model_width)
    grad_flat = grad_out.astype(f32)
    grad_hidden = jnp.einsum(
        "td,fd->tf",
        grad_out,
        lax.all_gather(w_down, "grp", axis=0, tiled=True),
        preferred_element_type=f32,
    )
    grad_gate = (
        grad_hidden * up_proj * sigmoid_gate * (1.0 + gate_proj * (1.0 - sigmoid_gate))
    ).astype(bf16)
    grad_up = (grad_hidden * swish).astype(bf16)
    rows_gate = lax.all_gather(w_gate, "grp", axis=0, tiled=True)
    rows_up = lax.all_gather(w_up, "grp", axis=0, tiled=True)
    rows_out = lax.all_gather(w_out, "grp", axis=0, tiled=True)
    row_term = against_rows(grad_gate, rows_gate) + against_rows(grad_up, rows_up)
    grad_two = row_term
    grad_mid, gain_ffn_term = norm_back(grad_flat, grad_two, unit_two, inv_two, gain_ffn)
    grad_mid_low = grad_mid.astype(bf16)
    grad_attended = against_rows(grad_mid_low, rows_out).astype(bf16)
    grad_grouped = grad_attended.reshape(seq_count, local_rows, kv_heads, group_size, HD)

    def spread(step_index, accum):
        key_rows, value_rows, allowed = block_keys(step_index)
        probabilities = jnp.exp(scores_of(key_rows, allowed) - log_total[..., None])
        prob_grad = jnp.einsum(
            "sqkgd,snkd->skgqn", grad_grouped, value_rows, preferred_element_type=f32
        )
        return accum + jnp.sum(probabilities * prob_grad, -1)

    center = lax.fori_loop(0, blocks, spread, jnp.zeros(stat_shape, f32))

    def back_block(step_index, state_now):
        grad_query, grad_keys, grad_values = state_now
        key_rows, value_rows, allowed = block_keys(step_index)
        probabilities = jnp.exp(scores_of(key_rows, allowed) - log_total[..., None])
        prob_grad = jnp.einsum(
            "sqkgd,snkd->skgqn", grad_grouped, value_rows, preferred_element_type=f32
        )
        grad_scores = (probabilities * (prob_grad - center[..., None])).astype(bf16)
        grad_query = grad_query + score_scale * jnp.einsum(
            "skgqn,snkd->sqkgd", grad_scores, key_rows, preferred_element_type=f32
        )
        key_term = score_scale * jnp.einsum(
            "skgqn,sqkgd->snkd", grad_scores, query_grouped, preferred_element_type=f32
        )
        value_term = jnp.einsum(
            "skgqn,sqkgd->snkd",
            probabilities.astype(bf16),
            grad_grouped,
            preferred_element_type=f32,
        )
        first_row = step_index * key_block
        grad_keys = lax.dynamic_update_slice_in_dim(
            grad_keys, key_term.reshape(seq_count, key_block, kv_width), first_row, 1
        )
        grad_values = lax.dynamic_update_slice_in_dim(
            grad_values, value_term.reshape(seq_count, key_block, kv_width), first_row, 1
        )
        return (grad_query, grad_keys, grad_values)

    back_start = (
        jnp.zeros((seq_count, local_rows, kv_heads, group_size, HD), f32),
        jnp.zeros((seq_count, length, kv_width), f32),
        jnp.zeros((seq_count, length, kv_width), f32),
    )
    grad_query_turned, grad_keys_all, grad_values_all = lax.fori_loop(
        0, blocks, back_block, back_start
    )
    grad_keys_own, grad_values_own = (
        lax.psum_scatter(
            grad_keys_all.astype(jnp.bfloat16), "grp", scatter_dimension=1, tiled=True
        ).astype(jnp.float32),
        lax.psum_scatter(
            grad_values_all.astype(jnp.bfloat16), "grp", scatter_dimension=1, tiled=True
        ).astype(jnp.float32),
    )
    grad_query = (
        rotate_back(
            grad_query_turned.reshape(seq_count, local_rows, head_count, HD), cosine, sine_table
        )
        .astype(bf16)
        .reshape(token_count, q_width)
    )
    grad_key = (
        rotate_back(grad_keys_own.reshape(seq_count, local_rows, kv_heads, HD), cosine, sine_table)
        .astype(bf16)
        .reshape(token_count, kv_width)
    )
    grad_value = grad_values_own.astype(bf16).reshape(token_count, kv_width)
    rows_query = lax.all_gather(w_query, "grp", axis=0, tiled=True)
    rows_key = lax.all_gather(w_key, "grp", axis=0, tiled=True)
    rows_value = lax.all_gather(w_value, "grp", axis=0, tiled=True)
    row_term = (
        against_rows(grad_query, rows_query)
        + against_rows(grad_key, rows_key)
        + against_rows(grad_value, rows_value)
    )
    grad_input, gain_attn_term = norm_back(grad_mid, row_term, unit_one, inv_one, gain_attn)
    grad_x = grad_input.astype(bf16).reshape(seq_count, local_rows, model_width)
    token_grads = (grad_query, grad_key, grad_value, grad_mid_low, grad_gate, grad_up, grad_out)
    grad_shard = lax.psum_scatter(
        seven_terms(
            normed_one,
            attended,
            normed_two,
            hidden,
            token_grads,
            rows_here * lax.axis_size("grp"),
            hidden_ratio,
            model_width,
        ).astype(jnp.bfloat16),
        "grp",
        scatter_dimension=0,
        tiled=True,
    ).astype(jnp.float32)
    grad_shard = lax.psum(grad_shard.astype(jnp.bfloat16), "rep").astype(jnp.float32)
    gain_total = lax.psum(jnp.stack([gain_attn_term, gain_ffn_term]), ("grp", "rep"))
    own_gains = lax.dynamic_slice_in_dim(gain_total, own_index * rows_here, rows_here, 1)
    widths = [q_width, kv_width, kv_width, model_width, hidden_width, hidden_width, hidden_width]
    offsets = [0]
    for column_count in widths:
        offsets.append(offsets[-1] + column_count)
    split_grads = [
        grad_shard[:, offsets[number] : offsets[number + 1]] for number in range(len(widths))
    ]
    grad_down = split_grads[6].reshape(rows_here * hidden_ratio, model_width)
    return (
        result,
        grad_x,
        split_grads[0],
        split_grads[1],
        split_grads[2],
        split_grads[3],
        split_grads[4],
        split_grads[5],
        grad_down,
        own_gains[0],
        own_gains[1],
    )


def solution(mesh):
    in_specs = (
        P("rep", "grp", None),
        P("rep", "grp", None),
        P("rep", None),
        P("rep", None),
        P("grp", None),
        P("grp", None),
        P("grp", None),
        P("grp", None),
        P("grp", None),
        P("grp", None),
        P("grp", None),
        P(),
        P(),
    )
    out_specs = (
        P("rep", "grp", None),
        P("rep", "grp", None),
        P("grp", None),
        P("grp", None),
        P("grp", None),
        P("grp", None),
        P("grp", None),
        P("grp", None),
        P("grp", None),
        P("grp"),
        P("grp"),
    )
    return jax.shard_map(
        on_device, mesh=mesh, in_specs=in_specs, out_specs=out_specs, check_vma=False
    )
```

profile of v0, /device:TPU:0, one launch (start us, length us, event | category | flops | bytes accessed | tf_op | source)
XLA Modules:
  0.0 2414.0 jit_solution(6027990927874666065)
XLA Ops:
  10.3 39.1 %all-gather.12.cloned.1.call-done = bf16[2048,1024]{1,0:T(8,128)(2,1)} async-done(((bf16[256,1024]{1,0:T(8,128)(2,1)}), bf16[2048,1024]{1,0:T(8,128)(2,1)}) %all-gather.12.cloned.1.call-update) | async-done | bytes 4194320 | tf_op jit(solution)/shard_map/all_gather | solution.py:129
  59.7 5.5 select_select_fusion
  65.2 11.8 gather_fusion
  77.7 10.3 all-gather.14.cloned.1.call-done
  98.6 28.6 %all-gather.26.cloned.1.call-done = bf16[2048,1024]{1,0:T(8,128)(2,1)} async-done(((bf16[256,1024]{1,0:T(8,128)(2,1)}), bf16[2048,1024]{1,0:T(8,128)(2,1)}) %all-gather.26.cloned.1.call-update) | async-done | bytes 4194320 | tf_op jit(solution)/shard_map/all_gather | solution.py:147
  127.2 6.4 copy.139
  133.6 32.6 %all-gather.28.cloned.1.call-done = bf16[2048,1024]{1,0:T(8,128)(2,1)} async-done(((bf16[256,1024]{1,0:T(8,128)(2,1)}), bf16[2048,1024]{1,0:T(8,128)(2,1)}) %all-gather.28.cloned.1.call-update) | async-done | bytes 4194320 | tf_op jit(solution)/shard_map/all_gather | solution.py:144
  166.3 6.5 copy.140
  172.8 49.6 %all-gather.16.cloned.1.call-done = bf16[2048,2048]{1,0:T(8,128)(2,1)} async-done(((bf16[256,2048]{1,0:T(8,128)(2,1)}), bf16[2048,2048]{1,0:T(8,128)(2,1)}) %all-gather.16.cloned.1.call-update) | async-done | bytes 8388624 | tf_op jit(solution)/shard_map/all_gather | solution.py:127
  222.5 7.1 fusion.95
  231.1 47.8 %while.62 = (s32[]{:T(128)}, f32[1,8,2,256]{3,2,1,0:T(2,128)S(1)}, f32[1,8,2,256]{3,2,1,0:T(2,128)S(1)}, s32[1,2048]{1,0:T(1,128)S(1)}, s32[1,256]{1,0:T(1,128)S...) while((s32[]{:T(128)}, f32[1,8,2,256]{3,2,1,0:T(2,128)S(1)}, ...), condition=%wide.region_4.5_spmd.clone, body=%wide.region_1.4_spmd.clone.sunk | while | flops 552096000 | bytes 21593796 | solution.py:185
  249.5 5.8 exponential_reduce_fusion.2
  278.9 36.6 %while.63 = (s32[]{:T(128)}, f32[1,256,8,2,128]{1,4,3,2,0:T(8,128)}, bf16[1,2048,1024]{1,2,0:T(8,128)(2,1)}, s32[1,2048]{1,0:T(1,128)S(1)}, s32[1,256]{1,0:T(1,1...) while((s32[]{:T(128)}, ...), condition=%wide.region_6.7_spmd.clone, body=%wide.region_5.6_spmd.clone.sunk | while | flops 1083703552 | bytes 11828941 | solution.py:197
  290.6 6.6 bitcast_add_fusion.10
  300.1 6.1 bitcast_add_fusion.10
  309.1 6.1 bitcast_add_fusion.10
  317.3 6.2 multiply_reduce_fusion.2
  325.1 116.2 %all-gather.20.cloned.1.call-done = bf16[2048,8192]{1,0:T(8,128)(2,1)} async-done(((bf16[256,8192]{1,0:T(8,128)(2,1)}), bf16[2048,8192]{1,0:T(8,128)(2,1)}) %all-gather.20.cloned.1.call-update) | async-done | bytes 33554448 | tf_op jit(solution)/shard_map/all_gather | solution.py:205
  441.3 20.2 fusion.109
  461.5 142.5 %all-gather.22.cloned.1.call-done = bf16[2048,8192]{1,0:T(8,128)(2,1)} async-done(((bf16[256,8192]{1,0:T(8,128)(2,1)}), bf16[2048,8192]{1,0:T(8,128)(2,1)}) %all-gather.22.cloned.1.call-update) | async-done | bytes 33554448 | tf_op jit(solution)/shard_map/all_gather | solution.py:206
  604.0 20.2 fusion.110
  624.2 142.5 %all-gather.24.cloned.1.call-done = bf16[8192,2048]{1,0:T(8,128)(2,1)} async-done(((bf16[1024,2048]{1,0:T(8,128)(2,1)}), bf16[8192,2048]{1,0:T(8,128)(2,1)}) %all-gather.24.cloned.1.call-update) | async-done | bytes 33554448 | tf_op jit(solution)/shard_map/all_gather | solution.py:214
  766.8 23.2 multiply_convert_fusion
  790.0 17.0 fusion.111
  807.0 18.8 multiply_reduce_fusion
  829.6 5.8 convolution_convert_fusion.5
  838.6 24.8 %while.64 = (s32[]{:T(128)}, f32[1,8,2,256]{3,2,1,0:T(2,128)S(1)}, s32[1,2048]{1,0:T(1,128)S(1)}, s32[1,256]{1,0:T(1,128)S(1)}, s32[1,256]{1,0:T(1,128)S(1)}, /*...) while((s32[]{:T(128)}, f32[1,8,2,256]{3,2,1,0:T(2,128)S(1)}, ...), condition=%wide.region_11.12_spmd.clone, body=%wide.region_9.11_spmd.clone.sunk | while | flops 1084756224 | bytes 25525972 | solution.py:246
  868.5 89.1 %while.65 = (s32[]{:T(128)}, f32[1,256,8,2,128]{1,4,3,2,0:T(8,128)S(1)}, bf16[1,2048,1024]{2,1,0:T(8,128)(2,1)}, bf16[1,2048,1024]{1,2,0:T(8,128)(2,1)}, bf16[1,...) while((s32[]{:T(128)}, ...), condition=%wide.region_13.14_spmd.clone, body=%wide.region_12.13_spmd.clone.sunk | while | flops 2708472064 | bytes 87490392 | solution.py:282
  961.3 6.2 convolution_convert_fusion.1
  967.5 12.5 copy.152
  980.1 7.1 convolution_convert_fusion.2
  987.2 12.3 copy.155
  999.5 16.6 convolution_convert_fusion
  1016.1 55.5 %reshape.1478 = bf16[2048,8192]{1,0:T(8,128)(2,1)} reshape(bf16[8192,2048]{1,0:T(8,128)(2,1)} %convolution_convert_fusion) | data formatting | bytes 67108864 | tf_op jit(solution)/shard_map/reshape | solution.py:76
  1071.6 8.4 constant_dynamic-update-slice_fusion.6
  1086.8 6.4 copy.153
  1097.6 6.6 copy.154
  1111.6 8.4 constant_dynamic-update-slice_fusion.3
  1120.1 16.1 convert_dynamic-update-slice_fusion.1
  1136.2 14.1 convert_dynamic-update-slice_fusion
  1150.3 23.0 constant_dynamic-update-slice_fusion.2
  1173.3 674.1 %reduce-scatter.10.cloned.1.call-done = bf16[256,30720]{1,0:T(8,128)(2,1)} async-done(((bf16[2048,30720]{1,0:T(8,128)(2,1)}), bf16[256,30720]{1,0:T(8,128)(2,1)}) %reduce-scatter.10.cloned.1.call-update) | async-done | bytes 15728656
  1850.9 7.3 fusion.112
  1858.2 16.7 fusion.56
  1882.7 51.4 %psum.15 = f32[2,2048]{1,0:T(2,128)S(1)} all-reduce(f32[2,2048]{1,0:T(2,128)S(1)} %pad_maximum_fusion.3), channel_id=1, replica_groups=mesh['grp'=8,'rep'=4] {'grp','rep'}, use_global_device_ids=true, to_apply=%region_21.22 | all-reduce | flops 4096 | bytes 32768 | tf_op jit(solution)/shard_map/psum | solution.py:333
  1938.0 440.7 %all-reduce.3.cloned.1.call-done = bf16[256,30720]{1,0:T(8,128)(2,1)} async-done(((bf16[256,30720]{1,0:T(8,128)(2,1)}), bf16[256,30720]{1,0:T(8,128)(2,1)}) %all-reduce.3.cloned.1.call-update) | async-done | bytes 15728656 | tf_op jit(solution)/shard_map/psum | solution.py:332
  2378.7 11.7 fusion.102
  2390.4 9.8 reshape.1479
  (344 shorter events, 257.4 us)
Async XLA Ops:
  7.2 58.0 %copy-start = (s32[1,2048]{1,0:T(1,128)S(1)}, s32[1,2048]{1,0:T(1,128)}, u32[]{:S(2)}) copy-start(s32[1,2048]{1,0:T(1,128)} %param.24) | copy-start | bytes 24580
  7.2 42.2 %all-gather.12.cloned.1.call-start = ((), (), s32[]{:S(2)}) async-start(), calls=%async_computation.3 | async-start | bytes 4718592 | tf_op jit(solution)/shard_map/all_gather | solution.py:129
  7.9 80.1 %all-gather.14.cloned.1.call-start = ((), (), s32[]{:S(2)}) async-start(), calls=%async_computation.4 | async-start | bytes 4718592 | tf_op jit(solution)/shard_map/all_gather | solution.py:128
  8.7 118.5 %all-gather.26.cloned.1.call-start = ((), (), s32[]{:S(2)}) async-start(), calls=%async_computation.13 | async-start | bytes 4718592 | tf_op jit(solution)/shard_map/all_gather | solution.py:147
  10.2 44.2 %copy-start.41 = (s32[1,16]{1,0:T(1,128)S(1)}, s32[1,16]{1,0:T(1,128)}, u32[]{:S(2)}) copy-start(s32[1,16]{1,0:T(1,128)} %param.23) | copy-start | bytes 196
  10.3 212.2 %copy-start.42 = (f32[256]{0:T(256)}, f32[256]{0:T(256)S(1)}, u32[]{:S(2)}) copy-start(f32[256]{0:T(256)S(1)} %add_rsqrt_fusion.1) | copy-start | bytes 3076
  54.0 112.3 %all-gather.28.cloned.1.call-start = ((), (), s32[]{:S(2)}) async-start(), calls=%async_computation.14 | async-start | bytes 4718592 | tf_op jit(solution)/shard_map/all_gather | solution.py:144
  65.2 22.8 copy-start.6
  65.2 22.8 copy-start.38
  77.4 152.3 %copy-start.26 = (f32[256,128]{0,1:T(8,128)}, f32[256,128]{0,1:T(8,128)S(1)}, u32[]{:S(2)}) copy-start(f32[256,128]{0,1:T(8,128)S(1)} %get-tuple-element.1233) | copy-start | bytes 393220
  77.4 152.3 %copy-start.29 = (f32[256,128]{0,1:T(8,128)}, f32[256,128]{0,1:T(8,128)S(1)}, u32[]{:S(2)}) copy-start(f32[256,128]{0,1:T(8,128)S(1)} %get-tuple-element.1234) | copy-start | bytes 393220
  77.5 14.9 copy-start.33
  77.7 14.8 copy-start.31
  94.9 127.6 %all-gather.16.cloned.1.call-start = ((), (), s32[]{:S(2)}) async-start(), calls=%async_computation.5 | async-start | bytes 9437184 | tf_op jit(solution)/shard_map/all_gather | solution.py:127
  95.5 221.8 %all-gather.18.cloned.1.call-start = ((), (), s32[]{:S(2)}) async-start(), calls=%async_computation.6 | async-start | bytes 9437184 | tf_op jit(solution)/shard_map/all_gather | solution.py:130
  96.0 345.3 %all-gather.20.cloned.1.call-start = ((), (), s32[]{:S(2)}) async-start(), calls=%async_computation.7 | async-start | bytes 37748736 | tf_op jit(solution)/shard_map/all_gather | solution.py:205
  96.8 507.2 %all-gather.22.cloned.1.call-start = ((), (), s32[]{:S(2)}) async-start(), calls=%async_computation.8 | async-start | bytes 37748736 | tf_op jit(solution)/shard_map/all_gather | solution.py:206
  97.5 669.2 %all-gather.24.cloned.1.call-start = ((), (), s32[]{:S(2)}) async-start(), calls=%async_computation.9 | async-start | bytes 37748736 | tf_op jit(solution)/shard_map/all_gather | solution.py:214
  98.3 981.7 %reduce-scatter.6.cloned.1.call-start = ((), (), s32[]{:S(2)}) async-start(), calls=%async_computation.10 | async-start | bytes 4718592 | tf_op jit(solution)/shard_map/reduce_scatter | solution.py:286
  317.3 6.3 copy-start.17
  317.3 7.6 copy-start.44
  325.1 278.9 %copy-start.35 = (bf16[256,2048]{1,0:T(8,128)(2,1)}, bf16[256,2048]{1,0:T(8,128)(2,1)S(1)}, u32[]{:S(2)}) copy-start(bf16[256,2048]{1,0:T(8,128)(2,1)S(1)} %multiply_convert_fusion.3) | copy-start | bytes 3145732
  461.5 305.2 %copy-start.21 = (bf16[1,256,2048]{2,1,0:T(8,128)(2,1)S(1)}, bf16[1,256,2048]{2,1,0:T(8,128)(2,1)}, u32[]{:S(2)}) copy-start(bf16[1,256,2048]{2,1,0:T(8,128)(2,1)} %param.22) | copy-start | bytes 3145732
  789.9 17.0 copy-start.14
  863.4 5.1 copy-start.3
  882.0 3.7 copy-start.9
  904.3 3.4 copy-start.2
  904.3 3.7 copy-start.9
  926.6 3.4 copy-start.2
  926.6 3.7 copy-start.9
  948.8 3.7 copy-start.9
  957.6 135.6 %reduce-scatter.8.cloned.1.call-start = ((), (), s32[]{:S(2)}) async-start(), calls=%async_computation.11 | async-start | bytes 4718592 | tf_op jit(solution)/shard_map/reduce_scatter | solution.py:289
  958.4 889.1 %reduce-scatter.10.cloned.1.call-start = ((), (), s32[]{:S(2)}) async-start(), calls=%async_computation.15 | async-start | bytes 141557760
  967.5 12.6 copy-start.11
  987.2 12.3 copy-start.22
  1071.6 9.8 copy-start.34
  1104.3 4.9 copy-start.16
  1111.6 8.4 copy-start.36
  1120.1 16.1 copy-start.46
  1173.3 1205.4 %all-reduce.3.cloned.1.call-start = ((), (), s32[]{:S(2)}) async-start(), calls=%async_computation.12 | async-start | bytes 31457280 | tf_op jit(solution)/shard_map/psum | solution.py:332
  1850.9 7.3 copy-start.15
  1850.9 7.3 copy-start.20
  1858.2 16.7 copy-start.19
  1858.2 16.7 copy-start.24
  1875.0 4.6 copy-start.23
  1875.0 4.6 copy-start.25
  1879.6 55.1 %copy-start.12 = (f32[256,2048]{1,0:T(8,128)S(1)}, f32[256,2048]{1,0:T(8,128)}, u32[]{:S(2)}) copy-start(f32[256,2048]{1,0:T(8,128)} %copy-done.10) | copy-start | bytes 6291460
  2400.2 6.9 copy-start.1
  (21 other events, 43.9 us)
Sparse Core Ops, SparseCore 0:
  9.9 39.4 all-gather.11
  51.3 36.7 all-gather.13
  90.5 36.7 all-gather.25
  129.5 36.7 all-gather.27
  168.0 54.3 all-gather.15
  224.2 54.3 all-gather.17
  280.5 160.7 all-gather.19
  443.2 160.7 all-gather.21
  605.9 160.7 all-gather.23
  957.7 51.3 reduce-scatter.5
  1012.8 51.3 reduce-scatter.7
  1173.4 673.9 reduce-scatter.9
  1850.0 528.6 all-reduce.2
where the time goes:
time: 2420 us; the launch traced here: 2410 us
  waiting for transfers between devices  1680 us (69%)
  matrix products  347 us (14%)
  local copies, waits for them, and re-layouts  262 us (11%)
  other arithmetic  54.5 us (2%)
  blocking collectives  51.4 us (2%)
    unnamed x14, waiting for transfers between devices  679 us
    psum x1, waiting for transfers between devices, on_device(): lax.psum(grad_shard.astype(jnp.bfloat16), 'rep').astype(jnp.float32)  441 us
    all_gather x1, waiting for transfers between devices, on_device(): lax.all_gather(w_down, 'grp', axis=0, tiled=True)  143 us
    all_gather x1, waiting for transfers between devices, on_device(): rows_up = lax.all_gather(w_up, 'grp', axis=0, tiled=True)  143 us
    all_gather x1, waiting for transfers between devices, on_device(): rows_gate = lax.all_gather(w_gate, 'grp', axis=0, tiled=True)  116 us
    dot_general x6, matrix products, matmul_f32(): return jnp.dot(first, second, preferred_element_type=jnp.float32)  71.5 us
    dot_general x7, matrix products, over_tokens(): jnp.einsum('tr,tc->rc', first, second, preferred_element_type=jnp.float32)  67.9 us
    dot_general x6, matrix products, against_rows(): jnp.einsum('tc,rc->tr', first, second, preferred_element_type=jnp.float32)  56.5 us
  transfers between devices with their start and end apart: 13, of which 10 were waited for; matrix products, arithmetic and copies ran while one was open for 15% of the time, Pallas kernels for 0%

commit v1 on v0

v1 whole, which is shorter than its diff:
```python
import functools

import jax
import jax.numpy as jnp
from jax import lax
from jax.experimental import pallas as pl
from jax.experimental.pallas import tpu as pltpu
from jax.sharding import PartitionSpec as P

HD = 128
EPS = 1e-05
ROPE_BASE = 1000000.0
SCORE_SCALE = HD**-0.5
LOG2E = 1.4426950408889634
TO_EXP2 = SCORE_SCALE * LOG2E
NEG = -1e30

f32 = jnp.float32
bf16 = jnp.bfloat16


def matmul_f32(first, second):
    return jnp.dot(first, second, preferred_element_type=f32)


def against_rows(first, second):
    return lax.dot_general(first, second, (((1,), (1,)), ((), ())), preferred_element_type=f32)


def over_tokens(first, second):
    return lax.dot_general(first, second, (((0,), (0,)), ((), ())), preferred_element_type=f32)


def turn_tables(length):
    half_size = HD // 2
    inverse = ROPE_BASE ** (-(jnp.arange(half_size, dtype=f32) * 2.0) / HD)
    angles = jnp.arange(length, dtype=jnp.int32).astype(f32)[:, None] * inverse
    cosine, sine = jnp.cos(angles), jnp.sin(angles)
    return jnp.concatenate([cosine, cosine], -1), jnp.concatenate([-sine, sine], -1)


def norm_back(upstream, grad_normed, unit_rows, inv_root, gain):
    scaled = grad_normed * gain
    center_term = jnp.mean(scaled * unit_rows, -1, keepdims=True)
    return (
        upstream + inv_root * (scaled - unit_rows * center_term),
        jnp.sum(grad_normed * unit_rows, 0),
    )


def fold_lanes(values, op):
    out = values[:, :HD]
    for at in range(HD, values.shape[1], HD):
        out = op(out, values[:, at : at + HD])
    return out


def as_row(column):
    return jnp.broadcast_to(column, (column.shape[0], HD)).T[0:1, :]


def attend_kernel(
    heads, cuts, block,
    order_ref, qkv_ref, cos_ref, sin_ref, piece_ref, piece_col_ref,
    out_ref, q_ref, k_ref, v_ref, lse_ref,
    scores, placed,
):
    length = qkv_ref.shape[0]
    cut = length // cuts
    blocks = length // block

    def place_cut(r, _):
        src = pl.ds(pl.multiple_of(r * cut, cut), cut)
        dst = pl.ds(pl.multiple_of(order_ref[0, r] * cut, cut), cut)
        cosine, sine = cos_ref[dst, :], sin_ref[dst, :]
        for h in range(heads + 1):
            part = qkv_ref[src, h * HD : (h + 1) * HD]
            turned = (part * cosine + pltpu.roll(part, HD // 2, 1) * sine).astype(bf16)
            if h < heads:
                q_ref[h, dst, :] = turned
            else:
                k_ref[dst, :] = turned
        v_ref[dst, :] = qkv_ref[src, (heads + 1) * HD :].astype(bf16)
        return 0

    lax.fori_loop(0, cuts, place_cut, 0)

    def one_block(i, _):
        rows = pl.ds(pl.multiple_of(i * block, block), block)
        query = q_ref[:, rows, :].reshape(heads * block, HD)

        def score(j, high):
            cols = pl.ds(pl.multiple_of(j * block, block), block)
            tile = against_rows(query, k_ref[cols, :])
            scores[j] = tile
            return jnp.maximum(high, fold_lanes(tile, jnp.maximum))

        high = lax.fori_loop(0, i, score, jnp.full((heads * block, HD), NEG, f32))
        tile = against_rows(query, k_ref[rows, :])
        q_at = lax.broadcasted_iota(jnp.int32, (block, block), 0)
        k_at = lax.broadcasted_iota(jnp.int32, (block, block), 1)
        q_piece, k_piece = piece_col_ref[rows, 0:1], piece_ref[0:1, rows]
        allowed = (k_at <= q_at) | ((q_piece != 0) & (q_piece == k_piece))
        tile = jnp.concatenate(
            [jnp.where(allowed, tile[h * block : (h + 1) * block], NEG) for h in range(heads)], 0
        )
        scores[i] = tile
        high = jnp.max(jnp.maximum(high, fold_lanes(tile, jnp.maximum)), 1, keepdims=True)

        def weigh(j, state):
            total, mixed = state
            cols = pl.ds(pl.multiple_of(j * block, block), block)
            prob = jnp.exp2((scores[j] - high) * TO_EXP2)
            total = total + fold_lanes(prob, jnp.add)
            return total, mixed + matmul_f32(prob.astype(bf16), v_ref[cols, :])

        zero = jnp.zeros((heads * block, HD), f32)
        total, mixed = lax.fori_loop(0, i + 1, weigh, (zero, zero))
        total = jnp.sum(total, 1, keepdims=True)
        mixed = (mixed / total).astype(bf16)
        log_total = high * TO_EXP2 + jnp.log2(total)
        for h in range(heads):
            placed[rows, h * HD : (h + 1) * HD] = mixed[h * block : (h + 1) * block]
            lse_ref[h : h + 1, rows] = as_row(log_total[h * block : (h + 1) * block])
        return 0

    lax.fori_loop(0, blocks, one_block, 0)

    def store_cut(r, _):
        dst = pl.ds(pl.multiple_of(r * cut, cut), cut)
        src = pl.ds(pl.multiple_of(order_ref[0, r] * cut, cut), cut)
        out_ref[dst, :] = placed[src, :]
        return 0

    lax.fori_loop(0, cuts, store_cut, 0)


def vmem_specs(count):
    return [pl.BlockSpec(memory_space=pltpu.VMEM)] * count


def attend(order, qkv, cosine, sine, piece, piece_col, heads):
    length = qkv.shape[0]
    block = min(512, length)
    return pl.pallas_call(
        functools.partial(attend_kernel, heads, order.shape[1], block),
        out_shape=(
            jax.ShapeDtypeStruct((length, heads * HD), bf16),
            jax.ShapeDtypeStruct((heads, length, HD), bf16),
            jax.ShapeDtypeStruct((length, HD), bf16),
            jax.ShapeDtypeStruct((length, HD), bf16),
            jax.ShapeDtypeStruct((heads, length), f32),
        ),
        in_specs=[pl.BlockSpec(memory_space=pltpu.SMEM)] + vmem_specs(5),
        out_specs=tuple(vmem_specs(5)),
        scratch_shapes=[
            pltpu.VMEM((length // block, heads * block, block), f32),
            pltpu.VMEM((length, heads * HD), bf16),
        ],
        compiler_params=pltpu.CompilerParams(vmem_limit_bytes=48 * 2**20),
        cost_estimate=pl.CostEstimate(
            flops=3 * heads * length * length * HD, bytes_accessed=10 * length * HD * heads * 4,
            transcendentals=heads * length * length // 2,
        ),
    )(order, qkv, cosine, sine, piece, piece_col)


def attend_back_kernel(
    heads, cuts, block,
    order_ref, grad_ref, out_ref, q_ref, k_ref, v_ref, lse_ref, cos_ref, sin_ref,
    piece_ref, piece_col_ref,
    grad_qkv_ref,
    grads, centers, grad_q, placed,
):
    length = grad_ref.shape[0]
    cut = length // cuts
    blocks = length // block

    def place_cut(r, _):
        src = pl.ds(pl.multiple_of(r * cut, cut), cut)
        dst = pl.ds(pl.multiple_of(order_ref[0, r] * cut, cut), cut)
        for h in range(heads):
            grad = grad_ref[src, h * HD : (h + 1) * HD].astype(bf16)
            grads[h, dst, :] = grad
            product = grad.astype(f32) * out_ref[src, h * HD : (h + 1) * HD].astype(f32)
            centers[h, dst, :] = jnp.broadcast_to(
                jnp.sum(product, 1, keepdims=True), (cut, HD)
            )
        return 0

    lax.fori_loop(0, cuts, place_cut, 0)
    grad_q[...] = jnp.zeros_like(grad_q)

    def key_block(j, _):
        cols = pl.ds(pl.multiple_of(j * block, block), block)
        key, value = k_ref[cols, :], v_ref[cols, :]

        def one(i, state, diagonal):
            grad_key, grad_value = state
            rows = pl.ds(pl.multiple_of(i * block, block), block)
            for h in range(heads):
                query, grad = q_ref[h, rows, :], grads[h, rows, :]
                log_total = lse_ref[h : h + 1, rows]
                center = centers[h, rows, :].T[0:1, :]
                prob = jnp.exp2(against_rows(key, query) * TO_EXP2 - log_total)
                if diagonal:
                    k_at = lax.broadcasted_iota(jnp.int32, (block, block), 0)
                    q_at = lax.broadcasted_iota(jnp.int32, (block, block), 1)
                    k_piece, q_piece = piece_col_ref[cols, 0:1], piece_ref[0:1, cols]
                    allowed = (k_at <= q_at) | ((q_piece != 0) & (q_piece == k_piece))
                    prob = jnp.where(allowed, prob, 0.0)
                grad_prob = against_rows(value, grad)
                grad_score = (prob * (grad_prob - center)).astype(bf16)
                grad_value = grad_value + matmul_f32(prob.astype(bf16), grad)
                grad_key = grad_key + matmul_f32(grad_score, query)
                grad_q[h, rows, :] += over_tokens(grad_score, key)
            return grad_key, grad_value

        zero = jnp.zeros((block, HD), f32)
        state = one(j, (zero, zero), True)
        grad_key, grad_value = lax.fori_loop(
            j + 1, blocks, functools.partial(one, diagonal=False), state
        )
        grad_key = grad_key * SCORE_SCALE
        grad_key = grad_key * cos_ref[cols, :] - pltpu.roll(grad_key, HD // 2, 1) * sin_ref[cols, :]
        placed[cols, heads * HD : (heads + 1) * HD] = grad_key.astype(bf16)
        placed[cols, (heads + 1) * HD :] = grad_value.astype(bf16)
        return 0

    lax.fori_loop(0, blocks, key_block, 0)

    def store_cut(r, _):
        dst = pl.ds(pl.multiple_of(r * cut, cut), cut)
        src = pl.ds(pl.multiple_of(order_ref[0, r] * cut, cut), cut)
        for h in range(heads):
            grad = grad_q[h, src, :] * SCORE_SCALE
            grad = grad * cos_ref[src, :] - pltpu.roll(grad, HD // 2, 1) * sin_ref[src, :]
            grad_qkv_ref[dst, h * HD : (h + 1) * HD] = grad.astype(bf16)
        grad_qkv_ref[dst, heads * HD :] = placed[src, heads * HD :]
        return 0

    lax.fori_loop(0, cuts, store_cut, 0)


def attend_back(order, grad, out, query, key, value, lse, cosine, sine, piece, piece_col, heads):
    length = grad.shape[0]
    block = min(512, length)
    return pl.pallas_call(
        functools.partial(attend_back_kernel, heads, order.shape[1], block),
        out_shape=jax.ShapeDtypeStruct((length, (heads + 2) * HD), bf16),
        in_specs=[pl.BlockSpec(memory_space=pltpu.SMEM)] + vmem_specs(10),
        out_specs=pl.BlockSpec(memory_space=pltpu.VMEM),
        scratch_shapes=[
            pltpu.VMEM((heads, length, HD), bf16),
            pltpu.VMEM((heads, length, HD), f32),
            pltpu.VMEM((heads, length, HD), f32),
            pltpu.VMEM((length, (heads + 2) * HD), bf16),
        ],
        compiler_params=pltpu.CompilerParams(vmem_limit_bytes=48 * 2**20),
        cost_estimate=pl.CostEstimate(
            flops=8 * heads * length * length * HD, bytes_accessed=14 * length * HD * heads * 4,
            transcendentals=heads * length * length // 2,
        ),
    )(order, grad, out, query, key, value, lse, cosine, sine, piece, piece_col)


def sum_over_sequences(term, reps):
    if reps != 4:
        return lax.psum(term, "rep").astype(f32)
    rank = lax.axis_index("rep")
    inward = lax.ppermute(term, "rep", [(0, 1), (3, 2)])
    pair = (term.astype(f32) + inward.astype(f32)).astype(bf16)
    other = lax.ppermute(pair, "rep", [(1, 2), (2, 1)])
    total = (pair.astype(f32) + other.astype(f32)).astype(bf16)
    outward = lax.ppermute(total, "rep", [(1, 0), (2, 3)])
    return jnp.where((rank == 0) | (rank == 3), outward, total).astype(f32)


def on_device(
    layer_input,
    cotangent,
    cut_order,
    piece_ids,
    w_query,
    w_key,
    w_value,
    w_out,
    w_gate,
    w_up,
    w_down,
    gain_attn,
    gain_ffn,
):
    groups = lax.axis_size("grp")
    reps = lax.axis_size("rep")
    own_index = lax.axis_index("grp")
    _, local_rows, model_width = layer_input.shape
    length = piece_ids.shape[1]
    rows_here = w_query.shape[0]
    q_width = w_query.shape[1]
    kv_heads = w_key.shape[1] // HD
    heads = q_width // HD // groups
    copies = groups // kv_heads
    hidden_here = w_down.shape[0]
    piece_col = jnp.broadcast_to(piece_ids.reshape(length, 1), (length, HD))
    cosine, sine = turn_tables(length)

    def gather(rows):
        return lax.all_gather(rows, "grp", axis=0, tiled=True)

    def scatter(terms):
        return lax.psum_scatter(terms.astype(bf16), "grp", scatter_dimension=0, tiled=True)

    def to_columns(parts):
        return lax.all_to_all(parts, "grp", 1, 0, tiled=True).reshape(-1, parts.shape[-1])

    def per_group(weight):
        return weight.reshape(rows_here, groups, -1)

    def per_kv_head(weight):
        return jnp.repeat(weight.reshape(rows_here, kv_heads, HD), copies, axis=1)

    x_flat = layer_input.reshape(local_rows, model_width).astype(f32)
    inv_one = lax.rsqrt(jnp.mean(x_flat * x_flat, -1, keepdims=True) + EPS)
    unit_one = x_flat * inv_one
    normed_one = gather((unit_one * gain_attn).astype(bf16))
    cols_qkv = to_columns(
        jnp.concatenate([per_group(w_query), per_kv_head(w_key), per_kv_head(w_value)], -1)
    )
    qkv = matmul_f32(normed_one, cols_qkv)
    attended, query, key, value, lse = attend(
        cut_order, qkv, cosine, sine, piece_ids, piece_col, heads
    )
    cols_gate_up = to_columns(jnp.concatenate([per_group(w_gate), per_group(w_up)], -1))
    mid = x_flat + scatter(matmul_f32(attended, w_out)).astype(f32)
    inv_two = lax.rsqrt(jnp.mean(mid * mid, -1, keepdims=True) + EPS)
    unit_two = mid * inv_two
    normed_two = gather((unit_two * gain_ffn).astype(bf16))
    grad_out = cotangent.reshape(local_rows, model_width)
    grad_all = gather(grad_out)
    gate_up = matmul_f32(normed_two, cols_gate_up)
    gate_proj, up_proj = gate_up[:, :hidden_here], gate_up[:, hidden_here:]
    sigmoid_gate = jax.nn.sigmoid(gate_proj)
    swish = gate_proj * sigmoid_gate
    hidden = (swish * up_proj).astype(bf16)
    down_term = sum_over_sequences(over_tokens(hidden, grad_all).astype(bf16), reps)
    grad_hidden = against_rows(grad_all, w_down)
    grad_gate = (
        grad_hidden * up_proj * sigmoid_gate * (1.0 + gate_proj * (1.0 - sigmoid_gate))
    ).astype(bf16)
    grad_up = (grad_hidden * swish).astype(bf16)
    grad_gate_up = jnp.concatenate([grad_gate, grad_up], 1)
    grad_two = scatter(against_rows(grad_gate_up, cols_gate_up)).astype(f32)
    grad_mid, gain_ffn_term = norm_back(
        grad_out.astype(f32), grad_two, unit_two, inv_two, gain_ffn
    )
    grad_mid_low = gather(grad_mid.astype(bf16))
    grad_attended = against_rows(grad_mid_low, w_out).astype(bf16)

    def to_rows(term):
        return lax.all_to_all(
            term.astype(bf16).reshape(groups, rows_here, -1), "grp", 0, 0, tiled=True
        )

    gate_up_term = sum_over_sequences(to_rows(over_tokens(normed_two, grad_gate_up)), reps)
    result = (mid + scatter(matmul_f32(hidden, w_down)).astype(f32)).astype(bf16)
    grad_qkv = attend_back(
        cut_order, grad_attended, attended, query, key, value, lse, cosine, sine,
        piece_ids, piece_col, heads,
    )
    out_term = sum_over_sequences(over_tokens(attended, grad_mid_low).astype(bf16), reps)
    qkv_term = sum_over_sequences(to_rows(over_tokens(normed_one, grad_qkv)), reps)
    grad_one = scatter(against_rows(grad_qkv, cols_qkv)).astype(f32)
    grad_input, gain_attn_term = norm_back(grad_mid, grad_one, unit_one, inv_one, gain_attn)
    gain_total = lax.psum(jnp.stack([gain_attn_term, gain_ffn_term]), ("grp", "rep"))
    own_gains = lax.dynamic_slice_in_dim(gain_total, own_index * rows_here, rows_here, 1)

    def whole_rows(term):
        return jnp.moveaxis(term, 0, 1).reshape(rows_here, -1)

    def kv_rows(term):
        return jnp.sum(
            jnp.moveaxis(term, 0, 1).reshape(rows_here, kv_heads, copies, HD), 2
        ).reshape(rows_here, -1)

    q_here = heads * HD
    return (
        result.reshape(layer_input.shape),
        grad_input.astype(bf16).reshape(layer_input.shape),
        whole_rows(qkv_term[..., :q_here]),
        kv_rows(qkv_term[..., q_here : q_here + HD]),
        kv_rows(qkv_term[..., q_here + HD :]),
        out_term,
        whole_rows(gate_up_term[..., :hidden_here]),
        whole_rows(gate_up_term[..., hidden_here:]),
        down_term,
        own_gains[0],
        own_gains[1],
    )


def solution(mesh):
    tokens, table, rows, whole = P("rep", "grp", None), P("rep", None), P("grp", None), P()
    return jax.shard_map(
        on_device,
        mesh=mesh,
        in_specs=(tokens, tokens, table, table) + (rows,) * 7 + (whole,) * 2,
        out_specs=(tokens, tokens) + (rows,) * 7 + (P("grp"),) * 2,
        check_vma=False,
    )
```

time: 2420 us -> 1460 us (0.60)
  waiting for transfers between devices: 1680 us -> 625 us
  blocking collectives: 51.4 us -> 295 us
  local copies, waits for them, and re-layouts: 262 us -> 60.7 us
  matrix products: 347 us -> 164 us
  starting transfers between devices: 0.89 us -> 163 us
  Pallas kernels: 0 us -> 43.3 us
  other arithmetic: 54.5 us -> 87.5 us
    unnamed x14 -> x8, waiting for transfers between devices: 679 us -> 0.64 us
    all_gather x9 -> x4, waiting for transfers between devices: 562 us -> 27.8 us  [gather(): return lax.all_gather(rows, 'grp', axis=0, tiled=True)]
    psum x1 -> x0, waiting for transfers between devices: 441 us -> none  [on_device(): lax.psum(grad_shard.astype(jnp.bfloat16), 'rep').astype(jnp.float32)]
    ppermute x0 -> x12, waiting for transfers between devices: none -> 421 us  [the longest x4 286 us: sum_over_sequences(): inward = lax.ppermute(term, 'rep', [(0, 1), (3, 2)])]
    all_to_all x0 -> x2, blocking collectives: none -> 254 us  [the longest x1 134 us: to_columns(): lax.all_to_all(parts, 'grp', 1, 0, tiled=True).reshape(-1, parts.shape[-1])]
    dot_general x56 -> x12, matrix products: 340 us -> 164 us  [the longest x4 60.6 us: against_rows(): lax.dot_general(first, second, (((1,), (1,)), ((), ())), preferred_elemen...]
    ppermute x0 -> x12, starting transfers between devices: none -> 153 us  [the longest x4 138 us: sum_over_sequences(): inward = lax.ppermute(term, 'rep', [(0, 1), (3, 2)])]
    reduce_scatter x2 -> x4, waiting for transfers between devices: 0.01 us -> 142 us  [scatter(): lax.psum_scatter(terms.astype(bf16), 'grp', scatter_dimension=0, tiled=True)]
  transfers between devices with their start and end apart: 13 -> 22, of which waited for: 10 -> 11; matrix products, arithmetic and copies ran while one was open for 15% -> 15% of each run, Pallas kernels for 0% -> 2%
where the time goes in v1:
time: 1460 us; the launch traced here: 1450 us
  waiting for transfers between devices  625 us (43%)
  blocking collectives  295 us (20%)
  matrix products  164 us (11%)
  starting transfers between devices  163 us (11%)
  other arithmetic  87.5 us (6%)
  local copies, waits for them, and re-layouts  60.7 us (4%)
  Pallas kernels  43.3 us (3%)
  between operations  14.9 us (1%)
    ppermute x4, waiting for transfers between devices, sum_over_sequences(): inward = lax.ppermute(term, 'rep', [(0, 1), (3, 2)])  286 us
    reduce_scatter x4, waiting for transfers between devices, scatter(): lax.psum_scatter(terms.astype(bf16), 'grp', scatter_dimension=0, tiled=True)  142 us
    ppermute x4, starting transfers between devices, sum_over_sequences(): inward = lax.ppermute(term, 'rep', [(0, 1), (3, 2)])  138 us
    ppermute x4, waiting for transfers between devices, sum_over_sequences(): outward = lax.ppermute(total, 'rep', [(1, 0), (2, 3)])  134 us
    all_to_all x1, blocking collectives, to_columns(): lax.all_to_all(parts, 'grp', 1, 0, tiled=True).reshape(-1, parts.shape[-1])  134 us
    all_to_all x1, blocking collectives, to_rows(): lax.all_to_all(term.astype(bf16).reshape(groups, rows_here, -1), 'grp', 0...  120 us
    dot_general x4, matrix products, against_rows(): lax.dot_general(first, second, (((1,), (1,)), ((), ())), preferred_elemen...  60.6 us
    dot_general x4, matrix products, matmul_f32(): return jnp.dot(first, second, preferred_element_type=f32)  52.2 us
  transfers between devices with their start and end apart: 22, of which 11 were waited for; matrix products, arithmetic and copies ran while one was open for 15% of the time, Pallas kernels for 2%

profile of v1, /device:TPU:0, one launch (start us, length us, event | category | flops | bytes accessed | tf_op | source)
XLA Modules:
  0.0 1452.9 jit_solution(8170989956819273544)
XLA Ops:
  15.4 5.2 all-to-all-start
  25.0 33.5 %all-to-all-done = bf16[256,8,512]{0,2,1:T(8,128)(2,1)} async-done(((bf16[256,8,512]{0,2,1:T(8,128)(2,1)}), bf16[256,8,512]{0,2,1:T(8,128)(2,1)}, u32[]{:S(2)}, u32[]{:S(2)}) %all-to-all-start) | async-done | bytes 2097184 | tf_op jit(solution)/shard_map/all_to_all | solution.py:315
  58.5 4.1 copy.37
  62.6 27.8 %all-gather.6.cloned.1.call-done = bf16[2048,2048]{1,0:T(8,128)(2,1)} async-done(((bf16[256,2048]{1,0:T(8,128)(2,1)}), bf16[2048,2048]{1,0:T(8,128)(2,1)}) %all-gather.6.cloned.1.call-update) | async-done | bytes 8388624 | tf_op jit(solution)/shard_map/all_gather | solution.py:309
  90.4 10.5 fusion.34.qkv_ref
  102.3 18.5 %shard_map.212 = (bf16[2048,256]{1,0:T(8,128)(2,1)S(1)}, bf16[2,2048,128]{2,1,0:T(8,128)(2,1)S(1)}, bf16[2048,128]{1,0:T(8,128)(2,1)S(1)}, bf16[2048,128]{1,0:T(8,128)(2,1)S(1)}, f32[2,2048]{1,0:T(2,128)S(1)}) custom-call(s32[1,16]{1,0:T(1,128)S(1)} %copy-done.9, f32[2048,512]{1,0:T(8,128)} %fusion.34.qkv_ref, f32[2048,128]{1,0:T(8,128)S(1)} %get-tuple-element.39.cos_ref, ...), custom_call_target="tpu_custom_call" | custom-call | flops 3221225472 | bytes 20971520 | tf_op jit(solution)/shard_map/pallas_call | solution.py:145
  123.4 5.8 convolution_convert_fusion.4
  130.2 71.4 %reduce-scatter.5.cloned.1.call-done = bf16[256,2048]{1,0:T(8,128)(2,1)} async-done(((bf16[2048,2048]{1,0:T(8,128)(2,1)}), bf16[256,2048]{1,0:T(8,128)(2,1)}) %reduce-scatter.5.cloned.1.call-update) | async-done | bytes 1048592 | tf_op jit(solution)/shard_map/reduce_scatter | solution.py:312
  206.5 6.4 copy.39
  212.8 6.5 copy.38
  219.3 7.4 pad_maximum_fusion
  226.8 133.7 %all_to_all.40 = bf16[256,8,2048]{0,2,1:T(8,128)(2,1)} all-to-all(bf16[256,8,2048]{0,2,1:T(8,128)(2,1)} %pad_maximum_fusion), channel_id=1, replica_groups=mesh['grp'=8,'rep'=4] {'grp'}, dimensions={1} | all-to-all | bytes 16777216 | tf_op jit(solution)/shard_map/all_to_all | solution.py:315
  360.4 11.4 copy.40
  371.8 24.4 %fusion.35 = f32[2048,2048]{0,1:T(8,128)} fusion(bf16[2048,2048]{1,0:T(8,128)(2,1)} %all-gather.8.cloned.1.call-done, bf16[2048,2048]{1,0:T(8,128)(2,1)} %bitcast.107), kind=kOutput, calls=%fused_computation.88 | convolution fusion | flops 17179869184 | bytes 33554432 | tf_op jit(solution)/shard_map/dot_general | solution.py:23
  396.2 22.1 %multiply_convert_fusion.1 = (bf16[2048,1024]{0,1:T(8,128)(2,1)}, bf16[2048,1024]{0,1:T(8,128)(2,1)}, bf16[2048,1024]{0,1:T(8,128)(2,1)}) fusion(f32[2048,2048]{0,1:T(8,128)} %fusion.35, bf16[1024,2048]{1,0:T(8,128)(2,1)} %param.23, bf16[1,2048,2048]{2,1,0:T(8,128)(2,1)} %all-gather.12.cloned.1.call-done), kind=kOutput, calls=%fused_computation.14 | convolution fusion | flops 8621391872 | bytes 41943040 | tf_op jit(solution)/shard_map/dot_general | solution.py:27
  418.3 24.1 %convolution_convert_fusion.2 = bf16[2048,2048]{1,0:T(8,128)(2,1)} fusion(bf16[2048,2048]{1,0:T(8,128)(2,1)} %bitcast.108, bf16[2048,1024]{0,1:T(8,128)(2,1)} %get-tuple-element.26, bf16[2048,1024]{0,1:T(8,128)(2,1)} %get-tuple-element.25), kind=kOutput, calls=%fused_computation.20 | convolution fusion | flops 17200840704 | bytes 25165824 | tf_op jit(solution)/shard_map/dot_general | solution.py:27
  442.5 70.9 %reduce-scatter.9.cloned.1.call-done = bf16[256,2048]{1,0:T(8,128)(2,1)} async-done(((bf16[2048,2048]{1,0:T(8,128)(2,1)}), bf16[256,2048]{1,0:T(8,128)(2,1)}) %reduce-scatter.9.cloned.1.call-update) | async-done | bytes 1048592 | tf_op jit(solution)/shard_map/reduce_scatter | solution.py:312
  520.3 23.0 %convolution_convert_fusion = bf16[2048,2048]{1,0:T(8,128)(2,1)S(1)} fusion(bf16[2048,2048]{1,0:T(8,128)(2,1)} %all-gather.8.cloned.1.call-done, bf16[2048,1024]{0,1:T(8,128)(2,1)} %get-tuple-element.26, bf16[2048,1024]{0,1:T(8,128)(2,1)} %get-tuple-element.25), kind=kOutput, calls=%fused_computation.18 | convolution fusion | flops 17200840704 | bytes 25165824 | tf_op jit(solution)/shard_map/dot_general | solution.py:31
  543.4 119.9 %all_to_all.41 = bf16[8,256,2048]{2,1,0:T(8,128)(2,1)} all-to-all(bf16[8,256,2048]{2,1,0:T(8,128)(2,1)S(1)} %bitcast.109), channel_id=1, replica_groups=mesh['grp'=8,'rep'=4] {'grp'}, dimensions={0} | all-to-all | bytes 16777216 | tf_op jit(solution)/shard_map/all_to_all | solution.py:361
  663.3 7.0 collective-permute-start.6
  670.3 5.9 convolution_convert_fusion.7.grad_ref
  676.3 24.8 %shard_map.213 = bf16[2048,512]{1,0:T(8,128)(2,1)} custom-call(s32[1,16]{1,0:T(1,128)S(1)} %copy-done.10, bf16[2048,256]{1,0:T(8,128)(2,1)S(1)} %convolution_convert_fusion.7.grad_ref, bf16[2048,256]{1,0:T(8,128)(2,1)S(1)} %copy-done.3, bf16[2,2048,128]{2,1,0:T(8,128)(2,1)S(1)} %copy-done.12, bf16[2048,128]{1,0:T(8,128)(2,1)S(1)} %copy-done.14, ...), custom_call_target="tpu_custom_call" | custom-call | flops 8589934592 | bytes 29360128 | tf_op jit(solution)/shard_map/pallas_call | solution.py:248
  701.1 8.5 convolution_convert_fusion.1
  709.6 136.4 %collective-permute-done.6 = bf16[8,256,2048]{2,1,0:T(8,128)(2,1)} collective-permute-done((bf16[8,256,2048]{2,1,0:T(8,128)(2,1)}, bf16[8,256,2048]{2,1,0:T(8,128)(2,1)}, u32[]{:S(2)}, u32[]{:S(2)}) %collective-permute-start.6) | collective-permute-done | bytes 8388640 | tf_op jit(solution)/shard_map/ppermute | solution.py:271
  846.1 10.4 add_convert_fusion.1
  856.5 4.1 collective-permute-start.7
  860.6 11.3 fusion.5
  872.0 4.4 collective-permute-start.9
  876.4 87.6 %collective-permute-done.9 = bf16[1024,2048]{1,0:T(8,128)(2,1)S(1)} collective-permute-done((bf16[1024,2048]{1,0:T(8,128)(2,1)S(1)}, bf16[1024,2048]{1,0:T(8,128)(2,1)S(1)}, u32[]{:S(2)}, u32[]{:S(2)}) %collective-permute-start.9) | collective-permute-done | bytes 4194336 | tf_op jit(solution)/shard_map/ppermute | solution.py:271
  970.7 11.4 convolution_convert_fusion.3
  982.2 11.2 add_convert_fusion
  995.1 10.6 convolution_convert_fusion.5
  1005.8 4.4 all-to-all-start.2
  1010.2 7.8 add_convert_fusion.2
  1019.3 6.0 convolution_convert_fusion.6
  1025.3 125.1 %collective-permute-start.3 = (bf16[256,2048]{1,0:T(8,128)(2,1)S(1)}, bf16[256,2048]{1,0:T(8,128)(2,1)S(1)}, u32[]{:S(2)}, u32[]{:S(2)}) collective-permute-start(bf16[256,2048]{1,0:T(8,128)(2,1)S(1)} %convolution_convert_fusion.6), channel_id=1, source_target_pairs={{0,1},{3,2},{4,5},{7,6},{8,9},{11,10},{12,13},{15,14},{16,17},{19,... | collective-permute-start | bytes 3145736 | tf_op jit(solution)/shard_map/ppermute | solution.py:271
  1151.8 22.1 %collective-permute-done.3 = bf16[256,2048]{1,0:T(8,128)(2,1)S(1)} collective-permute-done((bf16[256,2048]{1,0:T(8,128)(2,1)S(1)}, bf16[256,2048]{1,0:T(8,128)(2,1)S(1)}, u32[]{:S(2)}, u32[]{:S(2)}) %collective-permute-start.3) | collective-permute-done | bytes 1048608 | tf_op jit(solution)/shard_map/ppermute | solution.py:271
  1175.0 40.1 %collective-permute-done = bf16[8,256,512]{2,1,0:T(8,128)(2,1)S(1)} collective-permute-done((bf16[8,256,512]{2,1,0:T(8,128)(2,1)}, bf16[8,256,512]{2,1,0:T(8,128)(2,1)S(1)}, u32[]{:S(2)}, u32[]{:S(2)}) %collective-permute-start) | collective-permute-done | bytes 2097184 | tf_op jit(solution)/shard_map/ppermute | solution.py:271
  1221.1 106.8 %collective-permute-done.11 = bf16[1024,2048]{1,0:T(8,128)(2,1)} collective-permute-done((bf16[1024,2048]{1,0:T(8,128)(2,1)}, bf16[1024,2048]{1,0:T(8,128)(2,1)}, u32[]{:S(2)}, u32[]{:S(2)}) %collective-permute-start.11) | collective-permute-done | bytes 4194336 | tf_op jit(solution)/shard_map/ppermute | solution.py:275
  1327.9 6.1 select_convert_fusion.1
  1334.0 10.0 collective-permute-done.5
  1350.4 4.6 select_convert_fusion
  1354.9 6.7 slice_bitcast_fusion
  1361.6 8.6 copy.49
  1370.2 4.2 copy.50
  1374.5 17.6 %collective-permute-done.2 = bf16[8,256,512]{2,1,0:T(8,128)(2,1)S(1)} collective-permute-done((bf16[8,256,512]{2,1,0:T(8,128)(2,1)S(1)}, bf16[8,256,512]{2,1,0:T(8,128)(2,1)S(1)}, u32[]{:S(2)}, u32[]{:S(2)}) %collective-permute-start.2) | collective-permute-done | bytes 2097184 | tf_op jit(solution)/shard_map/ppermute | solution.py:275
  1398.7 41.2 %psum.7 = f32[2,2048]{1,0:T(2,128)S(1)} all-reduce(f32[2,2048]{1,0:T(2,128)S(1)} %pad_maximum_fusion.7), channel_id=1, replica_groups=mesh['grp'=8,'rep'=4] {'grp','rep'}, use_global_device_ids=true, to_apply=%region_10.11 | all-reduce | flops 4096 | bytes 32768 | tf_op jit(solution)/shard_map/psum | solution.py:375
  1440.6 5.3 fusion.28
  (145 shorter events, 61.1 us)
Async XLA Ops:
  7.2 116.2 %copy-start = (bf16[256,2048]{1,0:T(8,128)(2,1)S(1)}, bf16[256,2048]{1,0:T(8,128)(2,1)}, u32[]{:S(2)}) copy-start(bf16[256,2048]{1,0:T(8,128)(2,1)} %param.20) | copy-start | bytes 3145732
  7.2 83.2 %all-gather.6.cloned.1.call-start = ((), (), s32[]{:S(2)}) async-start(), calls=%async_computation.8 | async-start | bytes 9437184 | tf_op jit(solution)/shard_map/all_gather | solution.py:309
  15.4 43.1 %all-to-all-start = ((bf16[256,8,512]{0,2,1:T(8,128)(2,1)}), bf16[256,8,512]{0,2,1:T(8,128)(2,1)}, u32[]{:S(2)}, u32[]{:S(2)}) async-start(bf16[256,8,512]{0,2,1:T(8,128)(2,1)} %pad_maximum_fusion.4), calls=%async_computation | async-start | bytes 4194304 | tf_op jit(solution)/shard_map/all_to_all | solution.py:315
  20.6 181.0 %reduce-scatter.5.cloned.1.call-start = ((), (), s32[]{:S(2)}) async-start(), calls=%async_computation.9 | async-start | bytes 9437184 | tf_op jit(solution)/shard_map/reduce_scatter | solution.py:312
  25.0 77.3 %copy-start.4 = (f32[2048,128]{1,0:T(8,128)}, f32[2048,128]{1,0:T(8,128)S(1)}, u32[]{:S(2)}) copy-start(f32[2048,128]{1,0:T(8,128)S(1)} %get-tuple-element.39.cos_ref) | copy-start | bytes 3145732
  25.0 77.3 %copy-start.6 = (f32[2048,128]{1,0:T(8,128)}, f32[2048,128]{1,0:T(8,128)S(1)}, u32[]{:S(2)}) copy-start(f32[2048,128]{1,0:T(8,128)S(1)} %get-tuple-element.40.sin_ref) | copy-start | bytes 3145732
  90.4 10.5 copy-start.7
  90.4 11.9 copy-start.9
  130.1 71.4 %copy-start.17 = (bf16[1,256,2048]{2,1,0:T(8,128)(2,1)S(1)}, bf16[1,256,2048]{2,1,0:T(8,128)(2,1)}, u32[]{:S(2)}) copy-start(bf16[1,256,2048]{2,1,0:T(8,128)(2,1)} %param.13) | copy-start | bytes 3145732
  130.1 73.1 %copy-start.25 = (f32[2048]{0:T(1024)S(1)}, f32[2048]{0:T(1024)}, u32[]{:S(2)}) copy-start(f32[2048]{0:T(1024)} %param.25) | copy-start | bytes 24580
  130.2 241.6 %all-gather.8.cloned.1.call-start = ((), (), s32[]{:S(2)}) async-start(), calls=%async_computation.10 | async-start | bytes 9437184 | tf_op jit(solution)/shard_map/all_gather | solution.py:309
  203.2 312.9 %copy-start.29 = (f32[256]{0:T(256)}, f32[256]{0:T(256)S(1)}, u32[]{:S(2)}) copy-start(f32[256]{0:T(256)S(1)} %add_rsqrt_fusion) | copy-start | bytes 3076
  205.8 190.4 %all-gather.12.cloned.1.call-start = ((), (), s32[]{:S(2)}) async-start(), calls=%async_computation.15 | async-start | bytes 9437184 | tf_op jit(solution)/shard_map/all_gather | solution.py:309
  206.4 306.9 %reduce-scatter.9.cloned.1.call-start = ((), (), s32[]{:S(2)}) async-start(), calls=%async_computation.12 | async-start | bytes 9437184 | tf_op jit(solution)/shard_map/reduce_scatter | solution.py:312
  442.4 71.0 %copy-start.20 = (bf16[256,2048]{1,0:T(8,128)(2,1)S(1)}, bf16[256,2048]{1,0:T(8,128)(2,1)}, u32[]{:S(2)}) copy-start(bf16[256,2048]{1,0:T(8,128)(2,1)} %reduce-scatter.5.cloned.1.call-done) | copy-start | bytes 3145732
  442.4 227.8 %all-gather.10.cloned.1.call-start = ((), (), s32[]{:S(2)}) async-start(), calls=%async_computation.13 | async-start | bytes 9437184 | tf_op jit(solution)/shard_map/all_gather | solution.py:309
  520.3 876.3 %reduce-scatter.11.cloned.1.call-start = ((), (), s32[]{:S(2)}) async-start(), calls=%async_computation.14 | async-start | bytes 9437184 | tf_op jit(solution)/shard_map/reduce_scatter | solution.py:312
  663.3 12.9 copy-start.3
  663.3 12.9 copy-start.5
  663.3 12.9 copy-start.8
  663.3 12.9 copy-start.10
  663.3 182.8 %collective-permute-start.6 = (bf16[8,256,2048]{2,1,0:T(8,128)(2,1)}, bf16[8,256,2048]{2,1,0:T(8,128)(2,1)}, u32[]{:S(2)}, u32[]{:S(2)}) collective-permute-start(bf16[8,256,2048]{2,1,0:T(8,128)(2,1)} %all_to_all.41), channel_id=1, source_target_pairs={{0,1},{3,2},{4,5},{7,6},{8,9},{11,10},{12,13},{15,14},{16,17},{19,... | collective-permute-start | bytes 25165832 | tf_op jit(solution)/shard_map/ppermute | solution.py:271
  670.2 6.0 copy-start.12
  670.3 6.0 copy-start.14
  670.3 6.0 copy-start.16
  676.2 24.8 %copy-start.22 = (bf16[8,256,1,512]{3,1,0,2:T(8,128)(2,1)S(1)}, bf16[8,256,1,512]{3,1,0,2:T(8,128)(2,1)}, u32[]{:S(2)}) copy-start(bf16[8,256,1,512]{3,1,0,2:T(8,128)(2,1)} %copy.37) | copy-start | bytes 6291460
  709.6 730.9 %reduce-scatter.7.cloned.1.call-start = ((), (), s32[]{:S(2)}) async-start(), calls=%async_computation.11 | async-start | bytes 9437184 | tf_op jit(solution)/shard_map/reduce_scatter | solution.py:312
  709.6 151.0 %copy-start.37 = (bf16[2048,1024]{0,1:T(8,128)(2,1)S(1)}, bf16[2048,1024]{0,1:T(8,128)(2,1)}, u32[]{:S(2)}) copy-start(bf16[2048,1024]{0,1:T(8,128)(2,1)} %get-tuple-element.29) | copy-start | bytes 12582916
  856.5 125.7 %collective-permute-start.7 = (bf16[8,256,2048]{2,1,0:T(8,128)(2,1)}, bf16[8,256,2048]{2,1,0:T(8,128)(2,1)}, u32[]{:S(2)}, u32[]{:S(2)}) collective-permute-start(bf16[8,256,2048]{2,1,0:T(8,128)(2,1)} %add_convert_fusion.1), channel_id=1, source_target_pairs={{1,2},{2,1},{5,6},{6,5},{9,10},{10,9},{13,14},{14,13},{17,18},{18,... | collective-permute-start | bytes 25165832 | tf_op jit(solution)/shard_map/ppermute | solution.py:273
  871.9 98.7 %copy-start.35 = (bf16[1024,2048]{1,0:T(8,128)(2,1)S(1)}, bf16[1024,2048]{1,0:T(8,128)(2,1)}, u32[]{:S(2)}) copy-start(bf16[1024,2048]{1,0:T(8,128)(2,1)} %param.23) | copy-start | bytes 12582916
  872.0 92.0 %collective-permute-start.9 = (bf16[1024,2048]{1,0:T(8,128)(2,1)S(1)}, bf16[1024,2048]{1,0:T(8,128)(2,1)S(1)}, u32[]{:S(2)}, u32[]{:S(2)}) collective-permute-start(bf16[1024,2048]{1,0:T(8,128)(2,1)S(1)} %fusion.5), channel_id=1, source_target_pairs={{0,1},{3,2},{4,5},{7,6},{8,9},{11,10},{12,13},{15,14},{16,17},{19,... | collective-permute-start | bytes 12582920 | tf_op jit(solution)/shard_map/ppermute | solution.py:271
  968.0 42.2 %collective-permute-start.10 = (bf16[1024,2048]{1,0:T(8,128)(2,1)}, bf16[1024,2048]{1,0:T(8,128)(2,1)}, u32[]{:S(2)}, u32[]{:S(2)}) collective-permute-start(bf16[1024,2048]{1,0:T(8,128)(2,1)} %add_convert_fusion.3), channel_id=1, source_target_pairs={{1,2},{2,1},{5,6},{6,5},{9,10},{10,9},{13,14},{14,13},{17,18},{18,... | collective-permute-start | bytes 12582920 | tf_op jit(solution)/shard_map/ppermute | solution.py:273
  982.2 13.0 copy-start.36
  993.4 356.9 %collective-permute-start.8 = (bf16[8,256,2048]{2,1,0:T(8,128)(2,1)}, bf16[8,256,2048]{2,1,0:T(8,128)(2,1)}, u32[]{:S(2)}, u32[]{:S(2)}) collective-permute-start(bf16[8,256,2048]{2,1,0:T(8,128)(2,1)} %add_convert_fusion), channel_id=1, source_target_pairs={{1,0},{2,3},{5,4},{6,7},{9,8},{10,11},{13,12},{14,15},{17,16},{18,... | collective-permute-start | bytes 25165832 | tf_op jit(solution)/shard_map/ppermute | solution.py:275
  1005.8 144.6 %all-to-all-start.2 = ((bf16[8,256,512]{2,1,0:T(8,128)(2,1)}), bf16[8,256,512]{2,1,0:T(8,128)(2,1)}, u32[]{:S(2)}, u32[]{:S(2)}) async-start(bf16[8,256,512]{2,1,0:T(8,128)(2,1)} %bitcast.114), calls=%async_computation.6 | async-start | bytes 4194304 | tf_op jit(solution)/shard_map/all_to_all | solution.py:361
  1018.0 309.9 %collective-permute-start.11 = (bf16[1024,2048]{1,0:T(8,128)(2,1)}, bf16[1024,2048]{1,0:T(8,128)(2,1)}, u32[]{:S(2)}, u32[]{:S(2)}) collective-permute-start(bf16[1024,2048]{1,0:T(8,128)(2,1)} %add_convert_fusion.2), channel_id=1, source_target_pairs={{1,0},{2,3},{5,4},{6,7},{9,8},{10,11},{13,12},{14,15},{17,16},{18,... | collective-permute-start | bytes 12582920 | tf_op jit(solution)/shard_map/ppermute | solution.py:275
  1025.3 148.6 %collective-permute-start.3 = (bf16[256,2048]{1,0:T(8,128)(2,1)S(1)}, bf16[256,2048]{1,0:T(8,128)(2,1)S(1)}, u32[]{:S(2)}, u32[]{:S(2)}) collective-permute-start(bf16[256,2048]{1,0:T(8,128)(2,1)S(1)} %convolution_convert_fusion.6), channel_id=1, source_target_pairs={{0,1},{3,2},{4,5},{7,6},{8,9},{11,10},{12,13},{15,14},{16,17},{19,... | collective-permute-start | bytes 3145736 | tf_op jit(solution)/shard_map/ppermute | solution.py:271
  1150.4 64.8 %collective-permute-start = (bf16[8,256,512]{2,1,0:T(8,128)(2,1)}, bf16[8,256,512]{2,1,0:T(8,128)(2,1)S(1)}, u32[]{:S(2)}, u32[]{:S(2)}) collective-permute-start(bf16[8,256,512]{2,1,0:T(8,128)(2,1)} %all-to-all-done.2), channel_id=1, source_target_pairs={{0,1},{3,2},{4,5},{7,6},{8,9},{11,10},{12,13},{15,14},{16,17},{19,... | collective-permute-start | bytes 6291464 | tf_op jit(solution)/shard_map/ppermute | solution.py:271
  1174.3 45.1 %collective-permute-start.4 = (bf16[256,2048]{1,0:T(8,128)(2,1)S(1)}, bf16[256,2048]{1,0:T(8,128)(2,1)S(1)}, u32[]{:S(2)}, u32[]{:S(2)}) collective-permute-start(bf16[256,2048]{1,0:T(8,128)(2,1)S(1)} %add_convert_fusion.7), channel_id=1, source_target_pairs={{1,2},{2,1},{5,6},{6,5},{9,10},{10,9},{13,14},{14,13},{17,18},{18,... | collective-permute-start | bytes 3145736 | tf_op jit(solution)/shard_map/ppermute | solution.py:273
  1217.4 129.3 %collective-permute-start.1 = (bf16[8,256,512]{2,1,0:T(8,128)(2,1)S(1)}, bf16[8,256,512]{2,1,0:T(8,128)(2,1)}, u32[]{:S(2)}, u32[]{:S(2)}) collective-permute-start(bf16[8,256,512]{2,1,0:T(8,128)(2,1)S(1)} %add_convert_fusion.5), channel_id=1, source_target_pairs={{1,2},{2,1},{5,6},{6,5},{9,10},{10,9},{13,14},{14,13},{17,18},{18,... | collective-permute-start | bytes 6291464 | tf_op jit(solution)/shard_map/ppermute | solution.py:273
  1219.8 124.2 %collective-permute-start.5 = (bf16[256,2048]{1,0:T(8,128)(2,1)S(1)}, bf16[256,2048]{1,0:T(8,128)(2,1)}, u32[]{:S(2)}, u32[]{:S(2)}) collective-permute-start(bf16[256,2048]{1,0:T(8,128)(2,1)S(1)} %add_convert_fusion.6), channel_id=1, source_target_pairs={{1,0},{2,3},{5,4},{6,7},{9,8},{10,11},{13,12},{14,15},{17,16},{18,... | collective-permute-start | bytes 3145736 | tf_op jit(solution)/shard_map/ppermute | solution.py:275
  1348.9 43.2 %collective-permute-start.2 = (bf16[8,256,512]{2,1,0:T(8,128)(2,1)S(1)}, bf16[8,256,512]{2,1,0:T(8,128)(2,1)S(1)}, u32[]{:S(2)}, u32[]{:S(2)}) collective-permute-start(bf16[8,256,512]{2,1,0:T(8,128)(2,1)S(1)} %add_convert_fusion.4), channel_id=1, source_target_pairs={{1,0},{2,3},{5,4},{6,7},{9,8},{10,11},{13,12},{14,15},{17,16},{18,... | collective-permute-start | bytes 6291464 | tf_op jit(solution)/shard_map/ppermute | solution.py:275
  1361.6 8.6 copy-start.19
  1394.3 46.2 %copy-start.21 = (bf16[256,2048]{1,0:T(8,128)(2,1)S(1)}, bf16[256,2048]{1,0:T(8,128)(2,1)}, u32[]{:S(2)}) copy-start(bf16[256,2048]{1,0:T(8,128)(2,1)} %reduce-scatter.5.cloned.1.call-done) | copy-start | bytes 3145732
  1394.3 46.2 %copy-start.26 = (f32[2048]{0:T(1024)S(1)}, f32[2048]{0:T(1024)}, u32[]{:S(2)}) copy-start(f32[2048]{0:T(1024)} %param.25) | copy-start | bytes 24580
  1394.4 46.2 %copy-start.30 = (f32[256]{0:T(256)S(1)}, f32[256]{0:T(256)}, u32[]{:S(2)}) copy-start(f32[256]{0:T(256)} %copy-done.29) | copy-start | bytes 3076
  1394.4 46.2 %copy-start.34 = (f32[256]{0:T(256)S(1)}, f32[256]{0:T(256)}, u32[]{:S(2)}) copy-start(f32[256]{0:T(256)} %copy-done.33) | copy-start | bytes 3076
  1440.5 5.3 copy-start.1
  (12 other events, 26.2 us)
Sparse Core Ops, SparseCore 0:
  12.1 78.2 all-gather.5
  130.3 71.2 reduce-scatter.4
  206.0 97.9 all-gather.7
  305.8 79.5 all-gather.11
  442.5 70.7 reduce-scatter.8
  520.4 98.2 all-gather.9
  709.7 69.4 reduce-scatter.10
  982.3 94.4 reduce-scatter.6

commit v2 on v1

--- a/solution.py
+++ b/solution.py
@@ -262,6 +262,472 @@
             transcendentals=heads * length * length // 2,
         ),
     )(order, grad, out, query, key, value, lse, cosine, sine, piece, piece_col)
+
+
+MESH = pl.DeviceIdType.MESH
+
+
+def place_in_group():
+    me = lax.axis_index("grp")
+    return me // 4, (me // 2) % 2, me % 2
+
+
+def other(flip_y, flip_x, flip_core):
+    y, x, core = place_in_group()
+    return ((y + flip_y) % 2) * 4 + ((x + flip_x) % 2) * 2 + (core + flip_core) % 2
+
+
+def chip_rows(flip_y, flip_x, rows):
+    y, x, _ = place_in_group()
+    first = (((y + flip_y) % 2) * 2 + (x + flip_x) % 2) * (2 * rows)
+    return pl.ds(pl.multiple_of(first, 2 * rows), 2 * rows)
+
+
+def greet_group():
+    barrier = pltpu.get_barrier_semaphore()
+    for flips in ((0, 0, 1), (0, 1, 0), (1, 0, 0)):
+        pl.semaphore_signal(barrier, inc=1, device_id={"grp": other(*flips)}, device_id_type=MESH)
+    pl.semaphore_wait(barrier, 3)
+
+
+SIBLING, ALONG_X, ALONG_Y, ACROSS = (0, 0), (0, 1), (1, 0), (1, 1)
+
+
+def gather_rows(rows, all_ref, sends, recvs, on_chip):
+    half = rows // 2
+
+    def block(chip, core, part=None):
+        first = other(*chip, core) * rows
+        if part is None:
+            return pl.ds(pl.multiple_of(first, rows), rows)
+        return pl.ds(pl.multiple_of(first + part * half, half), half)
+
+    def copy(number, chip, core, part, target):
+        where = all_ref.at[block(chip, core, part), :]
+        return pltpu.make_async_remote_copy(
+            src_ref=where, dst_ref=where, send_sem=sends.at[number], recv_sem=recvs.at[number],
+            device_id={"grp": other(*target)}, device_id_type=MESH,
+        )
+
+    def landed(number, chip, core, part):
+        where = all_ref.at[block(chip, core, part), :]
+        pltpu.make_async_remote_copy(
+            src_ref=where, dst_ref=where, send_sem=sends.at[number], recv_sem=recvs.at[number],
+            device_id={"grp": other(0, 0, 1)}, device_id_type=MESH,
+        ).wait_recv()
+
+    to_s, to_x, to_y = (0, 0, 1), (0, 1, 0), (1, 0, 0)
+    started = []
+
+    def send(*what):
+        one = copy(*what)
+        one.start()
+        started.append(one)
+
+    send(1, SIBLING, 0, 1, to_x)
+    send(3, SIBLING, 0, 0, to_y)
+    send(0, SIBLING, 0, None, to_s)
+    send(2, SIBLING, 0, 0, to_x)
+    send(4, SIBLING, 0, 1, to_y)
+    landed(0, SIBLING, 1, None)
+    on_chip(*SIBLING)
+    landed(1, ALONG_X, 0, 1)
+    send(6, ALONG_X, 0, 1, to_y)
+    landed(3, ALONG_Y, 0, 0)
+    send(5, ALONG_Y, 0, 0, to_x)
+    send(7, ALONG_X, 0, 1, to_s)
+    send(8, ALONG_Y, 0, 0, to_s)
+    landed(2, ALONG_X, 0, 0)
+    send(9, ALONG_X, 0, 0, to_s)
+    landed(4, ALONG_Y, 0, 1)
+    send(10, ALONG_Y, 0, 1, to_s)
+    landed(7, ALONG_X, 1, 1)
+    landed(9, ALONG_X, 1, 0)
+    on_chip(*ALONG_X)
+    landed(5, ACROSS, 0, 0)
+    send(11, ACROSS, 0, 0, to_s)
+    landed(6, ACROSS, 0, 1)
+    send(12, ACROSS, 0, 1, to_s)
+    landed(8, ALONG_Y, 1, 0)
+    landed(10, ALONG_Y, 1, 1)
+    on_chip(*ALONG_Y)
+    landed(11, ACROSS, 1, 0)
+    landed(12, ACROSS, 1, 1)
+    on_chip(*ACROSS)
+    for one in started:
+        one.wait_send()
+
+
+GATHER_COPIES = 13
+
+
+def rms_normed(values, gain):
+    return values * lax.rsqrt(jnp.mean(values * values, -1, keepdims=True) + EPS) * gain
+
+
+class Moves:
+    def __init__(self, sems):
+        self.sems, self.count, self.open = sems, 0, []
+
+    def start(self, src, dst):
+        one = pltpu.make_async_copy(src, dst, self.sems.at[self.count])
+        self.count += 1
+        one.start()
+        return one
+
+    def later(self, src, dst):
+        self.open.append(self.start(src, dst))
+
+    def finish(self):
+        for one in self.open:
+            one.wait()
+
+
+def comm_params(number, vmem=56):
+    return pltpu.CompilerParams(
+        collective_id=number, has_side_effects=True, vmem_limit_bytes=vmem * 2**20
+    )
+
+
+def gather_scratch(rows, width, moves):
+    return [
+        pltpu.VMEM((8 * rows, width), bf16),
+        pltpu.SemaphoreType.DMA((GATHER_COPIES,)),
+        pltpu.SemaphoreType.DMA((GATHER_COPIES,)),
+        pltpu.SemaphoreType.DMA((moves,)),
+    ]
+
+
+def any_specs(count):
+    return [pl.BlockSpec(memory_space=pl.ANY)] * count
+
+
+def own_rows(rows):
+    return pl.ds(pl.multiple_of(other(0, 0, 0) * rows, rows), rows)
+
+
+def gather_normed_kernel(x_ref, gain_ref, all_ref, held, sends, recvs, sems):
+    rows = x_ref.shape[0]
+    moves = Moves(sems)
+    held[own_rows(rows), :] = rms_normed(x_ref[...].astype(f32), gain_ref[...]).astype(bf16)
+    greet_group()
+
+    def on_chip(*chip):
+        where = chip_rows(*chip, rows)
+        moves.later(held.at[where, :], all_ref.at[where, :])
+
+    gather_rows(rows, held, sends, recvs, on_chip)
+    moves.finish()
+
+
+def gather_normed(x, gain, number):
+    rows, width = x.shape
+    return pl.pallas_call(
+        gather_normed_kernel,
+        out_shape=jax.ShapeDtypeStruct((8 * rows, width), bf16),
+        in_specs=vmem_specs(2),
+        out_specs=pl.BlockSpec(memory_space=pl.ANY),
+        scratch_shapes=gather_scratch(rows, width, 4),
+        compiler_params=comm_params(number),
+        cost_estimate=pl.CostEstimate(
+            flops=0, bytes_accessed=150 * rows * width * 2, transcendentals=0
+        ),
+    )(x, gain)
+
+
+def feed_forward_kernel(
+    tile, mid_ref, gain_ref, w_ref, all_ref, hidden_ref, up_part_ref, gate_part_ref,
+    held, sends, recvs, sems, weight, hidden, up_part, gate_part,
+):
+    rows = mid_ref.shape[0]
+    inner = hidden.shape[1]
+    moves = Moves(sems)
+    weight_copy = moves.start(w_ref, weight)
+    held[own_rows(rows), :] = rms_normed(mid_ref[...], gain_ref[...]).astype(bf16)
+    greet_group()
+
+    def on_chip(*chip):
+        where = chip_rows(*chip, rows)
+        moves.later(held.at[where, :], all_ref.at[where, :])
+        if chip == SIBLING:
+            weight_copy.wait()
+
+        def column(t, _):
+            cols = pl.ds(pl.multiple_of(t * tile, tile), tile)
+            up_cols = pl.ds(pl.multiple_of(inner + t * tile, tile), tile)
+            lhs = held[where, :]
+            gate = matmul_f32(lhs, weight[:, cols])
+            up = matmul_f32(lhs, weight[:, up_cols])
+            sigma = 1.0 / (1.0 + jnp.exp(-gate))
+            swish = gate * sigma
+            hidden[where, cols] = (swish * up).astype(bf16)
+            up_part[where, cols] = swish.astype(bf16)
+            gate_part[where, cols] = (up * sigma * (1.0 + gate * (1.0 - sigma))).astype(bf16)
+            return 0
+
+        lax.fori_loop(0, inner // tile, column, 0)
+        for src, dst in ((hidden, hidden_ref), (up_part, up_part_ref), (gate_part, gate_part_ref)):
+            moves.later(src.at[where, :], dst.at[where, :])
+
+    gather_rows(rows, held, sends, recvs, on_chip)
+    moves.finish()
+
+
+def feed_forward(mid, gain, cols_gate_up, number):
+    rows, width = mid.shape
+    inner = cols_gate_up.shape[1] // 2
+    tall = jax.ShapeDtypeStruct((8 * rows, inner), bf16)
+    return pl.pallas_call(
+        functools.partial(feed_forward_kernel, min(256, inner)),
+        out_shape=(jax.ShapeDtypeStruct((8 * rows, width), bf16), tall, tall, tall),
+        in_specs=vmem_specs(2) + any_specs(1),
+        out_specs=tuple(any_specs(4)),
+        scratch_shapes=gather_scratch(rows, width, 17)
+        + [pltpu.VMEM(cols_gate_up.shape, bf16)]
+        + [pltpu.VMEM((8 * rows, inner), bf16)] * 3,
+        compiler_params=comm_params(number),
+        cost_estimate=pl.CostEstimate(
+            flops=32 * rows * width * inner, bytes_accessed=150 * rows * width * 2,
+            transcendentals=8 * rows * inner,
+        ),
+    )(mid, gain, cols_gate_up)
+
+
+def feed_forward_back_kernel(
+    tile, grad_ref, w_ref, hidden_ref, up_part_ref, gate_part_ref, grad_gate_up_ref, down_ref,
+    held, sends, recvs, sems, weight, hidden, up_part, gate_part, grads, down, down_low,
+):
+    rows = grad_ref.shape[0]
+    inner, width = weight.shape
+    moves = Moves(sems)
+    loads = [
+        moves.start(src, dst)
+        for src, dst in (
+            (w_ref, weight), (hidden_ref, hidden), (up_part_ref, up_part), (gate_part_ref, gate_part)
+        )
+    ]
+    held[own_rows(rows), :] = grad_ref[...]
+    greet_group()
+
+    def on_chip(*chip):
+        where = chip_rows(*chip, rows)
+        if chip == SIBLING:
+            for one in loads:
+                one.wait()
+
+        def column(t, _):
+            cols = pl.ds(pl.multiple_of(t * tile, tile), tile)
+            up_cols = pl.ds(pl.multiple_of(inner + t * tile, tile), tile)
+            incoming = held[where, :]
+            grad_hidden = against_rows(incoming, weight[cols, :])
+            grads[where, cols] = (grad_hidden * gate_part[where, cols].astype(f32)).astype(bf16)
+            grads[where, up_cols] = (grad_hidden * up_part[where, cols].astype(f32)).astype(bf16)
+            term = over_tokens(hidden[where, cols], incoming)
+            if chip == SIBLING:
+                down[cols, :] = term
+            elif chip == ACROSS:
+                down_low[cols, :] = (down[cols, :] + term).astype(bf16)
+            else:
+                down[cols, :] += term
+            return 0
+
+        lax.fori_loop(0, inner // tile, column, 0)
+        moves.later(grads.at[where, :], grad_gate_up_ref.at[where, :])
+
+    gather_rows(rows, held, sends, recvs, on_chip)
+    moves.later(down_low, down_ref)
+    moves.finish()
+
+
+def feed_forward_back(grad, w_down, hidden, up_part, gate_part, number):
+    rows, width = grad.shape
+    inner = w_down.shape[0]
+    return pl.pallas_call(
+        functools.partial(feed_forward_back_kernel, min(256, inner)),
+        out_shape=(
+            jax.ShapeDtypeStruct((8 * rows, 2 * inner), bf16),
+            jax.ShapeDtypeStruct((inner, width), bf16),
+        ),
+        in_specs=vmem_specs(1) + any_specs(4),
+        out_specs=tuple(any_specs(2)),
+        scratch_shapes=gather_scratch(rows, width, 9)
+        + [pltpu.VMEM(w_down.shape, bf16)]
+        + [pltpu.VMEM((8 * rows, inner), bf16)] * 3
+        + [
+            pltpu.VMEM((8 * rows, 2 * inner), bf16),
+            pltpu.VMEM(w_down.shape, f32),
+            pltpu.VMEM(w_down.shape, bf16),
+        ],
+        compiler_params=comm_params(number, 62),
+        cost_estimate=pl.CostEstimate(
+            flops=32 * rows * width * inner, bytes_accessed=150 * rows * width * 2,
+            transcendentals=0,
+        ),
+    )(grad, w_down, hidden, up_part, gate_part)
+
+
+def attended_back_kernel(
+    grad_ref, w_ref, attended_ref, grad_attended_ref, out_term_ref,
+    held, sends, recvs, sems, total,
+):
+    rows = grad_ref.shape[0]
+    moves = Moves(sems)
+    held[own_rows(rows), :] = grad_ref[...]
+    greet_group()
+
+    def on_chip(*chip):
+        where = chip_rows(*chip, rows)
+        incoming = held[where, :]
+        grad_attended_ref[where, :] = against_rows(incoming, w_ref[...]).astype(bf16)
+        term = over_tokens(attended_ref[where, :], incoming)
+        if chip == SIBLING:
+            total[...] = term
+        elif chip == ACROSS:
+            out_term_ref[...] = (total[...] + term).astype(bf16)
+        else:
+            total[...] += term
+
+    gather_rows(rows, held, sends, recvs, on_chip)
+    moves.finish()
+
+
+def attended_back(grad, w_out, attended, number):
+    rows, width = grad.shape
+    return pl.pallas_call(
+        attended_back_kernel,
+        out_shape=(
+            jax.ShapeDtypeStruct(attended.shape, bf16),
+            jax.ShapeDtypeStruct(w_out.shape, bf16),
+        ),
+        in_specs=vmem_specs(3),
+        out_specs=tuple(vmem_specs(2)),
+        scratch_shapes=gather_scratch(rows, width, 1) + [pltpu.VMEM(w_out.shape, f32)],
+        compiler_params=comm_params(number),
+        cost_estimate=pl.CostEstimate(
+            flops=32 * rows * width * w_out.shape[0], bytes_accessed=150 * rows * width * 2,
+            transcendentals=0,
+        ),
+    )(grad, w_out, attended)
+
+
+def scatter_kernel(
+    turned, tile,
+    a_ref, b_ref, out_ref,
+    part, to_s, from_s, to_chip, held, relay, last, sends, recvs,
+):
+    rows, width = out_ref.shape
+    half = rows // 2
+    _, _, core = place_in_group()
+    greet_group()
+    own_at = pl.multiple_of(core * rows, rows)
+    other_at = pl.multiple_of((1 - core) * rows, rows)
+    started = []
+
+    def send(number, src, dst, target):
+        one = pltpu.make_async_remote_copy(
+            src_ref=src, dst_ref=dst, send_sem=sends.at[number], recv_sem=recvs.at[number],
+            device_id={"grp": other(*target)}, device_id_type=MESH,
+        )
+        one.start()
+        started.append(one)
+        return one
+
+    def landed(number, where):
+        pltpu.make_async_remote_copy(
+            src_ref=where, dst_ref=where, send_sem=sends.at[number], recv_sem=recvs.at[number],
+            device_id={"grp": other(0, 0, 1)}, device_id_type=MESH,
+        ).wait_recv()
+
+    to_sib, to_x, to_y = (0, 0, 1), (0, 1, 0), (1, 0, 0)
+
+    def make(number, chip):
+        where = chip_rows(*chip, rows)
+
+        def column(t, _):
+            cols = pl.ds(pl.multiple_of(t * tile, tile), tile)
+            lhs = a_ref[where, :]
+            if turned:
+                part[:, cols] = against_rows(lhs, b_ref[cols, :])
+            else:
+                part[:, cols] = matmul_f32(lhs, b_ref[:, cols])
+            return 0
+
+        lax.fori_loop(0, width // tile, column, 0)
+        to_s[number] = part[pl.ds(other_at, rows), :].astype(bf16)
+        send(number, to_s.at[number], from_s.at[number], to_sib)
+
+    def own(low, number):
+        at = pl.ds(pl.multiple_of(core * rows + low * half, half), half)
+        return part[at, :] + from_s[number, low * half : (low + 1) * half, :].astype(f32)
+
+    first, second = slice(0, half), slice(half, rows)
+    make(0, ACROSS)
+    landed(0, from_s.at[0])
+    to_chip[0, first, :] = own(0, 0).astype(bf16)
+    send(4, to_chip.at[0, first, :], relay.at[0], to_x)
+    to_chip[0, second, :] = own(1, 0).astype(bf16)
+    send(5, to_chip.at[0, second, :], relay.at[1], to_y)
+    make(1, ALONG_X)
+    landed(1, from_s.at[1])
+    to_chip[1, first, :] = own(0, 1).astype(bf16)
+    send(6, to_chip.at[1, first, :], last.at[0, first, :], to_x)
+    held[0] = own(1, 1)
+    make(2, ALONG_Y)
+    landed(2, from_s.at[2])
+    to_chip[2, second, :] = own(1, 2).astype(bf16)
+    send(7, to_chip.at[2, second, :], last.at[1, second, :], to_y)
+    held[1] = own(0, 2)
+    landed(5, relay.at[1])
+    to_chip[1, second, :] = (held[0] + relay[1].astype(f32)).astype(bf16)
+    send(8, to_chip.at[1, second, :], last.at[0, second, :], to_x)
+    landed(4, relay.at[0])
+    to_chip[2, first, :] = (held[1] + relay[0].astype(f32)).astype(bf16)
+    send(9, to_chip.at[2, first, :], last.at[1, first, :], to_y)
+    make(3, SIBLING)
+    landed(3, from_s.at[3])
+    for low in (0, 1):
+        out_ref[low * half : (low + 1) * half, :] = own(low, 3)
+    landed(6, last.at[0, first, :])
+    out_ref[first, :] += last[0, first, :].astype(f32)
+    landed(7, last.at[1, second, :])
+    out_ref[second, :] += last[1, second, :].astype(f32)
+    landed(8, last.at[0, second, :])
+    out_ref[second, :] += last[0, second, :].astype(f32)
+    landed(9, last.at[1, first, :])
+    out_ref[first, :] += last[1, first, :].astype(f32)
+    for one in started:
+        one.wait_send()
+
+
+def product_scattered(a, b, turned, number):
+    length, depth = a.shape
+    width = b.shape[0] if turned else b.shape[1]
+    rows = length // 8
+    tile = min(256, width)
+    return pl.pallas_call(
+        functools.partial(scatter_kernel, turned, tile),
+        out_shape=jax.ShapeDtypeStruct((rows, width), f32),
+        in_specs=vmem_specs(2),
+        out_specs=pl.BlockSpec(memory_space=pltpu.VMEM),
+        scratch_shapes=[
+            pltpu.VMEM((2 * rows, width), f32),
+            pltpu.VMEM((4, rows, width), bf16),
+            pltpu.VMEM((4, rows, width), bf16),
+            pltpu.VMEM((3, rows, width), bf16),
+            pltpu.VMEM((2, rows // 2, width), f32),
+            pltpu.VMEM((2, rows // 2, width), bf16),
+            pltpu.VMEM((2, rows, width), bf16),
+            pltpu.SemaphoreType.DMA((10,)),
+            pltpu.SemaphoreType.DMA((10,)),
+        ],
+        compiler_params=pltpu.CompilerParams(
+            collective_id=number, has_side_effects=True, vmem_limit_bytes=56 * 2**20
+        ),
+        cost_estimate=pl.CostEstimate(
+            flops=2 * length * depth * width,
+            bytes_accessed=100 * rows * width * 2, transcendentals=0,
+        ),
+    )(a, b)
 
 
 def sum_over_sequences(term, reps):
@@ -305,11 +771,18 @@
     piece_col = jnp.broadcast_to(piece_ids.reshape(length, 1), (length, HD))
     cosine, sine = turn_tables(length)
 
+    near = groups == 8
+
     def gather(rows):
         return lax.all_gather(rows, "grp", axis=0, tiled=True)
 
-    def scatter(terms):
-        return lax.psum_scatter(terms.astype(bf16), "grp", scatter_dimension=0, tiled=True)
+    def scatter(first, second, turned, number):
+        if near:
+            return product_scattered(first, second, turned, number)
+        term = against_rows(first, second) if turned else matmul_f32(first, second)
+        return lax.psum_scatter(
+            term.astype(bf16), "grp", scatter_dimension=0, tiled=True
+        ).astype(f32)
 
     def to_columns(parts):
         return lax.all_to_all(parts, "grp", 1, 0, tiled=True).reshape(-1, parts.shape[-1])
@@ -320,42 +793,57 @@
     def per_kv_head(weight):
         return jnp.repeat(weight.reshape(rows_here, kv_heads, HD), copies, axis=1)
 
-    x_flat = layer_input.reshape(local_rows, model_width).astype(f32)
+    x_rows = layer_input.reshape(local_rows, model_width)
+    x_flat = x_rows.astype(f32)
     inv_one = lax.rsqrt(jnp.mean(x_flat * x_flat, -1, keepdims=True) + EPS)
     unit_one = x_flat * inv_one
-    normed_one = gather((unit_one * gain_attn).astype(bf16))
+    attn_gain, ffn_gain = gain_attn.reshape(1, -1), gain_ffn.reshape(1, -1)
     cols_qkv = to_columns(
         jnp.concatenate([per_group(w_query), per_kv_head(w_key), per_kv_head(w_value)], -1)
     )
+    if near:
+        normed_one = gather_normed(x_rows, attn_gain, 1)
+    else:
+        normed_one = gather(rms_normed(x_flat, attn_gain).astype(bf16))
     qkv = matmul_f32(normed_one, cols_qkv)
     attended, query, key, value, lse = attend(
         cut_order, qkv, cosine, sine, piece_ids, piece_col, heads
     )
     cols_gate_up = to_columns(jnp.concatenate([per_group(w_gate), per_group(w_up)], -1))
-    mid = x_flat + scatter(matmul_f32(attended, w_out)).astype(f32)
+    mid = x_flat + scatter(attended, w_out, False, 2)
     inv_two = lax.rsqrt(jnp.mean(mid * mid, -1, keepdims=True) + EPS)
     unit_two = mid * inv_two
-    normed_two = gather((unit_two * gain_ffn).astype(bf16))
     grad_out = cotangent.reshape(local_rows, model_width)
-    grad_all = gather(grad_out)
-    gate_up = matmul_f32(normed_two, cols_gate_up)
-    gate_proj, up_proj = gate_up[:, :hidden_here], gate_up[:, hidden_here:]
-    sigmoid_gate = jax.nn.sigmoid(gate_proj)
-    swish = gate_proj * sigmoid_gate
-    hidden = (swish * up_proj).astype(bf16)
-    down_term = sum_over_sequences(over_tokens(hidden, grad_all).astype(bf16), reps)
-    grad_hidden = against_rows(grad_all, w_down)
-    grad_gate = (
-        grad_hidden * up_proj * sigmoid_gate * (1.0 + gate_proj * (1.0 - sigmoid_gate))
-    ).astype(bf16)
-    grad_up = (grad_hidden * swish).astype(bf16)
-    grad_gate_up = jnp.concatenate([grad_gate, grad_up], 1)
-    grad_two = scatter(against_rows(grad_gate_up, cols_gate_up)).astype(f32)
+    if near:
+        normed_two, hidden, up_part, gate_part = feed_forward(mid, ffn_gain, cols_gate_up, 3)
+        grad_gate_up, down_term = feed_forward_back(
+            grad_out, w_down, hidden, up_part, gate_part, 4
+        )
+    else:
+        normed_two = gather((unit_two * ffn_gain).astype(bf16))
+        grad_all = gather(grad_out)
+        gate_up = matmul_f32(normed_two, cols_gate_up)
+        gate_proj, up_proj = gate_up[:, :hidden_here], gate_up[:, hidden_here:]
+        sigmoid_gate = jax.nn.sigmoid(gate_proj)
+        swish = gate_proj * sigmoid_gate
+        hidden = (swish * up_proj).astype(bf16)
+        gate_part = up_proj * sigmoid_gate * (1.0 + gate_proj * (1.0 - sigmoid_gate))
+        down_term = over_tokens(hidden, grad_all).astype(bf16)
+        grad_hidden = against_rows(grad_all, w_down)
+        grad_gate_up = jnp.concatenate([grad_hidden * gate_part, grad_hidden * swish], 1)
+        grad_gate_up = grad_gate_up.astype(bf16)
+    down_term = sum_over_sequences(down_term, reps)
+    grad_two = scatter(grad_gate_up, cols_gate_up, True, 5)
     grad_mid, gain_ffn_term = norm_back(
         grad_out.astype(f32), grad_two, unit_two, inv_two, gain_ffn
     )
-    grad_mid_low = gather(grad_mid.astype(bf16))
-    grad_attended = against_rows(grad_mid_low, w_out).astype(bf16)
+    grad_mid_low = grad_mid.astype(bf16)
+    if near:
+        grad_attended, out_term = attended_back(grad_mid_low, w_out, attended, 6)
+    else:
+        grad_mid_low = gather(grad_mid_low)
+        grad_attended = against_rows(grad_mid_low, w_out).astype(bf16)
+        out_term = over_tokens(attended, grad_mid_low).astype(bf16)
 
     def to_rows(term):
         return lax.all_to_all(
@@ -363,15 +851,15 @@
         )
 
     gate_up_term = sum_over_sequences(to_rows(over_tokens(normed_two, grad_gate_up)), reps)
-    result = (mid + scatter(matmul_f32(hidden, w_down)).astype(f32)).astype(bf16)
     grad_qkv = attend_back(
         cut_order, grad_attended, attended, query, key, value, lse, cosine, sine,
         piece_ids, piece_col, heads,
     )
-    out_term = sum_over_sequences(over_tokens(attended, grad_mid_low).astype(bf16), reps)
+    out_term = sum_over_sequences(out_term, reps)
     qkv_term = sum_over_sequences(to_rows(over_tokens(normed_one, grad_qkv)), reps)
-    grad_one = scatter(against_rows(grad_qkv, cols_qkv)).astype(f32)
+    grad_one = scatter(grad_qkv, cols_qkv, True, 7)
     grad_input, gain_attn_term = norm_back(grad_mid, grad_one, unit_one, inv_one, gain_attn)
+    result = (mid + scatter(hidden, w_down, False, 8)).astype(bf16)
     gain_total = lax.psum(jnp.stack([gain_attn_term, gain_ffn_term]), ("grp", "rep"))
     own_gains = lax.dynamic_slice_in_dim(gain_total, own_index * rows_here, rows_here, 1)
 

time: 1460 us -> 1280 us (0.88)
  Pallas kernels: 43.3 us -> 519 us
  waiting for transfers between devices: 625 us -> 306 us
  matrix products: 164 us -> 40.4 us
  starting transfers between devices: 163 us -> 52.4 us
  blocking collectives: 295 us -> 240 us
  local copies, waits for them, and re-layouts: 60.7 us -> 40.2 us
    pallas_call x0 -> x8, Pallas kernels: none -> 476 us  [the longest x4 198 us: product_scattered(): pl.pallas_call(functools.partial(scatter_kernel, turned, tile), out_shape...]
    reduce_scatter x4 -> x0, waiting for transfers between devices: 142 us -> none  [scatter(): lax.psum_scatter(terms.astype(bf16), 'grp', scatter_dimension=0, tiled=True)]
    all_to_all x1 -> x0, blocking collectives: 134 us -> none  [to_columns(): lax.all_to_all(parts, 'grp', 1, 0, tiled=True).reshape(-1, parts.shape[-1])]
    ppermute x4, starting transfers between devices: 138 us -> 22.1 us  [sum_over_sequences(): inward = lax.ppermute(term, 'rep', [(0, 1), (3, 2)])]
    ppermute x4, waiting for transfers between devices: 286 us -> 179 us  [sum_over_sequences(): inward = lax.ppermute(term, 'rep', [(0, 1), (3, 2)])]
    psum x1, blocking collectives: 41.2 us -> 144 us  [on_device(): lax.psum(jnp.stack([gain_attn_term, gain_ffn_term]), ('grp', 'rep'))]
    dot_general x4 -> x0, matrix products: 60.6 us -> none  [against_rows(): lax.dot_general(first, second, (((1,), (1,)), ((), ())), preferred_elemen...]
    dot_general x4 -> x1, matrix products: 52.2 us -> 7.98 us  [matmul_f32(): return jnp.dot(first, second, preferred_element_type=f32)]
  transfers between devices with their start and end apart: 22 -> 15, of which waited for: 11 -> 4; matrix products, arithmetic and copies ran while one was open for 15% -> 8% of each run, Pallas kernels for 2% -> 33%
where the time goes in v2:
time: 1280 us
  Pallas kernels  519 us (41%)
  waiting for transfers between devices  306 us (24%)
  blocking collectives  240 us (19%)
  other arithmetic  77.4 us (6%)
  starting transfers between devices  52.4 us (4%)
  matrix products  40.4 us (3%)
  local copies, waits for them, and re-layouts  40.2 us (3%)
    pallas_call x4, Pallas kernels, product_scattered(): pl.pallas_call(functools.partial(scatter_kernel, turned, tile), out_shape...  198 us
    ppermute x4, waiting for transfers between devices, sum_over_sequences(): inward = lax.ppermute(term, 'rep', [(0, 1), (3, 2)])  179 us
    psum x1, blocking collectives, on_device(): lax.psum(jnp.stack([gain_attn_term, gain_ffn_term]), ('grp', 'rep'))  144 us
    pallas_call x1, Pallas kernels, gather_normed(): pl.pallas_call(gather_normed_kernel, out_shape=jax.ShapeDtypeStruct((8 *...  130 us
    ppermute x4, waiting for transfers between devices, sum_over_sequences(): outward = lax.ppermute(total, 'rep', [(1, 0), (2, 3)])  99 us
    all_to_all x1, blocking collectives, to_rows(): lax.all_to_all(term.astype(bf16).reshape(groups, rows_here, -1), 'grp', 0...  96.6 us
    pallas_call x1, Pallas kernels, feed_forward(): pl.pallas_call(functools.partial(feed_forward_kernel, min(256, inner)), o...  51.6 us
    pallas_call x1, Pallas kernels, feed_forward_back(): pl.pallas_call(functools.partial(feed_forward_back_kernel, min(256, inner...  50.9 us
  transfers between devices with their start and end apart: 15, of which 4 were waited for; matrix products, arithmetic and copies ran while one was open for 8% of the time, Pallas kernels for 33%

profile of v2, /device:TPU:0, one launch (start us, length us, event | category | flops | bytes accessed | tf_op | source)
XLA Modules:
  0.0 1276.9 jit_solution(3293307452991495023)
XLA Ops:
  4.9 5.2 all-to-all-start
  10.0 6.2 copy_bitcast_fusion
  16.2 8.3 pad_maximum_fusion
  24.5 12.2 all-to-all-done
  38.0 5.5 all-to-all-start.1
  43.5 130.3 %shard_map.212 = bf16[2048,2048]{1,0:T(8,128)(2,1)} custom-call(bf16[256,2048]{1,0:T(8,128)(2,1)} %bitcast.87, f32[1,2048]{1,0:T(1,128)} %bitcast.103), custom_call_target="tpu_custom_call" | custom-call | bytes 157286400 | tf_op jit(solution)/shard_map/pallas_call | solution.py:425
  173.8 3.7 fusion.12
  178.2 8.0 fusion.15.qkv_ref
  187.5 18.5 %shard_map.213 = (bf16[2048,256]{1,0:T(8,128)(2,1)S(1)}, bf16[2,2048,128]{2,1,0:T(8,128)(2,1)S(1)}, bf16[2048,128]{1,0:T(8,128)(2,1)S(1)}, bf16[2048,128]{1,0:T(8,128)(2,1)S(1)}, f32[2,2048]{1,0:T(2,128)S(1)}) custom-call(s32[1,16]{1,0:T(1,128)S(1)} %copy-done.4, f32[2048,512]{1,0:T(8,128)} %fusion.15.qkv_ref, f32[2048,128]{1,0:T(8,128)S(1)} %get-tuple-element.57.cos_ref, ...), custom_call_target="tpu_custom_call" | custom-call | flops 3221225472 | bytes 20971520 | tf_op jit(solution)/shard_map/pallas_call | solution.py:145
  208.8 44.9 %shard_map.214 = f32[256,2048]{1,0:T(8,128)} custom-call(bf16[2048,256]{1,0:T(8,128)(2,1)} %copy-done.5, bf16[256,2048]{1,0:T(8,128)(2,1)} %w_ref.3), custom_call_target="tpu_custom_call" | custom-call | flops 2147483648 | bytes 104857600 | tf_op jit(solution)/shard_map/pallas_call | solution.py:707
  253.7 3.2 multiply_reduce_fusion.2
  256.9 51.6 %shard_map.215 = (bf16[2048,2048]{1,0:T(8,128)(2,1)}, bf16[2048,1024]{1,0:T(8,128)(2,1)}, bf16[2048,1024]{1,0:T(8,128)(2,1)}, bf16[2048,1024]{1,0:T(8,128)(2,1)}) custom-call(f32[256,2048]{1,0:T(8,128)} %get-tuple-element.42.mid_ref, f32[1,2048]{1,0:T(1,128)} %bitcast.102, bf16[2048,2048]{1,0:T(8,128)(2,1)} %bitcast.9.w_ref.b_ref), custom_call_target="tpu_custom_call" | custom-call | flops 17179869184 | bytes 157286400 | tf_op jit(solution)/shard_map/pallas_call | solution.py:480
  308.5 50.9 %shard_map.217 = (bf16[2048,2048]{1,0:T(8,128)(2,1)}, bf16[1024,2048]{1,0:T(8,128)(2,1)}) custom-call(bf16[256,2048]{1,0:T(8,128)(2,1)} %bitcast.91, bf16[1024,2048]{1,0:T(8,128)(2,1)} %w_ref.2, bf16[2048,1024]{1,0:T(8,128)(2,1)} %get-tuple-element.25.a_ref.hidden_ref, bf16[2048,1024]{1,0:T(8,128)(2,1)} %get-tuple-element.26.up_part_ref, ...), custom_call_target="tpu_custom_call" | custom-call | flops 17179869184 | bytes 157286400 | tf_op jit(solution)/shard_map/pallas_call | solution.py:545
  359.4 22.6 %convolution_convert_fusion = bf16[2048,2048]{1,0:T(8,128)(2,1)S(1)} fusion(bf16[2048,2048]{1,0:T(8,128)(2,1)} %get-tuple-element.35, bf16[2048,2048]{1,0:T(8,128)(2,1)} %get-tuple-element.28.a_ref), kind=kOutput, calls=%fused_computation.8 | convolution fusion | flops 17184063488 | bytes 25165824 | tf_op jit(solution)/shard_map/dot_general | solution.py:31
  382.0 96.6 %all_to_all.40 = bf16[8,256,2048]{2,1,0:T(8,128)(2,1)S(1)} all-to-all(bf16[8,256,2048]{2,1,0:T(8,128)(2,1)S(1)} %bitcast.90), channel_id=1, replica_groups=mesh['grp'=8,'rep'=4] {'grp'}, dimensions={0} | all-to-all | bytes 16777216 | tf_op jit(solution)/shard_map/all_to_all | solution.py:849
  478.6 4.0 collective-permute-start.6
  482.6 178.5 %collective-permute-done.6 = bf16[8,256,2048]{2,1,0:T(8,128)(2,1)S(1)} collective-permute-done((bf16[8,256,2048]{2,1,0:T(8,128)(2,1)S(1)}, bf16[8,256,2048]{2,1,0:T(8,128)(2,1)S(1)}, u32[]{:S(2)}, u32[]{:S(2)}) %collective-permute-start.6) | collective-permute-done | bytes 8388640 | tf_op jit(solution)/shard_map/ppermute | solution.py:737
  661.1 5.1 add_convert_fusion.1
  666.1 4.0 collective-permute-start.7
  670.1 6.1 collective-permute-start.9
  676.2 57.7 %shard_map.218 = f32[256,2048]{1,0:T(8,128)} custom-call(bf16[2048,2048]{1,0:T(8,128)(2,1)} %get-tuple-element.28.a_ref, bf16[2048,2048]{1,0:T(8,128)(2,1)} %bitcast.9.w_ref.b_ref), custom_call_target="tpu_custom_call" | custom-call | flops 17179869184 | bytes 104857600 | tf_op jit(solution)/shard_map/pallas_call | solution.py:707
  733.9 2.3 multiply_reduce_fusion
  737.9 44.3 %shard_map.219 = (bf16[2048,256]{1,0:T(8,128)(2,1)}, bf16[256,2048]{1,0:T(8,128)(2,1)}) custom-call(bf16[256,2048]{1,0:T(8,128)(2,1)} %fusion.13.grad_ref, bf16[256,2048]{1,0:T(8,128)(2,1)} %w_ref.3, bf16[2048,256]{1,0:T(8,128)(2,1)} %copy-done.5), custom_call_target="tpu_custom_call" | custom-call | flops 4294967296 | bytes 157286400 | tf_op jit(solution)/shard_map/pallas_call | solution.py:596
  783.5 24.8 %shard_map.220.a_ref = bf16[2048,512]{1,0:T(8,128)(2,1)} custom-call(s32[1,16]{1,0:T(1,128)S(1)} %copy-done.4, bf16[2048,256]{1,0:T(8,128)(2,1)S(1)} %copy-done.11, bf16[2048,256]{1,0:T(8,128)(2,1)S(1)} %copy-done.6, bf16[2,2048,128]{2,1,0:T(8,128)(2,1)S(1)} %copy-done.8, bf16[2048,128]{1,0:T(8,128)(2,1)S(1)} %get-tuple-element.31.k_ref, ...), custom_call_target="tpu_custom_call" | custom-call | flops 8589934592 | bytes 29360128 | tf_op jit(solution)/shard_map/pallas_call | solution.py:248
  808.4 9.9 convolution_convert_fusion.1
  818.2 3.6 all-to-all-start.2
  821.9 7.8 add_convert_fusion.3
  829.6 2.7 collective-permute-start.10
  832.3 16.1 %all-to-all-done.2 = bf16[8,256,512]{2,1,0:T(8,128)(2,1)S(1)} async-done(((bf16[8,256,512]{2,1,0:T(8,128)(2,1)}), bf16[8,256,512]{2,1,0:T(8,128)(2,1)S(1)}, u32[]{:S(2)}, u32[]{:S(2)}) %all-to-all-start.2) | async-done | bytes 2097184 | tf_op jit(solution)/shard_map/all_to_all | solution.py:849
  848.4 2.6 collective-permute-start
  851.0 10.4 add_convert_fusion
  862.8 9.5 collective-permute-start.3
  872.3 46.1 %shard_map.221 = f32[256,2048]{1,0:T(8,128)} custom-call(bf16[2048,512]{1,0:T(8,128)(2,1)} %shard_map.220.a_ref, bf16[2048,512]{1,0:T(8,128)(2,1)} %bitcast.96), custom_call_target="tpu_custom_call" | custom-call | flops 4294967296 | bytes 104857600 | tf_op jit(solution)/shard_map/pallas_call | solution.py:707
  918.4 2.3 fusion.8
  920.7 143.8 %psum.7 = f32[2,2048]{1,0:T(2,128)S(1)} all-reduce(f32[2,2048]{1,0:T(2,128)S(1)} %pad_maximum_fusion.4), channel_id=1, replica_groups=mesh['grp'=8,'rep'=4] {'grp','rep'}, use_global_device_ids=true, to_apply=%region_6.7 | all-reduce | flops 4096 | bytes 32768 | tf_op jit(solution)/shard_map/psum | solution.py:863
  1064.5 3.0 add_convert_fusion.5
  1067.4 2.1 collective-permute-start.1
  1069.5 2.6 add_convert_fusion.7
  1073.7 5.7 add_convert_fusion.2
  1080.8 49.7 %shard_map.216 = f32[256,2048]{1,0:T(8,128)} custom-call(bf16[2048,1024]{1,0:T(8,128)(2,1)} %get-tuple-element.25.a_ref.hidden_ref, bf16[1024,2048]{1,0:T(8,128)(2,1)} %w_ref.2), custom_call_target="tpu_custom_call" | custom-call | flops 8589934592 | bytes 104857600 | tf_op jit(solution)/shard_map/pallas_call | solution.py:707
  1130.6 2.4 add_convert_fusion.4
  1138.7 2.6 fusion.11
  1141.3 99.0 %collective-permute-done.5 = bf16[256,2048]{1,0:T(8,128)(2,1)S(1)} collective-permute-done((bf16[256,2048]{1,0:T(8,128)(2,1)S(1)}, bf16[256,2048]{1,0:T(8,128)(2,1)S(1)}, u32[]{:S(2)}, u32[]{:S(2)}) %collective-permute-start.5) | collective-permute-done | bytes 1048608 | tf_op jit(solution)/shard_map/ppermute | solution.py:741
  1246.3 6.1 select_convert_fusion.1
  1252.4 4.5 select_convert_fusion
  1256.9 6.8 slice_bitcast_fusion
  1263.8 8.6 copy.42
  1272.4 4.3 copy.43
  (96 shorter events, 29.1 us)
Async XLA Ops:
  0.6 1.4 copy-start
  4.9 31.8 %all-to-all-start = ((bf16[256,8,512]{2,0,1:T(8,128)(2,1)}), bf16[256,8,512]{2,0,1:T(8,128)(2,1)S(1)}, u32[]{:S(2)}, u32[]{:S(2)}) async-start(bf16[256,8,512]{2,0,1:T(8,128)(2,1)} %pad_maximum_fusion.1), calls=%async_computation | async-start | bytes 4194304 | tf_op jit(solution)/shard_map/all_to_all | solution.py:788
  36.7 1.3 copy-start.24
  38.0 218.9 %all-to-all-start.1 = ((bf16[256,8,2048]{2,0,1:T(8,128)(2,1)}), bf16[256,8,2048]{2,0,1:T(8,128)(2,1)}, u32[]{:S(2)}, u32[]{:S(2)}) async-start(bf16[256,8,2048]{2,0,1:T(8,128)(2,1)} %pad_maximum_fusion), calls=%async_computation.1 | async-start | bytes 16777216 | tf_op jit(solution)/shard_map/all_to_all | solution.py:788
  173.8 4.4 copy-start.20
  178.1 9.3 copy-start.2
  178.2 8.0 copy-start.3
  178.2 9.3 copy-start.4
  206.0 1.0 copy-start.5
  207.0 1.0 copy-start.7
  208.0 0.8 copy-start.9
  208.8 44.9 %copy-start.17 = (bf16[1,256,2048]{2,1,0:T(8,128)(2,1)S(1)}, bf16[1,256,2048]{2,1,0:T(8,128)(2,1)}, u32[]{:S(2)}) copy-start(bf16[1,256,2048]{2,1,0:T(8,128)(2,1)} %param.13) | copy-start | bytes 3145732
  478.6 182.5 %collective-permute-start.6 = (bf16[8,256,2048]{2,1,0:T(8,128)(2,1)S(1)}, bf16[8,256,2048]{2,1,0:T(8,128)(2,1)S(1)}, u32[]{:S(2)}, u32[]{:S(2)}) collective-permute-start(bf16[8,256,2048]{2,1,0:T(8,128)(2,1)S(1)} %all_to_all.40), channel_id=1, source_target_pairs={{0,1},{3,2},{4,5},{7,6},{8,9},{11,10},{12,13},{15,14},{16,17},{19,... | collective-permute-start | bytes 25165832 | tf_op jit(solution)/shard_map/ppermute | solution.py:737
  666.1 184.9 %collective-permute-start.7 = (bf16[8,256,2048]{2,1,0:T(8,128)(2,1)}, bf16[8,256,2048]{2,1,0:T(8,128)(2,1)}, u32[]{:S(2)}, u32[]{:S(2)}) collective-permute-start(bf16[8,256,2048]{2,1,0:T(8,128)(2,1)} %add_convert_fusion.1), channel_id=1, source_target_pairs={{1,2},{2,1},{5,6},{6,5},{9,10},{10,9},{13,14},{14,13},{17,18},{18,... | collective-permute-start | bytes 25165832 | tf_op jit(solution)/shard_map/ppermute | solution.py:739
  670.1 63.8 %copy-start.12 = (f32[256,2048]{1,0:T(8,128)S(1)}, f32[256,2048]{1,0:T(8,128)}, u32[]{:S(2)}) copy-start(f32[256,2048]{1,0:T(8,128)} %get-tuple-element.42.mid_ref) | copy-start | bytes 6291460
  670.1 63.8 %copy-start.27 = (f32[2048]{0:T(1024)S(1)}, f32[2048]{0:T(1024)}, u32[]{:S(2)}) copy-start(f32[2048]{0:T(1024)} %param.25) | copy-start | bytes 24580
  670.1 151.7 %collective-permute-start.9 = (bf16[1024,2048]{1,0:T(8,128)(2,1)}, bf16[1024,2048]{1,0:T(8,128)(2,1)}, u32[]{:S(2)}, u32[]{:S(2)}) collective-permute-start(bf16[1024,2048]{1,0:T(8,128)(2,1)} %get-tuple-element.36), channel_id=1, source_target_pairs={{0,1},{3,2},{4,5},{7,6},{8,9},{11,10},{12,13},{15,14},{16,17},{19,... | collective-permute-start | bytes 12582920 | tf_op jit(solution)/shard_map/ppermute | solution.py:737
  733.9 2.3 copy-start.15
  733.9 2.5 copy-start.22
  737.9 44.4 %copy-start.6 = (bf16[2048,256]{1,0:T(8,128)(2,1)S(1)}, bf16[2048,256]{1,0:T(8,128)(2,1)}, u32[]{:S(2)}) copy-start(bf16[2048,256]{1,0:T(8,128)(2,1)} %copy-done.5) | copy-start | bytes 3145732
  737.9 44.4 %copy-start.8 = (bf16[2,2048,128]{2,1,0:T(8,128)(2,1)S(1)}, bf16[2,2048,128]{2,1,0:T(8,128)(2,1)}, u32[]{:S(2)}) copy-start(bf16[2,2048,128]{2,1,0:T(8,128)(2,1)} %copy-done.7) | copy-start | bytes 3145732
  737.9 44.4 %copy-start.10 = (bf16[2048,128]{1,0:T(8,128)(2,1)S(1)}, bf16[2048,128]{1,0:T(8,128)(2,1)}, u32[]{:S(2)}) copy-start(bf16[2048,128]{1,0:T(8,128)(2,1)} %copy-done.9) | copy-start | bytes 1572868
  782.3 1.2 copy-start.11
  818.2 30.2 %all-to-all-start.2 = ((bf16[8,256,512]{2,1,0:T(8,128)(2,1)}), bf16[8,256,512]{2,1,0:T(8,128)(2,1)S(1)}, u32[]{:S(2)}, u32[]{:S(2)}) async-start(bf16[8,256,512]{2,1,0:T(8,128)(2,1)} %bitcast.98), calls=%async_computation.2 | async-start | bytes 4194304 | tf_op jit(solution)/shard_map/all_to_all | solution.py:849
  829.6 244.1 %collective-permute-start.10 = (bf16[1024,2048]{1,0:T(8,128)(2,1)}, bf16[1024,2048]{1,0:T(8,128)(2,1)}, u32[]{:S(2)}, u32[]{:S(2)}) collective-permute-start(bf16[1024,2048]{1,0:T(8,128)(2,1)} %add_convert_fusion.3), channel_id=1, source_target_pairs={{1,2},{2,1},{5,6},{6,5},{9,10},{10,9},{13,14},{14,13},{17,18},{18,... | collective-permute-start | bytes 12582920 | tf_op jit(solution)/shard_map/ppermute | solution.py:739
  848.4 13.1 %copy-start.19 = (bf16[8,256,512]{2,1,0:T(8,128)(2,1)}, bf16[8,256,512]{2,1,0:T(8,128)(2,1)S(1)}, u32[]{:S(2)}) copy-start(bf16[8,256,512]{2,1,0:T(8,128)(2,1)S(1)} %all-to-all-done.2) | copy-start | bytes 6291460
  848.4 216.0 %collective-permute-start = (bf16[8,256,512]{2,1,0:T(8,128)(2,1)S(1)}, bf16[8,256,512]{2,1,0:T(8,128)(2,1)}, u32[]{:S(2)}, u32[]{:S(2)}) collective-permute-start(bf16[8,256,512]{2,1,0:T(8,128)(2,1)S(1)} %all-to-all-done.2), channel_id=1, source_target_pairs={{0,1},{3,2},{4,5},{7,6},{8,9},{11,10},{12,13},{15,14},{16,17},{19,... | collective-permute-start | bytes 6291464 | tf_op jit(solution)/shard_map/ppermute | solution.py:737
  861.5 390.9 %collective-permute-start.8 = (bf16[8,256,2048]{2,1,0:T(8,128)(2,1)}, bf16[8,256,2048]{2,1,0:T(8,128)(2,1)}, u32[]{:S(2)}, u32[]{:S(2)}) collective-permute-start(bf16[8,256,2048]{2,1,0:T(8,128)(2,1)} %add_convert_fusion), channel_id=1, source_target_pairs={{1,0},{2,3},{5,4},{6,7},{9,8},{10,11},{13,12},{14,15},{17,16},{18,... | collective-permute-start | bytes 25165832 | tf_op jit(solution)/shard_map/ppermute | solution.py:741
  862.8 55.6 %copy-start.18 = (bf16[1,256,2048]{2,1,0:T(8,128)(2,1)S(1)}, bf16[1,256,2048]{2,1,0:T(8,128)(2,1)}, u32[]{:S(2)}) copy-start(bf16[1,256,2048]{2,1,0:T(8,128)(2,1)} %param.13) | copy-start | bytes 3145732
  862.8 55.6 %copy-start.28 = (f32[2048]{0:T(1024)S(1)}, f32[2048]{0:T(1024)}, u32[]{:S(2)}) copy-start(f32[2048]{0:T(1024)} %param.24) | copy-start | bytes 24580
  862.8 206.7 %collective-permute-start.3 = (bf16[256,2048]{1,0:T(8,128)(2,1)}, bf16[256,2048]{1,0:T(8,128)(2,1)}, u32[]{:S(2)}, u32[]{:S(2)}) collective-permute-start(bf16[256,2048]{1,0:T(8,128)(2,1)} %get-tuple-element.34), channel_id=1, source_target_pairs={{0,1},{3,2},{4,5},{7,6},{8,9},{11,10},{12,13},{15,14},{16,17},{19,... | collective-permute-start | bytes 3145736 | tf_op jit(solution)/shard_map/ppermute | solution.py:737
  1064.5 5.0 copy-start.26
  1067.4 63.1 %collective-permute-start.1 = (bf16[8,256,512]{2,1,0:T(8,128)(2,1)S(1)}, bf16[8,256,512]{2,1,0:T(8,128)(2,1)}, u32[]{:S(2)}, u32[]{:S(2)}) collective-permute-start(bf16[8,256,512]{2,1,0:T(8,128)(2,1)S(1)} %add_convert_fusion.5), channel_id=1, source_target_pairs={{1,2},{2,1},{5,6},{6,5},{9,10},{10,9},{13,14},{14,13},{17,18},{18,... | collective-permute-start | bytes 6291464 | tf_op jit(solution)/shard_map/ppermute | solution.py:739
  1072.1 62.4 %collective-permute-start.4 = (bf16[256,2048]{1,0:T(8,128)(2,1)}, bf16[256,2048]{1,0:T(8,128)(2,1)}, u32[]{:S(2)}, u32[]{:S(2)}) collective-permute-start(bf16[256,2048]{1,0:T(8,128)(2,1)} %add_convert_fusion.7), channel_id=1, source_target_pairs={{1,2},{2,1},{5,6},{6,5},{9,10},{10,9},{13,14},{14,13},{17,18},{18,... | collective-permute-start | bytes 3145736 | tf_op jit(solution)/shard_map/ppermute | solution.py:739
  1079.5 166.8 %collective-permute-start.11 = (bf16[1024,2048]{1,0:T(8,128)(2,1)S(1)}, bf16[1024,2048]{1,0:T(8,128)(2,1)}, u32[]{:S(2)}, u32[]{:S(2)}) collective-permute-start(bf16[1024,2048]{1,0:T(8,128)(2,1)S(1)} %add_convert_fusion.2), channel_id=1, source_target_pairs={{1,0},{2,3},{5,4},{6,7},{9,8},{10,11},{13,12},{14,15},{17,16},{18,... | collective-permute-start | bytes 12582920 | tf_op jit(solution)/shard_map/ppermute | solution.py:741
  1130.5 8.1 copy-start.13
  1130.5 8.1 copy-start.16
  1130.5 8.1 copy-start.21
  1130.5 8.1 copy-start.23
  1130.6 8.1 copy-start.25
  1132.9 108.8 %collective-permute-start.2 = (bf16[8,256,512]{2,1,0:T(8,128)(2,1)S(1)}, bf16[8,256,512]{2,1,0:T(8,128)(2,1)S(1)}, u32[]{:S(2)}, u32[]{:S(2)}) collective-permute-start(bf16[8,256,512]{2,1,0:T(8,128)(2,1)S(1)} %add_convert_fusion.4), channel_id=1, source_target_pairs={{1,0},{2,3},{5,4},{6,7},{9,8},{10,11},{13,12},{14,15},{17,16},{18,... | collective-permute-start | bytes 6291464 | tf_op jit(solution)/shard_map/ppermute | solution.py:741
  1136.4 103.8 %collective-permute-start.5 = (bf16[256,2048]{1,0:T(8,128)(2,1)S(1)}, bf16[256,2048]{1,0:T(8,128)(2,1)S(1)}, u32[]{:S(2)}, u32[]{:S(2)}) collective-permute-start(bf16[256,2048]{1,0:T(8,128)(2,1)S(1)} %add_convert_fusion.6), channel_id=1, source_target_pairs={{1,0},{2,3},{5,4},{6,7},{9,8},{10,11},{13,12},{14,15},{17,16},{18,... | collective-permute-start | bytes 3145736 | tf_op jit(solution)/shard_map/ppermute | solution.py:741
  1263.8 8.6 copy-start.14
  1272.4 4.3 copy-start.1

commit v3 on v2

--- a/solution.py
+++ b/solution.py
@@ -15,6 +15,7 @@
 TO_EXP2 = SCORE_SCALE * LOG2E
 NEG = -1e30
 
+MESH = pl.DeviceIdType.MESH
 f32 = jnp.float32
 bf16 = jnp.bfloat16
 
@@ -62,8 +63,8 @@
 def attend_kernel(
     heads, cuts, block,
     order_ref, qkv_ref, cos_ref, sin_ref, piece_ref, piece_col_ref,
-    out_ref, q_ref, k_ref, v_ref, lse_ref,
-    scores, placed,
+    out_ref, q_ref, k_ref, v_ref, lse_ref, placed,
+    scores,
 ):
     length = qkv_ref.shape[0]
     cut = length // cuts
@@ -150,13 +151,11 @@
             jax.ShapeDtypeStruct((length, HD), bf16),
             jax.ShapeDtypeStruct((length, HD), bf16),
             jax.ShapeDtypeStruct((heads, length), f32),
+            jax.ShapeDtypeStruct((length, heads * HD), bf16),
         ),
         in_specs=[pl.BlockSpec(memory_space=pltpu.SMEM)] + vmem_specs(5),
-        out_specs=tuple(vmem_specs(5)),
-        scratch_shapes=[
-            pltpu.VMEM((length // block, heads * block, block), f32),
-            pltpu.VMEM((length, heads * HD), bf16),
-        ],
+        out_specs=tuple(vmem_specs(6)),
+        scratch_shapes=[pltpu.VMEM((length // block, heads * block, block), f32)],
         compiler_params=pltpu.CompilerParams(vmem_limit_bytes=48 * 2**20),
         cost_estimate=pl.CostEstimate(
             flops=3 * heads * length * length * HD, bytes_accessed=10 * length * HD * heads * 4,
@@ -165,30 +164,275 @@
     )(order, qkv, cosine, sine, piece, piece_col)
 
 
+CHUNKS = 15
+
+
+def is_middle():
+    rank = lax.axis_index("rep")
+    return (rank == 1) | (rank == 2)
+
+
+def is_end():
+    rank = lax.axis_index("rep")
+    return (rank == 0) | (rank == 3)
+
+
+class NoLine:
+    ticks = 0
+
+    def greet(self, barrier, others):
+        if others:
+            pl.semaphore_wait(barrier, others)
+
+    def open(self, number):
+        pass
+
+    def close(self, number):
+        pass
+
+    def finish(self):
+        pass
+
+
+class Line:
+    def __init__(self, first, ticks, picks, refs, outs, scratch):
+        self.first, self.ticks, self.picks, self.refs, self.outs = first, ticks, picks, refs, outs
+        self.inward, self.across, self.own, self.pair, self.total, self.sems, self.local = scratch
+        rank = lax.axis_index("rep")
+        self.partner = {"rep": rank + 1 - 2 * (rank % 2)}
+        self.peer = {"rep": 3 - rank}
+        self.slots = line_slots(first, ticks)
+
+    def greet(self, barrier, others):
+        pl.semaphore_signal(barrier, inc=1, device_id=self.partner, device_id_type=MESH)
+
+        @pl.when(is_middle())
+        def _():
+            pl.semaphore_signal(barrier, inc=1, device_id=self.peer, device_id_type=MESH)
+            pl.semaphore_wait(barrier, others + 2)
+
+        @pl.when(is_end())
+        def _():
+            pl.semaphore_wait(barrier, others + 1)
+
+    def remote(self, hop, number, src, dst, device):
+        return pltpu.make_async_remote_copy(
+            src_ref=src, dst_ref=dst, send_sem=self.sems.at[0, hop, number],
+            recv_sem=self.sems.at[1, hop, number], device_id=device, device_id_type=MESH,
+        )
+
+    def hops(self, number):
+        tick = self.first + number
+        term = pair = total = None
+        if tick < CHUNKS:
+            which, pick = self.picks[tick]
+            term = (
+                lambda: self.remote(
+                    0, number, pick(self.refs[which]), self.inward.at[number], self.partner
+                ),
+                lambda: pltpu.make_async_copy(
+                    pick(self.refs[which]), self.own.at[number % 2], self.local.at[0, number]
+                ),
+            )
+        if 1 <= tick <= CHUNKS:
+            before = self.refs["pair"] if number == 0 else self.pair.at[(number - 1) % 2]
+            pair = (
+                lambda: self.remote(1, number, before, self.across.at[number], self.peer),
+                lambda: pltpu.make_async_copy(before, self.pair.at[2], self.local.at[1, number]),
+            )
+        if 2 <= tick <= CHUNKS + 1:
+            done = self.refs["total"] if number == 0 else self.total.at[(number - 1) % 2]
+            slot = self.outs[tick - 2]
+            total = (
+                lambda: self.remote(2, number, done, slot, self.partner),
+                lambda: pltpu.make_async_copy(done, slot, self.local.at[2, number]),
+            )
+        return term, pair, total
+
+    def open(self, number):
+        if number >= self.ticks:
+            return
+        term, pair, total = self.hops(number)
+
+        @pl.when(is_end())
+        def _():
+            if term:
+                term[0]().start()
+
+        @pl.when(is_middle())
+        def _():
+            if pair:
+                pair[0]().start()
+            if total:
+                total[0]().start()
+                total[1]().start()
+            if term:
+                term[1]().start()
+            if pair and number == 0:
+                pair[1]().start()
+
+    def close(self, number):
+        if number >= self.ticks:
+            return
+        term, pair, total = self.hops(number)
+
+        def add(into, first, second):
+            def one(g, _):
+                into[g] = (first[g].astype(f32) + second[g].astype(f32)).astype(bf16)
+                return 0
+
+            lax.fori_loop(0, into.shape[0], one, 0)
+
+        @pl.when(is_end())
+        def _():
+            if term:
+                term[0]().wait_send()
+            if total:
+                total[0]().wait_recv()
+
+        @pl.when(is_middle())
+        def _():
+            if total:
+                total[0]().wait_send()
+                total[1]().wait()
+            if pair:
+                pair[0]().wait_send()
+                pair[0]().wait_recv()
+                if number == 0:
+                    pair[1]().wait()
+                before = 2 if number == 0 else (number - 1) % 2
+                add(self.total.at[number % 2], self.pair.at[before], self.across.at[number])
+            if term:
+                term[1]().wait()
+                term[0]().wait_recv()
+                add(self.pair.at[number % 2], self.own.at[number % 2], self.inward.at[number])
+
+    def finish(self):
+        last = self.ticks - 1
+        tick = self.first + last
+
+        @pl.when(is_middle())
+        def _():
+            if tick < CHUNKS:
+                keep = pltpu.make_async_copy(
+                    self.pair.at[last % 2], self.outs["pair"], self.local.at[0, last]
+                )
+                keep.start()
+                keep.wait()
+            if 1 <= tick <= CHUNKS:
+                keep = pltpu.make_async_copy(
+                    self.total.at[last % 2], self.outs["total"], self.local.at[1, last]
+                )
+                keep.start()
+                keep.wait()
+
+
+def line_slots(first, ticks):
+    return [t - 2 for t in range(first, first + ticks) if 2 <= t <= CHUNKS + 1]
+
+
+class Sums:
+    def __init__(self, shape):
+        self.shape, self.tick, self.pair, self.total, self.done = shape, 0, None, None, {}
+
+
+def run(kernel, ins, outs, scratch, number, cost, sums=None, ticks=0, arrays=(), picks=None, vmem=58):
+    ins, outs, scratch = list(ins), list(outs), list(scratch)
+    counts = (len(ins), len(outs), len(scratch))
+    first = sums.tick if ticks else 0
+    names_in, names_out = [], []
+    if ticks:
+        last = first + ticks - 1
+        chunk = jax.ShapeDtypeStruct(sums.shape, bf16)
+        for name, array in arrays:
+            names_in.append(name)
+            ins.append((array, pl.ANY))
+        if 1 <= first <= CHUNKS:
+            names_in.append("pair")
+            ins.append((sums.pair, pl.ANY))
+        if 2 <= first <= CHUNKS + 1:
+            names_in.append("total")
+            ins.append((sums.total, pl.ANY))
+        names_out = line_slots(first, ticks)
+        if last < CHUNKS:
+            names_out.append("pair")
+        if 1 <= last <= CHUNKS:
+            names_out.append("total")
+        outs += [(chunk, pl.ANY)] * len(names_out)
+        scratch += [
+            pltpu.VMEM((ticks,) + sums.shape, bf16),
+            pltpu.VMEM((ticks,) + sums.shape, bf16),
+            pltpu.VMEM((2,) + sums.shape, bf16),
+            pltpu.VMEM((3,) + sums.shape, bf16),
+            pltpu.VMEM((2,) + sums.shape, bf16),
+            pltpu.SemaphoreType.DMA((2, 3, ticks)),
+            pltpu.SemaphoreType.DMA((3, ticks)),
+        ]
+
+    def body(*refs):
+        in_refs, rest = refs[: len(ins)], refs[len(ins) :]
+        out_refs, scratch_refs = rest[: len(outs)], rest[len(outs) :]
+        line = NoLine()
+        if ticks:
+            line = Line(
+                first, ticks, picks, dict(zip(names_in, in_refs[counts[0] :])),
+                dict(zip(names_out, out_refs[counts[1] :])), scratch_refs[counts[2] :],
+            )
+        kernel(in_refs[: counts[0]], out_refs[: counts[1]], scratch_refs[: counts[2]], line)
+
+    results = pl.pallas_call(
+        body,
+        out_shape=tuple(shape for shape, _ in outs),
+        in_specs=[pl.BlockSpec(memory_space=space) for _, space in ins],
+        out_specs=tuple(pl.BlockSpec(memory_space=space) for _, space in outs),
+        scratch_shapes=scratch,
+        compiler_params=pltpu.CompilerParams(
+            vmem_limit_bytes=vmem * 2**20,
+            **({} if number is None else {"collective_id": number, "has_side_effects": True}),
+        ),
+        cost_estimate=pl.CostEstimate(
+            flops=cost[0], bytes_accessed=cost[1], transcendentals=cost[2]
+        ),
+    )(*[array for array, _ in ins])
+    for name, result in zip(names_out, results[counts[1] :]):
+        if name == "pair":
+            sums.pair = result
+        elif name == "total":
+            sums.total = result
+        else:
+            sums.done[name] = result
+    if ticks:
+        sums.tick += ticks
+    return results[: counts[1]]
+
+
+SMEM, VMEM, ANY = pltpu.SMEM, pltpu.VMEM, pl.ANY
+
+
 def attend_back_kernel(
-    heads, cuts, block,
-    order_ref, grad_ref, out_ref, q_ref, k_ref, v_ref, lse_ref, cos_ref, sin_ref,
-    piece_ref, piece_col_ref,
-    grad_qkv_ref,
-    grads, centers, grad_q, placed,
+    heads, block, ins, outs, scratch, line
 ):
+    grad_ref, out_ref, q_ref, k_ref, v_ref, lse_ref, cos_ref, sin_ref, piece_ref, piece_col_ref = ins
+    (grad_qkv_ref,) = outs
+    grads, centers, grad_q = scratch
+    if line.ticks:
+        line.greet(pltpu.get_barrier_semaphore(), 0)
+        line.open(0)
     length = grad_ref.shape[0]
-    cut = length // cuts
     blocks = length // block
 
-    def place_cut(r, _):
-        src = pl.ds(pl.multiple_of(r * cut, cut), cut)
-        dst = pl.ds(pl.multiple_of(order_ref[0, r] * cut, cut), cut)
+    def take_block(i, _):
+        rows = pl.ds(pl.multiple_of(i * block, block), block)
         for h in range(heads):
-            grad = grad_ref[src, h * HD : (h + 1) * HD].astype(bf16)
-            grads[h, dst, :] = grad
-            product = grad.astype(f32) * out_ref[src, h * HD : (h + 1) * HD].astype(f32)
-            centers[h, dst, :] = jnp.broadcast_to(
-                jnp.sum(product, 1, keepdims=True), (cut, HD)
+            grad = grad_ref[rows, h * HD : (h + 1) * HD].astype(bf16)
+            grads[h, rows, :] = grad
+            product = grad.astype(f32) * out_ref[rows, h * HD : (h + 1) * HD].astype(f32)
+            centers[h, rows, :] = jnp.broadcast_to(
+                jnp.sum(product, 1, keepdims=True), (block, HD)
             )
         return 0
 
-    lax.fori_loop(0, cuts, place_cut, 0)
+    lax.fori_loop(0, blocks, take_block, 0)
     grad_q[...] = jnp.zeros_like(grad_q)
 
     def key_block(j, _):
@@ -223,48 +467,71 @@
         )
         grad_key = grad_key * SCORE_SCALE
         grad_key = grad_key * cos_ref[cols, :] - pltpu.roll(grad_key, HD // 2, 1) * sin_ref[cols, :]
-        placed[cols, heads * HD : (heads + 1) * HD] = grad_key.astype(bf16)
-        placed[cols, (heads + 1) * HD :] = grad_value.astype(bf16)
+        grad_qkv_ref[cols, heads * HD : (heads + 1) * HD] = grad_key.astype(bf16)
+        grad_qkv_ref[cols, (heads + 1) * HD :] = grad_value.astype(bf16)
         return 0
 
     lax.fori_loop(0, blocks, key_block, 0)
 
-    def store_cut(r, _):
-        dst = pl.ds(pl.multiple_of(r * cut, cut), cut)
-        src = pl.ds(pl.multiple_of(order_ref[0, r] * cut, cut), cut)
+    def turn_back(i, _):
+        rows = pl.ds(pl.multiple_of(i * block, block), block)
         for h in range(heads):
-            grad = grad_q[h, src, :] * SCORE_SCALE
-            grad = grad * cos_ref[src, :] - pltpu.roll(grad, HD // 2, 1) * sin_ref[src, :]
-            grad_qkv_ref[dst, h * HD : (h + 1) * HD] = grad.astype(bf16)
-        grad_qkv_ref[dst, heads * HD :] = placed[src, heads * HD :]
+            grad = grad_q[h, rows, :] * SCORE_SCALE
+            grad = grad * cos_ref[rows, :] - pltpu.roll(grad, HD // 2, 1) * sin_ref[rows, :]
+            grad_qkv_ref[rows, h * HD : (h + 1) * HD] = grad.astype(bf16)
         return 0
 
-    lax.fori_loop(0, cuts, store_cut, 0)
-
-
-def attend_back(order, grad, out, query, key, value, lse, cosine, sine, piece, piece_col, heads):
+    lax.fori_loop(0, blocks, turn_back, 0)
+    if line.ticks:
+        line.close(0)
+        line.finish()
+
+
+def take_cuts_kernel(cuts, holder_ref, rows_ref, out_ref):
+    cut = out_ref.shape[0] // cuts
+
+    def one(p, _):
+        src = pl.ds(pl.multiple_of(holder_ref[0, p] * cut, cut), cut)
+        out_ref[pl.ds(pl.multiple_of(p * cut, cut), cut), :] = rows_ref[src, :]
+        return 0
+
+    lax.fori_loop(0, cuts, one, 0)
+
+
+def take_cuts(holder, rows):
+    return pl.pallas_call(
+        functools.partial(take_cuts_kernel, holder.shape[1]),
+        out_shape=jax.ShapeDtypeStruct(rows.shape, rows.dtype),
+        in_specs=[pl.BlockSpec(memory_space=pltpu.SMEM)] + vmem_specs(1),
+        out_specs=pl.BlockSpec(memory_space=pltpu.VMEM),
+        cost_estimate=pl.CostEstimate(
+            flops=0, bytes_accessed=2 * rows.size * rows.dtype.itemsize, transcendentals=0
+        ),
+    )(holder, rows)
+
+
+def attend_back(
+    order, grad, out, query, key, value, lse, cosine, sine, piece, piece_col, heads, **line
+):
+    cuts = jnp.arange(order.shape[1], dtype=order.dtype)
+    holder = jnp.sum(jnp.where(order[0][None, :] == cuts[:, None], cuts[None, :], 0), 1)[None, :]
     length = grad.shape[0]
     block = min(512, length)
-    return pl.pallas_call(
-        functools.partial(attend_back_kernel, heads, order.shape[1], block),
-        out_shape=jax.ShapeDtypeStruct((length, (heads + 2) * HD), bf16),
-        in_specs=[pl.BlockSpec(memory_space=pltpu.SMEM)] + vmem_specs(10),
-        out_specs=pl.BlockSpec(memory_space=pltpu.VMEM),
-        scratch_shapes=[
+    tall = [take_cuts(holder, grad), out, query, key, value, lse, cosine, sine, piece, piece_col]
+    grad_qkv = run(
+        functools.partial(attend_back_kernel, heads, block),
+        [(array, VMEM) for array in tall],
+        [(jax.ShapeDtypeStruct((length, (heads + 2) * HD), bf16), VMEM)],
+        [
             pltpu.VMEM((heads, length, HD), bf16),
             pltpu.VMEM((heads, length, HD), f32),
             pltpu.VMEM((heads, length, HD), f32),
-            pltpu.VMEM((length, (heads + 2) * HD), bf16),
         ],
-        compiler_params=pltpu.CompilerParams(vmem_limit_bytes=48 * 2**20),
-        cost_estimate=pl.CostEstimate(
-            flops=8 * heads * length * length * HD, bytes_accessed=14 * length * HD * heads * 4,
-            transcendentals=heads * length * length // 2,
-        ),
-    )(order, grad, out, query, key, value, lse, cosine, sine, piece, piece_col)
-
-
-MESH = pl.DeviceIdType.MESH
+        line.pop("number", None),
+        (8 * heads * length * length * HD, 14 * length * HD * heads * 4, heads * length * length // 2),
+        **line,
+    )[0]
+    return take_cuts(order, grad_qkv)
 
 
 def place_in_group():
@@ -283,17 +550,21 @@
     return pl.ds(pl.multiple_of(first, 2 * rows), 2 * rows)
 
 
-def greet_group():
+NEIGHBOURS = ((0, 0, 1), (0, 1, 0), (1, 0, 0))
+EVERYONE = tuple((n // 4, (n // 2) % 2, n % 2) for n in range(1, 8))
+
+
+def greet_group(line, flips=NEIGHBOURS):
     barrier = pltpu.get_barrier_semaphore()
-    for flips in ((0, 0, 1), (0, 1, 0), (1, 0, 0)):
-        pl.semaphore_signal(barrier, inc=1, device_id={"grp": other(*flips)}, device_id_type=MESH)
-    pl.semaphore_wait(barrier, 3)
+    for flip in flips:
+        pl.semaphore_signal(barrier, inc=1, device_id={"grp": other(*flip)}, device_id_type=MESH)
+    line.greet(barrier, len(flips))
 
 
 SIBLING, ALONG_X, ALONG_Y, ACROSS = (0, 0), (0, 1), (1, 0), (1, 1)
 
 
-def gather_rows(rows, all_ref, sends, recvs, on_chip):
+def gather_rows(rows, all_ref, sends, recvs, on_chip, line):
     half = rows // 2
 
     def block(chip, core, part=None):
@@ -341,6 +612,8 @@
     send(9, ALONG_X, 0, 0, to_s)
     landed(4, ALONG_Y, 0, 1)
     send(10, ALONG_Y, 0, 1, to_s)
+    line.close(0)
+    line.open(1)
     landed(7, ALONG_X, 1, 1)
     landed(9, ALONG_X, 1, 0)
     on_chip(*ALONG_X)
@@ -356,6 +629,8 @@
     on_chip(*ACROSS)
     for one in started:
         one.wait_send()
+    line.close(1)
+    line.finish()
 
 
 GATHER_COPIES = 13
@@ -381,12 +656,6 @@
     def finish(self):
         for one in self.open:
             one.wait()
-
-
-def comm_params(number, vmem=56):
-    return pltpu.CompilerParams(
-        collective_id=number, has_side_effects=True, vmem_limit_bytes=vmem * 2**20
-    )
 
 
 def gather_scratch(rows, width, moves):
@@ -398,53 +667,52 @@
     ]
 
 
-def any_specs(count):
-    return [pl.BlockSpec(memory_space=pl.ANY)] * count
-
-
 def own_rows(rows):
     return pl.ds(pl.multiple_of(other(0, 0, 0) * rows, rows), rows)
 
 
-def gather_normed_kernel(x_ref, gain_ref, all_ref, held, sends, recvs, sems):
+def gather_normed_kernel(ins, outs, scratch, line):
+    x_ref, gain_ref = ins
+    (all_ref,) = outs
+    held, sends, recvs, sems = scratch
     rows = x_ref.shape[0]
     moves = Moves(sems)
     held[own_rows(rows), :] = rms_normed(x_ref[...].astype(f32), gain_ref[...]).astype(bf16)
-    greet_group()
+    greet_group(line)
+    line.open(0)
 
     def on_chip(*chip):
         where = chip_rows(*chip, rows)
         moves.later(held.at[where, :], all_ref.at[where, :])
 
-    gather_rows(rows, held, sends, recvs, on_chip)
+    gather_rows(rows, held, sends, recvs, on_chip, line)
     moves.finish()
 
 
-def gather_normed(x, gain, number):
+def gather_normed(x, gain, **line):
     rows, width = x.shape
-    return pl.pallas_call(
+    return run(
         gather_normed_kernel,
-        out_shape=jax.ShapeDtypeStruct((8 * rows, width), bf16),
-        in_specs=vmem_specs(2),
-        out_specs=pl.BlockSpec(memory_space=pl.ANY),
-        scratch_shapes=gather_scratch(rows, width, 4),
-        compiler_params=comm_params(number),
-        cost_estimate=pl.CostEstimate(
-            flops=0, bytes_accessed=150 * rows * width * 2, transcendentals=0
-        ),
-    )(x, gain)
-
-
-def feed_forward_kernel(
-    tile, mid_ref, gain_ref, w_ref, all_ref, hidden_ref, up_part_ref, gate_part_ref,
-    held, sends, recvs, sems, weight, hidden, up_part, gate_part,
-):
+        [(x, VMEM), (gain, VMEM)],
+        [(jax.ShapeDtypeStruct((8 * rows, width), bf16), ANY)],
+        gather_scratch(rows, width, 4),
+        line.pop("number"),
+        (0, 150 * rows * width * 2, 0),
+        **line,
+    )[0]
+
+
+def feed_forward_kernel(tile, ins, outs, scratch, line):
+    mid_ref, gain_ref, w_ref = ins
+    all_ref, hidden_ref, up_part_ref, gate_part_ref = outs
+    held, sends, recvs, sems, weight, hidden, up_part, gate_part = scratch
     rows = mid_ref.shape[0]
     inner = hidden.shape[1]
     moves = Moves(sems)
     weight_copy = moves.start(w_ref, weight)
     held[own_rows(rows), :] = rms_normed(mid_ref[...], gain_ref[...]).astype(bf16)
-    greet_group()
+    greet_group(line)
+    line.open(0)
 
     def on_chip(*chip):
         where = chip_rows(*chip, rows)
@@ -469,34 +737,31 @@
         for src, dst in ((hidden, hidden_ref), (up_part, up_part_ref), (gate_part, gate_part_ref)):
             moves.later(src.at[where, :], dst.at[where, :])
 
-    gather_rows(rows, held, sends, recvs, on_chip)
+    gather_rows(rows, held, sends, recvs, on_chip, line)
     moves.finish()
 
 
-def feed_forward(mid, gain, cols_gate_up, number):
+def feed_forward(mid, gain, cols_gate_up, **line):
     rows, width = mid.shape
     inner = cols_gate_up.shape[1] // 2
     tall = jax.ShapeDtypeStruct((8 * rows, inner), bf16)
-    return pl.pallas_call(
+    return run(
         functools.partial(feed_forward_kernel, min(256, inner)),
-        out_shape=(jax.ShapeDtypeStruct((8 * rows, width), bf16), tall, tall, tall),
-        in_specs=vmem_specs(2) + any_specs(1),
-        out_specs=tuple(any_specs(4)),
-        scratch_shapes=gather_scratch(rows, width, 17)
+        [(mid, VMEM), (gain, VMEM), (cols_gate_up, ANY)],
+        [(jax.ShapeDtypeStruct((8 * rows, width), bf16), ANY)] + [(tall, ANY)] * 3,
+        gather_scratch(rows, width, 17)
         + [pltpu.VMEM(cols_gate_up.shape, bf16)]
         + [pltpu.VMEM((8 * rows, inner), bf16)] * 3,
-        compiler_params=comm_params(number),
-        cost_estimate=pl.CostEstimate(
-            flops=32 * rows * width * inner, bytes_accessed=150 * rows * width * 2,
-            transcendentals=8 * rows * inner,
-        ),
-    )(mid, gain, cols_gate_up)
-
-
-def feed_forward_back_kernel(
-    tile, grad_ref, w_ref, hidden_ref, up_part_ref, gate_part_ref, grad_gate_up_ref, down_ref,
-    held, sends, recvs, sems, weight, hidden, up_part, gate_part, grads, down, down_low,
-):
+        line.pop("number"),
+        (32 * rows * width * inner, 150 * rows * width * 2, 8 * rows * inner),
+        **line,
+    )
+
+
+def feed_forward_back_kernel(tile, ins, outs, scratch, line):
+    grad_ref, w_ref, hidden_ref, up_part_ref, gate_part_ref = ins
+    grad_gate_up_ref, down_ref = outs
+    held, sends, recvs, sems, weight, hidden, up_part, gate_part, grads, down, down_low = scratch
     rows = grad_ref.shape[0]
     inner, width = weight.shape
     moves = Moves(sems)
@@ -507,7 +772,8 @@
         )
     ]
     held[own_rows(rows), :] = grad_ref[...]
-    greet_group()
+    greet_group(line)
+    line.open(0)
 
     def on_chip(*chip):
         where = chip_rows(*chip, rows)
@@ -534,23 +800,22 @@
         lax.fori_loop(0, inner // tile, column, 0)
         moves.later(grads.at[where, :], grad_gate_up_ref.at[where, :])
 
-    gather_rows(rows, held, sends, recvs, on_chip)
+    gather_rows(rows, held, sends, recvs, on_chip, line)
     moves.later(down_low, down_ref)
     moves.finish()
 
 
-def feed_forward_back(grad, w_down, hidden, up_part, gate_part, number):
+def feed_forward_back(grad, w_down, hidden, up_part, gate_part, **line):
     rows, width = grad.shape
     inner = w_down.shape[0]
-    return pl.pallas_call(
+    return run(
         functools.partial(feed_forward_back_kernel, min(256, inner)),
-        out_shape=(
-            jax.ShapeDtypeStruct((8 * rows, 2 * inner), bf16),
-            jax.ShapeDtypeStruct((inner, width), bf16),
-        ),
-        in_specs=vmem_specs(1) + any_specs(4),
-        out_specs=tuple(any_specs(2)),
-        scratch_shapes=gather_scratch(rows, width, 9)
+        [(grad, VMEM)] + [(array, ANY) for array in (w_down, hidden, up_part, gate_part)],
+        [
+            (jax.ShapeDtypeStruct((8 * rows, 2 * inner), bf16), ANY),
+            (jax.ShapeDtypeStruct((inner, width), bf16), ANY),
+        ],
+        gather_scratch(rows, width, 9)
         + [pltpu.VMEM(w_down.shape, bf16)]
         + [pltpu.VMEM((8 * rows, inner), bf16)] * 3
         + [
@@ -558,22 +823,22 @@
             pltpu.VMEM(w_down.shape, f32),
             pltpu.VMEM(w_down.shape, bf16),
         ],
-        compiler_params=comm_params(number, 62),
-        cost_estimate=pl.CostEstimate(
-            flops=32 * rows * width * inner, bytes_accessed=150 * rows * width * 2,
-            transcendentals=0,
-        ),
-    )(grad, w_down, hidden, up_part, gate_part)
-
-
-def attended_back_kernel(
-    grad_ref, w_ref, attended_ref, grad_attended_ref, out_term_ref,
-    held, sends, recvs, sems, total,
-):
+        line.pop("number"),
+        (32 * rows * width * inner, 150 * rows * width * 2, 0),
+        vmem=62,
+        **line,
+    )
+
+
+def attended_back_kernel(ins, outs, scratch, line):
+    grad_ref, w_ref, attended_ref = ins
+    grad_attended_ref, out_term_ref = outs
+    held, sends, recvs, sems, total = scratch
     rows = grad_ref.shape[0]
     moves = Moves(sems)
     held[own_rows(rows), :] = grad_ref[...]
-    greet_group()
+    greet_group(line)
+    line.open(0)
 
     def on_chip(*chip):
         where = chip_rows(*chip, rows)
@@ -587,38 +852,86 @@
         else:
             total[...] += term
 
-    gather_rows(rows, held, sends, recvs, on_chip)
+    gather_rows(rows, held, sends, recvs, on_chip, line)
     moves.finish()
 
 
-def attended_back(grad, w_out, attended, number):
+def attended_back(grad, w_out, attended, **line):
     rows, width = grad.shape
-    return pl.pallas_call(
+    return run(
         attended_back_kernel,
-        out_shape=(
-            jax.ShapeDtypeStruct(attended.shape, bf16),
-            jax.ShapeDtypeStruct(w_out.shape, bf16),
-        ),
-        in_specs=vmem_specs(3),
-        out_specs=tuple(vmem_specs(2)),
-        scratch_shapes=gather_scratch(rows, width, 1) + [pltpu.VMEM(w_out.shape, f32)],
-        compiler_params=comm_params(number),
-        cost_estimate=pl.CostEstimate(
-            flops=32 * rows * width * w_out.shape[0], bytes_accessed=150 * rows * width * 2,
-            transcendentals=0,
-        ),
-    )(grad, w_out, attended)
-
-
-def scatter_kernel(
-    turned, tile,
-    a_ref, b_ref, out_ref,
-    part, to_s, from_s, to_chip, held, relay, last, sends, recvs,
-):
+        [(array, VMEM) for array in (grad, w_out, attended)],
+        [
+            (jax.ShapeDtypeStruct(attended.shape, bf16), VMEM),
+            (jax.ShapeDtypeStruct(w_out.shape, bf16), VMEM),
+        ],
+        gather_scratch(rows, width, 1) + [pltpu.VMEM(w_out.shape, f32)],
+        line.pop("number"),
+        (32 * rows * width * w_out.shape[0], 150 * rows * width * 2, 0),
+        **line,
+    )
+
+
+class WeightTerm:
+    def __init__(self, rows_ref, columns_ref, term_ref, scratch):
+        self.rows_ref, self.columns_ref, self.term_ref = rows_ref, columns_ref, term_ref
+        self.loaded, self.ready, self.sems = scratch
+        self.tile = self.loaded.shape[2]
+        for number in (0, 1):
+            self.load(number).start()
+
+    def load(self, number):
+        cols = slice(number * self.tile, (number + 1) * self.tile)
+        return pltpu.make_async_copy(
+            self.rows_ref.at[:, cols], self.loaded.at[number % 2], self.sems.at[0, number % 2]
+        )
+
+    def store(self, number):
+        return pltpu.make_async_copy(
+            self.ready.at[number % 2], self.term_ref.at[number], self.sems.at[1, number % 2]
+        )
+
+    def work(self, numbers):
+        for number in numbers:
+            at = number % 2
+            self.load(number).wait()
+            if number >= 2:
+                self.store(number - 2).wait()
+            width = self.columns_ref.shape[1]
+            step = min(256, width)
+
+            def column(t, _):
+                cols = pl.ds(pl.multiple_of(t * step, step), step)
+                term = over_tokens(self.loaded[at], self.columns_ref[:, cols])
+                self.ready[at, :, cols] = term.astype(bf16)
+                return 0
+
+            lax.fori_loop(0, width // step, column, 0)
+            self.store(number).start()
+            if number + 2 < 8:
+                self.load(number + 2).start()
+
+    def finish(self):
+        for number in (6, 7):
+            self.store(number).wait()
+
+
+def scatter_kernel(turned, tile, extra, ins, outs, scratch, line):
+    a_ref, b_ref = ins[:2]
+    out_ref = outs[0]
+    part, to_s, from_s, to_chip, held, relay, last, sends, recvs = scratch[:9]
     rows, width = out_ref.shape
     half = rows // 2
     _, _, core = place_in_group()
-    greet_group()
+    greet_group(line)
+    line.open(0)
+    if extra:
+        columns_ref = a_ref
+        if extra == "loaded":
+            columns_ref = scratch[12]
+            columns_copy = pltpu.make_async_copy(ins[3], columns_ref, scratch[13].at[0])
+            columns_copy.start()
+        term = WeightTerm(ins[2], columns_ref, outs[1], scratch[9:12])
     own_at = pl.multiple_of(core * rows, rows)
     other_at = pl.multiple_of((1 - core) * rows, rows)
     started = []
@@ -677,13 +990,21 @@
     to_chip[2, second, :] = own(1, 2).astype(bf16)
     send(7, to_chip.at[2, second, :], last.at[1, second, :], to_y)
     held[1] = own(0, 2)
+    if extra:
+        if extra == "loaded":
+            columns_copy.wait()
+        term.work((0, 1, 2))
     landed(5, relay.at[1])
     to_chip[1, second, :] = (held[0] + relay[1].astype(f32)).astype(bf16)
     send(8, to_chip.at[1, second, :], last.at[0, second, :], to_x)
     landed(4, relay.at[0])
     to_chip[2, first, :] = (held[1] + relay[0].astype(f32)).astype(bf16)
     send(9, to_chip.at[2, first, :], last.at[1, first, :], to_y)
+    line.close(0)
+    line.open(1)
     make(3, SIBLING)
+    if extra:
+        term.work((3, 4, 5, 6, 7))
     landed(3, from_s.at[3])
     for low in (0, 1):
         out_ref[low * half : (low + 1) * half, :] = own(low, 3)
@@ -697,49 +1018,182 @@
     out_ref[first, :] += last[1, first, :].astype(f32)
     for one in started:
         one.wait_send()
-
-
-def product_scattered(a, b, turned, number):
+    if extra:
+        term.finish()
+    line.close(1)
+    line.finish()
+
+
+def product_scattered(a, b, turned, extra=None, **line):
     length, depth = a.shape
     width = b.shape[0] if turned else b.shape[1]
     rows = length // 8
     tile = min(256, width)
-    return pl.pallas_call(
-        functools.partial(scatter_kernel, turned, tile),
-        out_shape=jax.ShapeDtypeStruct((rows, width), f32),
-        in_specs=vmem_specs(2),
-        out_specs=pl.BlockSpec(memory_space=pltpu.VMEM),
-        scratch_shapes=[
-            pltpu.VMEM((2 * rows, width), f32),
-            pltpu.VMEM((4, rows, width), bf16),
-            pltpu.VMEM((4, rows, width), bf16),
-            pltpu.VMEM((3, rows, width), bf16),
-            pltpu.VMEM((2, rows // 2, width), f32),
-            pltpu.VMEM((2, rows // 2, width), bf16),
-            pltpu.VMEM((2, rows, width), bf16),
-            pltpu.SemaphoreType.DMA((10,)),
-            pltpu.SemaphoreType.DMA((10,)),
+    ins = [(a, VMEM), (b, VMEM)]
+    outs = [(jax.ShapeDtypeStruct((rows, width), f32), VMEM)]
+    scratch = [
+        pltpu.VMEM((2 * rows, width), f32),
+        pltpu.VMEM((4, rows, width), bf16),
+        pltpu.VMEM((4, rows, width), bf16),
+        pltpu.VMEM((3, rows, width), bf16),
+        pltpu.VMEM((2, rows // 2, width), f32),
+        pltpu.VMEM((2, rows // 2, width), bf16),
+        pltpu.VMEM((2, rows, width), bf16),
+        pltpu.SemaphoreType.DMA((10,)),
+        pltpu.SemaphoreType.DMA((10,)),
+    ]
+    flops, kind = 2 * length * depth * width, None
+    if extra:
+        first, second = extra
+        kind = "own" if second is None else "loaded"
+        ins.append((first, ANY))
+        columns = a if second is None else second
+        tall = first.shape[1] // 8
+        outs.append((jax.ShapeDtypeStruct((8, tall, columns.shape[1]), bf16), ANY))
+        scratch += [
+            pltpu.VMEM((2, length, tall), bf16),
+            pltpu.VMEM((2, tall, columns.shape[1]), bf16),
+            pltpu.SemaphoreType.DMA((2, 2)),
+        ]
+        if second is not None:
+            ins.append((second, ANY))
+            scratch += [pltpu.VMEM(second.shape, bf16), pltpu.SemaphoreType.DMA((1,))]
+        flops += 2 * length * first.shape[1] * columns.shape[1]
+    return run(
+        functools.partial(scatter_kernel, turned, tile, kind), ins, outs, scratch,
+        line.pop("number"), (flops, 150 * rows * width * 2, 0), vmem=60, **line,
+    )
+
+
+def tail_kernel(ready, later, ins, outs, scratch, line):
+    qkv_ref, gains_ref = ins[:2]
+    chunk_refs = dict(zip(ready, ins[2:]))
+    gate_ref, up_ref, qkv_rows_ref, gains_out_ref = outs
+    from_group, mine, from_rep, sends, recvs, chunk_sems, local = scratch
+    me, rank = other(0, 0, 0), lax.axis_index("rep")
+    inner = gate_ref.shape[1] // 8
+    part = qkv_ref.shape[-1]
+    high = line.outs[later[0]].shape[1]
+    barrier = pltpu.get_barrier_semaphore()
+    for flip in range(1, 4):
+        pl.semaphore_signal(
+            barrier, inc=1, device_id={"rep": (rank + flip) % 4}, device_id_type=MESH
+        )
+    for flip in EVERYONE:
+        pl.semaphore_signal(barrier, inc=1, device_id={"grp": other(*flip)}, device_id_type=MESH)
+    pl.semaphore_wait(barrier, 10)
+    waits, moves = [], Moves(local)
+    line.refs["qkv"] = qkv_rows_ref
+
+    def send(kind, number, src, dst, device):
+        return pltpu.make_async_remote_copy(
+            src_ref=src, dst_ref=dst, send_sem=sends.at[kind, number],
+            recv_sem=recvs.at[kind, number], device_id=device, device_id_type=MESH,
+        )
+
+    own_qkv = qkv_rows_ref.at[me // 4, :, :, pl.ds(pl.multiple_of((me % 4) * part, part), part)]
+    qkv_copies, gain_copies = [], []
+    for number, flip in enumerate(EVERYONE):
+        target = other(*flip)
+        qkv_copies.append(send(0, number, qkv_ref.at[target], own_qkv, {"grp": target}))
+        qkv_copies[-1].start()
+    moves.later(qkv_ref.at[me], own_qkv)
+    line.open(0)
+    for number, flip in enumerate(EVERYONE):
+        target = other(*flip)
+        gain_copies.append(
+            send(1, number, gains_ref.at[target], from_group.at[me], {"grp": target})
+        )
+        gain_copies[-1].start()
+    from_group[me] = gains_ref[me]
+
+    def spread(chunk):
+        src = chunk_refs[chunk] if chunk in chunk_refs else line.outs[chunk]
+        number = chunk - 4
+        rows = slice(number * high, (number + 1) * high)
+        cols = pl.ds(pl.multiple_of(me * inner, inner), inner)
+        for which, dst in enumerate((gate_ref, up_ref)):
+            there = dst.at[rows, cols]
+            for flip in EVERYONE:
+                target = other(*flip)
+                pltpu.make_async_remote_copy(
+                    src_ref=src.at[target, :, which * inner : (which + 1) * inner], dst_ref=there,
+                    send_sem=chunk_sems.at[0, which, number], recv_sem=chunk_sems.at[1, which, number],
+                    device_id={"grp": target}, device_id_type=MESH,
+                ).start()
+            moves.later(src.at[me, :, which * inner : (which + 1) * inner], there)
+            seven = dst.at[rows, : 7 * inner]
+            waits.append(
+                pltpu.make_async_remote_copy(
+                    src_ref=seven, dst_ref=seven, send_sem=chunk_sems.at[0, which, number],
+                    recv_sem=chunk_sems.at[1, which, number],
+                    device_id={"grp": other(0, 0, 1)}, device_id_type=MESH,
+                )
+            )
+
+    for chunk in ready:
+        spread(chunk)
+    for one in gain_copies:
+        one.wait()
+    mine[rank] = sum(from_group[g] for g in range(8))
+    rep_copies = []
+    for step in range(1, 4):
+        target = (rank + step) % 4
+        rep_copies.append(
+            send(2, step, mine.at[rank], from_rep.at[step], {"rep": target})
+        )
+        rep_copies[-1].start()
+    for step, one in zip(range(1, 4), rep_copies):
+        one.wait()
+        mine[(rank + 4 - step) % 4] = from_rep[step]
+    gains_out_ref[...] = (mine[0] + mine[1]) + (mine[2] + mine[3])
+    line.close(0)
+    for number in range(1, line.ticks):
+        if line.first + number == CHUNKS - 2:
+            for one in qkv_copies:
+                one.wait()
+            moves.open.pop(0).wait()
+        line.open(number)
+        chunk = line.first + number - 3
+        if chunk in later:
+            spread(chunk)
+        line.close(number)
+    for one in waits:
+        one.wait_send()
+        one.wait_recv()
+    moves.finish()
+
+
+def tail(qkv_term, gains, chunks, inner, number, sums, ticks, arrays, picks):
+    first = sums.tick
+    ready = sorted(chunks)
+    later = [c for c in line_slots(first, ticks) if c < 12]
+    _, high, width = sums.shape
+    part = qkv_term.shape[-1]
+    wide = jax.ShapeDtypeStruct((8 * high, 8 * inner), bf16)
+    moved = jax.ShapeDtypeStruct((2,) + sums.shape, bf16)
+    picks = dict(picks)
+    for half in (0, 1):
+        picks[CHUNKS - 2 + half] = ("qkv", lambda ref, half=half: ref.at[half])
+    return run(
+        functools.partial(tail_kernel, ready, later),
+        [(qkv_term, ANY), (gains, VMEM)] + [(chunks[c], ANY) for c in ready],
+        [(wide, ANY), (wide, ANY), (moved, ANY), (jax.ShapeDtypeStruct(gains.shape[1:], f32), VMEM)],
+        [
+            pltpu.VMEM(gains.shape, f32),
+            pltpu.VMEM((4,) + gains.shape[1:], f32),
+            pltpu.VMEM((4,) + gains.shape[1:], f32),
+            pltpu.SemaphoreType.DMA((3, 7)),
+            pltpu.SemaphoreType.DMA((3, 7)),
+            pltpu.SemaphoreType.DMA((2, 2, 8)),
+            pltpu.SemaphoreType.DMA((17,)),
         ],
-        compiler_params=pltpu.CompilerParams(
-            collective_id=number, has_side_effects=True, vmem_limit_bytes=56 * 2**20
-        ),
-        cost_estimate=pl.CostEstimate(
-            flops=2 * length * depth * width,
-            bytes_accessed=100 * rows * width * 2, transcendentals=0,
-        ),
-    )(a, b)
-
-
-def sum_over_sequences(term, reps):
-    if reps != 4:
-        return lax.psum(term, "rep").astype(f32)
-    rank = lax.axis_index("rep")
-    inward = lax.ppermute(term, "rep", [(0, 1), (3, 2)])
-    pair = (term.astype(f32) + inward.astype(f32)).astype(bf16)
-    other = lax.ppermute(pair, "rep", [(1, 2), (2, 1)])
-    total = (pair.astype(f32) + other.astype(f32)).astype(bf16)
-    outward = lax.ppermute(total, "rep", [(1, 0), (2, 3)])
-    return jnp.where((rank == 0) | (rank == 3), outward, total).astype(f32)
+        number, (0, 200 * 8 * high * width * 2, 0), sums=sums, ticks=ticks, arrays=arrays, picks=picks,
+    )
+
+
+def sum_over_sequences(term):
+    return lax.psum(term, "rep").astype(f32)
 
 
 def on_device(
@@ -771,14 +1225,12 @@
     piece_col = jnp.broadcast_to(piece_ids.reshape(length, 1), (length, HD))
     cosine, sine = turn_tables(length)
 
-    near = groups == 8
+    near = groups == 8 and reps == 4 and copies == 1
 
     def gather(rows):
         return lax.all_gather(rows, "grp", axis=0, tiled=True)
 
-    def scatter(first, second, turned, number):
-        if near:
-            return product_scattered(first, second, turned, number)
+    def scatter(first, second, turned):
         term = against_rows(first, second) if turned else matmul_f32(first, second)
         return lax.psum_scatter(
             term.astype(bf16), "grp", scatter_dimension=0, tiled=True
@@ -802,66 +1254,131 @@
         jnp.concatenate([per_group(w_query), per_kv_head(w_key), per_kv_head(w_value)], -1)
     )
     if near:
-        normed_one = gather_normed(x_rows, attn_gain, 1)
+        normed_one = gather_normed(x_rows, attn_gain, number=1)
     else:
         normed_one = gather(rms_normed(x_flat, attn_gain).astype(bf16))
     qkv = matmul_f32(normed_one, cols_qkv)
-    attended, query, key, value, lse = attend(
+    attended, query, key, value, lse, attended_placed = attend(
         cut_order, qkv, cosine, sine, piece_ids, piece_col, heads
     )
     cols_gate_up = to_columns(jnp.concatenate([per_group(w_gate), per_group(w_up)], -1))
-    mid = x_flat + scatter(attended, w_out, False, 2)
+    if near:
+        out_sum = product_scattered(attended, w_out, False, number=2)[0]
+    else:
+        out_sum = scatter(attended, w_out, False)
+    mid = x_flat + out_sum
     inv_two = lax.rsqrt(jnp.mean(mid * mid, -1, keepdims=True) + EPS)
     unit_two = mid * inv_two
     grad_out = cotangent.reshape(local_rows, model_width)
+
+    def finish_two(grad_two):
+        return norm_back(grad_out.astype(f32), grad_two, unit_two, inv_two, gain_ffn)
+
+    def finish_one(grad_mid, grad_one):
+        grad_input, gain_term = norm_back(grad_mid, grad_one, unit_one, inv_one, gain_attn)
+        return grad_input.astype(bf16).reshape(layer_input.shape), gain_term
+
+    def back_through_attention(grad_attended, **line):
+        return attend_back(
+            cut_order, grad_attended, attended_placed, query, key, value, lse, cosine, sine,
+            piece_ids, piece_col, heads, **line,
+        )
+
+    def result_of(down_sum):
+        return (mid + down_sum).astype(bf16).reshape(layer_input.shape)
+
+    q_here = heads * HD
     if near:
-        normed_two, hidden, up_part, gate_part = feed_forward(mid, ffn_gain, cols_gate_up, 3)
+        normed_two, hidden, up_part, gate_part = feed_forward(
+            mid, ffn_gain, cols_gate_up, number=3
+        )
         grad_gate_up, down_term = feed_forward_back(
-            grad_out, w_down, hidden, up_part, gate_part, 4
-        )
-    else:
-        normed_two = gather((unit_two * ffn_gain).astype(bf16))
-        grad_all = gather(grad_out)
-        gate_up = matmul_f32(normed_two, cols_gate_up)
-        gate_proj, up_proj = gate_up[:, :hidden_here], gate_up[:, hidden_here:]
-        sigmoid_gate = jax.nn.sigmoid(gate_proj)
-        swish = gate_proj * sigmoid_gate
-        hidden = (swish * up_proj).astype(bf16)
-        gate_part = up_proj * sigmoid_gate * (1.0 + gate_proj * (1.0 - sigmoid_gate))
-        down_term = over_tokens(hidden, grad_all).astype(bf16)
-        grad_hidden = against_rows(grad_all, w_down)
-        grad_gate_up = jnp.concatenate([grad_hidden * gate_part, grad_hidden * swish], 1)
-        grad_gate_up = grad_gate_up.astype(bf16)
-    down_term = sum_over_sequences(down_term, reps)
-    grad_two = scatter(grad_gate_up, cols_gate_up, True, 5)
-    grad_mid, gain_ffn_term = norm_back(
-        grad_out.astype(f32), grad_two, unit_two, inv_two, gain_ffn
-    )
-    grad_mid_low = grad_mid.astype(bf16)
-    if near:
-        grad_attended, out_term = attended_back(grad_mid_low, w_out, attended, 6)
-    else:
-        grad_mid_low = gather(grad_mid_low)
-        grad_attended = against_rows(grad_mid_low, w_out).astype(bf16)
-        out_term = over_tokens(attended, grad_mid_low).astype(bf16)
+            grad_out, w_down, hidden, up_part, gate_part, number=4
+        )
+        high = rows_here // 8
+        sums = Sums((8, high, model_width))
+        terms = {"down": down_term.reshape((4,) + sums.shape)}
+
+        def pick_down(number):
+            return "down", lambda ref: ref.at[number]
+
+        def pick_gate_up(number):
+            return "gate_up", lambda ref: ref.at[:, number * high : (number + 1) * high, :]
+
+        picks = [pick_down(n) for n in range(4)] + [pick_gate_up(n) for n in range(8)]
+        picks += [("out", lambda ref: ref)]
+
+        def line(number, ticks):
+            names = sorted(
+                {picks[t][0] for t in range(sums.tick, sums.tick + ticks) if t < len(picks)}
+            )
+            return dict(
+                number=number, ticks=ticks, sums=sums, picks=dict(enumerate(picks)),
+                arrays=[(name, terms[name]) for name in names],
+            )
+
+        down_sum, terms["gate_up"] = product_scattered(
+            hidden, w_down, False, extra=(normed_two, grad_gate_up), **line(5, 2)
+        )
+        result = result_of(down_sum)
+        grad_two = product_scattered(grad_gate_up, cols_gate_up, True, **line(6, 2))[0]
+        grad_mid, gain_ffn_term = finish_two(grad_two)
+        grad_attended, out_term = attended_back(
+            grad_mid.astype(bf16), w_out, attended, **line(7, 2)
+        )
+        terms["out"] = out_term.reshape(sums.shape)
+        grad_qkv = back_through_attention(grad_attended, **line(8, 1))
+        grad_one, qkv_term = product_scattered(
+            grad_qkv, cols_qkv, True, extra=(normed_one, None), **line(9, 2)
+        )
+        grad_x, gain_attn_term = finish_one(grad_mid, grad_one)
+        gains = jnp.stack([gain_attn_term, gain_ffn_term]).reshape(2, groups, rows_here)
+        gains = jnp.pad(jnp.moveaxis(gains, 0, 1), ((0, 0), (0, 6), (0, 0)))
+        rest = line(10, 8)
+        gate_rows, up_rows, qkv_rows, own_gains = tail(
+            qkv_term.reshape(8, 8, high, -1), gains,
+            {c: sums.done[c] for c in range(4, 7)}, hidden_here, **rest,
+        )
+        qkv_rows = jnp.stack([sums.done[13], sums.done[14]], 2).astype(f32)
+        qkv_rows = qkv_rows.reshape(8, high, 2, 4, -1)
+
+        def columns(low, above):
+            return qkv_rows[..., low:above].reshape(rows_here, -1)
+
+        return (
+            result,
+            grad_x,
+            columns(0, q_here),
+            columns(q_here, q_here + HD),
+            columns(q_here + HD, q_here + 2 * HD),
+            sums.done[12].reshape(rows_here, model_width).astype(f32),
+            gate_rows.astype(f32),
+            up_rows.astype(f32),
+            jnp.stack([sums.done[n] for n in range(4)]).reshape(hidden_here, -1).astype(f32),
+            own_gains[0],
+            own_gains[1],
+        )
+
+    normed_two = gather((unit_two * ffn_gain).astype(bf16))
+    grad_all = gather(grad_out)
+    gate_up = matmul_f32(normed_two, cols_gate_up)
+    gate_proj, up_proj = gate_up[:, :hidden_here], gate_up[:, hidden_here:]
+    sigmoid_gate = jax.nn.sigmoid(gate_proj)
+    swish = gate_proj * sigmoid_gate
+    hidden = (swish * up_proj).astype(bf16)
+    gate_part = up_proj * sigmoid_gate * (1.0 + gate_proj * (1.0 - sigmoid_gate))
+    down_term = over_tokens(hidden, grad_all).astype(bf16)
+    grad_hidden = against_rows(grad_all, w_down)
+    grad_gate_up = jnp.concatenate([grad_hidden * gate_part, grad_hidden * swish], 1).astype(bf16)
+    grad_mid, gain_ffn_term = finish_two(scatter(grad_gate_up, cols_gate_up, True))
+    grad_mid_low = gather(grad_mid.astype(bf16))
+    grad_qkv = back_through_attention(against_rows(grad_mid_low, w_out).astype(bf16))
+    grad_x, gain_attn_term = finish_one(grad_mid, scatter(grad_qkv, cols_qkv, True))
 
     def to_rows(term):
         return lax.all_to_all(
             term.astype(bf16).reshape(groups, rows_here, -1), "grp", 0, 0, tiled=True
         )
-
-    gate_up_term = sum_over_sequences(to_rows(over_tokens(normed_two, grad_gate_up)), reps)
-    grad_qkv = attend_back(
-        cut_order, grad_attended, attended, query, key, value, lse, cosine, sine,
-        piece_ids, piece_col, heads,
-    )
-    out_term = sum_over_sequences(out_term, reps)
-    qkv_term = sum_over_sequences(to_rows(over_tokens(normed_one, grad_qkv)), reps)
-    grad_one = scatter(grad_qkv, cols_qkv, True, 7)
-    grad_input, gain_attn_term = norm_back(grad_mid, grad_one, unit_one, inv_one, gain_attn)
-    result = (mid + scatter(hidden, w_down, False, 8)).astype(bf16)
-    gain_total = lax.psum(jnp.stack([gain_attn_term, gain_ffn_term]), ("grp", "rep"))
-    own_gains = lax.dynamic_slice_in_dim(gain_total, own_index * rows_here, rows_here, 1)
 
     def whole_rows(term):
         return jnp.moveaxis(term, 0, 1).reshape(rows_here, -1)
@@ -871,17 +1388,21 @@
             jnp.moveaxis(term, 0, 1).reshape(rows_here, kv_heads, copies, HD), 2
         ).reshape(rows_here, -1)
 
-    q_here = heads * HD
+    gate_up_term = sum_over_sequences(to_rows(over_tokens(normed_two, grad_gate_up)))
+    out_term = sum_over_sequences(over_tokens(attended, grad_mid_low).astype(bf16))
+    qkv_term = sum_over_sequences(to_rows(over_tokens(normed_one, grad_qkv)))
+    gain_total = lax.psum(jnp.stack([gain_attn_term, gain_ffn_term]), ("grp", "rep"))
+    own_gains = lax.dynamic_slice_in_dim(gain_total, own_index * rows_here, rows_here, 1)
     return (
-        result.reshape(layer_input.shape),
-        grad_input.astype(bf16).reshape(layer_input.shape),
+        result_of(scatter(hidden, w_down, False)),
+        grad_x,
         whole_rows(qkv_term[..., :q_here]),
         kv_rows(qkv_term[..., q_here : q_here + HD]),
         kv_rows(qkv_term[..., q_here + HD :]),
         out_term,
         whole_rows(gate_up_term[..., :hidden_here]),
         whole_rows(gate_up_term[..., hidden_here:]),
-        down_term,
+        sum_over_sequences(down_term),
         own_gains[0],
         own_gains[1],
     )

time: 1280 us -> 941 us (0.74)
  Pallas kernels: 519 us -> 819 us
  waiting for transfers between devices: 306 us -> 12.2 us
  blocking collectives: 240 us -> 0 us
  starting transfers between devices: 52.4 us -> 10.3 us
  matrix products: 40.4 us -> 5.99 us
  other arithmetic: 77.4 us -> 52.7 us
    pallas_call x9 -> x12, Pallas kernels: 500 us -> 800 us  [the longest x10 794 us: run(): pl.pallas_call(body, out_shape=tuple((shape for shape, _ in outs)), in_sp...]
    ppermute x12 -> x0, waiting for transfers between devices: 278 us -> none  [the longest x4 179 us: sum_over_sequences(): inward = lax.ppermute(term, 'rep', [(0, 1), (3, 2)])]
    psum x1 -> x0, blocking collectives: 144 us -> none  [on_device(): lax.psum(jnp.stack([gain_attn_term, gain_ffn_term]), ('grp', 'rep'))]
    all_to_all x1 -> x0, blocking collectives: 96.6 us -> none  [to_rows(): lax.all_to_all(term.astype(bf16).reshape(groups, rows_here, -1), 'grp', 0...]
    ppermute x12 -> x0, starting transfers between devices: 38.1 us -> none  [the longest x4 22.1 us: sum_over_sequences(): inward = lax.ppermute(term, 'rep', [(0, 1), (3, 2)])]
    dot_general x2 -> x0, matrix products: 32.4 us -> none  [over_tokens(): lax.dot_general(first, second, (((0,), (0,)), ((), ())), preferred_elemen...]
    convert_element_type x13 -> x6, other arithmetic: 52.8 us -> 22.9 us  [the longest x1 6.73 us: on_device(): gate_rows.astype(f32)]
    all_to_all x1 -> x0, waiting for transfers between devices: 16.1 us -> none  [to_rows(): lax.all_to_all(term.astype(bf16).reshape(groups, rows_here, -1), 'grp', 0...]
  transfers between devices with their start and end apart: 15 -> 2, of which waited for: 4 -> 1; matrix products, arithmetic and copies ran while one was open for 8% -> 3% of each run, Pallas kernels for 33% -> 21%
where the time goes in v3:
time: 941 us; the launch traced here: 938 us
  Pallas kernels  819 us (87%)
  other arithmetic  52.7 us (6%)
  local copies, waits for them, and re-layouts  37.1 us (4%)
  waiting for transfers between devices  12.2 us (1%)
  starting transfers between devices  10.3 us (1%)
    pallas_call x10, Pallas kernels, run(): pl.pallas_call(body, out_shape=tuple((shape for shape, _ in outs)), in_sp...  794 us
  transfers between devices with their start and end apart: 2, of which 1 were waited for; matrix products, arithmetic and copies ran while one was open for 3% of the time, Pallas kernels for 21%

profile of v3, /device:TPU:0, one launch (start us, length us, event | category | flops | bytes accessed | tf_op | source)
XLA Modules:
  0.0 938.2 jit_solution(11089188992430173150)
XLA Ops:
  0.7 1.4 copy.50
  2.4 1.5 pad_maximum_fusion.2
  3.9 5.2 all-to-all-start
  9.1 6.2 copy_bitcast_fusion
  15.3 8.3 pad_maximum_fusion
  23.6 12.2 %all-to-all-done = bf16[256,8,512]{2,0,1:T(8,128)(2,1)S(1)} async-done(((bf16[256,8,512]{2,0,1:T(8,128)(2,1)}), bf16[256,8,512]{2,0,1:T(8,128)(2,1)S(1)}, u32[]{:S(2)}, u32[]{:S(2)}) %all-to-all-start) | async-done | bytes 2097184 | tf_op jit(solution)/shard_map/all_to_all | solution.py:1240
  35.8 5.1 all-to-all-start.1
  40.9 130.3 %shard_map.212.refs_2_ = bf16[2048,2048]{1,0:T(8,128)(2,1)} custom-call(bf16[256,2048]{1,0:T(8,128)(2,1)} %bitcast.75, f32[1,2048]{1,0:T(1,128)} %bitcast.90), custom_call_target="tpu_custom_call" | custom-call | bytes 157286400 | tf_op jit(solution)/shard_map/pallas_call | solution.py:383
  171.8 3.7 fusion.12
  175.6 1.6 pad_maximum_fusion.3
  177.1 6.0 fusion.15.qkv_ref
  183.1 1.3 broadcast_in_dim.19.piece_col_ref.refs_9_
  184.4 18.8 %shard_map.213 = (bf16[2048,256]{1,0:T(8,128)(2,1)S(1)}, bf16[2,2048,128]{2,1,0:T(8,128)(2,1)S(1)}, bf16[2048,128]{1,0:T(8,128)(2,1)S(1)}, bf16[2048,128]{1,0:T(...) custom-call(s32[1,16]{1,0:T(1,128)S(1)} %copy-done.4, f32[2048,512]{1,0:T(8,128)} %fusion.15.qkv_ref, ...), custom_call_target="tpu_custom_call" | custom-call | flops 3221225472 | bytes 20971520 | tf_op jit(solution)/shard_map/pallas_call | solution.py:146
  203.2 1.0 copy-done.5
  204.2 1.0 copy-done.6
  205.1 1.0 copy-done.7
  208.3 45.0 %shard_map.214 = f32[256,2048]{1,0:T(8,128)} custom-call(bf16[2048,256]{1,0:T(8,128)(2,1)} %copy-done.5, bf16[256,2048]{1,0:T(8,128)(2,1)} %refs_1_.7), custom_call_target="tpu_custom_call" | custom-call | flops 2147483648 | bytes 157286400 | tf_op jit(solution)/shard_map/pallas_call | solution.py:383
  253.3 3.2 multiply_reduce_fusion.2
  256.5 51.6 %shard_map.215 = (bf16[2048,2048]{1,0:T(8,128)(2,1)}, bf16[2048,1024]{1,0:T(8,128)(2,1)}, bf16[2048,1024]{1,0:T(8,128)(2,1)}, bf16[2048,1024]{1,0:T(8,128)(2,1)}) custom-call(f32[256,2048]{1,0:T(8,128)} %get-tuple-element.102.refs_0_, f32[1,2048]{1,0:T(1,128)} %bitcast.89, bf16[2048,2048]{1,0:T(8,128)(2,1)} %bitcast.9.refs_2_.refs_1_), custom_call_target="tpu_custom_call" | custom-call | flops 17179869184 | bytes 157286400 | tf_op jit(solution)/shard_map/pallas_call | solution.py:383
  308.2 50.9 %shard_map.216 = (bf16[2048,2048]{1,0:T(8,128)(2,1)}, bf16[1024,2048]{1,0:T(8,128)(2,1)}) custom-call(bf16[256,2048]{1,0:T(8,128)(2,1)} %bitcast.76, bf16[1024,2048]{1,0:T(8,128)(2,1)} %refs_1_.6, bf16[2048,1024]{1,0:T(8,128)(2,1)} %get-tuple-element.55.refs_2_.refs_0_, bf16[2048,1024]{1,0:T(8,128)(2,1)} %get-tuple-element.57.refs_3_, ...), custom_call_target="tpu_custom_call" | custom-call | flops 17179869184 | bytes 157286400 | tf_op jit(solution)/shard_map/pallas_call | solution.py:383
  359.1 61.7 %shard_map.217 = (f32[256,2048]{1,0:T(8,128)}, bf16[8,256,2048]{2,1,0:T(8,128)(2,1)}, bf16[8,32,2048]{2,1,0:T(8,128)(2,1)}, bf16[8,32,2048]{2,1,0:T(8,128)(2,1)}) custom-call(bf16[2048,1024]{1,0:T(8,128)(2,1)} %get-tuple-element.55.refs_2_.refs_0_, bf16[1024,2048]{1,0:T(8,128)(2,1)} %refs_1_.6, bf16[2048,2048]{1,0:T(8,128)(2,1)} %get-tuple-element.56.refs_2_, ...), custom_call_target="tpu_custom_call" | custom-call | flops 25769803776 | bytes 157286400 | tf_op jit(solution)/shard_map/pallas_call | solution.py:383
  420.8 70.7 %shard_map.218 = (f32[256,2048]{1,0:T(8,128)}, bf16[8,32,2048]{2,1,0:T(8,128)(2,1)}, bf16[8,32,2048]{2,1,0:T(8,128)(2,1)}, bf16[8,32,2048]{2,1,0:T(8,128)(2,1)}, bf16[8,32,2048]{2,1,0:T(8,128)(2,1)}) custom-call(bf16[2048,2048]{1,0:T(8,128)(2,1)} %get-tuple-element.59.refs_3_.refs_0_, bf16[2048,2048]{1,0:T(8,128)(2,1)} %bitcast.9.refs_2_.refs_1_, ...), custom_call_target="tpu_custom_call" | custom-call | flops 17179869184 | bytes 157286400 | tf_op jit(solution)/shard_map/pallas_call | solution.py:383
  491.5 2.3 multiply_reduce_fusion
  494.0 1.6 fusion.13.refs_0_
  495.6 65.7 %shard_map.219 = (bf16[2048,256]{1,0:T(8,128)(2,1)}, bf16[256,2048]{1,0:T(8,128)(2,1)}, bf16[8,32,2048]{2,1,0:T(8,128)(2,1)}, bf16[8,32,2048]{2,1,0:T(8,128)(2,1...) custom-call(bf16[256,2048]{1,0:T(8,128)(2,1)} %fusion.13.refs_0_, bf16[256,2048]{1,0:T(8,128)(2,1)} %refs_1_.7, ...), custom_call_target="tpu_custom_call" | custom-call | flops 4294967296 | bytes 157286400 | tf_op jit(solution)/shard_map/pallas_call | solution.py:383
  561.3 2.3 shard_map.220.refs_0_
  563.6 31.4 %shard_map.221 = (bf16[2048,512]{1,0:T(8,128)(2,1)}, bf16[8,32,2048]{2,1,0:T(8,128)(2,1)}, bf16[8,32,2048]{2,1,0:T(8,128)(2,1)}, bf16[8,32,2048]{2,1,0:T(8,128)(2,1)}) custom-call(bf16[2048,256]{1,0:T(8,128)(2,1)} %shard_map.220.refs_0_, bf16[2048,256]{1,0:T(8,128)(2,1)} %copy-done.7, bf16[2,2048,128]{2,1,0:T(8,128)(2,1)} %copy-done.6, ...), custom_call_target="tpu_custom_call" | custom-call | flops 8589934592 | bytes 29360128 | tf_op jit(solution)/shard_map/pallas_call | solution.py:383
  595.0 3.1 shard_map.222.refs_0_
  598.2 74.5 %shard_map.223 = (f32[256,2048]{1,0:T(8,128)}, bf16[8,256,512]{2,1,0:T(8,128)(2,1)}, bf16[8,32,2048]{2,1,0:T(8,128)(2,1)}, bf16[8,32,2048]{2,1,0:T(8,128)(2,1)},...) custom-call(bf16[2048,512]{1,0:T(8,128)(2,1)} %shard_map.222.refs_0_, bf16[2048,512]{1,0:T(8,128)(2,1)} %bitcast.81, ...), custom_call_target="tpu_custom_call" | custom-call | flops 8589934592 | bytes 157286400 | tf_op jit(solution)/shard_map/pallas_call | solution.py:383
  672.7 2.5 fusion.8
  675.9 212.7 %shard_map.224 = (bf16[256,8192]{1,0:T(8,128)(2,1)}, bf16[256,8192]{1,0:T(8,128)(2,1)}, bf16[2,8,32,2048]{3,2,1,0:T(8,128)(2,1)}, f32[8,256]{1,0:T(8,128)}, bf16...) custom-call(bf16[8,8,32,512]{3,2,1,0:T(8,128)(2,1)} %bitcast.82, ...), custom_call_target="tpu_custom_call" | custom-call | bytes 209715200 | tf_op jit(solution)/shard_map/pallas_call | solution.py:383
  888.6 2.6 stack.36
  891.2 2.6 stack.37
  893.9 2.8 maximum_convert_fusion.1
  896.7 3.4 maximum_convert_fusion
  900.6 4.7 bitcast_convert_fusion
  905.4 1.2 copy.38
  906.5 2.6 reshape.145
  909.2 2.4 copy.39
  911.5 2.6 reshape.146
  914.1 1.6 slice-done
  915.7 1.7 copy.37
  917.4 3.3 reshape.144
  920.7 6.7 convert_element_type.61
  927.5 4.8 convert_element_type.62
  932.3 1.6 bitcast_convert_fusion.1
  933.9 1.3 fusion.14
  935.3 2.6 fusion.11
  (76 shorter events, 4.7 us)
Async XLA Ops:
  0.6 1.4 copy-start
  0.7 1.5 copy-start.30
  3.9 31.8 %all-to-all-start = ((bf16[256,8,512]{2,0,1:T(8,128)(2,1)}), bf16[256,8,512]{2,0,1:T(8,128)(2,1)S(1)}, u32[]{:S(2)}, u32[]{:S(2)}) async-start(bf16[256,8,512]{2,0,1:T(8,128)(2,1)} %pad_maximum_fusion.2), calls=%async_computation | async-start | bytes 4194304 | tf_op jit(solution)/shard_map/all_to_all | solution.py:1240
  35.8 141.4 %copy-start.23 = (bf16[256,8,512]{2,0,1:T(8,128)(2,1)}, bf16[256,8,512]{2,0,1:T(8,128)(2,1)S(1)}, u32[]{:S(2)}) copy-start(bf16[256,8,512]{2,0,1:T(8,128)(2,1)S(1)} %all-to-all-done) | copy-start | bytes 6291460
  35.8 220.7 %all-to-all-start.1 = ((bf16[256,8,2048]{2,0,1:T(8,128)(2,1)}), bf16[256,8,2048]{2,0,1:T(8,128)(2,1)}, u32[]{:S(2)}, u32[]{:S(2)}) async-start(bf16[256,8,2048]{2,0,1:T(8,128)(2,1)} %pad_maximum_fusion), calls=%async_computation.1 | async-start | bytes 16777216 | tf_op jit(solution)/shard_map/all_to_all | solution.py:1240
  40.9 130.3 %copy-start.4 = (s32[1,16]{1,0:T(1,128)S(1)}, s32[1,16]{1,0:T(1,128)}, u32[]{:S(2)}) copy-start(s32[1,16]{1,0:T(1,128)} %holder_ref.1) | copy-start | bytes 196
  171.8 5.3 copy-start.18
  177.1 7.3 copy-start.2
  177.1 6.0 copy-start.3
  203.2 1.0 copy-start.5
  204.2 1.0 copy-start.6
  205.1 1.0 copy-start.7
  206.1 0.8 copy-start.8
  206.9 0.8 copy-start.9
  207.7 0.6 copy-start.10
  208.3 45.0 %copy-start.14 = (bf16[1,256,2048]{2,1,0:T(8,128)(2,1)S(1)}, bf16[1,256,2048]{2,1,0:T(8,128)(2,1)}, u32[]{:S(2)}) copy-start(bf16[1,256,2048]{2,1,0:T(8,128)(2,1)} %param.13) | copy-start | bytes 3145732
  420.7 70.7 %copy-start.11 = (f32[256,2048]{1,0:T(8,128)S(1)}, f32[256,2048]{1,0:T(8,128)}, u32[]{:S(2)}) copy-start(f32[256,2048]{1,0:T(8,128)} %get-tuple-element.102.refs_0_) | copy-start | bytes 6291460
  420.7 70.7 %copy-start.31 = (f32[2048]{0:T(1024)S(1)}, f32[2048]{0:T(1024)}, u32[]{:S(2)}) copy-start(f32[2048]{0:T(1024)} %param.25) | copy-start | bytes 24580
  491.5 2.3 copy-start.12
  491.5 2.5 copy-start.21
  598.2 74.5 %copy-start.32 = (f32[2048]{0:T(1024)S(1)}, f32[2048]{0:T(1024)}, u32[]{:S(2)}) copy-start(f32[2048]{0:T(1024)} %param.24) | copy-start | bytes 24580
  893.9 2.8 copy-start.16
  893.9 2.8 copy-start.17
  896.7 3.4 copy-start.26
  896.7 3.4 copy-start.27
  896.7 3.4 copy-start.28
  896.7 3.4 copy-start.29
  914.1 1.6 slice-start
  920.7 6.7 copy-start.20
  927.5 4.8 copy-start.25
  927.5 7.8 copy-start.19
  927.5 7.8 copy-start.22
  927.5 7.8 copy-start.24
  932.3 3.0 copy-start.13
  932.3 3.0 copy-start.15
  935.3 2.6 copy-start.1

commit v4 on v3

--- a/solution.py
+++ b/solution.py
@@ -564,7 +564,7 @@
 SIBLING, ALONG_X, ALONG_Y, ACROSS = (0, 0), (0, 1), (1, 0), (1, 1)
 
 
-def gather_rows(rows, all_ref, sends, recvs, on_chip, line):
+def gather_rows(rows, all_ref, sends, recvs, on_chip, line, then=None):
     half = rows // 2
 
     def block(chip, core, part=None):
@@ -600,6 +600,8 @@
     send(0, SIBLING, 0, None, to_s)
     send(2, SIBLING, 0, 0, to_x)
     send(4, SIBLING, 0, 1, to_y)
+    if then:
+        then()
     landed(0, SIBLING, 1, None)
     on_chip(*SIBLING)
     landed(1, ALONG_X, 0, 1)
@@ -671,45 +673,120 @@
     return pl.ds(pl.multiple_of(other(0, 0, 0) * rows, rows), rows)
 
 
+def send_columns(pieces, sends, recvs, moves):
+    copies = []
+    for which, (rows_ref, width, there) in enumerate(pieces):
+        for number, flip in enumerate(EVERYONE):
+            target = other(*flip)
+            cols = pl.ds(pl.multiple_of(target * width, width), width)
+            one = pltpu.make_async_remote_copy(
+                src_ref=rows_ref.at[:, cols], dst_ref=there,
+                send_sem=sends.at[which, number], recv_sem=recvs.at[which, number],
+                device_id={"grp": target}, device_id_type=MESH,
+            )
+            one.start()
+            copies.append(one)
+        mine = pl.ds(pl.multiple_of(other(0, 0, 0) * width, width), width)
+        moves.later(rows_ref.at[:, mine], there)
+    return copies
+
+
 def gather_normed_kernel(ins, outs, scratch, line):
-    x_ref, gain_ref = ins
-    (all_ref,) = outs
-    held, sends, recvs, sems = scratch
+    x_ref, gain_ref = ins[:2]
+    weights = ins[2:]
+    all_ref, cols_ref = outs
+    held, sends, recvs, sems, col_sends, col_recvs = scratch
     rows = x_ref.shape[0]
     moves = Moves(sems)
     held[own_rows(rows), :] = rms_normed(x_ref[...].astype(f32), gain_ref[...]).astype(bf16)
-    greet_group(line)
-    line.open(0)
+    greet_group(line, EVERYONE)
+    col_copies = []
+
+    def send_weights():
+        pieces, low = [], 0
+        tall = weights[0].shape[0]
+        there = pl.ds(pl.multiple_of(other(0, 0, 0) * tall, tall), tall)
+        for weight in weights:
+            width = weight.shape[1] // 8
+            pieces.append((weight, width, cols_ref.at[there, low : low + width]))
+            low += width
+        col_copies.extend(send_columns(pieces, col_sends, col_recvs, moves))
 
     def on_chip(*chip):
         where = chip_rows(*chip, rows)
         moves.later(held.at[where, :], all_ref.at[where, :])
 
-    gather_rows(rows, held, sends, recvs, on_chip, line)
+    gather_rows(rows, held, sends, recvs, on_chip, line, send_weights)
+    for one in col_copies:
+        one.wait()
     moves.finish()
 
 
-def gather_normed(x, gain, **line):
+def gather_normed(x, gain, weights, **line):
     rows, width = x.shape
+    deep = sum(weight.shape[1] for weight in weights) // 8
     return run(
         gather_normed_kernel,
-        [(x, VMEM), (gain, VMEM)],
-        [(jax.ShapeDtypeStruct((8 * rows, width), bf16), ANY)],
-        gather_scratch(rows, width, 4),
+        [(x, VMEM), (gain, VMEM)] + [(weight, ANY) for weight in weights],
+        [
+            (jax.ShapeDtypeStruct((8 * rows, width), bf16), ANY),
+            (jax.ShapeDtypeStruct((8 * weights[0].shape[0], deep), bf16), ANY),
+        ],
+        gather_scratch(rows, width, 4 + len(weights))
+        + [pltpu.SemaphoreType.DMA((len(weights), 7))] * 2,
         line.pop("number"),
         (0, 150 * rows * width * 2, 0),
         **line,
+    )
+
+
+def columns_kernel(rows_here, ins, outs, scratch, line):
+    (cols_ref,) = outs
+    sends, recvs, sems = scratch
+    moves = Moves(sems)
+    barrier = pltpu.get_barrier_semaphore()
+    for flip in EVERYONE:
+        pl.semaphore_signal(barrier, inc=1, device_id={"grp": other(*flip)}, device_id_type=MESH)
+    pl.semaphore_wait(barrier, 7)
+    first = pl.multiple_of(lax.axis_index("rep") * rows_here, rows_here)
+    me = other(0, 0, 0)
+    pieces, low = [], 0
+    for weight in ins:
+        width = weight.shape[1] // 8
+        pieces.append(
+            (weight.at[pl.ds(first, rows_here), :], width, cols_ref.at[me, :, low : low + width])
+        )
+        low += width
+    for one in send_columns(pieces, sends, recvs, moves):
+        one.wait()
+    moves.finish()
+
+
+def columns_of_some(weights, rows_here, number):
+    deep = sum(weight.shape[1] for weight in weights) // 8
+    return run(
+        functools.partial(columns_kernel, rows_here),
+        [(weight, ANY) for weight in weights],
+        [(jax.ShapeDtypeStruct((8, rows_here, deep), bf16), ANY)],
+        [pltpu.SemaphoreType.DMA((len(weights), 7))] * 2
+        + [pltpu.SemaphoreType.DMA((len(weights),))],
+        number, (0, 50 * 8 * rows_here * deep, 0),
     )[0]
 
 
 def feed_forward_kernel(tile, ins, outs, scratch, line):
-    mid_ref, gain_ref, w_ref = ins
-    all_ref, hidden_ref, up_part_ref, gate_part_ref = outs
+    mid_ref, gain_ref, spread_ref, rest_ref = ins
+    all_ref, hidden_ref, up_part_ref, gate_part_ref, whole_ref = outs
     held, sends, recvs, sems, weight, hidden, up_part, gate_part = scratch
     rows = mid_ref.shape[0]
     inner = hidden.shape[1]
     moves = Moves(sems)
-    weight_copy = moves.start(w_ref, weight)
+    planes, _, tall, deep = spread_ref.shape
+    loads = [
+        moves.start(spread_ref.at[z], weight.at[:, z * tall : (z + 1) * tall, :])
+        for z in range(planes)
+    ]
+    loads.append(moves.start(rest_ref, weight.at[:, planes * tall :, :]))
     held[own_rows(rows), :] = rms_normed(mid_ref[...], gain_ref[...]).astype(bf16)
     greet_group(line)
     line.open(0)
@@ -718,14 +795,16 @@
         where = chip_rows(*chip, rows)
         moves.later(held.at[where, :], all_ref.at[where, :])
         if chip == SIBLING:
-            weight_copy.wait()
+            for one in loads:
+                one.wait()
+            moves.later(weight, whole_ref)
 
         def column(t, _):
             cols = pl.ds(pl.multiple_of(t * tile, tile), tile)
             up_cols = pl.ds(pl.multiple_of(inner + t * tile, tile), tile)
             lhs = held[where, :]
-            gate = matmul_f32(lhs, weight[:, cols])
-            up = matmul_f32(lhs, weight[:, up_cols])
+            gate = matmul_f32(lhs, weight[:, :, cols].reshape(-1, tile))
+            up = matmul_f32(lhs, weight[:, :, up_cols].reshape(-1, tile))
             sigma = 1.0 / (1.0 + jnp.exp(-gate))
             swish = gate * sigma
             hidden[where, cols] = (swish * up).astype(bf16)
@@ -741,16 +820,19 @@
     moves.finish()
 
 
-def feed_forward(mid, gain, cols_gate_up, **line):
+def feed_forward(mid, gain, spread, rest, **line):
     rows, width = mid.shape
-    inner = cols_gate_up.shape[1] // 2
+    inner = rest.shape[2] // 2
+    weight = (8, width // 8, 2 * inner)
     tall = jax.ShapeDtypeStruct((8 * rows, inner), bf16)
     return run(
         functools.partial(feed_forward_kernel, min(256, inner)),
-        [(mid, VMEM), (gain, VMEM), (cols_gate_up, ANY)],
-        [(jax.ShapeDtypeStruct((8 * rows, width), bf16), ANY)] + [(tall, ANY)] * 3,
-        gather_scratch(rows, width, 17)
-        + [pltpu.VMEM(cols_gate_up.shape, bf16)]
+        [(mid, VMEM), (gain, VMEM), (spread, ANY), (rest, ANY)],
+        [(jax.ShapeDtypeStruct((8 * rows, width), bf16), ANY)]
+        + [(tall, ANY)] * 3
+        + [(jax.ShapeDtypeStruct(weight, bf16), ANY)],
+        gather_scratch(rows, width, 22)
+        + [pltpu.VMEM(weight, bf16)]
         + [pltpu.VMEM((8 * rows, inner), bf16)] * 3,
         line.pop("number"),
         (32 * rows * width * inner, 150 * rows * width * 2, 8 * rows * inner),
@@ -1192,6 +1274,96 @@
     )
 
 
+def finish_kernel(heads, *refs):
+    ins, rest = refs[:9], refs[9:]
+    outs, (low, wide, load_sems, store_sems) = rest[:7], rest[7:]
+    down_refs, out_sum, qkv_refs, gate_rows, up_rows = ins[:4], ins[4], ins[5:7], ins[7], ins[8]
+    query, key, value, out, gate, up, down = outs
+    rows, width = down_refs[0].shape
+    jobs = []
+    for number, ref in enumerate(down_refs):
+        jobs.append((ref, [(slice(0, width), down.at[number * rows : (number + 1) * rows, :])]))
+    for ref, into in ((gate_rows, gate), (up_rows, up)):
+        for low_col in range(0, ref.shape[1], width):
+            cols = slice(low_col, low_col + width)
+            jobs.append((ref.at[:, cols], [(slice(0, width), into.at[:, cols])]))
+    jobs.append((out_sum, [(slice(0, width), out)]))
+    part = (heads + 2) * HD
+    for number, ref in enumerate(qkv_refs):
+        stores = []
+        for place in range(width // part):
+            at, device = place * part, number * (width // part) + place
+            for into, first, size in (
+                (query, 0, heads * HD), (key, heads * HD, HD), (value, (heads + 1) * HD, HD)
+            ):
+                stores.append(
+                    (
+                        slice(at + first, at + first + size),
+                        into.at[:, device * size : (device + 1) * size],
+                    )
+                )
+        jobs.append((ref, stores))
+
+    def load(number):
+        return pltpu.make_async_copy(
+            jobs[number][0], low.at[number % 3], load_sems.at[number % 3]
+        )
+
+    def stores(number):
+        return [
+            pltpu.make_async_copy(
+                wide.at[number % 3, :, cols], into, store_sems.at[number % 3, which]
+            )
+            for which, (cols, into) in enumerate(jobs[number][1])
+        ]
+
+    for number in range(min(2, len(jobs))):
+        load(number).start()
+    for number in range(len(jobs)):
+        if number + 2 < len(jobs):
+            load(number + 2).start()
+        load(number).wait()
+        if number >= 3:
+            for one in stores(number - 3):
+                one.wait()
+
+        def cast(g, _, at=number % 3):
+            some = pl.ds(pl.multiple_of(g * 32, 32), 32)
+            wide[at, some, :] = low[at, some, :].astype(f32)
+            return 0
+
+        lax.fori_loop(0, rows // 32, cast, 0)
+        for one in stores(number):
+            one.start()
+    for number in range(max(0, len(jobs) - 3), len(jobs)):
+        for one in stores(number):
+            one.wait()
+
+
+def finish(downs, out_sum, qkvs, gate_rows, up_rows, heads):
+    rows, width = out_sum.shape
+    wide = gate_rows.shape[1]
+    shapes = [
+        (rows, 8 * heads * HD), (rows, 8 * HD), (rows, 8 * HD), (rows, width), (rows, wide),
+        (rows, wide), (len(downs) * rows, width),
+    ]
+    size = len(downs) * rows * width + 2 * rows * wide + 3 * rows * width
+    return pl.pallas_call(
+        functools.partial(finish_kernel, heads),
+        out_shape=tuple(jax.ShapeDtypeStruct(shape, f32) for shape in shapes),
+        in_specs=[pl.BlockSpec(memory_space=pl.ANY)] * 9,
+        out_specs=tuple([pl.BlockSpec(memory_space=pl.ANY)] * 7),
+        scratch_shapes=[
+            pltpu.VMEM((3, rows, width), bf16),
+            pltpu.VMEM((3, rows, width), f32),
+            pltpu.SemaphoreType.DMA((3,)),
+            pltpu.SemaphoreType.DMA((3, 12)),
+        ],
+        compiler_params=pltpu.CompilerParams(vmem_limit_bytes=32 * 2**20),
+        cost_estimate=pl.CostEstimate(flops=0, bytes_accessed=6 * size, transcendentals=0),
+    )(*downs, out_sum, *qkvs, gate_rows, up_rows)
+
+
 def sum_over_sequences(term):
     return lax.psum(term, "rep").astype(f32)
 
@@ -1250,18 +1422,33 @@
     inv_one = lax.rsqrt(jnp.mean(x_flat * x_flat, -1, keepdims=True) + EPS)
     unit_one = x_flat * inv_one
     attn_gain, ffn_gain = gain_attn.reshape(1, -1), gain_ffn.reshape(1, -1)
-    cols_qkv = to_columns(
-        jnp.concatenate([per_group(w_query), per_kv_head(w_key), per_kv_head(w_value)], -1)
-    )
     if near:
-        normed_one = gather_normed(x_rows, attn_gain, number=1)
+        share = rows_here // (4 * reps) * 3
+        spread = columns_of_some((w_gate, w_up), share, 11)
+        x_first, spread = lax.optimization_barrier((x_rows, spread))
+        spread = lax.all_gather(spread, "rep", axis=0)
+        normed_one, cols_qkv = gather_normed(
+            x_first, attn_gain, (w_query, w_key, w_value), number=1
+        )
+        last_gate, last_up, normed_one = lax.optimization_barrier(
+            (w_gate[reps * share :], w_up[reps * share :], normed_one)
+        )
+        rest = to_columns(
+            jnp.concatenate(
+                [part.reshape(rows_here - reps * share, groups, -1) for part in (last_gate, last_up)],
+                -1,
+            )
+        ).reshape(groups, rows_here - reps * share, -1)
     else:
         normed_one = gather(rms_normed(x_flat, attn_gain).astype(bf16))
+        cols_qkv = to_columns(
+            jnp.concatenate([per_group(w_query), per_kv_head(w_key), per_kv_head(w_value)], -1)
+        )
+        cols_gate_up = to_columns(jnp.concatenate([per_group(w_gate), per_group(w_up)], -1))
     qkv = matmul_f32(normed_one, cols_qkv)
     attended, query, key, value, lse, attended_placed = attend(
         cut_order, qkv, cosine, sine, piece_ids, piece_col, heads
     )
-    cols_gate_up = to_columns(jnp.concatenate([per_group(w_gate), per_group(w_up)], -1))
     if near:
         out_sum = product_scattered(attended, w_out, False, number=2)[0]
     else:
@@ -1289,9 +1476,10 @@
 
     q_here = heads * HD
     if near:
-        normed_two, hidden, up_part, gate_part = feed_forward(
-            mid, ffn_gain, cols_gate_up, number=3
-        )
+        normed_two, hidden, up_part, gate_part, cols_gate_up = feed_forward(
+            mid, ffn_gain, spread, rest, number=3
+        )
+        cols_gate_up = cols_gate_up.reshape(model_width, -1)
         grad_gate_up, down_term = feed_forward_back(
             grad_out, w_down, hidden, up_part, gate_part, number=4
         )
@@ -1339,25 +1527,10 @@
             qkv_term.reshape(8, 8, high, -1), gains,
             {c: sums.done[c] for c in range(4, 7)}, hidden_here, **rest,
         )
-        qkv_rows = jnp.stack([sums.done[13], sums.done[14]], 2).astype(f32)
-        qkv_rows = qkv_rows.reshape(8, high, 2, 4, -1)
-
-        def columns(low, above):
-            return qkv_rows[..., low:above].reshape(rows_here, -1)
-
-        return (
-            result,
-            grad_x,
-            columns(0, q_here),
-            columns(q_here, q_here + HD),
-            columns(q_here + HD, q_here + 2 * HD),
-            sums.done[12].reshape(rows_here, model_width).astype(f32),
-            gate_rows.astype(f32),
-            up_rows.astype(f32),
-            jnp.stack([sums.done[n] for n in range(4)]).reshape(hidden_here, -1).astype(f32),
-            own_gains[0],
-            own_gains[1],
-        )
+        flat = [sums.done[n].reshape(rows_here, model_width) for n in range(4)]
+        last = [sums.done[n].reshape(rows_here, model_width) for n in (12, 13, 14)]
+        weight_grads = finish(flat, last[0], last[1:], gate_rows, up_rows, heads)
+        return (result, grad_x) + tuple(weight_grads) + (own_gains[0], own_gains[1])
 
     normed_two = gather((unit_two * ffn_gain).astype(bf16))
     grad_all = gather(grad_out)

time: 941 us -> 866 us (0.920)
  other arithmetic: 52.7 us -> 21.9 us
  Pallas kernels: 819 us -> 789 us
  local copies, waits for them, and re-layouts: 37.1 us -> 15.5 us
  between operations: 1.3 us -> 14.8 us
  waiting for transfers between devices: 12.2 us -> 0.04 us
    pallas_call x10 -> x11, Pallas kernels: 794 us -> 754 us  [run(): pl.pallas_call(body, out_shape=tuple((shape for shape, _ in outs)), in_sp...]
    convert_element_type x5 -> x0, other arithmetic: 21.3 us -> none  [the longest x1 6.73 us: on_device(): gate_rows.astype(f32)]
    reshape x5 -> x1, local copies, waits for them, and re-layouts: 16.1 us -> 0.21 us  [on_device(): part.reshape(rows_here - reps * share, groups, -1)]
    all_to_all x2 -> x1, waiting for transfers between devices: 12.2 us -> 0.01 us  [to_columns(): lax.all_to_all(parts, 'grp', 1, 0, tiled=True).reshape(-1, parts.shape[-1])]
    pallas_call x0 -> x1, Pallas kernels: none -> 10.9 us  [finish(): pl.pallas_call(functools.partial(finish_kernel, heads), out_shape=tuple((...]
  transfers between devices with their start and end apart: 2 -> 2, of which waited for: 1 -> 0; matrix products, arithmetic and copies ran while one was open for 3% -> 3% of each run, Pallas kernels for 21% -> 15%
where the time goes in v4:
time: 866 us; the launch traced here: 856 us
  Pallas kernels  789 us (91%)
  other arithmetic  21.9 us (3%)
  local copies, waits for them, and re-layouts  15.5 us (2%)
  between operations  14.8 us (2%)
  matrix products  10.5 us (1%)
    pallas_call x11, Pallas kernels, run(): pl.pallas_call(body, out_shape=tuple((shape for shape, _ in outs)), in_sp...  754 us
    pallas_call x1, Pallas kernels, attend(): pl.pallas_call(functools.partial(attend_kernel, heads, order.shape[1], bl...  18.9 us
  transfers between devices with their start and end apart: 2, of which 0 were waited for; matrix products, arithmetic and copies ran while one was open for 3% of the time, Pallas kernels for 15%

profile of v4, /device:TPU:0, one launch (start us, length us, event | category | flops | bytes accessed | tf_op | source)
XLA Modules:
  0.0 855.7 jit_solution(4389666570898488832)
XLA Ops:
  7.2 0.0 all-gather.3.cloned.1.call-start
  7.2 22.5 %shard_map.212 = bf16[8,48,2048]{2,1,0:T(8,128)(2,1)} custom-call(bf16[256,8192]{1,0:T(8,128)(2,1)} %refs_0_.1, bf16[256,8192]{1,0:T(8,128)(2,1)} %refs_1_.5), custom_call_target="tpu_custom_call" | custom-call | bytes 39321600 | tf_op jit(solution)/shard_map/pallas_call | solution.py:383
  29.8 66.1 %shard_map.213 = (bf16[2048,2048]{1,0:T(8,128)(2,1)}, bf16[2048,512]{1,0:T(8,128)(2,1)}) custom-call(bf16[256,2048]{1,0:T(8,128)(2,1)} %bitcast.62, f32[1,2048]{1,0:T(1,128)} %bitcast.69, bf16[256,2048]{1,0:T(8,128)(2,1)} %refs_2_.1, bf16[256,1024]{1,0:T(8,128)(2,1)} %refs_3_.1, bf16[256,1024]{1,0:T(8,128)(2,1)} %refs_4_.1), custom_call_target="tpu_custom_call" | custom-call | bytes 157286400 | tf_op jit(solution)/shard_map/pallas_call | solution.py:383
  95.9 0.2 copy_bitcast_fusion
  96.1 1.5 pad_maximum_fusion
  97.6 3.6 all-to-all-start
  101.3 10.5 %fusion.15.qkv_ref = f32[2048,512]{1,0:T(8,128)} fusion(bf16[2048,2048]{1,0:T(8,128)(2,1)} %get-tuple-element.71.refs_2_, bf16[2048,512]{1,0:T(8,128)(2,1)} %get-tuple-element.72.refs_1_), kind=kOutput, calls=%fused_computation.39 | convolution fusion | flops 4294967296 | bytes 14680064 | tf_op jit(solution)/shard_map/dot_general | solution.py:24
  111.8 3.7 fusion.12
  115.5 0.6 select_reduce_fusion
  116.1 1.6 pad_maximum_fusion.1
  117.7 1.3 broadcast_in_dim.19.piece_col_ref.refs_9_
  119.0 18.9 %shard_map.214 = (bf16[2048,256]{1,0:T(8,128)(2,1)S(1)}, bf16[2,2048,128]{2,1,0:T(8,128)(2,1)S(1)}, bf16[2048,128]{1,0:T(8,128)(2,1)S(1)}, bf16[2048,128]{1,0:T(...) custom-call(s32[1,16]{1,0:T(1,128)S(1)} %copy-done.11, f32[2048,512]{1,0:T(8,128)} %fusion.15.qkv_ref, ...), custom_call_target="tpu_custom_call" | custom-call | flops 3221225472 | bytes 20971520 | tf_op jit(solution)/shard_map/pallas_call | solution.py:146
  137.9 1.0 copy-done.12
  138.9 1.0 copy-done.13
  139.8 1.0 copy-done.14
  140.8 0.8 copy-done.15
  141.6 0.8 copy-done.16
  142.4 0.6 copy-done.17
  143.0 46.0 %shard_map.215 = f32[256,2048]{1,0:T(8,128)} custom-call(bf16[2048,256]{1,0:T(8,128)(2,1)} %copy-done.12, bf16[256,2048]{1,0:T(8,128)(2,1)} %refs_1_.9), custom_call_target="tpu_custom_call" | custom-call | flops 2147483648 | bytes 157286400 | tf_op jit(solution)/shard_map/pallas_call | solution.py:383
  189.1 3.2 multiply_reduce_fusion.2
  192.3 0.0 all-gather.3.cloned.1.call-done
  192.3 1.3 copy-done.23
  193.6 51.8 %shard_map.216 = (bf16[2048,2048]{1,0:T(8,128)(2,1)}, bf16[2048,1024]{1,0:T(8,128)(2,1)}, bf16[2048,1024]{1,0:T(8,128)(2,1)}, bf16[2048,1024]{1,0:T(8,128)(2,1)}, bf16[8,256,2048]{2,1,0:T(8,128)(2,1)}) custom-call(f32[256,2048]{1,0:T(8,128)} %get-tuple-element.132.refs_0_, f32[1,2048]{1,0:T(1,128)} %bitcast.70, bf16[4,8,48,2048]{3,2,1,0:T(8,128)(2,1)} %bitcast.76, ...), custom_call_target="tpu_custom_call" | custom-call | flops 17179869184 | bytes 157286400 | tf_op jit(solution)/shard_map/pallas_call | solution.py:383
  245.4 50.7 %shard_map.217 = (bf16[2048,2048]{1,0:T(8,128)(2,1)}, bf16[1024,2048]{1,0:T(8,128)(2,1)}) custom-call(bf16[256,2048]{1,0:T(8,128)(2,1)} %bitcast.65, bf16[1024,2048]{1,0:T(8,128)(2,1)} %refs_1_.8, bf16[2048,1024]{1,0:T(8,128)(2,1)} %get-tuple-element.77.refs_2_.refs_0_, bf16[2048,1024]{1,0:T(8,128)(2,1)} %get-tuple-element.79.refs_3_, ...), custom_call_target="tpu_custom_call" | custom-call | flops 17179869184 | bytes 157286400 | tf_op jit(solution)/shard_map/pallas_call | solution.py:383
  296.1 61.5 %shard_map.218 = (f32[256,2048]{1,0:T(8,128)}, bf16[8,256,2048]{2,1,0:T(8,128)(2,1)}, bf16[8,32,2048]{2,1,0:T(8,128)(2,1)}, bf16[8,32,2048]{2,1,0:T(8,128)(2,1)}) custom-call(bf16[2048,1024]{1,0:T(8,128)(2,1)} %get-tuple-element.77.refs_2_.refs_0_, bf16[1024,2048]{1,0:T(8,128)(2,1)} %refs_1_.8, bf16[2048,2048]{1,0:T(8,128)(2,1)} %get-tuple-element.78.refs_2_, ...), custom_call_target="tpu_custom_call" | custom-call | flops 25769803776 | bytes 157286400 | tf_op jit(solution)/shard_map/pallas_call | solution.py:383
  357.6 71.1 %shard_map.219 = (f32[256,2048]{1,0:T(8,128)}, bf16[8,32,2048]{2,1,0:T(8,128)(2,1)}, bf16[8,32,2048]{2,1,0:T(8,128)(2,1)}, bf16[8,32,2048]{2,1,0:T(8,128)(2,1)}, bf16[8,32,2048]{2,1,0:T(8,128)(2,1)}) custom-call(bf16[2048,2048]{1,0:T(8,128)(2,1)} %get-tuple-element.81.refs_3_.refs_0_, bf16[2048,2048]{1,0:T(8,128)(2,1)} %bitcast.77, ...), custom_call_target="tpu_custom_call" | custom-call | flops 17179869184 | bytes 157286400 | tf_op jit(solution)/shard_map/pallas_call | solution.py:383
  428.8 2.3 multiply_reduce_fusion
  431.1 0.1 copy-done.22
  431.2 1.6 fusion.13.refs_0_
  432.9 65.3 %shard_map.220 = (bf16[2048,256]{1,0:T(8,128)(2,1)}, bf16[256,2048]{1,0:T(8,128)(2,1)}, bf16[8,32,2048]{2,1,0:T(8,128)(2,1)}, bf16[8,32,2048]{2,1,0:T(8,128)(2,1...) custom-call(bf16[256,2048]{1,0:T(8,128)(2,1)} %fusion.13.refs_0_, bf16[256,2048]{1,0:T(8,128)(2,1)} %refs_1_.9, ...), custom_call_target="tpu_custom_call" | custom-call | flops 4294967296 | bytes 157286400 | tf_op jit(solution)/shard_map/pallas_call | solution.py:383
  498.2 2.3 shard_map.221.refs_0_
  500.6 31.3 %shard_map.222 = (bf16[2048,512]{1,0:T(8,128)(2,1)}, bf16[8,32,2048]{2,1,0:T(8,128)(2,1)}, bf16[8,32,2048]{2,1,0:T(8,128)(2,1)}, bf16[8,32,2048]{2,1,0:T(8,128)(2,1)}) custom-call(bf16[2048,256]{1,0:T(8,128)(2,1)} %shard_map.221.refs_0_, bf16[2048,256]{1,0:T(8,128)(2,1)} %copy-done.14, bf16[2,2048,128]{2,1,0:T(8,128)(2,1)} %copy-done.13, ...), custom_call_target="tpu_custom_call" | custom-call | flops 8589934592 | bytes 29360128 | tf_op jit(solution)/shard_map/pallas_call | solution.py:383
  531.8 3.1 shard_map.223.refs_0_
  535.0 74.6 %shard_map.224 = (f32[256,2048]{1,0:T(8,128)}, bf16[8,256,512]{2,1,0:T(8,128)(2,1)}, bf16[8,32,2048]{2,1,0:T(8,128)(2,1)}, bf16[8,32,2048]{2,1,0:T(8,128)(2,1)},...) custom-call(bf16[2048,512]{1,0:T(8,128)(2,1)} %shard_map.223.refs_0_, ...), custom_call_target="tpu_custom_call" | custom-call | flops 8589934592 | bytes 157286400 | tf_op jit(solution)/shard_map/pallas_call | solution.py:383
  609.6 2.2 fusion.8
  611.9 0.6 pad.4.refs_1_
  612.5 213.0 %shard_map.225 = (bf16[256,8192]{1,0:T(8,128)(2,1)}, bf16[256,8192]{1,0:T(8,128)(2,1)}, bf16[2,8,32,2048]{3,2,1,0:T(8,128)(2,1)}, f32[8,256]{1,0:T(8,128)}, bf16...) custom-call(bf16[8,8,32,512]{3,2,1,0:T(8,128)(2,1)} %bitcast.67, ...), custom_call_target="tpu_custom_call" | custom-call | bytes 209715200 | tf_op jit(solution)/shard_map/pallas_call | solution.py:383
  825.6 1.3 fusion.14
  827.0 5.1 fusion.11
  832.1 0.3 copy-done.1
  832.4 0.5 copy-done.3
  832.9 0.3 copy-done.4
  833.2 0.3 copy-done.5
  833.5 0.3 copy-done.6
  833.8 1.2 copy-done.7
  835.0 1.2 copy-done.8
  836.3 1.2 copy-done.9
  837.5 10.9 %shard_map.226 = (f32[256,2048]{1,0:T(8,128)}, f32[256,1024]{1,0:T(8,128)}, f32[256,1024]{1,0:T(8,128)}, f32[256,2048]{1,0:T(8,128)}, f32[256,8192]{1,0:T(8,128)...) custom-call(bf16[256,2048]{1,0:T(8,128)(2,1)S(1)} %bitcast.53, bf16[256,2048]{1,0:T(8,128)(2,1)S(1)} %bitcast.54, ...), custom_call_target="tpu_custom_call" | custom-call | bytes 47185920 | tf_op jit(solution)/shard_map/pallas_call | solution.py:1351
  (49 shorter events, 0.2 us)
Async XLA Ops:
  7.2 185.1 %all-gather.3.cloned.1.call-start = ((), (), s32[]{:S(2)}) async-start(), calls=%async_computation.1 | async-start | bytes 7864320 | tf_op jit(solution)/shard_map/all_gather | solution.py:1429
  29.8 66.1 %slice-start = ((bf16[256,8192]{1,0:T(8,128)(2,1)}), bf16[64,8192]{1,0:T(8,128)(2,1)S(1)}, s32[]{:S(2)}) async-start(bf16[256,8192]{1,0:T(8,128)(2,1)} %refs_0_.1), calls=%async_computation.2 | async-start | bytes 2097152 | tf_op jit(solution)/shard_map/slice | solution.py:1434
  29.8 66.1 %slice-start.1 = ((bf16[256,8192]{1,0:T(8,128)(2,1)}), bf16[64,8192]{1,0:T(8,128)(2,1)S(1)}, s32[]{:S(2)}) async-start(bf16[256,8192]{1,0:T(8,128)(2,1)} %refs_1_.5), calls=%async_computation.3 | async-start | bytes 2097152 | tf_op jit(solution)/shard_map/slice | solution.py:1434
  97.6 94.7 %all-to-all-start = ((bf16[64,8,2048]{2,0,1:T(8,128)(2,1)}), bf16[64,8,2048]{2,0,1:T(8,128)(2,1)S(1)}, u32[]{:S(2)}, u32[]{:S(2)}) async-start(bf16[64,8,2048]{2,0,1:T(8,128)(2,1)} %pad_maximum_fusion), calls=%async_computation | async-start | bytes 4194304 | tf_op jit(solution)/shard_map/all_to_all | solution.py:1412
  111.8 3.7 copy-start.11
  116.1 1.6 copy-start.10
  117.7 20.2 %copy-start.2 = (f32[2048,128]{1,0:T(8,128)}, f32[2048,128]{1,0:T(8,128)S(1)}, u32[]{:S(2)}) copy-start(f32[2048,128]{1,0:T(8,128)S(1)} %get-tuple-element.141.cos_ref.refs_6_) | copy-start | bytes 3145732
  137.9 1.0 copy-start.12
  138.9 1.0 copy-start.13
  139.8 1.0 copy-start.14
  140.8 0.8 copy-start.15
  141.6 0.8 copy-start.16
  142.4 0.6 copy-start.17
  143.0 46.1 %copy-start.21 = (bf16[1,256,2048]{2,1,0:T(8,128)(2,1)S(1)}, bf16[1,256,2048]{2,1,0:T(8,128)(2,1)}, u32[]{:S(2)}) copy-start(bf16[1,256,2048]{2,1,0:T(8,128)(2,1)} %param.13) | copy-start | bytes 3145732
  192.3 1.3 copy-start.23
  357.6 71.1 %copy-start.18 = (f32[256,2048]{1,0:T(8,128)S(1)}, f32[256,2048]{1,0:T(8,128)}, u32[]{:S(2)}) copy-start(f32[256,2048]{1,0:T(8,128)} %get-tuple-element.132.refs_0_) | copy-start | bytes 6291460
  357.6 71.1 %copy-start.25 = (f32[2048]{0:T(1024)S(1)}, f32[2048]{0:T(1024)}, u32[]{:S(2)}) copy-start(f32[2048]{0:T(1024)} %param.25) | copy-start | bytes 24580
  428.8 2.3 copy-start.19
  428.8 2.5 copy-start.22
  535.0 74.6 %copy-start.24 = (f32[2048]{0:T(1024)S(1)}, f32[2048]{0:T(1024)}, u32[]{:S(2)}) copy-start(f32[2048]{0:T(1024)} %param.24) | copy-start | bytes 24580
  612.5 214.4 %copy-start.20 = (f32[256,2048]{1,0:T(8,128)S(1)}, f32[256,2048]{1,0:T(8,128)}, u32[]{:S(2)}) copy-start(f32[256,2048]{1,0:T(8,128)} %get-tuple-element.87) | copy-start | bytes 6291460
  826.9 5.2 copy-start
  826.9 5.5 copy-start.1
  826.9 6.0 copy-start.3
  826.9 6.3 copy-start.4
  826.9 6.6 copy-start.5
  826.9 6.9 copy-start.6
  833.8 1.2 copy-start.7
  835.0 1.2 copy-start.8
  836.3 1.2 copy-start.9
Sparse Core Ops, SparseCore 0:
  29.9 116.5 all-gather.2

commit v5 on v4

--- a/solution.py
+++ b/solution.py
@@ -2,6 +2,7 @@
 
 import jax
 import jax.numpy as jnp
+import numpy as np
 from jax import lax
 from jax.experimental import pallas as pl
 from jax.experimental.pallas import tpu as pltpu
@@ -34,10 +35,11 @@
 
 def turn_tables(length):
     half_size = HD // 2
-    inverse = ROPE_BASE ** (-(jnp.arange(half_size, dtype=f32) * 2.0) / HD)
-    angles = jnp.arange(length, dtype=jnp.int32).astype(f32)[:, None] * inverse
-    cosine, sine = jnp.cos(angles), jnp.sin(angles)
-    return jnp.concatenate([cosine, cosine], -1), jnp.concatenate([-sine, sine], -1)
+    inverse = np.float32(ROPE_BASE) ** (-(np.arange(half_size, dtype=np.float32) * 2) / HD)
+    angles = np.arange(length, dtype=np.float32)[:, None] * inverse.astype(np.float32)
+    cosine, sine = np.cos(angles), np.sin(angles)
+    tables = np.concatenate([cosine, cosine], -1), np.concatenate([-sine, sine], -1)
+    return tuple(jnp.asarray(table.astype(np.float32)) for table in tables)
 
 
 def norm_back(upstream, grad_normed, unit_rows, inv_root, gain):
@@ -156,7 +158,7 @@
         in_specs=[pl.BlockSpec(memory_space=pltpu.SMEM)] + vmem_specs(5),
         out_specs=tuple(vmem_specs(6)),
         scratch_shapes=[pltpu.VMEM((length // block, heads * block, block), f32)],
-        compiler_params=pltpu.CompilerParams(vmem_limit_bytes=48 * 2**20),
+        compiler_params=pltpu.CompilerParams(vmem_limit_bytes=60 * 2**20),
         cost_estimate=pl.CostEstimate(
             flops=3 * heads * length * length * HD, bytes_accessed=10 * length * HD * heads * 4,
             transcendentals=heads * length * length // 2,
@@ -164,7 +166,12 @@
     )(order, qkv, cosine, sine, piece, piece_col)
 
 
-CHUNKS = 15
+DOWN, GATE_UP, OUT, QKV = 8, 16, 2, 4
+CHUNKS = DOWN + GATE_UP + OUT + QKV
+
+
+def is_chunk(number):
+    return 0 <= number < CHUNKS
 
 
 def is_middle():
@@ -184,24 +191,28 @@
         if others:
             pl.semaphore_wait(barrier, others)
 
-    def open(self, number):
+    def start(self):
         pass
 
-    def close(self, number):
+    def step(self):
         pass
 
-    def finish(self):
+    def end(self):
         pass
 
 
 class Line:
     def __init__(self, first, ticks, picks, refs, outs, scratch):
         self.first, self.ticks, self.picks, self.refs, self.outs = first, ticks, picks, refs, outs
-        self.inward, self.across, self.own, self.pair, self.total, self.sems, self.local = scratch
+        (
+            self.inward, self.across, self.own, self.pair, self.total, self.sems, self.local,
+            self.carries,
+        ) = scratch
         rank = lax.axis_index("rep")
         self.partner = {"rep": rank + 1 - 2 * (rank % 2)}
         self.peer = {"rep": 3 - rank}
-        self.slots = line_slots(first, ticks)
+        self.now = 0
+        self.kept = []
 
     def greet(self, barrier, others):
         pl.semaphore_signal(barrier, inc=1, device_id=self.partner, device_id_type=MESH)
@@ -224,34 +235,34 @@
     def hops(self, number):
         tick = self.first + number
         term = pair = total = None
-        if tick < CHUNKS:
+        if is_chunk(tick):
             which, pick = self.picks[tick]
             term = (
                 lambda: self.remote(
                     0, number, pick(self.refs[which]), self.inward.at[number], self.partner
                 ),
                 lambda: pltpu.make_async_copy(
-                    pick(self.refs[which]), self.own.at[number % 2], self.local.at[0, number]
+                    pick(self.refs[which]), self.own.at[tick % 2], self.local.at[0, number]
                 ),
             )
-        if 1 <= tick <= CHUNKS:
-            before = self.refs["pair"] if number == 0 else self.pair.at[(number - 1) % 2]
+        if is_chunk(tick - 2):
+            before = self.refs[f"pair{number}"] if number < 2 else self.pair.at[(tick - 2) % 3]
             pair = (
                 lambda: self.remote(1, number, before, self.across.at[number], self.peer),
-                lambda: pltpu.make_async_copy(before, self.pair.at[2], self.local.at[1, number]),
+                lambda: pltpu.make_async_copy(
+                    before, self.pair.at[(tick - 2) % 3], self.carries.at[number]
+                ),
             )
-        if 2 <= tick <= CHUNKS + 1:
-            done = self.refs["total"] if number == 0 else self.total.at[(number - 1) % 2]
-            slot = self.outs[tick - 2]
+        if is_chunk(tick - 4):
+            done = self.refs[f"total{number}"] if number < 2 else self.total.at[(tick - 4) % 3]
+            slot = self.outs[tick - 4]
             total = (
                 lambda: self.remote(2, number, done, slot, self.partner),
-                lambda: pltpu.make_async_copy(done, slot, self.local.at[2, number]),
+                lambda: pltpu.make_async_copy(done, slot, self.local.at[1, number]),
             )
         return term, pair, total
 
     def open(self, number):
-        if number >= self.ticks:
-            return
         term, pair, total = self.hops(number)
 
         @pl.when(is_end())
@@ -265,23 +276,15 @@
                 pair[0]().start()
             if total:
                 total[0]().start()
-                total[1]().start()
             if term:
                 term[1]().start()
-            if pair and number == 0:
+            if total:
+                total[1]().start()
+            if pair and number < 2:
                 pair[1]().start()
 
     def close(self, number):
-        if number >= self.ticks:
-            return
         term, pair, total = self.hops(number)
-
-        def add(into, first, second):
-            def one(g, _):
-                into[g] = (first[g].astype(f32) + second[g].astype(f32)).astype(bf16)
-                return 0
-
-            lax.fori_loop(0, into.shape[0], one, 0)
 
         @pl.when(is_end())
         def _():
@@ -298,42 +301,85 @@
             if pair:
                 pair[0]().wait_send()
                 pair[0]().wait_recv()
-                if number == 0:
+            if term:
+                term[0]().wait_recv()
+
+    def add(self, number):
+        term, pair, _ = self.hops(number)
+        tick = self.first + number
+
+        def sum_of(into, first, second):
+            def one(g, _):
+                into[g] = (first[g].astype(f32) + second[g].astype(f32)).astype(bf16)
+                return 0
+
+            lax.fori_loop(0, into.shape[0], one, 0)
+
+        @pl.when(is_middle())
+        def _():
+            if pair:
+                if number < 2:
                     pair[1]().wait()
-                before = 2 if number == 0 else (number - 1) % 2
-                add(self.total.at[number % 2], self.pair.at[before], self.across.at[number])
+                sum_of(
+                    self.total.at[(tick - 2) % 3], self.pair.at[(tick - 2) % 3],
+                    self.across.at[number],
+                )
             if term:
                 term[1]().wait()
-                term[0]().wait_recv()
-                add(self.pair.at[number % 2], self.own.at[number % 2], self.inward.at[number])
-
-    def finish(self):
-        last = self.ticks - 1
-        tick = self.first + last
+                sum_of(self.pair.at[tick % 3], self.own.at[tick % 2], self.inward.at[number])
+
+    def keep(self, number):
+        tick = self.first + number
+        which = number - (self.ticks - 2)
+        made = []
+        if is_chunk(tick):
+            made.append((self.pair.at[tick % 3], self.outs[f"pair{which}"], 2 + which))
+        if is_chunk(tick - 2):
+            made.append((self.total.at[(tick - 2) % 3], self.outs[f"total{which}"], 4 + which))
+        copies = [
+            lambda src=src, dst=dst, at=at: pltpu.make_async_copy(src, dst, self.carries.at[at])
+            for src, dst, at in made
+        ]
 
         @pl.when(is_middle())
         def _():
-            if tick < CHUNKS:
-                keep = pltpu.make_async_copy(
-                    self.pair.at[last % 2], self.outs["pair"], self.local.at[0, last]
-                )
-                keep.start()
-                keep.wait()
-            if 1 <= tick <= CHUNKS:
-                keep = pltpu.make_async_copy(
-                    self.total.at[last % 2], self.outs["total"], self.local.at[1, last]
-                )
-                keep.start()
-                keep.wait()
+            for copy in copies:
+                copy().start()
+
+        self.kept += copies
+
+    def start(self):
+        self.open(0)
+
+    def step(self):
+        if self.now + 1 < self.ticks:
+            self.close(self.now)
+            self.open(self.now + 1)
+            self.add(self.now)
+            if self.now == self.ticks - 2:
+                self.keep(self.now)
+            self.now += 1
+
+    def end(self):
+        while self.now + 1 < self.ticks:
+            self.step()
+        self.close(self.now)
+        self.add(self.now)
+        self.keep(self.now)
+
+        @pl.when(is_middle())
+        def _():
+            for copy in self.kept:
+                copy().wait()
 
 
 def line_slots(first, ticks):
-    return [t - 2 for t in range(first, first + ticks) if 2 <= t <= CHUNKS + 1]
+    return [t - 4 for t in range(first, first + ticks) if is_chunk(t - 4)]
 
 
 class Sums:
     def __init__(self, shape):
-        self.shape, self.tick, self.pair, self.total, self.done = shape, 0, None, None, {}
+        self.shape, self.tick, self.kept, self.done = shape, 0, {}, {}
 
 
 def run(kernel, ins, outs, scratch, number, cost, sums=None, ticks=0, arrays=(), picks=None, vmem=58):
@@ -347,26 +393,26 @@
         for name, array in arrays:
             names_in.append(name)
             ins.append((array, pl.ANY))
-        if 1 <= first <= CHUNKS:
-            names_in.append("pair")
-            ins.append((sums.pair, pl.ANY))
-        if 2 <= first <= CHUNKS + 1:
-            names_in.append("total")
-            ins.append((sums.total, pl.ANY))
+        for which in (0, 1):
+            for name, chunk_at in ((f"pair{which}", first - 2), (f"total{which}", first - 4)):
+                if is_chunk(chunk_at + which):
+                    names_in.append(name)
+                    ins.append((sums.kept[name], pl.ANY))
         names_out = line_slots(first, ticks)
-        if last < CHUNKS:
-            names_out.append("pair")
-        if 1 <= last <= CHUNKS:
-            names_out.append("total")
+        for which in (0, 1):
+            for name, chunk_at in ((f"pair{which}", last - 1), (f"total{which}", last - 3)):
+                if is_chunk(chunk_at + which):
+                    names_out.append(name)
         outs += [(chunk, pl.ANY)] * len(names_out)
         scratch += [
             pltpu.VMEM((ticks,) + sums.shape, bf16),
             pltpu.VMEM((ticks,) + sums.shape, bf16),
             pltpu.VMEM((2,) + sums.shape, bf16),
             pltpu.VMEM((3,) + sums.shape, bf16),
-            pltpu.VMEM((2,) + sums.shape, bf16),
+            pltpu.VMEM((3,) + sums.shape, bf16),
             pltpu.SemaphoreType.DMA((2, 3, ticks)),
-            pltpu.SemaphoreType.DMA((3, ticks)),
+            pltpu.SemaphoreType.DMA((2, ticks)),
+            pltpu.SemaphoreType.DMA((6,)),
         ]
 
     def body(*refs):
@@ -395,12 +441,10 @@
         ),
     )(*[array for array, _ in ins])
     for name, result in zip(names_out, results[counts[1] :]):
-        if name == "pair":
-            sums.pair = result
-        elif name == "total":
-            sums.total = result
+        if name in line_slots(first, ticks):
+            sums.done[name] = result
         else:
-            sums.done[name] = result
+            sums.kept[name] = result
     if ticks:
         sums.tick += ticks
     return results[: counts[1]]
@@ -417,7 +461,7 @@
     grads, centers, grad_q = scratch
     if line.ticks:
         line.greet(pltpu.get_barrier_semaphore(), 0)
-        line.open(0)
+        line.start()
     length = grad_ref.shape[0]
     blocks = length // block
 
@@ -471,7 +515,10 @@
         grad_qkv_ref[cols, (heads + 1) * HD :] = grad_value.astype(bf16)
         return 0
 
-    lax.fori_loop(0, blocks, key_block, 0)
+    for j in range(min(2, blocks - 1)):
+        lax.fori_loop(j, j + 1, key_block, 0)
+        line.step()
+    lax.fori_loop(min(2, blocks - 1), blocks, key_block, 0)
 
     def turn_back(i, _):
         rows = pl.ds(pl.multiple_of(i * block, block), block)
@@ -482,9 +529,7 @@
         return 0
 
     lax.fori_loop(0, blocks, turn_back, 0)
-    if line.ticks:
-        line.close(0)
-        line.finish()
+    line.end()
 
 
 def take_cuts_kernel(cuts, holder_ref, rows_ref, out_ref):
@@ -610,12 +655,12 @@
     send(5, ALONG_Y, 0, 0, to_x)
     send(7, ALONG_X, 0, 1, to_s)
     send(8, ALONG_Y, 0, 0, to_s)
+    line.step()
     landed(2, ALONG_X, 0, 0)
     send(9, ALONG_X, 0, 0, to_s)
     landed(4, ALONG_Y, 0, 1)
     send(10, ALONG_Y, 0, 1, to_s)
-    line.close(0)
-    line.open(1)
+    line.step()
     landed(7, ALONG_X, 1, 1)
     landed(9, ALONG_X, 1, 0)
     on_chip(*ALONG_X)
@@ -623,6 +668,7 @@
     send(11, ACROSS, 0, 0, to_s)
     landed(6, ACROSS, 0, 1)
     send(12, ACROSS, 0, 1, to_s)
+    line.step()
     landed(8, ALONG_Y, 1, 0)
     landed(10, ALONG_Y, 1, 1)
     on_chip(*ALONG_Y)
@@ -631,8 +677,7 @@
     on_chip(*ACROSS)
     for one in started:
         one.wait_send()
-    line.close(1)
-    line.finish()
+    line.end()
 
 
 GATHER_COPIES = 13
@@ -789,7 +834,7 @@
     loads.append(moves.start(rest_ref, weight.at[:, planes * tall :, :]))
     held[own_rows(rows), :] = rms_normed(mid_ref[...], gain_ref[...]).astype(bf16)
     greet_group(line)
-    line.open(0)
+    line.start()
 
     def on_chip(*chip):
         where = chip_rows(*chip, rows)
@@ -855,7 +900,7 @@
     ]
     held[own_rows(rows), :] = grad_ref[...]
     greet_group(line)
-    line.open(0)
+    line.start()
 
     def on_chip(*chip):
         where = chip_rows(*chip, rows)
@@ -920,7 +965,7 @@
     moves = Moves(sems)
     held[own_rows(rows), :] = grad_ref[...]
     greet_group(line)
-    line.open(0)
+    line.start()
 
     def on_chip(*chip):
         where = chip_rows(*chip, rows)
@@ -1006,7 +1051,7 @@
     half = rows // 2
     _, _, core = place_in_group()
     greet_group(line)
-    line.open(0)
+    line.start()
     if extra:
         columns_ref = a_ref
         if extra == "loaded":
@@ -1067,6 +1112,7 @@
     to_chip[1, first, :] = own(0, 1).astype(bf16)
     send(6, to_chip.at[1, first, :], last.at[0, first, :], to_x)
     held[0] = own(1, 1)
+    line.step()
     make(2, ALONG_Y)
     landed(2, from_s.at[2])
     to_chip[2, second, :] = own(1, 2).astype(bf16)
@@ -1082,11 +1128,12 @@
     landed(4, relay.at[0])
     to_chip[2, first, :] = (held[1] + relay[0].astype(f32)).astype(bf16)
     send(9, to_chip.at[2, first, :], last.at[1, first, :], to_y)
-    line.close(0)
-    line.open(1)
+    line.step()
     make(3, SIBLING)
     if extra:
-        term.work((3, 4, 5, 6, 7))
+        term.work((3, 4))
+        line.step()
+        term.work((5, 6, 7))
     landed(3, from_s.at[3])
     for low in (0, 1):
         out_ref[low * half : (low + 1) * half, :] = own(low, 3)
@@ -1094,6 +1141,7 @@
     out_ref[first, :] += last[0, first, :].astype(f32)
     landed(7, last.at[1, second, :])
     out_ref[second, :] += last[1, second, :].astype(f32)
+    line.step()
     landed(8, last.at[0, second, :])
     out_ref[second, :] += last[0, second, :].astype(f32)
     landed(9, last.at[1, first, :])
@@ -1102,8 +1150,7 @@
         one.wait_send()
     if extra:
         term.finish()
-    line.close(1)
-    line.finish()
+    line.end()
 
 
 def product_scattered(a, b, turned, extra=None, **line):
@@ -1180,7 +1227,7 @@
         qkv_copies.append(send(0, number, qkv_ref.at[target], own_qkv, {"grp": target}))
         qkv_copies[-1].start()
     moves.later(qkv_ref.at[me], own_qkv)
-    line.open(0)
+    line.start()
     for number, flip in enumerate(EVERYONE):
         target = other(*flip)
         gain_copies.append(
@@ -1191,7 +1238,7 @@
 
     def spread(chunk):
         src = chunk_refs[chunk] if chunk in chunk_refs else line.outs[chunk]
-        number = chunk - 4
+        number = chunk - DOWN
         rows = slice(number * high, (number + 1) * high)
         cols = pl.ds(pl.multiple_of(me * inner, inner), inner)
         for which, dst in enumerate((gate_ref, up_ref)):
@@ -1229,17 +1276,16 @@
         one.wait()
         mine[(rank + 4 - step) % 4] = from_rep[step]
     gains_out_ref[...] = (mine[0] + mine[1]) + (mine[2] + mine[3])
-    line.close(0)
     for number in range(1, line.ticks):
-        if line.first + number == CHUNKS - 2:
+        if line.first + number == CHUNKS - QKV:
             for one in qkv_copies:
                 one.wait()
             moves.open.pop(0).wait()
-        line.open(number)
-        chunk = line.first + number - 3
+        line.step()
+        chunk = line.first + number - 5
         if chunk in later:
             spread(chunk)
-        line.close(number)
+    line.end()
     for one in waits:
         one.wait_send()
         one.wait_recv()
@@ -1249,14 +1295,16 @@
 def tail(qkv_term, gains, chunks, inner, number, sums, ticks, arrays, picks):
     first = sums.tick
     ready = sorted(chunks)
-    later = [c for c in line_slots(first, ticks) if c < 12]
+    later = [c for c in line_slots(first, ticks) if c < DOWN + GATE_UP]
     _, high, width = sums.shape
-    part = qkv_term.shape[-1]
-    wide = jax.ShapeDtypeStruct((8 * high, 8 * inner), bf16)
-    moved = jax.ShapeDtypeStruct((2,) + sums.shape, bf16)
+    wide = jax.ShapeDtypeStruct((GATE_UP * high, 8 * inner), bf16)
+    moved = jax.ShapeDtypeStruct((2, 8, 2 * high, width), bf16)
     picks = dict(picks)
-    for half in (0, 1):
-        picks[CHUNKS - 2 + half] = ("qkv", lambda ref, half=half: ref.at[half])
+    for n in range(QKV):
+        picks[CHUNKS - QKV + n] = (
+            "qkv",
+            lambda ref, n=n: ref.at[n // 2, :, (n % 2) * high : (n % 2 + 1) * high, :],
+        )
     return run(
         functools.partial(tail_kernel, ready, later),
         [(qkv_term, ANY), (gains, VMEM)] + [(chunks[c], ANY) for c in ready],
@@ -1267,101 +1315,110 @@
             pltpu.VMEM((4,) + gains.shape[1:], f32),
             pltpu.SemaphoreType.DMA((3, 7)),
             pltpu.SemaphoreType.DMA((3, 7)),
-            pltpu.SemaphoreType.DMA((2, 2, 8)),
-            pltpu.SemaphoreType.DMA((17,)),
+            pltpu.SemaphoreType.DMA((2, 2, GATE_UP)),
+            pltpu.SemaphoreType.DMA((1 + 2 * GATE_UP,)),
         ],
         number, (0, 200 * 8 * high * width * 2, 0), sums=sums, ticks=ticks, arrays=arrays, picks=picks,
     )
 
 
 def finish_kernel(heads, *refs):
-    ins, rest = refs[:9], refs[9:]
-    outs, (low, wide, load_sems, store_sems) = rest[:7], rest[7:]
-    down_refs, out_sum, qkv_refs, gate_rows, up_rows = ins[:4], ins[4], ins[5:7], ins[7], ins[8]
-    query, key, value, out, gate, up, down = outs
-    rows, width = down_refs[0].shape
-    jobs = []
-    for number, ref in enumerate(down_refs):
-        jobs.append((ref, [(slice(0, width), down.at[number * rows : (number + 1) * rows, :])]))
+    chunks, rest = refs[: DOWN + OUT + QKV], refs[DOWN + OUT + QKV :]
+    gate_rows, up_rows = rest[:2]
+    query, key, value, out, gate, up, down = rest[2:9]
+    low, wide, load_sems, store_sems = rest[9:]
+    _, high, width = chunks[0].shape
+    depth = low.shape[0]
+
+    def half(number):
+        return slice(number * high, (number + 1) * high)
+
+    whole = slice(0, width)
+    jobs = [(ref, [(whole, down.at[number])]) for number, ref in enumerate(chunks[:DOWN])]
     for ref, into in ((gate_rows, gate), (up_rows, up)):
-        for low_col in range(0, ref.shape[1], width):
+        for low_col in range(0, ref.shape[2], width):
             cols = slice(low_col, low_col + width)
-            jobs.append((ref.at[:, cols], [(slice(0, width), into.at[:, cols])]))
-    jobs.append((out_sum, [(slice(0, width), out)]))
+            for number in (0, 1):
+                where = (slice(None), half(number), cols)
+                jobs.append((ref.at[where], [(whole, into.at[where])]))
+    for number, ref in enumerate(chunks[DOWN : DOWN + OUT]):
+        jobs.append((ref, [(whole, out.at[:, half(number), :])]))
     part = (heads + 2) * HD
-    for number, ref in enumerate(qkv_refs):
+    for number, ref in enumerate(chunks[DOWN + OUT :]):
         stores = []
         for place in range(width // part):
-            at, device = place * part, number * (width // part) + place
+            at, device = place * part, (number // 2) * (width // part) + place
             for into, first, size in (
                 (query, 0, heads * HD), (key, heads * HD, HD), (value, (heads + 1) * HD, HD)
             ):
-                stores.append(
-                    (
-                        slice(at + first, at + first + size),
-                        into.at[:, device * size : (device + 1) * size],
-                    )
-                )
+                there = into.at[:, half(number % 2), device * size : (device + 1) * size]
+                stores.append((slice(at + first, at + first + size), there))
         jobs.append((ref, stores))
 
     def load(number):
-        return pltpu.make_async_copy(
-            jobs[number][0], low.at[number % 3], load_sems.at[number % 3]
-        )
+        at = number % depth
+        return pltpu.make_async_copy(jobs[number][0], low.at[at], load_sems.at[at])
 
     def stores(number):
+        at = number % depth
         return [
-            pltpu.make_async_copy(
-                wide.at[number % 3, :, cols], into, store_sems.at[number % 3, which]
-            )
+            pltpu.make_async_copy(wide.at[at, :, :, cols], into, store_sems.at[at, which])
             for which, (cols, into) in enumerate(jobs[number][1])
         ]
 
-    for number in range(min(2, len(jobs))):
+    for number in range(depth - 1):
         load(number).start()
     for number in range(len(jobs)):
-        if number + 2 < len(jobs):
-            load(number + 2).start()
+        if number + depth - 1 < len(jobs):
+            load(number + depth - 1).start()
         load(number).wait()
-        if number >= 3:
-            for one in stores(number - 3):
+        if number >= depth:
+            for one in stores(number - depth):
                 one.wait()
 
-        def cast(g, _, at=number % 3):
-            some = pl.ds(pl.multiple_of(g * 32, 32), 32)
-            wide[at, some, :] = low[at, some, :].astype(f32)
+        def cast(g, _, at=number % depth):
+            wide[at, g] = low[at, g].astype(f32)
             return 0
 
-        lax.fori_loop(0, rows // 32, cast, 0)
+        lax.fori_loop(0, low.shape[1], cast, 0)
         for one in stores(number):
             one.start()
-    for number in range(max(0, len(jobs) - 3), len(jobs)):
+    for number in range(len(jobs) - depth, len(jobs)):
         for one in stores(number):
             one.wait()
 
 
-def finish(downs, out_sum, qkvs, gate_rows, up_rows, heads):
-    rows, width = out_sum.shape
-    wide = gate_rows.shape[1]
-    shapes = [
-        (rows, 8 * heads * HD), (rows, 8 * HD), (rows, 8 * HD), (rows, width), (rows, wide),
-        (rows, wide), (len(downs) * rows, width),
-    ]
-    size = len(downs) * rows * width + 2 * rows * wide + 3 * rows * width
-    return pl.pallas_call(
+def finish(chunks, gate_rows, up_rows, heads):
+    eight, high, width = chunks[0].shape
+    rows, wide = gate_rows.shape
+
+    def split(columns):
+        return jax.ShapeDtypeStruct((eight, rows // eight, columns), f32)
+
+    shapes = [split(columns) for columns in (8 * heads * HD, 8 * HD, 8 * HD, width, wide, wide)]
+    shapes.append(jax.ShapeDtypeStruct((DOWN, eight, high, width), f32))
+    depth = 4
+    results = pl.pallas_call(
         functools.partial(finish_kernel, heads),
-        out_shape=tuple(jax.ShapeDtypeStruct(shape, f32) for shape in shapes),
-        in_specs=[pl.BlockSpec(memory_space=pl.ANY)] * 9,
+        out_shape=tuple(shapes),
+        in_specs=[pl.BlockSpec(memory_space=pl.ANY)] * (len(chunks) + 2),
         out_specs=tuple([pl.BlockSpec(memory_space=pl.ANY)] * 7),
         scratch_shapes=[
-            pltpu.VMEM((3, rows, width), bf16),
-            pltpu.VMEM((3, rows, width), f32),
-            pltpu.SemaphoreType.DMA((3,)),
-            pltpu.SemaphoreType.DMA((3, 12)),
+            pltpu.VMEM((depth, eight, high, width), bf16),
+            pltpu.VMEM((depth, eight, high, width), f32),
+            pltpu.SemaphoreType.DMA((depth,)),
+            pltpu.SemaphoreType.DMA((depth, 12)),
         ],
         compiler_params=pltpu.CompilerParams(vmem_limit_bytes=32 * 2**20),
-        cost_estimate=pl.CostEstimate(flops=0, bytes_accessed=6 * size, transcendentals=0),
-    )(*downs, out_sum, *qkvs, gate_rows, up_rows)
+        cost_estimate=pl.CostEstimate(
+            flops=0, bytes_accessed=6 * CHUNKS * eight * high * width, transcendentals=0
+        ),
+    )(
+        *chunks, gate_rows.reshape(eight, rows // eight, wide),
+        up_rows.reshape(eight, rows // eight, wide),
+    )
+    flat = [result.reshape(rows, -1) for result in results[:6]]
+    return flat + [results[6].reshape(DOWN * eight * high, width)]
 
 
 def sum_over_sequences(term):
@@ -1483,18 +1540,19 @@
         grad_gate_up, down_term = feed_forward_back(
             grad_out, w_down, hidden, up_part, gate_part, number=4
         )
-        high = rows_here // 8
+        high = rows_here // GATE_UP
         sums = Sums((8, high, model_width))
-        terms = {"down": down_term.reshape((4,) + sums.shape)}
-
-        def pick_down(number):
+        terms = {"down": down_term.reshape((DOWN,) + sums.shape)}
+
+        def pick_whole(number):
             return "down", lambda ref: ref.at[number]
 
-        def pick_gate_up(number):
-            return "gate_up", lambda ref: ref.at[:, number * high : (number + 1) * high, :]
-
-        picks = [pick_down(n) for n in range(4)] + [pick_gate_up(n) for n in range(8)]
-        picks += [("out", lambda ref: ref)]
+        def pick_rows(name, number):
+            return name, lambda ref: ref.at[:, number * high : (number + 1) * high, :]
+
+        picks = [pick_whole(n) for n in range(DOWN)]
+        picks += [pick_rows("gate_up", n) for n in range(GATE_UP)]
+        picks += [pick_rows("out", n) for n in range(OUT)]
 
         def line(number, ticks):
             names = sorted(
@@ -1506,30 +1564,29 @@
             )
 
         down_sum, terms["gate_up"] = product_scattered(
-            hidden, w_down, False, extra=(normed_two, grad_gate_up), **line(5, 2)
+            hidden, w_down, False, extra=(normed_two, grad_gate_up), **line(5, 4)
         )
         result = result_of(down_sum)
-        grad_two = product_scattered(grad_gate_up, cols_gate_up, True, **line(6, 2))[0]
+        grad_two = product_scattered(grad_gate_up, cols_gate_up, True, **line(6, 5))[0]
         grad_mid, gain_ffn_term = finish_two(grad_two)
         grad_attended, out_term = attended_back(
-            grad_mid.astype(bf16), w_out, attended, **line(7, 2)
-        )
-        terms["out"] = out_term.reshape(sums.shape)
-        grad_qkv = back_through_attention(grad_attended, **line(8, 1))
+            grad_mid.astype(bf16), w_out, attended, **line(7, 4)
+        )
+        terms["out"] = out_term.reshape(8, OUT * high, model_width)
+        grad_qkv = back_through_attention(grad_attended, **line(8, 2))
         grad_one, qkv_term = product_scattered(
-            grad_qkv, cols_qkv, True, extra=(normed_one, None), **line(9, 2)
+            grad_qkv, cols_qkv, True, extra=(normed_one, None), **line(9, 4)
         )
         grad_x, gain_attn_term = finish_one(grad_mid, grad_one)
         gains = jnp.stack([gain_attn_term, gain_ffn_term]).reshape(2, groups, rows_here)
         gains = jnp.pad(jnp.moveaxis(gains, 0, 1), ((0, 0), (0, 6), (0, 0)))
-        rest = line(10, 8)
+        rest = line(10, CHUNKS + 4 - sums.tick)
         gate_rows, up_rows, qkv_rows, own_gains = tail(
-            qkv_term.reshape(8, 8, high, -1), gains,
-            {c: sums.done[c] for c in range(4, 7)}, hidden_here, **rest,
-        )
-        flat = [sums.done[n].reshape(rows_here, model_width) for n in range(4)]
-        last = [sums.done[n].reshape(rows_here, model_width) for n in (12, 13, 14)]
-        weight_grads = finish(flat, last[0], last[1:], gate_rows, up_rows, heads)
+            qkv_term.reshape(8, 8, 2 * high, -1), gains,
+            {c: sums.done[c] for c in sums.done if c >= DOWN}, hidden_here, **rest,
+        )
+        straight = [n for n in range(CHUNKS) if n < DOWN or n >= DOWN + GATE_UP]
+        weight_grads = finish([sums.done[n] for n in straight], gate_rows, up_rows, heads)
         return (result, grad_x) + tuple(weight_grads) + (own_gains[0], own_gains[1])
 
     normed_two = gather((unit_two * ffn_gain).astype(bf16))

time: 866 us -> 881 us (1.017)
  Pallas kernels: 789 us -> 813 us
    pallas_call x11, Pallas kernels: 754 us -> 775 us  [run(): pl.pallas_call(body, out_shape=tuple((shape for shape, _ in outs)), in_sp...]
  transfers between devices with their start and end apart: 2 -> 2, of which waited for: 0 -> 0; matrix products, arithmetic and copies ran while one was open for 3% -> 2% of each run, Pallas kernels for 15% -> 15%
where the time goes in v5:
time: 881 us; the launch traced here: 871 us
  Pallas kernels  813 us (92%)
  other arithmetic  16.6 us (2%)
  between operations  14.6 us (2%)
  local copies, waits for them, and re-layouts  12.9 us (1%)
  matrix products  10.5 us (1%)
    pallas_call x11, Pallas kernels, run(): pl.pallas_call(body, out_shape=tuple((shape for shape, _ in outs)), in_sp...  775 us
    pallas_call x1, Pallas kernels, attend(): pl.pallas_call(functools.partial(attend_kernel, heads, order.shape[1], bl...  21.2 us
  transfers between devices with their start and end apart: 2, of which 0 were waited for; matrix products, arithmetic and copies ran while one was open for 2% of the time, Pallas kernels for 15%

profile of v5, /device:TPU:0, one launch (start us, length us, event | category | flops | bytes accessed | tf_op | source)
XLA Modules:
  0.0 871.2 jit_solution(12461026822727336908)
XLA Ops:
  7.2 0.0 all-gather.3.cloned.1.call-start
  7.2 22.5 %shard_map.230 = bf16[8,48,2048]{2,1,0:T(8,128)(2,1)} custom-call(bf16[256,8192]{1,0:T(8,128)(2,1)} %refs_0_.1, bf16[256,8192]{1,0:T(8,128)(2,1)} %refs_1_.5), custom_call_target="tpu_custom_call" | custom-call | bytes 39321600 | tf_op jit(solution)/shard_map/pallas_call | solution.py:429
  29.7 0.0 all-gather.3.cloned.1.call-update
  29.8 66.0 %shard_map.231 = (bf16[2048,2048]{1,0:T(8,128)(2,1)}, bf16[2048,512]{1,0:T(8,128)(2,1)}) custom-call(bf16[256,2048]{1,0:T(8,128)(2,1)} %bitcast.57, f32[1,2048]{1,0:T(1,128)} %bitcast.64, bf16[256,2048]{1,0:T(8,128)(2,1)} %refs_2_.1, bf16[256,1024]{1,0:T(8,128)(2,1)} %refs_3_.1, bf16[256,1024]{1,0:T(8,128)(2,1)} %refs_4_.1), custom_call_target="tpu_custom_call" | custom-call | bytes 157286400 | tf_op jit(solution)/shard_map/pallas_call | solution.py:429
  95.8 0.2 copy_bitcast_fusion
  96.0 1.5 pad_maximum_fusion
  97.5 3.7 all-to-all-start
  101.3 0.6 select_reduce_fusion
  101.9 10.5 %fusion.14.qkv_ref = f32[2048,512]{1,0:T(8,128)} fusion(bf16[2048,2048]{1,0:T(8,128)(2,1)} %get-tuple-element.92.refs_2_, bf16[2048,512]{1,0:T(8,128)(2,1)} %get-tuple-element.93.refs_1_), kind=kOutput, calls=%fused_computation.32 | convolution fusion | flops 4294967296 | bytes 14680064 | tf_op jit(solution)/shard_map/dot_general | solution.py:25
  112.5 1.3 broadcast_in_dim.19.piece_col_ref.refs_9_
  113.8 21.2 %shard_map.232 = (bf16[2048,256]{1,0:T(8,128)(2,1)}, bf16[2,2048,128]{2,1,0:T(8,128)(2,1)}, bf16[2048,128]{1,0:T(8,128)(2,1)}, bf16[2048,128]{1,0:T(8,128)(2,1)}...) custom-call(s32[1,16]{1,0:T(1,128)} %holder_ref.1, f32[2048,512]{1,0:T(8,128)} %fusion.14.qkv_ref, ...), custom_call_target="tpu_custom_call" | custom-call | flops 3221225472 | bytes 20971520 | tf_op jit(solution)/shard_map/pallas_call | solution.py:148
  135.0 46.1 %shard_map.233 = f32[256,2048]{1,0:T(8,128)} custom-call(bf16[2048,256]{1,0:T(8,128)(2,1)} %get-tuple-element.94.refs_0_.refs_2_, bf16[256,2048]{1,0:T(8,128)(2,1)} %refs_1_.9), custom_call_target="tpu_custom_call" | custom-call | flops 2147483648 | bytes 157286400 | tf_op jit(solution)/shard_map/pallas_call | solution.py:429
  181.1 3.2 multiply_reduce_fusion.2
  184.3 0.0 all-gather.3.cloned.1.call-done
  184.3 1.3 copy-done.21
  185.6 52.3 %shard_map.234 = (bf16[2048,2048]{1,0:T(8,128)(2,1)}, bf16[2048,1024]{1,0:T(8,128)(2,1)}, bf16[2048,1024]{1,0:T(8,128)(2,1)}, bf16[2048,1024]{1,0:T(8,128)(2,1)}, bf16[8,256,2048]{2,1,0:T(8,128)(2,1)}) custom-call(f32[256,2048]{1,0:T(8,128)} %get-tuple-element.174.refs_0_, f32[1,2048]{1,0:T(1,128)} %bitcast.65, bf16[4,8,48,2048]{3,2,1,0:T(8,128)(2,1)} %bitcast.76, ...), custom_call_target="tpu_custom_call" | custom-call | flops 17179869184 | bytes 157286400 | tf_op jit(solution)/shard_map/pallas_call | solution.py:429
  237.9 50.7 %shard_map.235 = (bf16[2048,2048]{1,0:T(8,128)(2,1)}, bf16[1024,2048]{1,0:T(8,128)(2,1)}) custom-call(bf16[256,2048]{1,0:T(8,128)(2,1)} %bitcast.60, bf16[1024,2048]{1,0:T(8,128)(2,1)} %refs_1_.8, bf16[2048,1024]{1,0:T(8,128)(2,1)} %get-tuple-element.98.refs_2_.refs_0_, bf16[2048,1024]{1,0:T(8,128)(2,1)} %get-tuple-element.100.refs_3_, ...), custom_call_target="tpu_custom_call" | custom-call | flops 17179869184 | bytes 157286400 | tf_op jit(solution)/shard_map/pallas_call | solution.py:429
  288.6 61.8 %shard_map.236 = (f32[256,2048]{1,0:T(8,128)}, bf16[8,256,2048]{2,1,0:T(8,128)(2,1)}, bf16[8,16,2048]{2,1,0:T(8,128)(2,1)}, bf16[8,16,2048]{2,1,0:T(8,128)(2,1)}...) custom-call(bf16[2048,1024]{1,0:T(8,128)(2,1)} %get-tuple-element.98.refs_2_.refs_0_, ...), custom_call_target="tpu_custom_call" | custom-call | flops 25769803776 | bytes 157286400 | tf_op jit(solution)/shard_map/pallas_call | solution.py:429
  350.4 87.4 %shard_map.237 = (f32[256,2048]{1,0:T(8,128)}, bf16[8,16,2048]{2,1,0:T(8,128)(2,1)}, bf16[8,16,2048]{2,1,0:T(8,128)(2,1)}, bf16[8,16,2048]{2,1,0:T(8,128)(2,1)},...) custom-call(bf16[2048,2048]{1,0:T(8,128)(2,1)} %get-tuple-element.10, ...), custom_call_target="tpu_custom_call" | custom-call | flops 17179869184 | bytes 157286400 | tf_op jit(solution)/shard_map/pallas_call | solution.py:429
  437.9 2.3 multiply_reduce_fusion
  440.2 0.1 copy-done.20
  440.3 1.6 fusion.12.refs_0_
  442.0 65.7 %shard_map.238 = (bf16[2048,256]{1,0:T(8,128)(2,1)}, bf16[256,2048]{1,0:T(8,128)(2,1)}, bf16[8,16,2048]{2,1,0:T(8,128)(2,1)}, bf16[8,16,2048]{2,1,0:T(8,128)(2,1...) custom-call(bf16[256,2048]{1,0:T(8,128)(2,1)} %fusion.12.refs_0_, ...), custom_call_target="tpu_custom_call" | custom-call | flops 4294967296 | bytes 157286400 | tf_op jit(solution)/shard_map/pallas_call | solution.py:429
  507.6 2.3 shard_map.239.refs_0_
  510.0 36.6 %shard_map.240 = (bf16[2048,512]{1,0:T(8,128)(2,1)}, bf16[8,16,2048]{2,1,0:T(8,128)(2,1)}, bf16[8,16,2048]{2,1,0:T(8,128)(2,1)}, bf16[8,16,2048]{2,1,0:T(8,128)(...) custom-call(bf16[2048,256]{1,0:T(8,128)(2,1)} %shard_map.239.refs_0_, ...), custom_call_target="tpu_custom_call" | custom-call | flops 8589934592 | bytes 29360128 | tf_op jit(solution)/shard_map/pallas_call | solution.py:429
  546.6 3.1 shard_map.241.refs_0_
  549.8 69.5 %shard_map.242 = (f32[256,2048]{1,0:T(8,128)}, bf16[8,256,512]{2,1,0:T(8,128)(2,1)}, bf16[8,16,2048]{2,1,0:T(8,128)(2,1)}, bf16[8,16,2048]{2,1,0:T(8,128)(2,1)},...) custom-call(bf16[2048,512]{1,0:T(8,128)(2,1)} %shard_map.241.refs_0_, ...), custom_call_target="tpu_custom_call" | custom-call | flops 8589934592 | bytes 157286400 | tf_op jit(solution)/shard_map/pallas_call | solution.py:429
  619.3 2.2 fusion.8
  621.6 0.6 pad.4.refs_1_
  622.2 216.6 %shard_map.243 = (bf16[256,8192]{1,0:T(8,128)(2,1)}, bf16[256,8192]{1,0:T(8,128)(2,1)}, bf16[2,8,32,2048]{3,2,1,0:T(8,128)(2,1)}, f32[8,256]{1,0:T(8,128)}, bf16...) custom-call(bf16[8,8,32,512]{3,2,1,0:T(8,128)(2,1)} %bitcast.61, ...), custom_call_target="tpu_custom_call" | custom-call | bytes 104857600 | tf_op jit(solution)/shard_map/pallas_call | solution.py:429
  838.8 1.3 fusion.13
  840.2 5.1 fusion.11
  845.3 0.2 copy-done.1
  845.5 0.4 copy-done.2
  845.9 0.2 copy-done.3
  846.1 0.1 copy-done.4
  846.3 0.2 copy-done.5
  846.4 0.2 copy-done.6
  846.6 0.2 copy-done.7
  846.7 0.2 copy-done.8
  846.9 0.2 copy-done.9
  847.0 1.0 copy-done.10
  848.1 1.0 copy-done.11
  849.1 1.0 copy-done.12
  850.1 1.0 copy-done.13
  851.2 1.0 copy-done.14
  852.2 1.0 copy-done.15
  853.3 10.9 %shard_map.244 = (f32[8,32,2048]{2,1,0:T(8,128)}, f32[8,32,1024]{2,1,0:T(8,128)}, f32[8,32,1024]{2,1,0:T(8,128)}, f32[8,32,2048]{2,1,0:T(8,128)}, f32[8,32,8192]...) custom-call(bf16[8,16,2048]{2,1,0:T(8,128)(2,1)S(1)} %copy-done.2, ...), custom_call_target="tpu_custom_call" | custom-call | bytes 47185920 | tf_op jit(solution)/shard_map/pallas_call | solution.py:1401
  (44 shorter events, 0.1 us)
Async XLA Ops:
  7.2 177.1 %all-gather.3.cloned.1.call-start = ((), (), s32[]{:S(2)}) async-start(), calls=%async_computation.1 | async-start | bytes 7864320 | tf_op jit(solution)/shard_map/all_gather | solution.py:1486
  29.8 66.0 %slice-start = ((bf16[256,8192]{1,0:T(8,128)(2,1)}), bf16[64,8192]{1,0:T(8,128)(2,1)S(1)}, s32[]{:S(2)}) async-start(bf16[256,8192]{1,0:T(8,128)(2,1)} %refs_0_.1), calls=%async_computation.2 | async-start | bytes 2097152 | tf_op jit(solution)/shard_map/slice | solution.py:1491
  29.8 66.0 %slice-start.1 = ((bf16[256,8192]{1,0:T(8,128)(2,1)}), bf16[64,8192]{1,0:T(8,128)(2,1)S(1)}, s32[]{:S(2)}) async-start(bf16[256,8192]{1,0:T(8,128)(2,1)} %refs_1_.5), calls=%async_computation.3 | async-start | bytes 2097152 | tf_op jit(solution)/shard_map/slice | solution.py:1491
  97.5 3.8 copy-start.25
  97.5 86.7 %all-to-all-start = ((bf16[64,8,2048]{2,0,1:T(8,128)(2,1)}), bf16[64,8,2048]{2,0,1:T(8,128)(2,1)S(1)}, u32[]{:S(2)}, u32[]{:S(2)}) async-start(bf16[64,8,2048]{2,0,1:T(8,128)(2,1)} %pad_maximum_fusion), calls=%async_computation | async-start | bytes 4194304 | tf_op jit(solution)/shard_map/all_to_all | solution.py:1469
  101.9 10.5 %copy-start.24 = (s32[1,2048]{1,0:T(1,128)S(1)}, s32[1,2048]{1,0:T(1,128)}, u32[]{:S(2)}) copy-start(s32[1,2048]{1,0:T(1,128)} %refs_8_.1) | copy-start | bytes 24580
  135.0 46.1 %copy-start.19 = (bf16[1,256,2048]{2,1,0:T(8,128)(2,1)S(1)}, bf16[1,256,2048]{2,1,0:T(8,128)(2,1)}, u32[]{:S(2)}) copy-start(bf16[1,256,2048]{2,1,0:T(8,128)(2,1)} %param.15) | copy-start | bytes 3145732
  184.3 1.3 copy-start.21
  350.4 87.4 %copy-start.16 = (f32[256,2048]{1,0:T(8,128)S(1)}, f32[256,2048]{1,0:T(8,128)}, u32[]{:S(2)}) copy-start(f32[256,2048]{1,0:T(8,128)} %get-tuple-element.174.refs_0_) | copy-start | bytes 6291460
  350.4 87.4 %copy-start.23 = (f32[2048]{0:T(1024)S(1)}, f32[2048]{0:T(1024)}, u32[]{:S(2)}) copy-start(f32[2048]{0:T(1024)} %param.27) | copy-start | bytes 24580
  437.8 2.3 copy-start.17
  437.8 2.5 copy-start.20
  549.8 69.5 %copy-start.22 = (f32[2048]{0:T(1024)S(1)}, f32[2048]{0:T(1024)}, u32[]{:S(2)}) copy-start(f32[2048]{0:T(1024)} %param.26) | copy-start | bytes 24580
  622.2 217.9 %copy-start.18 = (f32[256,2048]{1,0:T(8,128)S(1)}, f32[256,2048]{1,0:T(8,128)}, u32[]{:S(2)}) copy-start(f32[256,2048]{1,0:T(8,128)} %get-tuple-element.111) | copy-start | bytes 6291460
  840.1 5.2 copy-start
  840.1 5.4 copy-start.1
  840.1 5.7 copy-start.2
  840.2 5.9 copy-start.3
  840.2 6.1 copy-start.4
  840.2 6.2 copy-start.5
  840.2 6.4 copy-start.6
  840.2 6.5 copy-start.7
  840.2 6.6 copy-start.8
  840.2 6.8 copy-start.9
  847.0 1.0 copy-start.10
  848.1 1.0 copy-start.11
  849.1 1.0 copy-start.12
  850.1 1.0 copy-start.13
  851.2 1.0 copy-start.14
  852.2 1.0 copy-start.15
Sparse Core Ops, SparseCore 0:
  29.9 116.5 all-gather.2

commit v6 on v5

--- a/solution.py
+++ b/solution.py
@@ -187,6 +187,9 @@
 class NoLine:
     ticks = 0
 
+    def signal(self, barrier):
+        pass
+
     def greet(self, barrier, others):
         if others:
             pl.semaphore_wait(barrier, others)
@@ -214,12 +217,16 @@
         self.now = 0
         self.kept = []
 
-    def greet(self, barrier, others):
+    def signal(self, barrier):
         pl.semaphore_signal(barrier, inc=1, device_id=self.partner, device_id_type=MESH)
 
         @pl.when(is_middle())
         def _():
             pl.semaphore_signal(barrier, inc=1, device_id=self.peer, device_id_type=MESH)
+
+    def greet(self, barrier, others):
+        @pl.when(is_middle())
+        def _():
             pl.semaphore_wait(barrier, others + 2)
 
         @pl.when(is_end())
@@ -350,22 +357,26 @@
 
     def start(self):
         self.open(0)
+        if self.ticks > 1:
+            self.open(1)
 
     def step(self):
-        if self.now + 1 < self.ticks:
-            self.close(self.now)
+        if self.now + 2 < self.ticks:
+            self.settle()
             self.open(self.now + 1)
-            self.add(self.now)
-            if self.now == self.ticks - 2:
-                self.keep(self.now)
-            self.now += 1
-
-    def end(self):
-        while self.now + 1 < self.ticks:
-            self.step()
+
+    def settle(self):
         self.close(self.now)
         self.add(self.now)
-        self.keep(self.now)
+        if self.now >= self.ticks - 2:
+            self.keep(self.now)
+        self.now += 1
+
+    def end(self):
+        while self.now + 2 < self.ticks:
+            self.step()
+        while self.now < self.ticks:
+            self.settle()
 
         @pl.when(is_middle())
         def _():
@@ -460,6 +471,7 @@
     (grad_qkv_ref,) = outs
     grads, centers, grad_q = scratch
     if line.ticks:
+        line.signal(pltpu.get_barrier_semaphore())
         line.greet(pltpu.get_barrier_semaphore(), 0)
         line.start()
     length = grad_ref.shape[0]
@@ -599,10 +611,13 @@
 EVERYONE = tuple((n // 4, (n // 2) % 2, n % 2) for n in range(1, 8))
 
 
-def greet_group(line, flips=NEIGHBOURS):
+def greet_group(line, flips=NEIGHBOURS, between=None):
     barrier = pltpu.get_barrier_semaphore()
     for flip in flips:
         pl.semaphore_signal(barrier, inc=1, device_id={"grp": other(*flip)}, device_id_type=MESH)
+    line.signal(barrier)
+    if between:
+        between()
     line.greet(barrier, len(flips))
 
 
@@ -743,8 +758,11 @@
     held, sends, recvs, sems, col_sends, col_recvs = scratch
     rows = x_ref.shape[0]
     moves = Moves(sems)
-    held[own_rows(rows), :] = rms_normed(x_ref[...].astype(f32), gain_ref[...]).astype(bf16)
-    greet_group(line, EVERYONE)
+
+    def fill():
+        held[own_rows(rows), :] = rms_normed(x_ref[...].astype(f32), gain_ref[...]).astype(bf16)
+
+    greet_group(line, EVERYONE, fill)
     col_copies = []
 
     def send_weights():
@@ -832,9 +850,11 @@
         for z in range(planes)
     ]
     loads.append(moves.start(rest_ref, weight.at[:, planes * tall :, :]))
-    held[own_rows(rows), :] = rms_normed(mid_ref[...], gain_ref[...]).astype(bf16)
-    greet_group(line)
-    line.start()
+
+    def fill():
+        held[own_rows(rows), :] = rms_normed(mid_ref[...], gain_ref[...]).astype(bf16)
+
+    greet_group(line, between=fill)
 
     def on_chip(*chip):
         where = chip_rows(*chip, rows)
@@ -898,9 +918,9 @@
             (w_ref, weight), (hidden_ref, hidden), (up_part_ref, up_part), (gate_part_ref, gate_part)
         )
     ]
-    held[own_rows(rows), :] = grad_ref[...]
     greet_group(line)
     line.start()
+    held[own_rows(rows), :] = grad_ref[...]
 
     def on_chip(*chip):
         where = chip_rows(*chip, rows)
@@ -963,9 +983,9 @@
     held, sends, recvs, sems, total = scratch
     rows = grad_ref.shape[0]
     moves = Moves(sems)
-    held[own_rows(rows), :] = grad_ref[...]
     greet_group(line)
     line.start()
+    held[own_rows(rows), :] = grad_ref[...]
 
     def on_chip(*chip):
         where = chip_rows(*chip, rows)
@@ -1044,9 +1064,15 @@
 
 
 def scatter_kernel(turned, tile, extra, ins, outs, scratch, line):
-    a_ref, b_ref = ins[:2]
     out_ref = outs[0]
     part, to_s, from_s, to_chip, held, relay, last, sends, recvs = scratch[:9]
+    a_ref, b_ref, loads = scratch[-3:]
+    loading = [
+        pltpu.make_async_copy(src, dst, loads.at[number])
+        for number, (src, dst) in enumerate(((ins[1], b_ref), (ins[0], a_ref)))
+    ]
+    for one in loading:
+        one.start()
     rows, width = out_ref.shape
     half = rows // 2
     _, _, core = place_in_group()
@@ -1059,6 +1085,8 @@
             columns_copy = pltpu.make_async_copy(ins[3], columns_ref, scratch[13].at[0])
             columns_copy.start()
         term = WeightTerm(ins[2], columns_ref, outs[1], scratch[9:12])
+    for one in loading:
+        one.wait()
     own_at = pl.multiple_of(core * rows, rows)
     other_at = pl.multiple_of((1 - core) * rows, rows)
     started = []
@@ -1158,7 +1186,7 @@
     width = b.shape[0] if turned else b.shape[1]
     rows = length // 8
     tile = min(256, width)
-    ins = [(a, VMEM), (b, VMEM)]
+    ins = [(a, ANY), (b, ANY)]
     outs = [(jax.ShapeDtypeStruct((rows, width), f32), VMEM)]
     scratch = [
         pltpu.VMEM((2 * rows, width), f32),
@@ -1188,6 +1216,9 @@
             ins.append((second, ANY))
             scratch += [pltpu.VMEM(second.shape, bf16), pltpu.SemaphoreType.DMA((1,))]
         flops += 2 * length * first.shape[1] * columns.shape[1]
+    scratch += [
+        pltpu.VMEM(a.shape, bf16), pltpu.VMEM(b.shape, bf16), pltpu.SemaphoreType.DMA((2,))
+    ]
     return run(
         functools.partial(scatter_kernel, turned, tile, kind), ins, outs, scratch,
         line.pop("number"), (flops, 150 * rows * width * 2, 0), vmem=60, **line,
@@ -1277,7 +1308,7 @@
         mine[(rank + 4 - step) % 4] = from_rep[step]
     gains_out_ref[...] = (mine[0] + mine[1]) + (mine[2] + mine[3])
     for number in range(1, line.ticks):
-        if line.first + number == CHUNKS - QKV:
+        if line.first + number + 1 == CHUNKS - QKV:
             for one in qkv_copies:
                 one.wait()
             moves.open.pop(0).wait()
@@ -1409,7 +1440,7 @@
             pltpu.SemaphoreType.DMA((depth,)),
             pltpu.SemaphoreType.DMA((depth, 12)),
         ],
-        compiler_params=pltpu.CompilerParams(vmem_limit_bytes=32 * 2**20),
+        compiler_params=pltpu.CompilerParams(vmem_limit_bytes=60 * 2**20),
         cost_estimate=pl.CostEstimate(
             flops=0, bytes_accessed=6 * CHUNKS * eight * high * width, transcendentals=0
         ),
@@ -1567,7 +1598,7 @@
             hidden, w_down, False, extra=(normed_two, grad_gate_up), **line(5, 4)
         )
         result = result_of(down_sum)
-        grad_two = product_scattered(grad_gate_up, cols_gate_up, True, **line(6, 5))[0]
+        grad_two = product_scattered(grad_gate_up, cols_gate_up, True, **line(6, 4))[0]
         grad_mid, gain_ffn_term = finish_two(grad_two)
         grad_attended, out_term = attended_back(
             grad_mid.astype(bf16), w_out, attended, **line(7, 4)

time: 881 us -> 802 us (0.910)
  Pallas kernels: 813 us -> 742 us
    pallas_call x11, Pallas kernels: 775 us -> 698 us  [run(): pl.pallas_call(body, out_shape=tuple((shape for shape, _ in outs)), in_sp...]
  transfers between devices with their start and end apart: 2 -> 2, of which waited for: 0 -> 0; matrix products, arithmetic and copies ran while one was open for 2% -> 2% of each run, Pallas kernels for 15% -> 17%
where the time goes in v6:
time: 802 us; the launch traced here: 792 us
  Pallas kernels  742 us (93%)
  other arithmetic  16.5 us (2%)
  between operations  14.5 us (2%)
  matrix products  10.5 us (1%)
    pallas_call x11, Pallas kernels, run(): pl.pallas_call(body, out_shape=tuple((shape for shape, _ in outs)), in_sp...  698 us
    pallas_call x1, Pallas kernels, attend(): pl.pallas_call(functools.partial(attend_kernel, heads, order.shape[1], bl...  21.2 us
    pallas_call x1, Pallas kernels, finish(): pl.pallas_call(functools.partial(finish_kernel, heads), out_shape=tuple(s...  17.1 us
  transfers between devices with their start and end apart: 2, of which 0 were waited for; matrix products, arithmetic and copies ran while one was open for 2% of the time, Pallas kernels for 17%

profile of v6, /device:TPU:0, one launch (start us, length us, event | category | flops | bytes accessed | tf_op | source)
XLA Modules:
  0.0 792.0 jit_solution(1428557634503151609)
XLA Ops:
  7.2 0.0 all-gather.3.cloned.1.call-start
  7.2 22.5 %shard_map.230 = bf16[8,48,2048]{2,1,0:T(8,128)(2,1)} custom-call(bf16[256,8192]{1,0:T(8,128)(2,1)} %refs_0_.1, bf16[256,8192]{1,0:T(8,128)(2,1)} %refs_1_.5), custom_call_target="tpu_custom_call" | custom-call | bytes 39321600 | tf_op jit(solution)/shard_map/pallas_call | solution.py:440
  29.7 0.0 all-gather.3.cloned.1.call-update
  29.8 0.0 slice-start
  29.8 0.0 slice-start.1
  29.8 65.6 %shard_map.231 = (bf16[2048,2048]{1,0:T(8,128)(2,1)}, bf16[2048,512]{1,0:T(8,128)(2,1)}) custom-call(bf16[256,2048]{1,0:T(8,128)(2,1)} %bitcast.55, f32[1,2048]{1,0:T(1,128)} %bitcast.64, bf16[256,2048]{1,0:T(8,128)(2,1)} %refs_2_.1, bf16[256,1024]{1,0:T(8,128)(2,1)} %refs_3_.1, bf16[256,1024]{1,0:T(8,128)(2,1)} %refs_4_.1), custom_call_target="tpu_custom_call" | custom-call | bytes 157286400 | tf_op jit(solution)/shard_map/pallas_call | solution.py:440
  95.4 0.0 slice-done
  95.4 0.0 slice-done.1
  95.4 0.2 copy_bitcast_fusion
  95.6 1.5 pad_maximum_fusion
  97.1 3.7 all-to-all-start
  100.8 0.0 copy-done.9
  100.9 0.6 select_reduce_fusion
  101.5 10.5 %fusion.14.qkv_ref = f32[2048,512]{1,0:T(8,128)} fusion(bf16[2048,2048]{1,0:T(8,128)(2,1)} %get-tuple-element.91.refs_2_, bf16[2048,512]{1,0:T(8,128)(2,1)} %get-tuple-element.92.refs_1_), kind=kOutput, calls=%fused_computation.32 | convolution fusion | flops 4294967296 | bytes 14680064 | tf_op jit(solution)/shard_map/dot_general | solution.py:25
  112.0 0.0 copy-done.8
  112.0 1.3 broadcast_in_dim.19.piece_col_ref.refs_9_
  113.3 21.2 %shard_map.232 = (bf16[2048,256]{1,0:T(8,128)(2,1)}, bf16[2,2048,128]{2,1,0:T(8,128)(2,1)}, bf16[2048,128]{1,0:T(8,128)(2,1)}, bf16[2048,128]{1,0:T(8,128)(2,1)}...) custom-call(s32[1,16]{1,0:T(1,128)} %holder_ref.1, f32[2048,512]{1,0:T(8,128)} %fusion.14.qkv_ref, ...), custom_call_target="tpu_custom_call" | custom-call | flops 3221225472 | bytes 20971520 | tf_op jit(solution)/shard_map/pallas_call | solution.py:148
  134.5 44.6 %shard_map.233 = f32[256,2048]{1,0:T(8,128)} custom-call(bf16[2048,256]{1,0:T(8,128)(2,1)} %get-tuple-element.93.refs_0_.refs_2_, bf16[256,2048]{1,0:T(8,128)(2,1)} %refs_1_.9), custom_call_target="tpu_custom_call" | custom-call | flops 2147483648 | bytes 157286400 | tf_op jit(solution)/shard_map/pallas_call | solution.py:440
  179.1 0.0 copy-done.3
  179.1 3.2 multiply_reduce_fusion.2
  182.3 0.0 all-to-all-done
  182.3 0.0 copy-start.5
  182.3 0.0 all-gather.3.cloned.1.call-done
  182.4 1.3 copy-done.5
  183.7 52.0 %shard_map.234 = (bf16[2048,2048]{1,0:T(8,128)(2,1)}, bf16[2048,1024]{1,0:T(8,128)(2,1)}, bf16[2048,1024]{1,0:T(8,128)(2,1)}, bf16[2048,1024]{1,0:T(8,128)(2,1)}, bf16[8,256,2048]{2,1,0:T(8,128)(2,1)}) custom-call(f32[256,2048]{1,0:T(8,128)} %get-tuple-element.172.refs_0_, f32[1,2048]{1,0:T(1,128)} %bitcast.65, bf16[4,8,48,2048]{3,2,1,0:T(8,128)(2,1)} %bitcast.76, ...), custom_call_target="tpu_custom_call" | custom-call | flops 17179869184 | bytes 157286400 | tf_op jit(solution)/shard_map/pallas_call | solution.py:440
  235.7 51.1 %shard_map.235 = (bf16[2048,2048]{1,0:T(8,128)(2,1)}, bf16[1024,2048]{1,0:T(8,128)(2,1)}) custom-call(bf16[256,2048]{1,0:T(8,128)(2,1)} %bitcast.58, bf16[1024,2048]{1,0:T(8,128)(2,1)} %refs_1_.8, bf16[2048,1024]{1,0:T(8,128)(2,1)} %get-tuple-element.97.refs_2_.refs_0_, bf16[2048,1024]{1,0:T(8,128)(2,1)} %get-tuple-element.99.refs_3_, ...), custom_call_target="tpu_custom_call" | custom-call | flops 17179869184 | bytes 157286400 | tf_op jit(solution)/shard_map/pallas_call | solution.py:440
  286.8 60.1 %shard_map.236 = (f32[256,2048]{1,0:T(8,128)}, bf16[8,256,2048]{2,1,0:T(8,128)(2,1)}, bf16[8,16,2048]{2,1,0:T(8,128)(2,1)}, bf16[8,16,2048]{2,1,0:T(8,128)(2,1)}...) custom-call(bf16[2048,1024]{1,0:T(8,128)(2,1)} %get-tuple-element.97.refs_2_.refs_0_, ...), custom_call_target="tpu_custom_call" | custom-call | flops 25769803776 | bytes 157286400 | tf_op jit(solution)/shard_map/pallas_call | solution.py:440
  346.9 0.0 copy-start
  346.9 0.0 copy-start.7
  346.9 58.3 %shard_map.237 = (f32[256,2048]{1,0:T(8,128)}, bf16[8,16,2048]{2,1,0:T(8,128)(2,1)}, bf16[8,16,2048]{2,1,0:T(8,128)(2,1)}, bf16[8,16,2048]{2,1,0:T(8,128)(2,1)},...) custom-call(bf16[2048,2048]{1,0:T(8,128)(2,1)} %get-tuple-element.10, ...), custom_call_target="tpu_custom_call" | custom-call | flops 17179869184 | bytes 157286400 | tf_op jit(solution)/shard_map/pallas_call | solution.py:440
  405.2 0.0 copy-done
  405.2 0.0 copy-done.7
  405.2 0.0 copy-start.4
  405.3 2.3 multiply_reduce_fusion
  407.6 0.1 copy-done.4
  407.7 1.6 fusion.12.refs_0_
  409.4 55.8 %shard_map.238 = (bf16[2048,256]{1,0:T(8,128)(2,1)}, bf16[256,2048]{1,0:T(8,128)(2,1)}, bf16[8,16,2048]{2,1,0:T(8,128)(2,1)}, bf16[8,16,2048]{2,1,0:T(8,128)(2,1...) custom-call(bf16[256,2048]{1,0:T(8,128)(2,1)} %fusion.12.refs_0_, ...), custom_call_target="tpu_custom_call" | custom-call | flops 4294967296 | bytes 157286400 | tf_op jit(solution)/shard_map/pallas_call | solution.py:440
  465.2 2.3 shard_map.239.refs_0_
  467.6 30.7 %shard_map.240 = (bf16[2048,512]{1,0:T(8,128)(2,1)}, bf16[8,16,2048]{2,1,0:T(8,128)(2,1)}, bf16[8,16,2048]{2,1,0:T(8,128)(2,1)}, bf16[8,16,2048]{2,1,0:T(8,128)(...) custom-call(bf16[2048,256]{1,0:T(8,128)(2,1)} %shard_map.239.refs_0_, ...), custom_call_target="tpu_custom_call" | custom-call | flops 8589934592 | bytes 29360128 | tf_op jit(solution)/shard_map/pallas_call | solution.py:440
  498.3 3.1 shard_map.241.refs_0_
  501.5 60.4 %shard_map.242 = (f32[256,2048]{1,0:T(8,128)}, bf16[8,256,512]{2,1,0:T(8,128)(2,1)}, bf16[8,16,2048]{2,1,0:T(8,128)(2,1)}, bf16[8,16,2048]{2,1,0:T(8,128)(2,1)},...) custom-call(bf16[2048,512]{1,0:T(8,128)(2,1)} %shard_map.241.refs_0_, ...), custom_call_target="tpu_custom_call" | custom-call | flops 8589934592 | bytes 157286400 | tf_op jit(solution)/shard_map/pallas_call | solution.py:440
  561.9 0.0 copy-done.6
  561.9 2.2 fusion.8
  564.1 0.6 pad.4.refs_1_
  564.8 196.7 %shard_map.243 = (bf16[256,8192]{1,0:T(8,128)(2,1)}, bf16[256,8192]{1,0:T(8,128)(2,1)}, bf16[2,8,32,2048]{3,2,1,0:T(8,128)(2,1)}, f32[8,256]{1,0:T(8,128)}, bf16...) custom-call(bf16[8,8,32,512]{3,2,1,0:T(8,128)(2,1)} %bitcast.62, ...), custom_call_target="tpu_custom_call" | custom-call | bytes 104857600 | tf_op jit(solution)/shard_map/pallas_call | solution.py:440
  761.5 1.3 fusion.13
  762.9 5.0 fusion.11
  767.8 17.1 %shard_map.244 = (f32[8,32,2048]{2,1,0:T(8,128)}, f32[8,32,1024]{2,1,0:T(8,128)}, f32[8,32,1024]{2,1,0:T(8,128)}, f32[8,32,2048]{2,1,0:T(8,128)}, f32[8,32,8192]...) custom-call(bf16[8,16,2048]{2,1,0:T(8,128)(2,1)} %get-tuple-element.131.refs_0_, ...), custom_call_target="tpu_custom_call" | custom-call | bytes 47185920 | tf_op jit(solution)/shard_map/pallas_call | solution.py:1432
  (12 shorter events, 0.1 us)
Async XLA Ops:
  7.2 175.2 %all-gather.3.cloned.1.call-start = ((), (), s32[]{:S(2)}) async-start(), calls=%async_computation.1 | async-start | bytes 7864320 | tf_op jit(solution)/shard_map/all_gather | solution.py:1517
  29.8 65.6 %slice-start = ((bf16[256,8192]{1,0:T(8,128)(2,1)}), bf16[64,8192]{1,0:T(8,128)(2,1)S(1)}, s32[]{:S(2)}) async-start(bf16[256,8192]{1,0:T(8,128)(2,1)} %refs_0_.1), calls=%async_computation.2 | async-start | bytes 2097152 | tf_op jit(solution)/shard_map/slice | solution.py:1522
  29.8 65.6 %slice-start.1 = ((bf16[256,8192]{1,0:T(8,128)(2,1)}), bf16[64,8192]{1,0:T(8,128)(2,1)S(1)}, s32[]{:S(2)}) async-start(bf16[256,8192]{1,0:T(8,128)(2,1)} %refs_1_.5), calls=%async_computation.3 | async-start | bytes 2097152 | tf_op jit(solution)/shard_map/slice | solution.py:1522
  97.1 3.8 copy-start.9
  97.1 85.2 %all-to-all-start = ((bf16[64,8,2048]{2,0,1:T(8,128)(2,1)}), bf16[64,8,2048]{2,0,1:T(8,128)(2,1)S(1)}, u32[]{:S(2)}, u32[]{:S(2)}) async-start(bf16[64,8,2048]{2,0,1:T(8,128)(2,1)} %pad_maximum_fusion), calls=%async_computation | async-start | bytes 4194304 | tf_op jit(solution)/shard_map/all_to_all | solution.py:1500
  101.5 10.5 %copy-start.8 = (s32[1,2048]{1,0:T(1,128)S(1)}, s32[1,2048]{1,0:T(1,128)}, u32[]{:S(2)}) copy-start(s32[1,2048]{1,0:T(1,128)} %refs_8_.1) | copy-start | bytes 24580
  134.5 44.6 %copy-start.3 = (bf16[1,256,2048]{2,1,0:T(8,128)(2,1)S(1)}, bf16[1,256,2048]{2,1,0:T(8,128)(2,1)}, u32[]{:S(2)}) copy-start(bf16[1,256,2048]{2,1,0:T(8,128)(2,1)} %param.15) | copy-start | bytes 3145732
  182.3 1.3 copy-start.5
  346.9 58.4 %copy-start = (f32[256,2048]{1,0:T(8,128)S(1)}, f32[256,2048]{1,0:T(8,128)}, u32[]{:S(2)}) copy-start(f32[256,2048]{1,0:T(8,128)} %get-tuple-element.172.refs_0_) | copy-start | bytes 6291460
  346.9 58.3 %copy-start.7 = (f32[2048]{0:T(1024)S(1)}, f32[2048]{0:T(1024)}, u32[]{:S(2)}) copy-start(f32[2048]{0:T(1024)} %param.27) | copy-start | bytes 24580
  405.2 2.3 copy-start.1
  405.2 2.5 copy-start.4
  501.5 60.4 %copy-start.6 = (f32[2048]{0:T(1024)S(1)}, f32[2048]{0:T(1024)}, u32[]{:S(2)}) copy-start(f32[2048]{0:T(1024)} %param.26) | copy-start | bytes 24580
  564.8 198.1 %copy-start.2 = (f32[256,2048]{1,0:T(8,128)S(1)}, f32[256,2048]{1,0:T(8,128)}, u32[]{:S(2)}) copy-start(f32[256,2048]{1,0:T(8,128)} %get-tuple-element.109) | copy-start | bytes 6291460
Sparse Core Ops, SparseCore 0:
  29.9 116.5 all-gather.2

commit v7 on v6

--- a/solution.py
+++ b/solution.py
@@ -166,12 +166,16 @@
     )(order, qkv, cosine, sine, piece, piece_col)
 
 
-DOWN, GATE_UP, OUT, QKV = 8, 16, 2, 4
+DOWN, GATE_UP, OUT, QKV = 8, 16, 2, 8
 CHUNKS = DOWN + GATE_UP + OUT + QKV
 
 
 def is_chunk(number):
     return 0 <= number < CHUNKS
+
+
+def chunk_shape(shape, number):
+    return shape[:2] + (shape[2] // 2,) if number >= CHUNKS - QKV else shape
 
 
 def is_middle():
@@ -239,6 +243,10 @@
             recv_sem=self.sems.at[1, hop, number], device_id=device, device_id_type=MESH,
         )
 
+    def part(self, ref, at, chunk):
+        width = chunk_shape(ref.shape[1:], chunk)[2]
+        return ref.at[at] if width == ref.shape[3] else ref.at[at, :, :, :width]
+
     def hops(self, number):
         tick = self.first + number
         term = pair = total = None
@@ -246,22 +254,30 @@
             which, pick = self.picks[tick]
             term = (
                 lambda: self.remote(
-                    0, number, pick(self.refs[which]), self.inward.at[number], self.partner
+                    0, number, pick(self.refs[which]), self.part(self.inward, number, tick), self.partner
                 ),
                 lambda: pltpu.make_async_copy(
-                    pick(self.refs[which]), self.own.at[tick % 2], self.local.at[0, number]
+                    pick(self.refs[which]), self.part(self.own, tick % 2, tick), self.local.at[0, number]
                 ),
             )
         if is_chunk(tick - 2):
-            before = self.refs[f"pair{number}"] if number < 2 else self.pair.at[(tick - 2) % 3]
+            before = (
+                self.refs[f"pair{number}"]
+                if number < 2
+                else self.part(self.pair, (tick - 2) % 3, tick - 2)
+            )
             pair = (
-                lambda: self.remote(1, number, before, self.across.at[number], self.peer),
+                lambda: self.remote(1, number, before, self.part(self.across, number, tick - 2), self.peer),
                 lambda: pltpu.make_async_copy(
-                    before, self.pair.at[(tick - 2) % 3], self.carries.at[number]
+                    before, self.part(self.pair, (tick - 2) % 3, tick - 2), self.carries.at[number]
                 ),
             )
         if is_chunk(tick - 4):
-            done = self.refs[f"total{number}"] if number < 2 else self.total.at[(tick - 4) % 3]
+            done = (
+                self.refs[f"total{number}"]
+                if number < 2
+                else self.part(self.total, (tick - 4) % 3, tick - 4)
+            )
             slot = self.outs[tick - 4]
             total = (
                 lambda: self.remote(2, number, done, slot, self.partner),
@@ -328,12 +344,16 @@
                 if number < 2:
                     pair[1]().wait()
                 sum_of(
-                    self.total.at[(tick - 2) % 3], self.pair.at[(tick - 2) % 3],
-                    self.across.at[number],
+                    self.part(self.total, (tick - 2) % 3, tick - 2),
+                    self.part(self.pair, (tick - 2) % 3, tick - 2),
+                    self.part(self.across, number, tick - 2),
                 )
             if term:
                 term[1]().wait()
-                sum_of(self.pair.at[tick % 3], self.own.at[tick % 2], self.inward.at[number])
+                sum_of(
+                    self.part(self.pair, tick % 3, tick), self.part(self.own, tick % 2, tick),
+                    self.part(self.inward, number, tick),
+                )
 
     def keep(self, number):
         tick = self.first + number
@@ -400,7 +420,6 @@
     names_in, names_out = [], []
     if ticks:
         last = first + ticks - 1
-        chunk = jax.ShapeDtypeStruct(sums.shape, bf16)
         for name, array in arrays:
             names_in.append(name)
             ins.append((array, pl.ANY))
@@ -414,7 +433,16 @@
             for name, chunk_at in ((f"pair{which}", last - 1), (f"total{which}", last - 3)):
                 if is_chunk(chunk_at + which):
                     names_out.append(name)
-        outs += [(chunk, pl.ANY)] * len(names_out)
+        slots = line_slots(first, ticks)
+        outs += [
+            (
+                jax.ShapeDtypeStruct(
+                    chunk_shape(sums.shape, name) if name in slots else sums.shape, bf16
+                ),
+                pl.ANY,
+            )
+            for name in names_out
+        ]
         scratch += [
             pltpu.VMEM((ticks,) + sums.shape, bf16),
             pltpu.VMEM((ticks,) + sums.shape, bf16),
@@ -920,7 +948,7 @@
     ]
     greet_group(line)
     line.start()
-    held[own_rows(rows), :] = grad_ref[...]
+    held[own_rows(rows), :] = grad_ref[...].astype(bf16)
 
     def on_chip(*chip):
         where = chip_rows(*chip, rows)
@@ -985,7 +1013,7 @@
     moves = Moves(sems)
     greet_group(line)
     line.start()
-    held[own_rows(rows), :] = grad_ref[...]
+    held[own_rows(rows), :] = grad_ref[...].astype(bf16)
 
     def on_chip(*chip):
         where = chip_rows(*chip, rows)
@@ -1063,8 +1091,9 @@
             self.store(number).wait()
 
 
-def scatter_kernel(turned, tile, extra, ins, outs, scratch, line):
-    out_ref = outs[0]
+def scatter_kernel(turned, tile, extra, after, ins, outs, scratch, line):
+    out_ref = outs[0] if after == "base" else scratch[-4]
+    finals = ins[len(ins) - {"base": 1, "cast": 1, "back": 3}[after] :]
     part, to_s, from_s, to_chip, held, relay, last, sends, recvs = scratch[:9]
     a_ref, b_ref, loads = scratch[-3:]
     loading = [
@@ -1084,7 +1113,7 @@
             columns_ref = scratch[12]
             columns_copy = pltpu.make_async_copy(ins[3], columns_ref, scratch[13].at[0])
             columns_copy.start()
-        term = WeightTerm(ins[2], columns_ref, outs[1], scratch[9:12])
+        term = WeightTerm(ins[2], columns_ref, outs[-1], scratch[9:12])
     for one in loading:
         one.wait()
     own_at = pl.multiple_of(core * rows, rows)
@@ -1164,7 +1193,11 @@
         term.work((5, 6, 7))
     landed(3, from_s.at[3])
     for low in (0, 1):
-        out_ref[low * half : (low + 1) * half, :] = own(low, 3)
+        at = slice(low * half, (low + 1) * half)
+        if after == "back":
+            out_ref[at, :] = own(low, 3)
+        else:
+            out_ref[at, :] = own(low, 3) + finals[0][at, :].astype(f32)
     landed(6, last.at[0, first, :])
     out_ref[first, :] += last[0, first, :].astype(f32)
     landed(7, last.at[1, second, :])
@@ -1174,6 +1207,23 @@
     out_ref[second, :] += last[0, second, :].astype(f32)
     landed(9, last.at[1, first, :])
     out_ref[first, :] += last[1, first, :].astype(f32)
+    if after == "cast":
+        outs[0][...] = out_ref[...].astype(outs[0].dtype)
+    if after == "back":
+        upstream_ref, rows_ref, gain_ref = finals
+        some = min(64, rows)
+
+        def norm_rows(number, gain_term):
+            at = pl.ds(pl.multiple_of(number * some, some), some)
+            values, incoming = rows_ref[at, :].astype(f32), out_ref[at, :]
+            inv = lax.rsqrt(jnp.mean(values * values, -1, keepdims=True) + EPS)
+            grad, term = norm_back(
+                upstream_ref[at, :].astype(f32), incoming, values * inv, inv, gain_ref[...]
+            )
+            outs[0][at, :] = grad.astype(outs[0].dtype)
+            return gain_term + term[None, :]
+
+        outs[1][...] = lax.fori_loop(0, rows // some, norm_rows, jnp.zeros((1, width), f32))
     for one in started:
         one.wait_send()
     if extra:
@@ -1181,13 +1231,16 @@
     line.end()
 
 
-def product_scattered(a, b, turned, extra=None, **line):
+def product_scattered(a, b, turned, extra=None, base=None, back=None, dtype=f32, **line):
     length, depth = a.shape
     width = b.shape[0] if turned else b.shape[1]
     rows = length // 8
     tile = min(256, width)
     ins = [(a, ANY), (b, ANY)]
-    outs = [(jax.ShapeDtypeStruct((rows, width), f32), VMEM)]
+    outs = [(jax.ShapeDtypeStruct((rows, width), dtype), VMEM)]
+    after = "back" if back else "base" if dtype == f32 else "cast"
+    if back:
+        outs.append((jax.ShapeDtypeStruct((1, width), f32), VMEM))
     scratch = [
         pltpu.VMEM((2 * rows, width), f32),
         pltpu.VMEM((4, rows, width), bf16),
@@ -1216,12 +1269,15 @@
             ins.append((second, ANY))
             scratch += [pltpu.VMEM(second.shape, bf16), pltpu.SemaphoreType.DMA((1,))]
         flops += 2 * length * first.shape[1] * columns.shape[1]
+    ins += [(array, VMEM) for array in (back or (base,))]
+    if after != "base":
+        scratch.append(pltpu.VMEM((rows, width), f32))
     scratch += [
         pltpu.VMEM(a.shape, bf16), pltpu.VMEM(b.shape, bf16), pltpu.SemaphoreType.DMA((2,))
     ]
     return run(
-        functools.partial(scatter_kernel, turned, tile, kind), ins, outs, scratch,
-        line.pop("number"), (flops, 150 * rows * width * 2, 0), vmem=60, **line,
+        functools.partial(scatter_kernel, turned, tile, kind, after), ins, outs, scratch,
+        line.pop("number"), (flops, 150 * rows * width * 2, 0), vmem=61, **line,
     )
 
 
@@ -1334,7 +1390,10 @@
     for n in range(QKV):
         picks[CHUNKS - QKV + n] = (
             "qkv",
-            lambda ref, n=n: ref.at[n // 2, :, (n % 2) * high : (n % 2 + 1) * high, :],
+            lambda ref, n=n: ref.at[
+                n // 4, :, n // 2 % 2 * high : (n // 2 % 2 + 1) * high,
+                n % 2 * (width // 2) : (n % 2 + 1) * (width // 2),
+            ],
         )
     return run(
         functools.partial(tail_kernel, ready, later),
@@ -1377,18 +1436,19 @@
     part = (heads + 2) * HD
     for number, ref in enumerate(chunks[DOWN + OUT :]):
         stores = []
-        for place in range(width // part):
-            at, device = place * part, (number // 2) * (width // part) + place
+        places = ref.shape[2] // part
+        for place in range(places):
+            at, device = place * part, (number // 4 * 2 + number % 2) * places + place
             for into, first, size in (
                 (query, 0, heads * HD), (key, heads * HD, HD), (value, (heads + 1) * HD, HD)
             ):
-                there = into.at[:, half(number % 2), device * size : (device + 1) * size]
+                there = into.at[:, half(number // 2 % 2), device * size : (device + 1) * size]
                 stores.append((slice(at + first, at + first + size), there))
         jobs.append((ref, stores))
 
     def load(number):
-        at = number % depth
-        return pltpu.make_async_copy(jobs[number][0], low.at[at], load_sems.at[at])
+        at, ref = number % depth, jobs[number][0]
+        return pltpu.make_async_copy(ref, low.at[at, :, :, : ref.shape[2]], load_sems.at[at])
 
     def stores(number):
         at = number % depth
@@ -1407,8 +1467,8 @@
             for one in stores(number - depth):
                 one.wait()
 
-        def cast(g, _, at=number % depth):
-            wide[at, g] = low[at, g].astype(f32)
+        def cast(g, _, at=number % depth, cols=slice(0, jobs[number][0].shape[2])):
+            wide[at, g, :, cols] = low[at, g, :, cols].astype(f32)
             return 0
 
         lax.fori_loop(0, low.shape[1], cast, 0)
@@ -1428,7 +1488,7 @@
 
     shapes = [split(columns) for columns in (8 * heads * HD, 8 * HD, 8 * HD, width, wide, wide)]
     shapes.append(jax.ShapeDtypeStruct((DOWN, eight, high, width), f32))
-    depth = 4
+    depth = 6
     results = pl.pallas_call(
         functools.partial(finish_kernel, heads),
         out_shape=tuple(shapes),
@@ -1538,29 +1598,16 @@
         cut_order, qkv, cosine, sine, piece_ids, piece_col, heads
     )
     if near:
-        out_sum = product_scattered(attended, w_out, False, number=2)[0]
+        mid = product_scattered(attended, w_out, False, base=x_rows, number=2)[0]
     else:
-        out_sum = scatter(attended, w_out, False)
-    mid = x_flat + out_sum
-    inv_two = lax.rsqrt(jnp.mean(mid * mid, -1, keepdims=True) + EPS)
-    unit_two = mid * inv_two
+        mid = x_flat + scatter(attended, w_out, False)
     grad_out = cotangent.reshape(local_rows, model_width)
-
-    def finish_two(grad_two):
-        return norm_back(grad_out.astype(f32), grad_two, unit_two, inv_two, gain_ffn)
-
-    def finish_one(grad_mid, grad_one):
-        grad_input, gain_term = norm_back(grad_mid, grad_one, unit_one, inv_one, gain_attn)
-        return grad_input.astype(bf16).reshape(layer_input.shape), gain_term
 
     def back_through_attention(grad_attended, **line):
         return attend_back(
             cut_order, grad_attended, attended_placed, query, key, value, lse, cosine, sine,
             piece_ids, piece_col, heads, **line,
         )
-
-    def result_of(down_sum):
-        return (mid + down_sum).astype(bf16).reshape(layer_input.shape)
 
     q_here = heads * HD
     if near:
@@ -1594,21 +1641,20 @@
                 arrays=[(name, terms[name]) for name in names],
             )
 
-        down_sum, terms["gate_up"] = product_scattered(
-            hidden, w_down, False, extra=(normed_two, grad_gate_up), **line(5, 4)
-        )
-        result = result_of(down_sum)
-        grad_two = product_scattered(grad_gate_up, cols_gate_up, True, **line(6, 4))[0]
-        grad_mid, gain_ffn_term = finish_two(grad_two)
-        grad_attended, out_term = attended_back(
-            grad_mid.astype(bf16), w_out, attended, **line(7, 4)
-        )
+        result, terms["gate_up"] = product_scattered(
+            hidden, w_down, False, extra=(normed_two, grad_gate_up), base=mid, dtype=bf16,
+            **line(5, 5),
+        )
+        grad_mid, gain_ffn_term = product_scattered(
+            grad_gate_up, cols_gate_up, True, back=(grad_out, mid, ffn_gain), **line(6, 5)
+        )
+        grad_attended, out_term = attended_back(grad_mid, w_out, attended, **line(7, 4))
         terms["out"] = out_term.reshape(8, OUT * high, model_width)
-        grad_qkv = back_through_attention(grad_attended, **line(8, 2))
-        grad_one, qkv_term = product_scattered(
-            grad_qkv, cols_qkv, True, extra=(normed_one, None), **line(9, 4)
-        )
-        grad_x, gain_attn_term = finish_one(grad_mid, grad_one)
+        grad_qkv = back_through_attention(grad_attended, **line(8, 3))
+        grad_x, gain_attn_term, qkv_term = product_scattered(
+            grad_qkv, cols_qkv, True, extra=(normed_one, None), dtype=bf16,
+            back=(grad_mid, x_rows, attn_gain), **line(9, 4),
+        )
         gains = jnp.stack([gain_attn_term, gain_ffn_term]).reshape(2, groups, rows_here)
         gains = jnp.pad(jnp.moveaxis(gains, 0, 1), ((0, 0), (0, 6), (0, 0)))
         rest = line(10, CHUNKS + 4 - sums.tick)
@@ -1618,8 +1664,12 @@
         )
         straight = [n for n in range(CHUNKS) if n < DOWN or n >= DOWN + GATE_UP]
         weight_grads = finish([sums.done[n] for n in straight], gate_rows, up_rows, heads)
-        return (result, grad_x) + tuple(weight_grads) + (own_gains[0], own_gains[1])
-
+        shaped = tuple(rows.reshape(layer_input.shape) for rows in (result, grad_x))
+        return shaped + tuple(weight_grads) + (own_gains[0], own_gains[1])
+
+    unit_one = x_flat * inv_one
+    inv_two = lax.rsqrt(jnp.mean(mid * mid, -1, keepdims=True) + EPS)
+    unit_two = mid * inv_two
     normed_two = gather((unit_two * ffn_gain).astype(bf16))
     grad_all = gather(grad_out)
     gate_up = matmul_f32(normed_two, cols_gate_up)
@@ -1631,10 +1681,14 @@
     down_term = over_tokens(hidden, grad_all).astype(bf16)
     grad_hidden = against_rows(grad_all, w_down)
     grad_gate_up = jnp.concatenate([grad_hidden * gate_part, grad_hidden * swish], 1).astype(bf16)
-    grad_mid, gain_ffn_term = finish_two(scatter(grad_gate_up, cols_gate_up, True))
+    grad_mid, gain_ffn_term = norm_back(
+        grad_out.astype(f32), scatter(grad_gate_up, cols_gate_up, True), unit_two, inv_two, gain_ffn
+    )
     grad_mid_low = gather(grad_mid.astype(bf16))
     grad_qkv = back_through_attention(against_rows(grad_mid_low, w_out).astype(bf16))
-    grad_x, gain_attn_term = finish_one(grad_mid, scatter(grad_qkv, cols_qkv, True))
+    grad_x, gain_attn_term = norm_back(
+        grad_mid, scatter(grad_qkv, cols_qkv, True), unit_one, inv_one, gain_attn
+    )
 
     def to_rows(term):
         return lax.all_to_all(
@@ -1655,8 +1709,8 @@
     gain_total = lax.psum(jnp.stack([gain_attn_term, gain_ffn_term]), ("grp", "rep"))
     own_gains = lax.dynamic_slice_in_dim(gain_total, own_index * rows_here, rows_here, 1)
     return (
-        result_of(scatter(hidden, w_down, False)),
-        grad_x,
+        (mid + scatter(hidden, w_down, False)).astype(bf16).reshape(layer_input.shape),
+        grad_x.astype(bf16).reshape(layer_input.shape),
         whole_rows(qkv_term[..., :q_here]),
         kv_rows(qkv_term[..., q_here : q_here + HD]),
         kv_rows(qkv_term[..., q_here + HD :]),

time: 802 us -> 770 us (0.960)
  Pallas kernels: 742 us -> 722 us
  other arithmetic: 16.5 us -> 2.85 us
    pallas_call x11, Pallas kernels: 698 us -> 678 us  [run(): pl.pallas_call(body, out_shape=tuple((shape for shape, _ in outs)), in_sp...]
where the time goes in v7:
time: 770 us; the launch traced here: 760 us
  Pallas kernels  722 us (94%)
  between operations  14.7 us (2%)
  matrix products  10.5 us (1%)
    pallas_call x11, Pallas kernels, run(): pl.pallas_call(body, out_shape=tuple((shape for shape, _ in outs)), in_sp...  678 us
    pallas_call x1, Pallas kernels, attend(): pl.pallas_call(functools.partial(attend_kernel, heads, order.shape[1], bl...  21.2 us
    pallas_call x1, Pallas kernels, finish(): pl.pallas_call(functools.partial(finish_kernel, heads), out_shape=tuple(s...  17.3 us
  transfers between devices with their start and end apart: 2, of which 0 were waited for; matrix products, arithmetic and copies ran while one was open for 2% of the time, Pallas kernels for 17%

profile of v7, /device:TPU:0, one launch (start us, length us, event | category | flops | bytes accessed | tf_op | source)
XLA Modules:
  0.0 760.4 jit_solution(6448348236482868389)
XLA Ops:
  7.2 0.0 all-gather.3.cloned.1.call-start
  7.2 22.5 %shard_map.230 = bf16[8,48,2048]{2,1,0:T(8,128)(2,1)} custom-call(bf16[256,8192]{1,0:T(8,128)(2,1)} %refs_0_.1, bf16[256,8192]{1,0:T(8,128)(2,1)} %refs_1_.5), custom_call_target="tpu_custom_call" | custom-call | bytes 39321600 | tf_op jit(solution)/shard_map/pallas_call | solution.py:468
  29.7 0.0 slice-start
  29.7 0.0 slice-start.1
  29.8 0.0 all-gather.3.cloned.1.call-update
  29.8 65.6 %shard_map.231 = (bf16[2048,2048]{1,0:T(8,128)(2,1)}, bf16[2048,512]{1,0:T(8,128)(2,1)}) custom-call(bf16[256,2048]{1,0:T(8,128)(2,1)} %bitcast.48, f32[1,2048]{1,0:T(1,128)} %bitcast.55, bf16[256,2048]{1,0:T(8,128)(2,1)} %refs_2_.1, bf16[256,1024]{1,0:T(8,128)(2,1)} %refs_3_.1, bf16[256,1024]{1,0:T(8,128)(2,1)} %refs_4_.1), custom_call_target="tpu_custom_call" | custom-call | bytes 157286400 | tf_op jit(solution)/shard_map/pallas_call | solution.py:468
  95.4 0.0 slice-done
  95.4 0.0 slice-done.1
  95.4 0.2 copy_bitcast_fusion
  95.7 0.0 copy-start.5
  95.7 1.5 pad_maximum_fusion
  97.2 3.6 all-to-all-start
  100.8 0.0 copy-done.5
  100.8 0.6 select_reduce_fusion
  101.4 0.0 copy-start.3
  101.4 10.5 %fusion.1.qkv_ref = f32[2048,512]{1,0:T(8,128)} fusion(bf16[2048,2048]{1,0:T(8,128)(2,1)} %get-tuple-element.100.refs_2_, bf16[2048,512]{1,0:T(8,128)(2,1)} %get-tuple-element.101.refs_1_), kind=kOutput, calls=%fused_computation.7 | convolution fusion | flops 4294967296 | bytes 14680064 | tf_op jit(solution)/shard_map/dot_general | solution.py:25
  112.0 0.0 copy-done.3
  112.0 1.3 broadcast_in_dim.25.piece_col_ref.refs_9_
  113.3 21.2 %shard_map.232 = (bf16[2048,256]{1,0:T(8,128)(2,1)}, bf16[2,2048,128]{2,1,0:T(8,128)(2,1)}, bf16[2048,128]{1,0:T(8,128)(2,1)}, bf16[2048,128]{1,0:T(8,128)(2,1)}...) custom-call(s32[1,16]{1,0:T(1,128)} %holder_ref.1, f32[2048,512]{1,0:T(8,128)} %fusion.1.qkv_ref, ...), custom_call_target="tpu_custom_call" | custom-call | flops 3221225472 | bytes 20971520 | tf_op jit(solution)/shard_map/pallas_call | solution.py:148
  134.5 45.8 %shard_map.233.refs_0_.refs_4_.refs_3_ = f32[256,2048]{1,0:T(8,128)} custom-call(bf16[2048,256]{1,0:T(8,128)(2,1)} %get-tuple-element.102.refs_0_.refs_2_, bf16[256,2048]{1,0:T(8,128)(2,1)} %refs_1_.9, bf16[256,2048]{1,0:T(8,128)(2,1)} %bitcast.49), custom_call_target="tpu_custom_call" | custom-call | flops 2147483648 | bytes 157286400 | tf_op jit(solution)/shard_map/pallas_call | solution.py:468
  180.3 0.0 all-to-all-done
  180.3 0.0 copy-start
  180.3 0.0 all-gather.3.cloned.1.call-done
  180.3 1.3 copy-done
  181.6 51.8 %shard_map.234 = (bf16[2048,2048]{1,0:T(8,128)(2,1)}, bf16[2048,1024]{1,0:T(8,128)(2,1)}, bf16[2048,1024]{1,0:T(8,128)(2,1)}, bf16[2048,1024]{1,0:T(8,128)(2,1)}, bf16[8,256,2048]{2,1,0:T(8,128)(2,1)}) custom-call(f32[256,2048]{1,0:T(8,128)} %shard_map.233.refs_0_.refs_4_.refs_3_, f32[1,2048]{1,0:T(1,128)} %bitcast.73, bf16[4,8,48,2048]{3,2,1,0:T(8,128)(2,1)} %bitcast.66, ...), custom_call_target="tpu_custom_call" | custom-call | flops 17179869184 | bytes 157286400 | tf_op jit(solution)/shard_map/pallas_call | solution.py:468
  233.5 51.0 %shard_map.235 = (bf16[2048,2048]{1,0:T(8,128)(2,1)}, bf16[1024,2048]{1,0:T(8,128)(2,1)}) custom-call(bf16[256,2048]{1,0:T(8,128)(2,1)} %bitcast.69, bf16[1024,2048]{1,0:T(8,128)(2,1)} %refs_1_.8, bf16[2048,1024]{1,0:T(8,128)(2,1)} %get-tuple-element.106.refs_2_.refs_0_, bf16[2048,1024]{1,0:T(8,128)(2,1)} %get-tuple-element.108.refs_3_, ...), custom_call_target="tpu_custom_call" | custom-call | flops 17179869184 | bytes 157286400 | tf_op jit(solution)/shard_map/pallas_call | solution.py:468
  284.4 62.2 %shard_map.236 = (bf16[256,2048]{1,0:T(8,128)(2,1)}, bf16[8,256,2048]{2,1,0:T(8,128)(2,1)}, bf16[8,16,2048]{2,1,0:T(8,128)(2,1)}, bf16[8,16,2048]{2,1,0:T(8,128)...) custom-call(bf16[2048,1024]{1,0:T(8,128)(2,1)} %get-tuple-element.106.refs_2_.refs_0, ...), custom_call_target="tpu_custom_call" | custom-call | flops 25769803776 | bytes 157286400 | tf_op jit(solution)/shard_map/pallas_call | solution.py:468
  346.7 66.9 %shard_map.237 = (f32[256,2048]{1,0:T(8,128)}, f32[1,2048]{1,0:T(1,128)}, bf16[8,16,2048]{2,1,0:T(8,128)(2,1)}, bf16[8,16,2048]{2,1,0:T(8,128)(2,1)}, bf16[8,16,...) custom-call(bf16[2048,2048]{1,0:T(8,128)(2,1)} %get-tuple-element.11, ...), custom_call_target="tpu_custom_call" | custom-call | flops 17179869184 | bytes 157286400 | tf_op jit(solution)/shard_map/pallas_call | solution.py:468
  413.6 53.6 %shard_map.238 = (bf16[2048,256]{1,0:T(8,128)(2,1)}, bf16[256,2048]{1,0:T(8,128)(2,1)}, bf16[8,16,2048]{2,1,0:T(8,128)(2,1)}, bf16[8,16,2048]{2,1,0:T(8,128)(2,1...) custom-call(f32[256,2048]{1,0:T(8,128)} %get-tuple-element.119.refs_, ...), custom_call_target="tpu_custom_call" | custom-call | flops 4294967296 | bytes 157286400 | tf_op jit(solution)/shard_map/pallas_call | solution.py:468
  467.3 2.3 shard_map.239.refs_0_
  469.6 41.9 %shard_map.240 = (bf16[2048,512]{1,0:T(8,128)(2,1)}, bf16[8,16,2048]{2,1,0:T(8,128)(2,1)}, bf16[8,16,2048]{2,1,0:T(8,128)(2,1)}, bf16[8,16,2048]{2,1,0:T(8,128)(...) custom-call(bf16[2048,256]{1,0:T(8,128)(2,1)} %shard_map.239.refs_0_, ...), custom_call_target="tpu_custom_call" | custom-call | flops 8589934592 | bytes 29360128 | tf_op jit(solution)/shard_map/pallas_call | solution.py:468
  511.6 3.1 shard_map.241.refs_0_
  514.7 0.0 copy-start.4
  514.7 52.5 %shard_map.242 = (bf16[256,2048]{1,0:T(8,128)(2,1)}, f32[1,2048]{1,0:T(1,128)}, bf16[8,256,512]{2,1,0:T(8,128)(2,1)}, bf16[8,16,2048]{2,1,0:T(8,128)(2,1)}, bf16...) custom-call(bf16[2048,512]{1,0:T(8,128)(2,1)} %shard_map.241.refs_0_, ...), custom_call_target="tpu_custom_call" | custom-call | flops 8589934592 | bytes 157286400 | tf_op jit(solution)/shard_map/pallas_call | solution.py:468
  567.2 0.0 copy-done.4
  567.2 0.7 maximum_bitcast_fusion
  567.9 0.6 pad.4.refs_1_
  568.6 163.9 %shard_map.243 = (bf16[256,8192]{1,0:T(8,128)(2,1)}, bf16[256,8192]{1,0:T(8,128)(2,1)}, bf16[2,8,32,2048]{3,2,1,0:T(8,128)(2,1)}, f32[8,256]{1,0:T(8,128)}, bf16...) custom-call(bf16[8,8,32,512]{3,2,1,0:T(8,128)(2,1)} %bitcast.46, ...), custom_call_target="tpu_custom_call" | custom-call | bytes 104857600 | tf_op jit(solution)/shard_map/pallas_call | solution.py:468
  732.5 1.3 fusion
  733.8 0.0 copy-start.1
  733.8 0.0 copy-start.2
  733.8 17.3 %shard_map.244 = (f32[8,32,2048]{2,1,0:T(8,128)}, f32[8,32,1024]{2,1,0:T(8,128)}, f32[8,32,1024]{2,1,0:T(8,128)}, f32[8,32,2048]{2,1,0:T(8,128)}, f32[8,32,8192]...) custom-call(bf16[8,16,2048]{2,1,0:T(8,128)(2,1)} %get-tuple-element.140.refs_0_, ...), custom_call_target="tpu_custom_call" | custom-call | bytes 53477376 | tf_op jit(solution)/shard_map/pallas_call | solution.py:1492
  751.1 0.0 copy-done.1
  751.1 1.0 copy.38
  752.1 0.0 copy-done.2
  752.1 1.0 copy.39
Async XLA Ops:
  7.2 173.2 %all-gather.3.cloned.1.call-start = ((), (), s32[]{:S(2)}) async-start(), calls=%async_computation.1 | async-start | bytes 7864320 | tf_op jit(solution)/shard_map/all_gather | solution.py:1577
  29.7 65.7 %slice-start = ((bf16[256,8192]{1,0:T(8,128)(2,1)}), bf16[64,8192]{1,0:T(8,128)(2,1)S(1)}, s32[]{:S(2)}) async-start(bf16[256,8192]{1,0:T(8,128)(2,1)} %refs_0_.1), calls=%async_computation.2 | async-start | bytes 2097152 | tf_op jit(solution)/shard_map/slice | solution.py:1582
  29.7 65.7 %slice-start.1 = ((bf16[256,8192]{1,0:T(8,128)(2,1)}), bf16[64,8192]{1,0:T(8,128)(2,1)S(1)}, s32[]{:S(2)}) async-start(bf16[256,8192]{1,0:T(8,128)(2,1)} %refs_1_.5), calls=%async_computation.3 | async-start | bytes 2097152 | tf_op jit(solution)/shard_map/slice | solution.py:1582
  95.7 5.1 copy-start.5
  97.2 83.1 %all-to-all-start = ((bf16[64,8,2048]{2,0,1:T(8,128)(2,1)}), bf16[64,8,2048]{2,0,1:T(8,128)(2,1)S(1)}, u32[]{:S(2)}, u32[]{:S(2)}) async-start(bf16[64,8,2048]{2,0,1:T(8,128)(2,1)} %pad_maximum_fusion), calls=%async_computation | async-start | bytes 4194304 | tf_op jit(solution)/shard_map/all_to_all | solution.py:1560
  101.4 10.5 %copy-start.3 = (s32[1,2048]{1,0:T(1,128)S(1)}, s32[1,2048]{1,0:T(1,128)}, u32[]{:S(2)}) copy-start(s32[1,2048]{1,0:T(1,128)} %refs_8_.1) | copy-start | bytes 24580
  180.3 1.3 copy-start
  514.7 52.5 %copy-start.4 = (f32[1,2048]{1,0:T(1,128)S(1)}, f32[1,2048]{1,0:T(1,128)}, u32[]{:S(2)}) copy-start(f32[1,2048]{1,0:T(1,128)} %get-tuple-element.150) | copy-start | bytes 24580
  733.8 17.3 %copy-start.1 = (bf16[256,2048]{1,0:T(8,128)(2,1)S(1)}, bf16[256,2048]{1,0:T(8,128)(2,1)}, u32[]{:S(2)}) copy-start(bf16[256,2048]{1,0:T(8,128)(2,1)} %get-tuple-element.112) | copy-start | bytes 3145732
  733.8 18.3 %copy-start.2 = (bf16[256,2048]{1,0:T(8,128)(2,1)S(1)}, bf16[256,2048]{1,0:T(8,128)(2,1)}, u32[]{:S(2)}) copy-start(bf16[256,2048]{1,0:T(8,128)(2,1)} %get-tuple-element.139) | copy-start | bytes 3145732
Sparse Core Ops, SparseCore 0:
  29.9 116.5 all-gather.2

commit v8 on v7

--- a/solution.py
+++ b/solution.py
@@ -58,23 +58,33 @@
     return out
 
 
+def as_column(row):
+    return jnp.broadcast_to(row, (HD, row.shape[1])).T[:, 0:1]
+
+
 def as_row(column):
     return jnp.broadcast_to(column, (column.shape[0], HD)).T[0:1, :]
 
 
 def attend_kernel(
     heads, cuts, block,
-    order_ref, qkv_ref, cos_ref, sin_ref, piece_ref, piece_col_ref,
+    order_ref, rows_hbm, weight_hbm, cos_ref, sin_ref, piece_ref,
     out_ref, q_ref, k_ref, v_ref, lse_ref, placed,
-    scores,
+    scores, rows_ref, weight_ref, qkv_ref, sems,
 ):
-    length = qkv_ref.shape[0]
+    length = rows_ref.shape[0]
     cut = length // cuts
     blocks = length // block
-
-    def place_cut(r, _):
+    loads = [pltpu.make_async_copy(weight_hbm, weight_ref, sems.at[blocks])]
+    for i in range(blocks):
+        at = slice(i * block, (i + 1) * block)
+        loads.append(pltpu.make_async_copy(rows_hbm.at[at, :], rows_ref.at[at, :], sems.at[i]))
+    for load in loads:
+        load.start()
+
+    def place_cut(r, first):
         src = pl.ds(pl.multiple_of(r * cut, cut), cut)
-        dst = pl.ds(pl.multiple_of(order_ref[0, r] * cut, cut), cut)
+        dst = pl.ds(pl.multiple_of(order_ref[0, first + r] * cut, cut), cut)
         cosine, sine = cos_ref[dst, :], sin_ref[dst, :]
         for h in range(heads + 1):
             part = qkv_ref[src, h * HD : (h + 1) * HD]
@@ -84,9 +94,13 @@
             else:
                 k_ref[dst, :] = turned
         v_ref[dst, :] = qkv_ref[src, (heads + 1) * HD :].astype(bf16)
-        return 0
-
-    lax.fori_loop(0, cuts, place_cut, 0)
+        return first
+
+    loads[0].wait()
+    for i in range(blocks):
+        loads[1 + i].wait()
+        qkv_ref[...] = matmul_f32(rows_ref[i * block : (i + 1) * block, :], weight_ref[...])
+        lax.fori_loop(0, block // cut, place_cut, i * (block // cut))
 
     def one_block(i, _):
         rows = pl.ds(pl.multiple_of(i * block, block), block)
@@ -102,7 +116,8 @@
         tile = against_rows(query, k_ref[rows, :])
         q_at = lax.broadcasted_iota(jnp.int32, (block, block), 0)
         k_at = lax.broadcasted_iota(jnp.int32, (block, block), 1)
-        q_piece, k_piece = piece_col_ref[rows, 0:1], piece_ref[0:1, rows]
+        k_piece = piece_ref[0:1, rows].astype(f32)
+        q_piece = as_column(k_piece)
         allowed = (k_at <= q_at) | ((q_piece != 0) & (q_piece == k_piece))
         tile = jnp.concatenate(
             [jnp.where(allowed, tile[h * block : (h + 1) * block], NEG) for h in range(heads)], 0
@@ -142,8 +157,8 @@
     return [pl.BlockSpec(memory_space=pltpu.VMEM)] * count
 
 
-def attend(order, qkv, cosine, sine, piece, piece_col, heads):
-    length = qkv.shape[0]
+def attend(order, rows, weight, cosine, sine, piece, heads):
+    length, width = rows.shape
     block = min(512, length)
     return pl.pallas_call(
         functools.partial(attend_kernel, heads, order.shape[1], block),
@@ -155,18 +170,27 @@
             jax.ShapeDtypeStruct((heads, length), f32),
             jax.ShapeDtypeStruct((length, heads * HD), bf16),
         ),
-        in_specs=[pl.BlockSpec(memory_space=pltpu.SMEM)] + vmem_specs(5),
+        in_specs=[pl.BlockSpec(memory_space=pltpu.SMEM)]
+        + [pl.BlockSpec(memory_space=pl.ANY)] * 2
+        + vmem_specs(3),
         out_specs=tuple(vmem_specs(6)),
-        scratch_shapes=[pltpu.VMEM((length // block, heads * block, block), f32)],
+        scratch_shapes=[
+            pltpu.VMEM((length // block, heads * block, block), f32),
+            pltpu.VMEM(rows.shape, bf16),
+            pltpu.VMEM(weight.shape, bf16),
+            pltpu.VMEM((block, weight.shape[1]), f32),
+            pltpu.SemaphoreType.DMA((length // block + 1,)),
+        ],
         compiler_params=pltpu.CompilerParams(vmem_limit_bytes=60 * 2**20),
         cost_estimate=pl.CostEstimate(
-            flops=3 * heads * length * length * HD, bytes_accessed=10 * length * HD * heads * 4,
+            flops=3 * heads * length * length * HD + 2 * length * width * weight.shape[1],
+            bytes_accessed=10 * length * HD * heads * 4 + rows.size * 2,
             transcendentals=heads * length * length // 2,
         ),
-    )(order, qkv, cosine, sine, piece, piece_col)
-
-
-DOWN, GATE_UP, OUT, QKV = 8, 16, 2, 8
+    )(order, rows, weight, cosine, sine, piece)
+
+
+DOWN, GATE_UP, OUT, QKV = 8, 16, 2, 12
 CHUNKS = DOWN + GATE_UP + OUT + QKV
 
 
@@ -175,7 +199,17 @@
 
 
 def chunk_shape(shape, number):
-    return shape[:2] + (shape[2] // 2,) if number >= CHUNKS - QKV else shape
+    left = CHUNKS - number
+    return shape[:2] + (shape[2] // (4 if left <= 8 else 2 if left <= QKV else 1),)
+
+
+def qkv_parts(width):
+    return [
+        (half, low, n * (width // parts), width // parts)
+        for half, parts in ((0, 2), (1, 4))
+        for low in (0, 1)
+        for n in range(parts)
+    ]
 
 
 def is_middle():
@@ -495,7 +529,7 @@
 def attend_back_kernel(
     heads, block, ins, outs, scratch, line
 ):
-    grad_ref, out_ref, q_ref, k_ref, v_ref, lse_ref, cos_ref, sin_ref, piece_ref, piece_col_ref = ins
+    grad_ref, out_ref, q_ref, k_ref, v_ref, lse_ref, cos_ref, sin_ref, piece_ref = ins
     (grad_qkv_ref,) = outs
     grads, centers, grad_q = scratch
     if line.ticks:
@@ -534,7 +568,8 @@
                 if diagonal:
                     k_at = lax.broadcasted_iota(jnp.int32, (block, block), 0)
                     q_at = lax.broadcasted_iota(jnp.int32, (block, block), 1)
-                    k_piece, q_piece = piece_col_ref[cols, 0:1], piece_ref[0:1, cols]
+                    q_piece = piece_ref[0:1, cols].astype(f32)
+                    k_piece = as_column(q_piece)
                     allowed = (k_at <= q_at) | ((q_piece != 0) & (q_piece == k_piece))
                     prob = jnp.where(allowed, prob, 0.0)
                 grad_prob = against_rows(value, grad)
@@ -596,13 +631,13 @@
 
 
 def attend_back(
-    order, grad, out, query, key, value, lse, cosine, sine, piece, piece_col, heads, **line
+    order, grad, out, query, key, value, lse, cosine, sine, piece, heads, **line
 ):
     cuts = jnp.arange(order.shape[1], dtype=order.dtype)
     holder = jnp.sum(jnp.where(order[0][None, :] == cuts[:, None], cuts[None, :], 0), 1)[None, :]
     length = grad.shape[0]
     block = min(512, length)
-    tall = [take_cuts(holder, grad), out, query, key, value, lse, cosine, sine, piece, piece_col]
+    tall = [take_cuts(holder, grad), out, query, key, value, lse, cosine, sine, piece]
     grad_qkv = run(
         functools.partial(attend_back_kernel, heads, block),
         [(array, VMEM) for array in tall],
@@ -652,74 +687,101 @@
 SIBLING, ALONG_X, ALONG_Y, ACROSS = (0, 0), (0, 1), (1, 0), (1, 1)
 
 
+class Gather:
+    TO_S, TO_X, TO_Y = (0, 0, 1), (0, 1, 0), (1, 0, 0)
+
+    def __init__(self, rows, all_ref, sends, recvs):
+        self.rows, self.all_ref, self.sends, self.recvs = rows, all_ref, sends, recvs
+        self.started = []
+
+    def copy(self, number, chip, core, part, target):
+        first = other(*chip, core) * self.rows
+        if part is None:
+            where = pl.ds(pl.multiple_of(first, self.rows), self.rows)
+        else:
+            half = self.rows // 2
+            where = pl.ds(pl.multiple_of(first + part * half, half), half)
+        where = self.all_ref.at[where, :]
+        return pltpu.make_async_remote_copy(
+            src_ref=where, dst_ref=where, send_sem=self.sends.at[number],
+            recv_sem=self.recvs.at[number], device_id={"grp": other(*target)}, device_id_type=MESH,
+        )
+
+    def send(self, *what):
+        one = self.copy(*what)
+        one.start()
+        self.started.append(one)
+
+    def landed(self, number, chip, core, part):
+        self.copy(number, chip, core, part, self.TO_S).wait_recv()
+
+    def send_own(self):
+        self.send(1, SIBLING, 0, 1, self.TO_X)
+        self.send(3, SIBLING, 0, 0, self.TO_Y)
+        self.send(0, SIBLING, 0, None, self.TO_S)
+        self.send(2, SIBLING, 0, 0, self.TO_X)
+        self.send(4, SIBLING, 0, 1, self.TO_Y)
+
+    def sibling(self):
+        self.landed(0, SIBLING, 1, None)
+
+    def relay(self):
+        self.landed(1, ALONG_X, 0, 1)
+        self.send(6, ALONG_X, 0, 1, self.TO_Y)
+        self.landed(3, ALONG_Y, 0, 0)
+        self.send(5, ALONG_Y, 0, 0, self.TO_X)
+        self.send(7, ALONG_X, 0, 1, self.TO_S)
+        self.send(8, ALONG_Y, 0, 0, self.TO_S)
+
+    def pass_second(self):
+        self.landed(2, ALONG_X, 0, 0)
+        self.send(9, ALONG_X, 0, 0, self.TO_S)
+        self.landed(4, ALONG_Y, 0, 1)
+        self.send(10, ALONG_Y, 0, 1, self.TO_S)
+
+    def along_x(self):
+        self.landed(7, ALONG_X, 1, 1)
+        self.landed(9, ALONG_X, 1, 0)
+
+    def pass_across(self):
+        self.landed(5, ACROSS, 0, 0)
+        self.send(11, ACROSS, 0, 0, self.TO_S)
+        self.landed(6, ACROSS, 0, 1)
+        self.send(12, ACROSS, 0, 1, self.TO_S)
+
+    def along_y(self):
+        self.landed(8, ALONG_Y, 1, 0)
+        self.landed(10, ALONG_Y, 1, 1)
+
+    def across(self):
+        self.landed(11, ACROSS, 1, 0)
+        self.landed(12, ACROSS, 1, 1)
+
+    def finish(self):
+        for one in self.started:
+            one.wait_send()
+
+
 def gather_rows(rows, all_ref, sends, recvs, on_chip, line, then=None):
-    half = rows // 2
-
-    def block(chip, core, part=None):
-        first = other(*chip, core) * rows
-        if part is None:
-            return pl.ds(pl.multiple_of(first, rows), rows)
-        return pl.ds(pl.multiple_of(first + part * half, half), half)
-
-    def copy(number, chip, core, part, target):
-        where = all_ref.at[block(chip, core, part), :]
-        return pltpu.make_async_remote_copy(
-            src_ref=where, dst_ref=where, send_sem=sends.at[number], recv_sem=recvs.at[number],
-            device_id={"grp": other(*target)}, device_id_type=MESH,
-        )
-
-    def landed(number, chip, core, part):
-        where = all_ref.at[block(chip, core, part), :]
-        pltpu.make_async_remote_copy(
-            src_ref=where, dst_ref=where, send_sem=sends.at[number], recv_sem=recvs.at[number],
-            device_id={"grp": other(0, 0, 1)}, device_id_type=MESH,
-        ).wait_recv()
-
-    to_s, to_x, to_y = (0, 0, 1), (0, 1, 0), (1, 0, 0)
-    started = []
-
-    def send(*what):
-        one = copy(*what)
-        one.start()
-        started.append(one)
-
-    send(1, SIBLING, 0, 1, to_x)
-    send(3, SIBLING, 0, 0, to_y)
-    send(0, SIBLING, 0, None, to_s)
-    send(2, SIBLING, 0, 0, to_x)
-    send(4, SIBLING, 0, 1, to_y)
+    rows_of = Gather(rows, all_ref, sends, recvs)
+    rows_of.send_own()
     if then:
         then()
-    landed(0, SIBLING, 1, None)
+    rows_of.sibling()
     on_chip(*SIBLING)
-    landed(1, ALONG_X, 0, 1)
-    send(6, ALONG_X, 0, 1, to_y)
-    landed(3, ALONG_Y, 0, 0)
-    send(5, ALONG_Y, 0, 0, to_x)
-    send(7, ALONG_X, 0, 1, to_s)
-    send(8, ALONG_Y, 0, 0, to_s)
+    rows_of.relay()
     line.step()
-    landed(2, ALONG_X, 0, 0)
-    send(9, ALONG_X, 0, 0, to_s)
-    landed(4, ALONG_Y, 0, 1)
-    send(10, ALONG_Y, 0, 1, to_s)
+    rows_of.pass_second()
     line.step()
-    landed(7, ALONG_X, 1, 1)
-    landed(9, ALONG_X, 1, 0)
+    rows_of.along_x()
     on_chip(*ALONG_X)
-    landed(5, ACROSS, 0, 0)
-    send(11, ACROSS, 0, 0, to_s)
-    landed(6, ACROSS, 0, 1)
-    send(12, ACROSS, 0, 1, to_s)
+    rows_of.pass_across()
     line.step()
-    landed(8, ALONG_Y, 1, 0)
-    landed(10, ALONG_Y, 1, 1)
+    rows_of.along_y()
     on_chip(*ALONG_Y)
-    landed(11, ACROSS, 1, 0)
-    landed(12, ACROSS, 1, 1)
+    rows_of.across()
     on_chip(*ACROSS)
-    for one in started:
-        one.wait_send()
+    rows_of.finish()
     line.end()
 
 
@@ -866,31 +928,33 @@
 
 
 def feed_forward_kernel(tile, ins, outs, scratch, line):
-    mid_ref, gain_ref, spread_ref, rest_ref = ins
-    all_ref, hidden_ref, up_part_ref, gate_part_ref, whole_ref = outs
-    held, sends, recvs, sems, weight, hidden, up_part, gate_part = scratch
+    mid_ref, gain_ref, grad_ref, spread_ref, rest_ref, w_down_ref = ins
+    all_ref, hidden_ref, whole_ref, grad_gate_up_ref, down_ref = outs
+    held, grads_held, sends, recvs, grad_sends, grad_recvs, sems = scratch[:7]
+    weight, w_down, hidden, up_part, gate_part, grads, down = scratch[7:]
     rows = mid_ref.shape[0]
     inner = hidden.shape[1]
     moves = Moves(sems)
-    planes, _, tall, deep = spread_ref.shape
+    planes, _, tall, _ = spread_ref.shape
     loads = [
         moves.start(spread_ref.at[z], weight.at[:, z * tall : (z + 1) * tall, :])
         for z in range(planes)
     ]
     loads.append(moves.start(rest_ref, weight.at[:, planes * tall :, :]))
+    down_load = moves.start(w_down_ref, w_down)
 
     def fill():
         held[own_rows(rows), :] = rms_normed(mid_ref[...], gain_ref[...]).astype(bf16)
+        grads_held[own_rows(rows), :] = grad_ref[...]
 
     greet_group(line, between=fill)
-
-    def on_chip(*chip):
+    first = Gather(rows, held, sends, recvs)
+    second = Gather(rows, grads_held, grad_sends, grad_recvs)
+    stored = []
+
+    def forward(*chip):
         where = chip_rows(*chip, rows)
         moves.later(held.at[where, :], all_ref.at[where, :])
-        if chip == SIBLING:
-            for one in loads:
-                one.wait()
-            moves.later(weight, whole_ref)
 
         def column(t, _):
             cols = pl.ds(pl.multiple_of(t * tile, tile), tile)
@@ -906,101 +970,96 @@
             return 0
 
         lax.fori_loop(0, inner // tile, column, 0)
-        for src, dst in ((hidden, hidden_ref), (up_part, up_part_ref), (gate_part, gate_part_ref)):
-            moves.later(src.at[where, :], dst.at[where, :])
-
-    gather_rows(rows, held, sends, recvs, on_chip, line)
-    moves.finish()
-
-
-def feed_forward(mid, gain, spread, rest, **line):
-    rows, width = mid.shape
-    inner = rest.shape[2] // 2
-    weight = (8, width // 8, 2 * inner)
-    tall = jax.ShapeDtypeStruct((8 * rows, inner), bf16)
-    return run(
-        functools.partial(feed_forward_kernel, min(256, inner)),
-        [(mid, VMEM), (gain, VMEM), (spread, ANY), (rest, ANY)],
-        [(jax.ShapeDtypeStruct((8 * rows, width), bf16), ANY)]
-        + [(tall, ANY)] * 3
-        + [(jax.ShapeDtypeStruct(weight, bf16), ANY)],
-        gather_scratch(rows, width, 22)
-        + [pltpu.VMEM(weight, bf16)]
-        + [pltpu.VMEM((8 * rows, inner), bf16)] * 3,
-        line.pop("number"),
-        (32 * rows * width * inner, 150 * rows * width * 2, 8 * rows * inner),
-        **line,
-    )
-
-
-def feed_forward_back_kernel(tile, ins, outs, scratch, line):
-    grad_ref, w_ref, hidden_ref, up_part_ref, gate_part_ref = ins
-    grad_gate_up_ref, down_ref = outs
-    held, sends, recvs, sems, weight, hidden, up_part, gate_part, grads, down, down_low = scratch
-    rows = grad_ref.shape[0]
-    inner, width = weight.shape
-    moves = Moves(sems)
-    loads = [
-        moves.start(src, dst)
-        for src, dst in (
-            (w_ref, weight), (hidden_ref, hidden), (up_part_ref, up_part), (gate_part_ref, gate_part)
-        )
-    ]
-    greet_group(line)
-    line.start()
-    held[own_rows(rows), :] = grad_ref[...].astype(bf16)
-
-    def on_chip(*chip):
+        moves.later(hidden.at[where, :], hidden_ref.at[where, :])
+
+    def backward(*chip):
         where = chip_rows(*chip, rows)
-        if chip == SIBLING:
-            for one in loads:
-                one.wait()
+        slot = len(stored) % 2
+        if len(stored) >= 2:
+            stored[len(stored) - 2].wait()
 
         def column(t, _):
             cols = pl.ds(pl.multiple_of(t * tile, tile), tile)
             up_cols = pl.ds(pl.multiple_of(inner + t * tile, tile), tile)
-            incoming = held[where, :]
-            grad_hidden = against_rows(incoming, weight[cols, :])
-            grads[where, cols] = (grad_hidden * gate_part[where, cols].astype(f32)).astype(bf16)
-            grads[where, up_cols] = (grad_hidden * up_part[where, cols].astype(f32)).astype(bf16)
+            incoming = grads_held[where, :]
+            grad_hidden = against_rows(incoming, w_down[cols, :])
+            grads[slot, :, cols] = (grad_hidden * gate_part[where, cols].astype(f32)).astype(bf16)
+            grads[slot, :, up_cols] = (grad_hidden * up_part[where, cols].astype(f32)).astype(bf16)
             term = over_tokens(hidden[where, cols], incoming)
             if chip == SIBLING:
                 down[cols, :] = term
             elif chip == ACROSS:
-                down_low[cols, :] = (down[cols, :] + term).astype(bf16)
+                weight[t] = (down[cols, :] + term).astype(bf16)
             else:
                 down[cols, :] += term
             return 0
 
         lax.fori_loop(0, inner // tile, column, 0)
-        moves.later(grads.at[where, :], grad_gate_up_ref.at[where, :])
-
-    gather_rows(rows, held, sends, recvs, on_chip, line)
-    moves.later(down_low, down_ref)
+        stored.append(moves.start(grads.at[slot], grad_gate_up_ref.at[where, :]))
+
+    first.send_own()
+    for one in loads:
+        one.wait()
+    whole = moves.start(weight, whole_ref)
+    first.sibling()
+    forward(*SIBLING)
+    first.relay()
+    first.pass_second()
+    second.send_own()
+    first.along_x()
+    forward(*ALONG_X)
+    first.pass_across()
+    first.along_y()
+    forward(*ALONG_Y)
+    second.relay()
+    first.across()
+    forward(*ACROSS)
+    down_load.wait()
+    second.sibling()
+    backward(*SIBLING)
+    second.pass_second()
+    second.along_x()
+    backward(*ALONG_X)
+    second.pass_across()
+    second.along_y()
+    backward(*ALONG_Y)
+    second.across()
+    whole.wait()
+    backward(*ACROSS)
+    moves.later(weight.at[: inner // tile], down_ref)
+    first.finish()
+    second.finish()
+    for one in stored[-2:]:
+        one.wait()
     moves.finish()
 
 
-def feed_forward_back(grad, w_down, hidden, up_part, gate_part, **line):
-    rows, width = grad.shape
+def feed_forward(mid, gain, grad, spread, rest, w_down, **line):
+    rows, width = mid.shape
     inner = w_down.shape[0]
+    weight = (8, width // 8, 2 * inner)
     return run(
-        functools.partial(feed_forward_back_kernel, min(256, inner)),
-        [(grad, VMEM)] + [(array, ANY) for array in (w_down, hidden, up_part, gate_part)],
+        functools.partial(feed_forward_kernel, weight[1]),
+        [(mid, VMEM), (gain, VMEM), (grad, VMEM), (spread, ANY), (rest, ANY), (w_down, ANY)],
         [
+            (jax.ShapeDtypeStruct((8 * rows, width), bf16), ANY),
+            (jax.ShapeDtypeStruct((8 * rows, inner), bf16), ANY),
+            (jax.ShapeDtypeStruct(weight, bf16), ANY),
             (jax.ShapeDtypeStruct((8 * rows, 2 * inner), bf16), ANY),
-            (jax.ShapeDtypeStruct((inner, width), bf16), ANY),
+            (jax.ShapeDtypeStruct((inner // weight[1], weight[1], width), bf16), ANY),
         ],
-        gather_scratch(rows, width, 9)
-        + [pltpu.VMEM(w_down.shape, bf16)]
+        [pltpu.VMEM((8 * rows, width), bf16)] * 2
+        + [pltpu.SemaphoreType.DMA((GATHER_COPIES,))] * 4
+        + [pltpu.SemaphoreType.DMA((20,))]
+        + [pltpu.VMEM(weight, bf16), pltpu.VMEM(w_down.shape, bf16)]
         + [pltpu.VMEM((8 * rows, inner), bf16)] * 3
         + [
-            pltpu.VMEM((8 * rows, 2 * inner), bf16),
+            pltpu.VMEM((2, 2 * rows, 2 * inner), bf16),
             pltpu.VMEM(w_down.shape, f32),
-            pltpu.VMEM(w_down.shape, bf16),
         ],
         line.pop("number"),
-        (32 * rows * width * inner, 150 * rows * width * 2, 0),
-        vmem=62,
+        (64 * rows * width * inner, 300 * rows * width * 2, 8 * rows * inner),
+        vmem=61,
         **line,
     )
 
@@ -1387,14 +1446,9 @@
     wide = jax.ShapeDtypeStruct((GATE_UP * high, 8 * inner), bf16)
     moved = jax.ShapeDtypeStruct((2, 8, 2 * high, width), bf16)
     picks = dict(picks)
-    for n in range(QKV):
-        picks[CHUNKS - QKV + n] = (
-            "qkv",
-            lambda ref, n=n: ref.at[
-                n // 4, :, n // 2 % 2 * high : (n // 2 % 2 + 1) * high,
-                n % 2 * (width // 2) : (n % 2 + 1) * (width // 2),
-            ],
-        )
+    for n, (half, low, column, columns) in enumerate(qkv_parts(width)):
+        where = (half, slice(None), slice(low * high, (low + 1) * high), slice(column, column + columns))
+        picks[CHUNKS - QKV + n] = ("qkv", lambda ref, where=where: ref.at[where])
     return run(
         functools.partial(tail_kernel, ready, later),
         [(qkv_term, ANY), (gains, VMEM)] + [(chunks[c], ANY) for c in ready],
@@ -1434,15 +1488,14 @@
     for number, ref in enumerate(chunks[DOWN : DOWN + OUT]):
         jobs.append((ref, [(whole, out.at[:, half(number), :])]))
     part = (heads + 2) * HD
-    for number, ref in enumerate(chunks[DOWN + OUT :]):
+    for ref, (devices, low_rows, column, columns) in zip(chunks[DOWN + OUT :], qkv_parts(width)):
         stores = []
-        places = ref.shape[2] // part
-        for place in range(places):
-            at, device = place * part, (number // 4 * 2 + number % 2) * places + place
+        for place in range(columns // part):
+            at, device = place * part, devices * (width // part) + column // part + place
             for into, first, size in (
                 (query, 0, heads * HD), (key, heads * HD, HD), (value, (heads + 1) * HD, HD)
             ):
-                there = into.at[:, half(number // 2 % 2), device * size : (device + 1) * size]
+                there = into.at[:, half(low_rows), device * size : (device + 1) * size]
                 stores.append((slice(at + first, at + first + size), there))
         jobs.append((ref, stores))
 
@@ -1542,7 +1595,6 @@
     heads = q_width // HD // groups
     copies = groups // kv_heads
     hidden_here = w_down.shape[0]
-    piece_col = jnp.broadcast_to(piece_ids.reshape(length, 1), (length, HD))
     cosine, sine = turn_tables(length)
 
     near = groups == 8 and reps == 4 and copies == 1
@@ -1593,9 +1645,8 @@
             jnp.concatenate([per_group(w_query), per_kv_head(w_key), per_kv_head(w_value)], -1)
         )
         cols_gate_up = to_columns(jnp.concatenate([per_group(w_gate), per_group(w_up)], -1))
-    qkv = matmul_f32(normed_one, cols_qkv)
     attended, query, key, value, lse, attended_placed = attend(
-        cut_order, qkv, cosine, sine, piece_ids, piece_col, heads
+        cut_order, normed_one, cols_qkv, cosine, sine, piece_ids, heads
     )
     if near:
         mid = product_scattered(attended, w_out, False, base=x_rows, number=2)[0]
@@ -1606,18 +1657,15 @@
     def back_through_attention(grad_attended, **line):
         return attend_back(
             cut_order, grad_attended, attended_placed, query, key, value, lse, cosine, sine,
-            piece_ids, piece_col, heads, **line,
+            piece_ids, heads, **line,
         )
 
     q_here = heads * HD
     if near:
-        normed_two, hidden, up_part, gate_part, cols_gate_up = feed_forward(
-            mid, ffn_gain, spread, rest, number=3
+        normed_two, hidden, cols_gate_up, grad_gate_up, down_term = feed_forward(
+            mid, ffn_gain, grad_out, spread, rest, w_down, number=3
         )
         cols_gate_up = cols_gate_up.reshape(model_width, -1)
-        grad_gate_up, down_term = feed_forward_back(
-            grad_out, w_down, hidden, up_part, gate_part, number=4
-        )
         high = rows_here // GATE_UP
         sums = Sums((8, high, model_width))
         terms = {"down": down_term.reshape((DOWN,) + sums.shape)}

time: 770 us -> 749 us (0.973)
  matrix products: 10.5 us -> 0 us
  Pallas kernels: 722 us -> 712 us
    pallas_call x11 -> x10, Pallas kernels: 678 us -> 662 us  [run(): pl.pallas_call(body, out_shape=tuple((shape for shape, _ in outs)), in_sp...]
    dot_general x1 -> x0, matrix products: 10.5 us -> none  [matmul_f32(): return jnp.dot(first, second, preferred_element_type=f32)]
  transfers between devices with their start and end apart: 2 -> 2, of which waited for: 0 -> 0; matrix products, arithmetic and copies ran while one was open for 2% -> 0% of each run, Pallas kernels for 17% -> 19%
where the time goes in v8:
time: 749 us; the launch traced here: 739 us
  Pallas kernels  712 us (95%)
  between operations  14.7 us (2%)
    pallas_call x10, Pallas kernels, run(): pl.pallas_call(body, out_shape=tuple((shape for shape, _ in outs)), in_sp...  662 us
    pallas_call x1, Pallas kernels, attend(): pl.pallas_call(functools.partial(attend_kernel, heads, order.shape[1], bl...  27.2 us
    pallas_call x1, Pallas kernels, finish(): pl.pallas_call(functools.partial(finish_kernel, heads), out_shape=tuple(s...  17.6 us
  transfers between devices with their start and end apart: 2, of which 0 were waited for; matrix products, arithmetic and copies ran while one was open for 0% of the time, Pallas kernels for 19%

profile of v8, /device:TPU:0, one launch (start us, length us, event | category | flops | bytes accessed | tf_op | source)
XLA Modules:
  0.0 738.7 jit_solution(3860822603097263565)
XLA Ops:
  7.2 0.0 all-gather.3.cloned.1.call-start
  7.2 22.5 %shard_map.230 = bf16[8,48,2048]{2,1,0:T(8,128)(2,1)} custom-call(bf16[256,8192]{1,0:T(8,128)(2,1)} %refs_0_.1, bf16[256,8192]{1,0:T(8,128)(2,1)} %refs_1_.4), custom_call_target="tpu_custom_call" | custom-call | bytes 39321600 | tf_op jit(solution)/shard_map/pallas_call | solution.py:502
  29.7 0.0 slice-start
  29.7 0.0 slice-start.1
  29.8 0.0 all-gather.3.cloned.1.call-update
  29.8 65.6 %shard_map.231 = (bf16[2048,2048]{1,0:T(8,128)(2,1)}, bf16[2048,512]{1,0:T(8,128)(2,1)}) custom-call(bf16[256,2048]{1,0:T(8,128)(2,1)} %bitcast.45, f32[1,2048]{1,0:T(1,128)} %bitcast.51, bf16[256,2048]{1,0:T(8,128)(2,1)} %refs_2_.1, bf16[256,1024]{1,0:T(8,128)(2,1)} %refs_3_.1, bf16[256,1024]{1,0:T(8,128)(2,1)} %refs_4_.1), custom_call_target="tpu_custom_call" | custom-call | bytes 157286400 | tf_op jit(solution)/shard_map/pallas_call | solution.py:502
  95.4 0.0 slice-done
  95.4 0.0 slice-done.1
  95.4 0.2 copy_bitcast_fusion
  95.6 0.0 copy-start.4
  95.6 1.5 pad_maximum_fusion
  97.1 3.6 all-to-all-start
  100.7 0.0 copy-done.4
  100.7 0.6 select_reduce_fusion
  101.4 27.2 %shard_map.232 = (bf16[2048,256]{1,0:T(8,128)(2,1)}, bf16[2,2048,128]{2,1,0:T(8,128)(2,1)}, bf16[2048,128]{1,0:T(8,128)(2,1)}, bf16[2048,128]{1,0:T(8,128)(2,1)}...) custom-call(s32[1,16]{1,0:T(1,128)} %holder_ref.1, bf16[2048,2048]{1,0:T(8,128)(2,1)} %get-tuple-element.102.rows_hbm.refs_2_, ...), custom_call_target="tpu_custom_call" | custom-call | flops 7516192768 | bytes 29360128 | tf_op jit(solution)/shard_map/pallas_call | solution.py:163
  128.5 45.8 %shard_map.233.refs_0_.refs_4_.refs_3_ = f32[256,2048]{1,0:T(8,128)} custom-call(bf16[2048,256]{1,0:T(8,128)(2,1)} %get-tuple-element.104.refs_0_.refs_2_, bf16[256,2048]{1,0:T(8,128)(2,1)} %refs_1_.7, bf16[256,2048]{1,0:T(8,128)(2,1)} %bitcast.46), custom_call_target="tpu_custom_call" | custom-call | flops 2147483648 | bytes 157286400 | tf_op jit(solution)/shard_map/pallas_call | solution.py:502
  174.3 0.0 all-to-all-done
  174.3 0.0 copy-start
  174.4 0.0 all-gather.3.cloned.1.call-done
  174.4 1.3 copy-done
  175.7 86.1 %shard_map.234 = (bf16[2048,2048]{1,0:T(8,128)(2,1)}, bf16[2048,1024]{1,0:T(8,128)(2,1)}, bf16[8,256,2048]{2,1,0:T(8,128)(2,1)}, bf16[2048,2048]{1,0:T(8,128)(2,1)}, bf16[4,256,2048]{2,1,0:T(8,128)(2,1)}) custom-call(f32[256,2048]{1,0:T(8,128)} %shard_map.233.refs_0_.refs_4_.refs_3_, f32[1,2048]{1,0:T(1,128)} %bitcast.69, bf16[256,2048]{1,0:T(8,128)(2,1)} %bitcast.65, ...), custom_call_target="tpu_custom_call" | custom-call | flops 34359738368 | bytes 314572800 | tf_op jit(solution)/shard_map/pallas_call | solution.py:502
  261.8 63.5 %shard_map.235 = (bf16[256,2048]{1,0:T(8,128)(2,1)}, bf16[8,256,2048]{2,1,0:T(8,128)(2,1)}, bf16[8,16,2048]{2,1,0:T(8,128)(2,1)}, bf16[8,16,2048]{2,1,0:T(8,128)...) custom-call(bf16[2048,1024]{1,0:T(8,128)(2,1)} %get-tuple-element.108.refs_0_, ...), custom_call_target="tpu_custom_call" | custom-call | flops 25769803776 | bytes 157286400 | tf_op jit(solution)/shard_map/pallas_call | solution.py:502
  325.3 66.1 %shard_map.236 = (f32[256,2048]{1,0:T(8,128)}, f32[1,2048]{1,0:T(1,128)}, bf16[8,16,2048]{2,1,0:T(8,128)(2,1)}, bf16[8,16,2048]{2,1,0:T(8,128)(2,1)}, bf16[8,16,...) custom-call(bf16[2048,2048]{1,0:T(8,128)(2,1)} %get-tuple-element.11, ...), custom_call_target="tpu_custom_call" | custom-call | flops 17179869184 | bytes 157286400 | tf_op jit(solution)/shard_map/pallas_call | solution.py:502
  391.4 53.4 %shard_map.237 = (bf16[2048,256]{1,0:T(8,128)(2,1)}, bf16[256,2048]{1,0:T(8,128)(2,1)}, bf16[8,16,2048]{2,1,0:T(8,128)(2,1)}, bf16[8,16,2048]{2,1,0:T(8,128)(2,1...) custom-call(f32[256,2048]{1,0:T(8,128)} %get-tuple-element.119.refs_, ...), custom_call_target="tpu_custom_call" | custom-call | flops 4294967296 | bytes 157286400 | tf_op jit(solution)/shard_map/pallas_call | solution.py:502
  444.8 2.3 shard_map.238.refs_0_
  447.2 41.9 %shard_map.239 = (bf16[2048,512]{1,0:T(8,128)(2,1)}, bf16[8,16,2048]{2,1,0:T(8,128)(2,1)}, bf16[8,16,2048]{2,1,0:T(8,128)(2,1)}, bf16[8,16,2048]{2,1,0:T(8,128)(...) custom-call(bf16[2048,256]{1,0:T(8,128)(2,1)} %shard_map.238.refs_0_, ...), custom_call_target="tpu_custom_call" | custom-call | flops 8589934592 | bytes 29360128 | tf_op jit(solution)/shard_map/pallas_call | solution.py:502
  489.1 3.1 shard_map.240.refs_0_
  492.2 0.0 copy-start.3
  492.2 51.7 %shard_map.241 = (bf16[256,2048]{1,0:T(8,128)(2,1)}, f32[1,2048]{1,0:T(1,128)}, bf16[8,256,512]{2,1,0:T(8,128)(2,1)}, bf16[8,16,2048]{2,1,0:T(8,128)(2,1)}, bf16...) custom-call(bf16[2048,512]{1,0:T(8,128)(2,1)} %shard_map.240.refs_0_, ...), custom_call_target="tpu_custom_call" | custom-call | flops 8589934592 | bytes 157286400 | tf_op jit(solution)/shard_map/pallas_call | solution.py:502
  543.9 0.0 copy-done.3
  543.9 0.7 maximum_bitcast_fusion
  544.6 0.6 pad.4.refs_1_
  545.2 165.3 %shard_map.242 = (bf16[256,8192]{1,0:T(8,128)(2,1)}, bf16[256,8192]{1,0:T(8,128)(2,1)}, bf16[2,8,32,2048]{3,2,1,0:T(8,128)(2,1)}, f32[8,256]{1,0:T(8,128)}, bf16...) custom-call(bf16[8,8,32,512]{3,2,1,0:T(8,128)(2,1)} %bitcast.43, ...), custom_call_target="tpu_custom_call" | custom-call | bytes 104857600 | tf_op jit(solution)/shard_map/pallas_call | solution.py:502
  710.6 1.3 fusion
  711.9 0.0 copy-start.1
  711.9 0.0 copy-start.2
  711.9 17.6 %shard_map.243 = (f32[8,32,2048]{2,1,0:T(8,128)}, f32[8,32,1024]{2,1,0:T(8,128)}, f32[8,32,1024]{2,1,0:T(8,128)}, f32[8,32,2048]{2,1,0:T(8,128)}, f32[8,32,8192]...) custom-call(bf16[8,16,2048]{2,1,0:T(8,128)(2,1)} %get-tuple-element.140.refs_0_, ...), custom_call_target="tpu_custom_call" | custom-call | bytes 59768832 | tf_op jit(solution)/shard_map/pallas_call | solution.py:1545
  729.5 0.0 copy-done.1
  729.5 1.0 copy.38
  730.5 0.0 copy-done.2
  730.5 1.0 copy.39
Async XLA Ops:
  7.2 167.2 %all-gather.3.cloned.1.call-start = ((), (), s32[]{:S(2)}) async-start(), calls=%async_computation.1 | async-start | bytes 7864320 | tf_op jit(solution)/shard_map/all_gather | solution.py:1629
  29.7 65.6 %slice-start = ((bf16[256,8192]{1,0:T(8,128)(2,1)}), bf16[64,8192]{1,0:T(8,128)(2,1)S(1)}, s32[]{:S(2)}) async-start(bf16[256,8192]{1,0:T(8,128)(2,1)} %refs_0_.1), calls=%async_computation.2 | async-start | bytes 2097152 | tf_op jit(solution)/shard_map/slice | solution.py:1634
  29.7 65.6 %slice-start.1 = ((bf16[256,8192]{1,0:T(8,128)(2,1)}), bf16[64,8192]{1,0:T(8,128)(2,1)S(1)}, s32[]{:S(2)}) async-start(bf16[256,8192]{1,0:T(8,128)(2,1)} %refs_1_.4), calls=%async_computation.3 | async-start | bytes 2097152 | tf_op jit(solution)/shard_map/slice | solution.py:1634
  95.6 5.1 copy-start.4
  97.1 77.2 %all-to-all-start = ((bf16[64,8,2048]{2,0,1:T(8,128)(2,1)}), bf16[64,8,2048]{2,0,1:T(8,128)(2,1)S(1)}, u32[]{:S(2)}, u32[]{:S(2)}) async-start(bf16[64,8,2048]{2,0,1:T(8,128)(2,1)} %pad_maximum_fusion), calls=%async_computation | async-start | bytes 4194304 | tf_op jit(solution)/shard_map/all_to_all | solution.py:1612
  174.3 1.3 copy-start
  492.2 51.7 %copy-start.3 = (f32[1,2048]{1,0:T(1,128)S(1)}, f32[1,2048]{1,0:T(1,128)}, u32[]{:S(2)}) copy-start(f32[1,2048]{1,0:T(1,128)} %get-tuple-element.150) | copy-start | bytes 24580
  711.9 17.6 %copy-start.1 = (bf16[256,2048]{1,0:T(8,128)(2,1)S(1)}, bf16[256,2048]{1,0:T(8,128)(2,1)}, u32[]{:S(2)}) copy-start(bf16[256,2048]{1,0:T(8,128)(2,1)} %get-tuple-element.112) | copy-start | bytes 3145732
  711.9 18.6 %copy-start.2 = (bf16[256,2048]{1,0:T(8,128)(2,1)S(1)}, bf16[256,2048]{1,0:T(8,128)(2,1)}, u32[]{:S(2)}) copy-start(bf16[256,2048]{1,0:T(8,128)(2,1)} %get-tuple-element.139) | copy-start | bytes 3145732
Sparse Core Ops, SparseCore 0:
  29.9 116.5 all-gather.2

commit v9 on v8

--- a/solution.py
+++ b/solution.py
@@ -190,26 +190,13 @@
     )(order, rows, weight, cosine, sine, piece)
 
 
-DOWN, GATE_UP, OUT, QKV = 8, 16, 2, 12
+DOWN, GATE_UP, OUT, QKV = 16, 32, 4, 8
 CHUNKS = DOWN + GATE_UP + OUT + QKV
+LAG = 3
 
 
 def is_chunk(number):
     return 0 <= number < CHUNKS
-
-
-def chunk_shape(shape, number):
-    left = CHUNKS - number
-    return shape[:2] + (shape[2] // (4 if left <= 8 else 2 if left <= QKV else 1),)
-
-
-def qkv_parts(width):
-    return [
-        (half, low, n * (width // parts), width // parts)
-        for half, parts in ((0, 2), (1, 4))
-        for low in (0, 1)
-        for n in range(parts)
-    ]
 
 
 def is_middle():
@@ -235,7 +222,7 @@
     def start(self):
         pass
 
-    def step(self):
+    def step(self, times=1):
         pass
 
     def end(self):
@@ -277,10 +264,6 @@
             recv_sem=self.sems.at[1, hop, number], device_id=device, device_id_type=MESH,
         )
 
-    def part(self, ref, at, chunk):
-        width = chunk_shape(ref.shape[1:], chunk)[2]
-        return ref.at[at] if width == ref.shape[3] else ref.at[at, :, :, :width]
-
     def hops(self, number):
         tick = self.first + number
         term = pair = total = None
@@ -288,31 +271,23 @@
             which, pick = self.picks[tick]
             term = (
                 lambda: self.remote(
-                    0, number, pick(self.refs[which]), self.part(self.inward, number, tick), self.partner
+                    0, number, pick(self.refs[which]), self.inward.at[number], self.partner
                 ),
                 lambda: pltpu.make_async_copy(
-                    pick(self.refs[which]), self.part(self.own, tick % 2, tick), self.local.at[0, number]
+                    pick(self.refs[which]), self.own.at[tick % LAG], self.local.at[0, number]
                 ),
             )
-        if is_chunk(tick - 2):
-            before = (
-                self.refs[f"pair{number}"]
-                if number < 2
-                else self.part(self.pair, (tick - 2) % 3, tick - 2)
+        if is_chunk(tick - LAG):
+            held = self.pair.at[(tick - LAG) % (LAG + 1)]
+            before = self.refs[f"pair{number}"] if number < LAG else held
+            pair = (
+                lambda: self.remote(1, number, before, self.across.at[number], self.peer),
+                lambda: pltpu.make_async_copy(before, held, self.carries.at[0, number]),
             )
-            pair = (
-                lambda: self.remote(1, number, before, self.part(self.across, number, tick - 2), self.peer),
-                lambda: pltpu.make_async_copy(
-                    before, self.part(self.pair, (tick - 2) % 3, tick - 2), self.carries.at[number]
-                ),
-            )
-        if is_chunk(tick - 4):
-            done = (
-                self.refs[f"total{number}"]
-                if number < 2
-                else self.part(self.total, (tick - 4) % 3, tick - 4)
-            )
-            slot = self.outs[tick - 4]
+        if is_chunk(tick - 2 * LAG):
+            held_total = self.total.at[(tick - 2 * LAG) % (LAG + 1)]
+            done = self.refs[f"total{number}"] if number < LAG else held_total
+            slot = self.outs[tick - 2 * LAG]
             total = (
                 lambda: self.remote(2, number, done, slot, self.partner),
                 lambda: pltpu.make_async_copy(done, slot, self.local.at[1, number]),
@@ -337,7 +312,7 @@
                 term[1]().start()
             if total:
                 total[1]().start()
-            if pair and number < 2:
+            if pair and number < LAG:
                 pair[1]().start()
 
     def close(self, number):
@@ -375,30 +350,28 @@
         @pl.when(is_middle())
         def _():
             if pair:
-                if number < 2:
+                if number < LAG:
                     pair[1]().wait()
+                before = tick - LAG
                 sum_of(
-                    self.part(self.total, (tick - 2) % 3, tick - 2),
-                    self.part(self.pair, (tick - 2) % 3, tick - 2),
-                    self.part(self.across, number, tick - 2),
+                    self.total.at[before % (LAG + 1)], self.pair.at[before % (LAG + 1)],
+                    self.across.at[number],
                 )
             if term:
                 term[1]().wait()
-                sum_of(
-                    self.part(self.pair, tick % 3, tick), self.part(self.own, tick % 2, tick),
-                    self.part(self.inward, number, tick),
-                )
+                sum_of(self.pair.at[tick % (LAG + 1)], self.own.at[tick % LAG], self.inward.at[number])
 
     def keep(self, number):
         tick = self.first + number
-        which = number - (self.ticks - 2)
+        which = number - (self.ticks - LAG)
         made = []
         if is_chunk(tick):
-            made.append((self.pair.at[tick % 3], self.outs[f"pair{which}"], 2 + which))
-        if is_chunk(tick - 2):
-            made.append((self.total.at[(tick - 2) % 3], self.outs[f"total{which}"], 4 + which))
+            made.append((self.pair.at[tick % (LAG + 1)], self.outs[f"pair{which}"], (1, which)))
+        if is_chunk(tick - LAG):
+            held = self.total.at[(tick - LAG) % (LAG + 1)]
+            made.append((held, self.outs[f"total{which}"], (2, which)))
         copies = [
-            lambda src=src, dst=dst, at=at: pltpu.make_async_copy(src, dst, self.carries.at[at])
+            lambda src=src, dst=dst, at=at: pltpu.make_async_copy(src, dst, self.carries.at[*at])
             for src, dst, at in made
         ]
 
@@ -410,24 +383,24 @@
         self.kept += copies
 
     def start(self):
-        self.open(0)
-        if self.ticks > 1:
-            self.open(1)
-
-    def step(self):
-        if self.now + 2 < self.ticks:
-            self.settle()
-            self.open(self.now + 1)
+        for number in range(LAG):
+            self.open(number)
+
+    def step(self, times=1):
+        for _ in range(times):
+            if self.now + LAG < self.ticks:
+                self.settle()
+                self.open(self.now + LAG - 1)
 
     def settle(self):
         self.close(self.now)
         self.add(self.now)
-        if self.now >= self.ticks - 2:
+        if self.now >= self.ticks - LAG:
             self.keep(self.now)
         self.now += 1
 
     def end(self):
-        while self.now + 2 < self.ticks:
+        while self.now + LAG < self.ticks:
             self.step()
         while self.now < self.ticks:
             self.settle()
@@ -439,7 +412,7 @@
 
 
 def line_slots(first, ticks):
-    return [t - 4 for t in range(first, first + ticks) if is_chunk(t - 4)]
+    return [t - 2 * LAG for t in range(first, first + ticks) if is_chunk(t - 2 * LAG)]
 
 
 class Sums:
@@ -453,39 +426,30 @@
     first = sums.tick if ticks else 0
     names_in, names_out = [], []
     if ticks:
-        last = first + ticks - 1
         for name, array in arrays:
             names_in.append(name)
             ins.append((array, pl.ANY))
-        for which in (0, 1):
-            for name, chunk_at in ((f"pair{which}", first - 2), (f"total{which}", first - 4)):
+        for which in range(LAG):
+            for name, chunk_at in ((f"pair{which}", first - LAG), (f"total{which}", first - 2 * LAG)):
                 if is_chunk(chunk_at + which):
                     names_in.append(name)
                     ins.append((sums.kept[name], pl.ANY))
         names_out = line_slots(first, ticks)
-        for which in (0, 1):
-            for name, chunk_at in ((f"pair{which}", last - 1), (f"total{which}", last - 3)):
+        after = first + ticks
+        for which in range(LAG):
+            for name, chunk_at in ((f"pair{which}", after - LAG), (f"total{which}", after - 2 * LAG)):
                 if is_chunk(chunk_at + which):
                     names_out.append(name)
-        slots = line_slots(first, ticks)
-        outs += [
-            (
-                jax.ShapeDtypeStruct(
-                    chunk_shape(sums.shape, name) if name in slots else sums.shape, bf16
-                ),
-                pl.ANY,
-            )
-            for name in names_out
-        ]
+        outs += [(jax.ShapeDtypeStruct(sums.shape, bf16), pl.ANY)] * len(names_out)
         scratch += [
             pltpu.VMEM((ticks,) + sums.shape, bf16),
             pltpu.VMEM((ticks,) + sums.shape, bf16),
-            pltpu.VMEM((2,) + sums.shape, bf16),
-            pltpu.VMEM((3,) + sums.shape, bf16),
-            pltpu.VMEM((3,) + sums.shape, bf16),
+            pltpu.VMEM((LAG,) + sums.shape, bf16),
+            pltpu.VMEM((LAG + 1,) + sums.shape, bf16),
+            pltpu.VMEM((LAG + 1,) + sums.shape, bf16),
             pltpu.SemaphoreType.DMA((2, 3, ticks)),
             pltpu.SemaphoreType.DMA((2, ticks)),
-            pltpu.SemaphoreType.DMA((6,)),
+            pltpu.SemaphoreType.DMA((3, LAG)),
         ]
 
     def body(*refs):
@@ -592,7 +556,7 @@
 
     for j in range(min(2, blocks - 1)):
         lax.fori_loop(j, j + 1, key_block, 0)
-        line.step()
+        line.step(1 + j)
     lax.fori_loop(min(2, blocks - 1), blocks, key_block, 0)
 
     def turn_back(i, _):
@@ -770,9 +734,9 @@
     rows_of.sibling()
     on_chip(*SIBLING)
     rows_of.relay()
-    line.step()
+    line.step(2)
     rows_of.pass_second()
-    line.step()
+    line.step(2)
     rows_of.along_x()
     on_chip(*ALONG_X)
     rows_of.pass_across()
@@ -1150,7 +1114,7 @@
             self.store(number).wait()
 
 
-def scatter_kernel(turned, tile, extra, after, ins, outs, scratch, line):
+def scatter_kernel(turned, tile, extra, after, steps, ins, outs, scratch, line):
     out_ref = outs[0] if after == "base" else scratch[-4]
     finals = ins[len(ins) - {"base": 1, "cast": 1, "back": 3}[after] :]
     part, to_s, from_s, to_chip, held, relay, last, sends, recvs = scratch[:9]
@@ -1217,39 +1181,45 @@
         return part[at, :] + from_s[number, low * half : (low + 1) * half, :].astype(f32)
 
     first, second = slice(0, half), slice(half, rows)
+    step = lambda point: line.step(steps.get(point, 0))
     make(0, ACROSS)
     landed(0, from_s.at[0])
     to_chip[0, first, :] = own(0, 0).astype(bf16)
     send(4, to_chip.at[0, first, :], relay.at[0], to_x)
     to_chip[0, second, :] = own(1, 0).astype(bf16)
     send(5, to_chip.at[0, second, :], relay.at[1], to_y)
+    step("across")
     make(1, ALONG_X)
     landed(1, from_s.at[1])
     to_chip[1, first, :] = own(0, 1).astype(bf16)
     send(6, to_chip.at[1, first, :], last.at[0, first, :], to_x)
     held[0] = own(1, 1)
-    line.step()
+    step("x")
     make(2, ALONG_Y)
     landed(2, from_s.at[2])
     to_chip[2, second, :] = own(1, 2).astype(bf16)
     send(7, to_chip.at[2, second, :], last.at[1, second, :], to_y)
     held[1] = own(0, 2)
+    step("y")
     if extra:
         if extra == "loaded":
             columns_copy.wait()
         term.work((0, 1, 2))
+        step("work")
     landed(5, relay.at[1])
     to_chip[1, second, :] = (held[0] + relay[1].astype(f32)).astype(bf16)
     send(8, to_chip.at[1, second, :], last.at[0, second, :], to_x)
     landed(4, relay.at[0])
     to_chip[2, first, :] = (held[1] + relay[0].astype(f32)).astype(bf16)
     send(9, to_chip.at[2, first, :], last.at[1, first, :], to_y)
-    line.step()
+    step("relayed")
     make(3, SIBLING)
+    step("sibling")
     if extra:
         term.work((3, 4))
-        line.step()
+        step("work2")
         term.work((5, 6, 7))
+        step("work3")
     landed(3, from_s.at[3])
     for low in (0, 1):
         at = slice(low * half, (low + 1) * half)
@@ -1261,7 +1231,7 @@
     out_ref[first, :] += last[0, first, :].astype(f32)
     landed(7, last.at[1, second, :])
     out_ref[second, :] += last[1, second, :].astype(f32)
-    line.step()
+    step("halves")
     landed(8, last.at[0, second, :])
     out_ref[second, :] += last[0, second, :].astype(f32)
     landed(9, last.at[1, first, :])
@@ -1290,7 +1260,9 @@
     line.end()
 
 
-def product_scattered(a, b, turned, extra=None, base=None, back=None, dtype=f32, **line):
+def product_scattered(
+    a, b, turned, extra=None, base=None, back=None, dtype=f32, steps=None, **line
+):
     length, depth = a.shape
     width = b.shape[0] if turned else b.shape[1]
     rows = length // 8
@@ -1335,7 +1307,7 @@
         pltpu.VMEM(a.shape, bf16), pltpu.VMEM(b.shape, bf16), pltpu.SemaphoreType.DMA((2,))
     ]
     return run(
-        functools.partial(scatter_kernel, turned, tile, kind, after), ins, outs, scratch,
+        functools.partial(scatter_kernel, turned, tile, kind, after, steps or {}), ins, outs, scratch,
         line.pop("number"), (flops, 150 * rows * width * 2, 0), vmem=61, **line,
     )
 
@@ -1385,26 +1357,24 @@
     def spread(chunk):
         src = chunk_refs[chunk] if chunk in chunk_refs else line.outs[chunk]
         number = chunk - DOWN
-        rows = slice(number * high, (number + 1) * high)
-        cols = pl.ds(pl.multiple_of(me * inner, inner), inner)
-        for which, dst in enumerate((gate_ref, up_ref)):
-            there = dst.at[rows, cols]
-            for flip in EVERYONE:
-                target = other(*flip)
-                pltpu.make_async_remote_copy(
-                    src_ref=src.at[target, :, which * inner : (which + 1) * inner], dst_ref=there,
-                    send_sem=chunk_sems.at[0, which, number], recv_sem=chunk_sems.at[1, which, number],
-                    device_id={"grp": target}, device_id_type=MESH,
-                ).start()
-            moves.later(src.at[me, :, which * inner : (which + 1) * inner], there)
-            seven = dst.at[rows, : 7 * inner]
-            waits.append(
-                pltpu.make_async_remote_copy(
-                    src_ref=seven, dst_ref=seven, send_sem=chunk_sems.at[0, which, number],
-                    recv_sem=chunk_sems.at[1, which, number],
-                    device_id={"grp": other(0, 0, 1)}, device_id_type=MESH,
-                )
+        rows = slice(number // 2 * high, (number // 2 + 1) * high)
+        dst = (gate_ref, up_ref)[number % 2]
+        there = dst.at[rows, pl.ds(pl.multiple_of(me * inner, inner), inner)]
+        for flip in EVERYONE:
+            target = other(*flip)
+            pltpu.make_async_remote_copy(
+                src_ref=src.at[target], dst_ref=there, send_sem=chunk_sems.at[0, number],
+                recv_sem=chunk_sems.at[1, number], device_id={"grp": target}, device_id_type=MESH,
+            ).start()
+        moves.later(src.at[me], there)
+        seven = dst.at[rows, : 7 * inner]
+        waits.append(
+            pltpu.make_async_remote_copy(
+                src_ref=seven, dst_ref=seven, send_sem=chunk_sems.at[0, number],
+                recv_sem=chunk_sems.at[1, number], device_id={"grp": other(0, 0, 1)},
+                device_id_type=MESH,
             )
+        )
 
     for chunk in ready:
         spread(chunk)
@@ -1422,13 +1392,13 @@
         one.wait()
         mine[(rank + 4 - step) % 4] = from_rep[step]
     gains_out_ref[...] = (mine[0] + mine[1]) + (mine[2] + mine[3])
-    for number in range(1, line.ticks):
-        if line.first + number + 1 == CHUNKS - QKV:
+    for settled in range(line.ticks - LAG):
+        if line.first + settled + LAG == CHUNKS - QKV:
             for one in qkv_copies:
                 one.wait()
             moves.open.pop(0).wait()
         line.step()
-        chunk = line.first + number - 5
+        chunk = line.first + settled - 2 * LAG
         if chunk in later:
             spread(chunk)
     line.end()
@@ -1443,11 +1413,14 @@
     ready = sorted(chunks)
     later = [c for c in line_slots(first, ticks) if c < DOWN + GATE_UP]
     _, high, width = sums.shape
-    wide = jax.ShapeDtypeStruct((GATE_UP * high, 8 * inner), bf16)
-    moved = jax.ShapeDtypeStruct((2, 8, 2 * high, width), bf16)
+    wide = jax.ShapeDtypeStruct((GATE_UP // 2 * high, 8 * inner), bf16)
+    moved = jax.ShapeDtypeStruct((2, 8, 2 * high, 2 * width), bf16)
     picks = dict(picks)
-    for n, (half, low, column, columns) in enumerate(qkv_parts(width)):
-        where = (half, slice(None), slice(low * high, (low + 1) * high), slice(column, column + columns))
+    for n in range(QKV):
+        where = (
+            n // 4, slice(None), slice(n // 2 % 2 * high, (n // 2 % 2 + 1) * high),
+            slice(n % 2 * width, (n % 2 + 1) * width),
+        )
         picks[CHUNKS - QKV + n] = ("qkv", lambda ref, where=where: ref.at[where])
     return run(
         functools.partial(tail_kernel, ready, later),
@@ -1459,8 +1432,8 @@
             pltpu.VMEM((4,) + gains.shape[1:], f32),
             pltpu.SemaphoreType.DMA((3, 7)),
             pltpu.SemaphoreType.DMA((3, 7)),
-            pltpu.SemaphoreType.DMA((2, 2, GATE_UP)),
-            pltpu.SemaphoreType.DMA((1 + 2 * GATE_UP,)),
+            pltpu.SemaphoreType.DMA((2, GATE_UP)),
+            pltpu.SemaphoreType.DMA((1 + GATE_UP,)),
         ],
         number, (0, 200 * 8 * high * width * 2, 0), sums=sums, ticks=ticks, arrays=arrays, picks=picks,
     )
@@ -1477,25 +1450,28 @@
     def half(number):
         return slice(number * high, (number + 1) * high)
 
-    whole = slice(0, width)
-    jobs = [(ref, [(whole, down.at[number])]) for number, ref in enumerate(chunks[:DOWN])]
+    def side(number):
+        return slice(number * width, (number + 1) * width)
+
+    jobs = []
+    for n, ref in enumerate(chunks[:DOWN]):
+        jobs.append((ref, [(slice(0, width), down.at[n // 2, :, :, side(n % 2)])]))
     for ref, into in ((gate_rows, gate), (up_rows, up)):
-        for low_col in range(0, ref.shape[2], width):
-            cols = slice(low_col, low_col + width)
+        for low_col in range(0, ref.shape[2], low.shape[3]):
             for number in (0, 1):
-                where = (slice(None), half(number), cols)
-                jobs.append((ref.at[where], [(whole, into.at[where])]))
-    for number, ref in enumerate(chunks[DOWN : DOWN + OUT]):
-        jobs.append((ref, [(whole, out.at[:, half(number), :])]))
+                where = (slice(None), half(number), slice(low_col, low_col + low.shape[3]))
+                jobs.append((ref.at[where], [(slice(0, low.shape[3]), into.at[where])]))
+    for n, ref in enumerate(chunks[DOWN : DOWN + OUT]):
+        jobs.append((ref, [(slice(0, width), out.at[:, half(n // 2), side(n % 2)])]))
     part = (heads + 2) * HD
-    for ref, (devices, low_rows, column, columns) in zip(chunks[DOWN + OUT :], qkv_parts(width)):
+    for n, ref in enumerate(chunks[DOWN + OUT :]):
         stores = []
-        for place in range(columns // part):
-            at, device = place * part, devices * (width // part) + column // part + place
+        for place in range(width // part):
+            at, device = place * part, (n // 4 * 2 + n % 2) * (width // part) + place
             for into, first, size in (
                 (query, 0, heads * HD), (key, heads * HD, HD), (value, (heads + 1) * HD, HD)
             ):
-                there = into.at[:, half(low_rows), device * size : (device + 1) * size]
+                there = into.at[:, half(n // 2 % 2), device * size : (device + 1) * size]
                 stores.append((slice(at + first, at + first + size), there))
         jobs.append((ref, stores))
 
@@ -1534,13 +1510,14 @@
 
 def finish(chunks, gate_rows, up_rows, heads):
     eight, high, width = chunks[0].shape
+    width = 2 * width
     rows, wide = gate_rows.shape
 
     def split(columns):
         return jax.ShapeDtypeStruct((eight, rows // eight, columns), f32)
 
     shapes = [split(columns) for columns in (8 * heads * HD, 8 * HD, 8 * HD, width, wide, wide)]
-    shapes.append(jax.ShapeDtypeStruct((DOWN, eight, high, width), f32))
+    shapes.append(jax.ShapeDtypeStruct((DOWN // 2, eight, high, width), f32))
     depth = 6
     results = pl.pallas_call(
         functools.partial(finish_kernel, heads),
@@ -1555,14 +1532,14 @@
         ],
         compiler_params=pltpu.CompilerParams(vmem_limit_bytes=60 * 2**20),
         cost_estimate=pl.CostEstimate(
-            flops=0, bytes_accessed=6 * CHUNKS * eight * high * width, transcendentals=0
+            flops=0, bytes_accessed=3 * CHUNKS * eight * high * width, transcendentals=0
         ),
     )(
         *chunks, gate_rows.reshape(eight, rows // eight, wide),
         up_rows.reshape(eight, rows // eight, wide),
     )
     flat = [result.reshape(rows, -1) for result in results[:6]]
-    return flat + [results[6].reshape(DOWN * eight * high, width)]
+    return flat + [results[6].reshape(-1, width)]
 
 
 def sum_over_sequences(term):
@@ -1597,7 +1574,7 @@
     hidden_here = w_down.shape[0]
     cosine, sine = turn_tables(length)
 
-    near = groups == 8 and reps == 4 and copies == 1
+    near = groups == 8 and reps == 4 and copies == 1 and 2 * hidden_here == model_width
 
     def gather(rows):
         return lax.all_gather(rows, "grp", axis=0, tiled=True)
@@ -1666,15 +1643,16 @@
             mid, ffn_gain, grad_out, spread, rest, w_down, number=3
         )
         cols_gate_up = cols_gate_up.reshape(model_width, -1)
-        high = rows_here // GATE_UP
-        sums = Sums((8, high, model_width))
-        terms = {"down": down_term.reshape((DOWN,) + sums.shape)}
-
-        def pick_whole(number):
-            return "down", lambda ref: ref.at[number]
-
-        def pick_rows(name, number):
-            return name, lambda ref: ref.at[:, number * high : (number + 1) * high, :]
+        high, half_width = 2 * rows_here // GATE_UP, model_width // 2
+        sums = Sums((8, high, half_width))
+        terms = {"down": down_term.reshape(DOWN // 2, 8, high, model_width)}
+
+        def pick_whole(n):
+            return "down", lambda ref: ref.at[n // 2, :, :, n % 2 * half_width : (n % 2 + 1) * half_width]
+
+        def pick_rows(name, n):
+            rows, side = n // 2 * high, n % 2 * half_width
+            return name, lambda ref: ref.at[:, rows : rows + high, side : side + half_width]
 
         picks = [pick_whole(n) for n in range(DOWN)]
         picks += [pick_rows("gate_up", n) for n in range(GATE_UP)]
@@ -1691,21 +1669,23 @@
 
         result, terms["gate_up"] = product_scattered(
             hidden, w_down, False, extra=(normed_two, grad_gate_up), base=mid, dtype=bf16,
-            **line(5, 5),
+            steps={"x": 1, "y": 1, "work": 1, "relayed": 1, "work2": 1, "work3": 2}, **line(5, 10),
         )
         grad_mid, gain_ffn_term = product_scattered(
-            grad_gate_up, cols_gate_up, True, back=(grad_out, mid, ffn_gain), **line(6, 5)
-        )
-        grad_attended, out_term = attended_back(grad_mid, w_out, attended, **line(7, 4))
-        terms["out"] = out_term.reshape(8, OUT * high, model_width)
-        grad_qkv = back_through_attention(grad_attended, **line(8, 3))
+            grad_gate_up, cols_gate_up, True, back=(grad_out, mid, ffn_gain),
+            steps={"across": 1, "x": 1, "y": 1, "relayed": 1, "sibling": 1, "halves": 1}, **line(6, 10),
+        )
+        grad_attended, out_term = attended_back(grad_mid, w_out, attended, **line(7, 8))
+        terms["out"] = out_term.reshape(8, OUT // 2 * high, model_width)
+        grad_qkv = back_through_attention(grad_attended, **line(8, 6))
         grad_x, gain_attn_term, qkv_term = product_scattered(
             grad_qkv, cols_qkv, True, extra=(normed_one, None), dtype=bf16,
-            back=(grad_mid, x_rows, attn_gain), **line(9, 4),
+            back=(grad_mid, x_rows, attn_gain),
+            steps={"y": 1, "work": 1, "relayed": 2, "work2": 1, "work3": 1}, **line(9, 8),
         )
         gains = jnp.stack([gain_attn_term, gain_ffn_term]).reshape(2, groups, rows_here)
         gains = jnp.pad(jnp.moveaxis(gains, 0, 1), ((0, 0), (0, 6), (0, 0)))
-        rest = line(10, CHUNKS + 4 - sums.tick)
+        rest = line(10, CHUNKS + 2 * LAG - sums.tick)
         gate_rows, up_rows, qkv_rows, own_gains = tail(
             qkv_term.reshape(8, 8, 2 * high, -1), gains,
             {c: sums.done[c] for c in sums.done if c >= DOWN}, hidden_here, **rest,

time: 749 us -> 756 us (level)
  no operation moved by 1% of the time
where the time goes in v9:
time: 756 us; the launch traced here: 746 us
  Pallas kernels  719 us (95%)
  between operations  14.4 us (2%)
    pallas_call x10, Pallas kernels, run(): pl.pallas_call(body, out_shape=tuple((shape for shape, _ in outs)), in_sp...  669 us
    pallas_call x1, Pallas kernels, attend(): pl.pallas_call(functools.partial(attend_kernel, heads, order.shape[1], bl...  27.2 us
    pallas_call x1, Pallas kernels, finish(): pl.pallas_call(functools.partial(finish_kernel, heads), out_shape=tuple(s...  17.4 us
  transfers between devices with their start and end apart: 2, of which 0 were waited for; matrix products, arithmetic and copies ran while one was open for 0% of the time, Pallas kernels for 19%

profile of v9, /device:TPU:0, one launch (start us, length us, event | category | flops | bytes accessed | tf_op | source)
XLA Modules:
  0.0 745.6 jit_solution(11235909853757888847)
XLA Ops:
  7.2 0.0 all-gather.3.cloned.1.call-start
  7.2 22.5 %shard_map.230 = bf16[8,48,2048]{2,1,0:T(8,128)(2,1)} custom-call(bf16[256,8192]{1,0:T(8,128)(2,1)} %refs_0_.1, bf16[256,8192]{1,0:T(8,128)(2,1)} %refs_1_.4), custom_call_target="tpu_custom_call" | custom-call | bytes 39321600 | tf_op jit(solution)/shard_map/pallas_call | solution.py:466
  29.7 0.0 slice-start
  29.7 0.0 slice-start.1
  29.8 0.0 all-gather.3.cloned.1.call-update
  29.8 65.6 %shard_map.231 = (bf16[2048,2048]{1,0:T(8,128)(2,1)}, bf16[2048,512]{1,0:T(8,128)(2,1)}) custom-call(bf16[256,2048]{1,0:T(8,128)(2,1)} %bitcast.45, f32[1,2048]{1,0:T(1,128)} %bitcast.51, bf16[256,2048]{1,0:T(8,128)(2,1)} %refs_2_.1, bf16[256,1024]{1,0:T(8,128)(2,1)} %refs_3_.1, bf16[256,1024]{1,0:T(8,128)(2,1)} %refs_4_.1), custom_call_target="tpu_custom_call" | custom-call | bytes 157286400 | tf_op jit(solution)/shard_map/pallas_call | solution.py:466
  95.4 0.0 slice-done
  95.4 0.0 slice-done.1
  95.4 0.2 copy_bitcast_fusion
  95.6 0.0 copy-start.4
  95.6 1.5 pad_maximum_fusion
  97.1 3.6 all-to-all-start
  100.7 0.0 copy-done.4
  100.7 0.6 select_reduce_fusion
  101.4 27.2 %shard_map.232 = (bf16[2048,256]{1,0:T(8,128)(2,1)}, bf16[2,2048,128]{2,1,0:T(8,128)(2,1)}, bf16[2048,128]{1,0:T(8,128)(2,1)}, bf16[2048,128]{1,0:T(8,128)(2,1)}...) custom-call(s32[1,16]{1,0:T(1,128)} %holder_ref.1, bf16[2048,2048]{1,0:T(8,128)(2,1)} %get-tuple-element.129.rows_hbm.refs_2_, ...), custom_call_target="tpu_custom_call" | custom-call | flops 7516192768 | bytes 29360128 | tf_op jit(solution)/shard_map/pallas_call | solution.py:163
  128.5 45.8 %shard_map.233.refs_0_.refs_4_.refs_3_ = f32[256,2048]{1,0:T(8,128)} custom-call(bf16[2048,256]{1,0:T(8,128)(2,1)} %get-tuple-element.131.refs_0_.refs_2_, bf16[256,2048]{1,0:T(8,128)(2,1)} %refs_1_.7, bf16[256,2048]{1,0:T(8,128)(2,1)} %bitcast.46), custom_call_target="tpu_custom_call" | custom-call | flops 2147483648 | bytes 157286400 | tf_op jit(solution)/shard_map/pallas_call | solution.py:466
  174.3 0.0 all-to-all-done
  174.3 0.0 copy-start
  174.4 0.0 all-gather.3.cloned.1.call-done
  174.4 1.3 copy-done
  175.7 86.1 %shard_map.234 = (bf16[2048,2048]{1,0:T(8,128)(2,1)}, bf16[2048,1024]{1,0:T(8,128)(2,1)}, bf16[8,256,2048]{2,1,0:T(8,128)(2,1)}, bf16[2048,2048]{1,0:T(8,128)(2,1)}, bf16[4,256,2048]{2,1,0:T(8,128)(2,1)}) custom-call(f32[256,2048]{1,0:T(8,128)} %shard_map.233.refs_0_.refs_4_.refs_3_, f32[1,2048]{1,0:T(1,128)} %bitcast.69, bf16[256,2048]{1,0:T(8,128)(2,1)} %bitcast.65, ...), custom_call_target="tpu_custom_call" | custom-call | flops 34359738368 | bytes 314572800 | tf_op jit(solution)/shard_map/pallas_call | solution.py:466
  261.8 76.2 %shard_map.235 = (bf16[256,2048]{1,0:T(8,128)(2,1)}, bf16[8,256,2048]{2,1,0:T(8,128)(2,1)}, bf16[8,16,1024]{2,1,0:T(8,128)(2,1)}, bf16[8,16,1024]{2,1,0:T(8,128)...) custom-call(bf16[2048,1024]{1,0:T(8,128)(2,1)} %get-tuple-element.13, ...), custom_call_target="tpu_custom_call" | custom-call | flops 25769803776 | bytes 157286400 | tf_op jit(solution)/shard_map/pallas_call | solution.py:466
  338.1 69.8 %shard_map.236 = (f32[256,2048]{1,0:T(8,128)}, f32[1,2048]{1,0:T(1,128)}, bf16[8,16,1024]{2,1,0:T(8,128)(2,1)}, bf16[8,16,1024]{2,1,0:T(8,128)(2,1)}, bf16[8,16,...) custom-call(bf16[2048,2048]{1,0:T(8,128)(2,1)} %get-tuple-element.13, ...), custom_call_target="tpu_custom_call" | custom-call | flops 17179869184 | bytes 157286400 | tf_op jit(solution)/shard_map/pallas_call | solution.py:466
  407.9 54.7 %shard_map.237 = (bf16[2048,256]{1,0:T(8,128)(2,1)}, bf16[256,2048]{1,0:T(8,128)(2,1)}, bf16[8,16,1024]{2,1,0:T(8,128)(2,1)}, bf16[8,16,1024]{2,1,0:T(8,128)(2,1...) custom-call(f32[256,2048]{1,0:T(8,128)} %get-tuple-element.148.refs_, ...), custom_call_target="tpu_custom_call" | custom-call | flops 4294967296 | bytes 157286400 | tf_op jit(solution)/shard_map/pallas_call | solution.py:466
  462.6 2.3 shard_map.238.refs_0_
  464.9 40.0 %shard_map.239 = (bf16[2048,512]{1,0:T(8,128)(2,1)}, bf16[8,16,1024]{2,1,0:T(8,128)(2,1)}, bf16[8,16,1024]{2,1,0:T(8,128)(2,1)}, bf16[8,16,1024]{2,1,0:T(8,128)(...) custom-call(bf16[2048,256]{1,0:T(8,128)(2,1)} %shard_map.238.refs_0_, ...), custom_call_target="tpu_custom_call" | custom-call | flops 8589934592 | bytes 29360128 | tf_op jit(solution)/shard_map/pallas_call | solution.py:466
  505.0 3.1 shard_map.240.refs_0_
  508.1 0.0 copy-start.3
  508.1 51.6 %shard_map.241 = (bf16[256,2048]{1,0:T(8,128)(2,1)}, f32[1,2048]{1,0:T(1,128)}, bf16[8,256,512]{2,1,0:T(8,128)(2,1)}, bf16[8,16,1024]{2,1,0:T(8,128)(2,1)}, bf16...) custom-call(bf16[2048,512]{1,0:T(8,128)(2,1)} %shard_map.240.refs_0_, ...), custom_call_target="tpu_custom_call" | custom-call | flops 8589934592 | bytes 157286400 | tf_op jit(solution)/shard_map/pallas_call | solution.py:466
  559.7 0.0 copy-done.3
  559.7 0.7 maximum_bitcast_fusion
  560.4 0.6 pad.4.refs_1_
  561.1 156.8 %shard_map.242 = (bf16[256,8192]{1,0:T(8,128)(2,1)}, bf16[256,8192]{1,0:T(8,128)(2,1)}, bf16[2,8,32,2048]{3,2,1,0:T(8,128)(2,1)}, f32[8,256]{1,0:T(8,128)}, bf16...) custom-call(bf16[8,8,32,512]{3,2,1,0:T(8,128)(2,1)} %bitcast.43, ...), custom_call_target="tpu_custom_call" | custom-call | bytes 52428800 | tf_op jit(solution)/shard_map/pallas_call | solution.py:466
  717.9 1.3 fusion
  719.2 0.0 copy-start.1
  719.2 0.0 copy-start.2
  719.2 17.4 %shard_map.243 = (f32[8,32,2048]{2,1,0:T(8,128)}, f32[8,32,1024]{2,1,0:T(8,128)}, f32[8,32,1024]{2,1,0:T(8,128)}, f32[8,32,2048]{2,1,0:T(8,128)}, f32[8,32,8192]...) custom-call(bf16[8,16,1024]{2,1,0:T(8,128)(2,1)} %get-tuple-element.175.refs_0_, ...), custom_call_target="tpu_custom_call" | custom-call | bytes 47185920 | tf_op jit(solution)/shard_map/pallas_call | solution.py:1522
  736.6 0.0 copy-done.1
  736.6 1.0 copy.38
  737.6 0.0 copy-done.2
  737.6 1.0 copy.39
Async XLA Ops:
  7.2 167.2 %all-gather.3.cloned.1.call-start = ((), (), s32[]{:S(2)}) async-start(), calls=%async_computation.1 | async-start | bytes 7864320 | tf_op jit(solution)/shard_map/all_gather | solution.py:1606
  29.7 65.6 %slice-start = ((bf16[256,8192]{1,0:T(8,128)(2,1)}), bf16[64,8192]{1,0:T(8,128)(2,1)S(1)}, s32[]{:S(2)}) async-start(bf16[256,8192]{1,0:T(8,128)(2,1)} %refs_0_.1), calls=%async_computation.2 | async-start | bytes 2097152 | tf_op jit(solution)/shard_map/slice | solution.py:1611
  29.7 65.6 %slice-start.1 = ((bf16[256,8192]{1,0:T(8,128)(2,1)}), bf16[64,8192]{1,0:T(8,128)(2,1)S(1)}, s32[]{:S(2)}) async-start(bf16[256,8192]{1,0:T(8,128)(2,1)} %refs_1_.4), calls=%async_computation.3 | async-start | bytes 2097152 | tf_op jit(solution)/shard_map/slice | solution.py:1611
  95.6 5.1 copy-start.4
  97.1 77.2 %all-to-all-start = ((bf16[64,8,2048]{2,0,1:T(8,128)(2,1)}), bf16[64,8,2048]{2,0,1:T(8,128)(2,1)S(1)}, u32[]{:S(2)}, u32[]{:S(2)}) async-start(bf16[64,8,2048]{2,0,1:T(8,128)(2,1)} %pad_maximum_fusion), calls=%async_computation | async-start | bytes 4194304 | tf_op jit(solution)/shard_map/all_to_all | solution.py:1589
  174.3 1.3 copy-start
  508.1 51.6 %copy-start.3 = (f32[1,2048]{1,0:T(1,128)S(1)}, f32[1,2048]{1,0:T(1,128)}, u32[]{:S(2)}) copy-start(f32[1,2048]{1,0:T(1,128)} %get-tuple-element.193) | copy-start | bytes 24580
  719.2 17.4 %copy-start.1 = (bf16[256,2048]{1,0:T(8,128)(2,1)S(1)}, bf16[256,2048]{1,0:T(8,128)(2,1)}, u32[]{:S(2)}) copy-start(bf16[256,2048]{1,0:T(8,128)(2,1)} %get-tuple-element.139) | copy-start | bytes 3145732
  719.2 18.4 %copy-start.2 = (bf16[256,2048]{1,0:T(8,128)(2,1)S(1)}, bf16[256,2048]{1,0:T(8,128)(2,1)}, u32[]{:S(2)}) copy-start(bf16[256,2048]{1,0:T(8,128)(2,1)} %get-tuple-element.174) | copy-start | bytes 3145732
Sparse Core Ops, SparseCore 0:
  29.9 116.5 all-gather.2

commit v10 on v9

--- a/solution.py
+++ b/solution.py
@@ -493,9 +493,9 @@
 def attend_back_kernel(
     heads, block, ins, outs, scratch, line
 ):
-    grad_ref, out_ref, q_ref, k_ref, v_ref, lse_ref, cos_ref, sin_ref, piece_ref = ins
+    grad_ref, out_ref, q_ref, k_ref, v_ref, lse_ref, cos_ref, sin_ref, piece_ref, place_ref = ins
     (grad_qkv_ref,) = outs
-    grads, centers, grad_q = scratch
+    grads, centers, grad_q, placed = scratch
     if line.ticks:
         line.signal(pltpu.get_barrier_semaphore())
         line.greet(pltpu.get_barrier_semaphore(), 0)
@@ -505,8 +505,11 @@
 
     def take_block(i, _):
         rows = pl.ds(pl.multiple_of(i * block, block), block)
+        position = lax.broadcasted_iota(jnp.int32, (block, length), 0) + i * block
+        chosen = jnp.where(place_ref[...] == position, 1.0, 0.0).astype(bf16)
+        taken = matmul_f32(chosen, grad_ref[...]).astype(bf16)
         for h in range(heads):
-            grad = grad_ref[rows, h * HD : (h + 1) * HD].astype(bf16)
+            grad = taken[:, h * HD : (h + 1) * HD]
             grads[h, rows, :] = grad
             product = grad.astype(f32) * out_ref[rows, h * HD : (h + 1) * HD].astype(f32)
             centers[h, rows, :] = jnp.broadcast_to(
@@ -550,8 +553,8 @@
         )
         grad_key = grad_key * SCORE_SCALE
         grad_key = grad_key * cos_ref[cols, :] - pltpu.roll(grad_key, HD // 2, 1) * sin_ref[cols, :]
-        grad_qkv_ref[cols, heads * HD : (heads + 1) * HD] = grad_key.astype(bf16)
-        grad_qkv_ref[cols, (heads + 1) * HD :] = grad_value.astype(bf16)
+        placed[cols, heads * HD : (heads + 1) * HD] = grad_key.astype(bf16)
+        placed[cols, (heads + 1) * HD :] = grad_value.astype(bf16)
         return 0
 
     for j in range(min(2, blocks - 1)):
@@ -564,45 +567,33 @@
         for h in range(heads):
             grad = grad_q[h, rows, :] * SCORE_SCALE
             grad = grad * cos_ref[rows, :] - pltpu.roll(grad, HD // 2, 1) * sin_ref[rows, :]
-            grad_qkv_ref[rows, h * HD : (h + 1) * HD] = grad.astype(bf16)
+            placed[rows, h * HD : (h + 1) * HD] = grad.astype(bf16)
         return 0
 
     lax.fori_loop(0, blocks, turn_back, 0)
+    line.step()
+
+    def store_block(i, _):
+        rows = pl.ds(pl.multiple_of(i * block, block), block)
+        place = as_column(place_ref[0:1, rows].astype(f32)).astype(jnp.int32)
+        position = lax.broadcasted_iota(jnp.int32, (block, length), 1)
+        chosen = jnp.where(place == position, 1.0, 0.0).astype(bf16)
+        grad_qkv_ref[rows, :] = matmul_f32(chosen, placed[...]).astype(bf16)
+        return 0
+
+    lax.fori_loop(0, blocks, store_block, 0)
     line.end()
-
-
-def take_cuts_kernel(cuts, holder_ref, rows_ref, out_ref):
-    cut = out_ref.shape[0] // cuts
-
-    def one(p, _):
-        src = pl.ds(pl.multiple_of(holder_ref[0, p] * cut, cut), cut)
-        out_ref[pl.ds(pl.multiple_of(p * cut, cut), cut), :] = rows_ref[src, :]
-        return 0
-
-    lax.fori_loop(0, cuts, one, 0)
-
-
-def take_cuts(holder, rows):
-    return pl.pallas_call(
-        functools.partial(take_cuts_kernel, holder.shape[1]),
-        out_shape=jax.ShapeDtypeStruct(rows.shape, rows.dtype),
-        in_specs=[pl.BlockSpec(memory_space=pltpu.SMEM)] + vmem_specs(1),
-        out_specs=pl.BlockSpec(memory_space=pltpu.VMEM),
-        cost_estimate=pl.CostEstimate(
-            flops=0, bytes_accessed=2 * rows.size * rows.dtype.itemsize, transcendentals=0
-        ),
-    )(holder, rows)
 
 
 def attend_back(
     order, grad, out, query, key, value, lse, cosine, sine, piece, heads, **line
 ):
-    cuts = jnp.arange(order.shape[1], dtype=order.dtype)
-    holder = jnp.sum(jnp.where(order[0][None, :] == cuts[:, None], cuts[None, :], 0), 1)[None, :]
     length = grad.shape[0]
     block = min(512, length)
-    tall = [take_cuts(holder, grad), out, query, key, value, lse, cosine, sine, piece]
-    grad_qkv = run(
+    cut = length // order.shape[1]
+    place = (order.reshape(-1, 1) * cut + jnp.arange(cut, dtype=order.dtype)).reshape(1, length)
+    tall = [grad, out, query, key, value, lse, cosine, sine, piece, place]
+    return run(
         functools.partial(attend_back_kernel, heads, block),
         [(array, VMEM) for array in tall],
         [(jax.ShapeDtypeStruct((length, (heads + 2) * HD), bf16), VMEM)],
@@ -610,12 +601,12 @@
             pltpu.VMEM((heads, length, HD), bf16),
             pltpu.VMEM((heads, length, HD), f32),
             pltpu.VMEM((heads, length, HD), f32),
+            pltpu.VMEM((length, (heads + 2) * HD), bf16),
         ],
         line.pop("number", None),
         (8 * heads * length * length * HD, 14 * length * HD * heads * 4, heads * length * length // 2),
         **line,
     )[0]
-    return take_cuts(order, grad_qkv)
 
 
 def place_in_group():
@@ -1023,7 +1014,7 @@
         ],
         line.pop("number"),
         (64 * rows * width * inner, 300 * rows * width * 2, 8 * rows * inner),
-        vmem=61,
+        vmem=63,
         **line,
     )
 
@@ -1073,7 +1064,7 @@
 class WeightTerm:
     def __init__(self, rows_ref, columns_ref, term_ref, scratch):
         self.rows_ref, self.columns_ref, self.term_ref = rows_ref, columns_ref, term_ref
-        self.loaded, self.ready, self.sems = scratch
+        self.loaded, self.flipped, self.ready, self.sems = scratch
         self.tile = self.loaded.shape[2]
         for number in (0, 1):
             self.load(number).start()
@@ -1097,10 +1088,11 @@
                 self.store(number - 2).wait()
             width = self.columns_ref.shape[1]
             step = min(256, width)
+            self.flipped[...] = self.loaded[at].T
 
             def column(t, _):
                 cols = pl.ds(pl.multiple_of(t * step, step), step)
-                term = over_tokens(self.loaded[at], self.columns_ref[:, cols])
+                term = matmul_f32(self.flipped[...], self.columns_ref[:, cols])
                 self.ready[at, :, cols] = term.astype(bf16)
                 return 0
 
@@ -1133,10 +1125,10 @@
     if extra:
         columns_ref = a_ref
         if extra == "loaded":
-            columns_ref = scratch[12]
-            columns_copy = pltpu.make_async_copy(ins[3], columns_ref, scratch[13].at[0])
+            columns_ref = scratch[13]
+            columns_copy = pltpu.make_async_copy(ins[3], columns_ref, scratch[14].at[0])
             columns_copy.start()
-        term = WeightTerm(ins[2], columns_ref, outs[-1], scratch[9:12])
+        term = WeightTerm(ins[2], columns_ref, outs[-1], scratch[9:13])
     for one in loading:
         one.wait()
     own_at = pl.multiple_of(core * rows, rows)
@@ -1293,6 +1285,7 @@
         outs.append((jax.ShapeDtypeStruct((8, tall, columns.shape[1]), bf16), ANY))
         scratch += [
             pltpu.VMEM((2, length, tall), bf16),
+            pltpu.VMEM((tall, length), bf16),
             pltpu.VMEM((2, tall, columns.shape[1]), bf16),
             pltpu.SemaphoreType.DMA((2, 2)),
         ]
@@ -1669,7 +1662,7 @@
 
         result, terms["gate_up"] = product_scattered(
             hidden, w_down, False, extra=(normed_two, grad_gate_up), base=mid, dtype=bf16,
-            steps={"x": 1, "y": 1, "work": 1, "relayed": 1, "work2": 1, "work3": 2}, **line(5, 10),
+            steps={"x": 1, "y": 1, "work": 1, "relayed": 1, "sibling": 1, "work2": 1, "work3": 1}, **line(5, 10),
         )
         grad_mid, gain_ffn_term = product_scattered(
             grad_gate_up, cols_gate_up, True, back=(grad_out, mid, ffn_gain),
@@ -1677,7 +1670,7 @@
         )
         grad_attended, out_term = attended_back(grad_mid, w_out, attended, **line(7, 8))
         terms["out"] = out_term.reshape(8, OUT // 2 * high, model_width)
-        grad_qkv = back_through_attention(grad_attended, **line(8, 6))
+        grad_qkv = back_through_attention(grad_attended, **line(8, 7))
         grad_x, gain_attn_term, qkv_term = product_scattered(
             grad_qkv, cols_qkv, True, extra=(normed_one, None), dtype=bf16,
             back=(grad_mid, x_rows, attn_gain),

time: 756 us -> 746 us (0.987)
  Pallas kernels: 719 us -> 710 us
where the time goes in v10:
time: 746 us; the launch traced here: 736 us
  Pallas kernels  710 us (95%)
  between operations  14.4 us (2%)
    pallas_call x10, Pallas kernels, run(): pl.pallas_call(body, out_shape=tuple((shape for shape, _ in outs)), in_sp...  665 us
    pallas_call x1, Pallas kernels, attend(): pl.pallas_call(functools.partial(attend_kernel, heads, order.shape[1], bl...  27.2 us
    pallas_call x1, Pallas kernels, finish(): pl.pallas_call(functools.partial(finish_kernel, heads), out_shape=tuple(s...  17.4 us
  transfers between devices with their start and end apart: 2, of which 0 were waited for; matrix products, arithmetic and copies ran while one was open for 0% of the time, Pallas kernels for 19%

profile of v10, /device:TPU:0, one launch (start us, length us, event | category | flops | bytes accessed | tf_op | source)
XLA Modules:
  0.0 735.5 jit_solution(2287652570981374211)
XLA Ops:
  7.2 0.0 all-gather.3.cloned.1.call-start
  7.2 22.5 %shard_map.230 = bf16[8,48,2048]{2,1,0:T(8,128)(2,1)} custom-call(bf16[256,8192]{1,0:T(8,128)(2,1)} %refs_0_.1, bf16[256,8192]{1,0:T(8,128)(2,1)} %refs_1_.4), custom_call_target="tpu_custom_call" | custom-call | bytes 39321600 | tf_op jit(solution)/shard_map/pallas_call | solution.py:466
  29.7 0.0 slice-start
  29.7 0.0 slice-start.1
  29.8 0.0 all-gather.3.cloned.1.call-update
  29.8 65.6 %shard_map.231 = (bf16[2048,2048]{1,0:T(8,128)(2,1)}, bf16[2048,512]{1,0:T(8,128)(2,1)}) custom-call(bf16[256,2048]{1,0:T(8,128)(2,1)} %bitcast.45, f32[1,2048]{1,0:T(1,128)} %bitcast.51, bf16[256,2048]{1,0:T(8,128)(2,1)} %refs_2_.1, bf16[256,1024]{1,0:T(8,128)(2,1)} %refs_3_.1, bf16[256,1024]{1,0:T(8,128)(2,1)} %refs_4_.1), custom_call_target="tpu_custom_call" | custom-call | bytes 157286400 | tf_op jit(solution)/shard_map/pallas_call | solution.py:466
  95.4 0.0 slice-done
  95.4 0.0 slice-done.1
  95.4 0.2 copy_bitcast_fusion
  95.6 1.5 pad_maximum_fusion
  97.1 4.4 all-to-all-start
  101.5 27.2 %shard_map.232 = (bf16[2048,256]{1,0:T(8,128)(2,1)}, bf16[2,2048,128]{2,1,0:T(8,128)(2,1)}, bf16[2048,128]{1,0:T(8,128)(2,1)}, bf16[2048,128]{1,0:T(8,128)(2,1)}...) custom-call(s32[1,16]{1,0:T(1,128)} %order_ref.1, bf16[2048,2048]{1,0:T(8,128)(2,1)} %get-tuple-element.130.rows_hbm.refs_2_, ...), custom_call_target="tpu_custom_call" | custom-call | flops 7516192768 | bytes 29360128 | tf_op jit(solution)/shard_map/pallas_call | solution.py:163
  128.6 0.0 copy-start.3
  128.6 45.8 %shard_map.233.refs_0_.refs_4_.refs_3_ = f32[256,2048]{1,0:T(8,128)} custom-call(bf16[2048,256]{1,0:T(8,128)(2,1)} %get-tuple-element.132.refs_0_.refs_2_, bf16[256,2048]{1,0:T(8,128)(2,1)} %refs_1_.7, bf16[256,2048]{1,0:T(8,128)(2,1)} %bitcast.46), custom_call_target="tpu_custom_call" | custom-call | flops 2147483648 | bytes 157286400 | tf_op jit(solution)/shard_map/pallas_call | solution.py:466
  174.4 0.0 copy-done.3
  174.4 0.7 iota_add_fusion
  175.1 0.0 all-to-all-done
  175.1 0.0 all-gather.3.cloned.1.call-done
  175.1 86.1 %shard_map.234 = (bf16[2048,2048]{1,0:T(8,128)(2,1)}, bf16[2048,1024]{1,0:T(8,128)(2,1)}, bf16[8,256,2048]{2,1,0:T(8,128)(2,1)}, bf16[2048,2048]{1,0:T(8,128)(2,1)}, bf16[4,256,2048]{2,1,0:T(8,128)(2,1)}) custom-call(f32[256,2048]{1,0:T(8,128)} %shard_map.233.refs_0_.refs_4_.refs_3_, f32[1,2048]{1,0:T(1,128)} %bitcast.68, bf16[256,2048]{1,0:T(8,128)(2,1)} %bitcast.64, ...), custom_call_target="tpu_custom_call" | custom-call | flops 34359738368 | bytes 314572800 | tf_op jit(solution)/shard_map/pallas_call | solution.py:466
  261.2 71.7 %shard_map.235 = (bf16[256,2048]{1,0:T(8,128)(2,1)}, bf16[8,256,2048]{2,1,0:T(8,128)(2,1)}, bf16[8,16,1024]{2,1,0:T(8,128)(2,1)}, bf16[8,16,1024]{2,1,0:T(8,128)...) custom-call(bf16[2048,1024]{1,0:T(8,128)(2,1)} %get-tuple-element.13, ...), custom_call_target="tpu_custom_call" | custom-call | flops 25769803776 | bytes 157286400 | tf_op jit(solution)/shard_map/pallas_call | solution.py:466
  332.9 69.9 %shard_map.236 = (f32[256,2048]{1,0:T(8,128)}, f32[1,2048]{1,0:T(1,128)}, bf16[8,16,1024]{2,1,0:T(8,128)(2,1)}, bf16[8,16,1024]{2,1,0:T(8,128)(2,1)}, bf16[8,16,...) custom-call(bf16[2048,2048]{1,0:T(8,128)(2,1)} %get-tuple-element.13, ...), custom_call_target="tpu_custom_call" | custom-call | flops 17179869184 | bytes 157286400 | tf_op jit(solution)/shard_map/pallas_call | solution.py:466
  402.8 53.7 %shard_map.237 = (bf16[2048,256]{1,0:T(8,128)(2,1)}, bf16[256,2048]{1,0:T(8,128)(2,1)}, bf16[8,16,1024]{2,1,0:T(8,128)(2,1)}, bf16[8,16,1024]{2,1,0:T(8,128)(2,1...) custom-call(f32[256,2048]{1,0:T(8,128)} %get-tuple-element.149.refs_, ...), custom_call_target="tpu_custom_call" | custom-call | flops 4294967296 | bytes 157286400 | tf_op jit(solution)/shard_map/pallas_call | solution.py:466
  456.5 46.2 %shard_map.238 = (bf16[2048,512]{1,0:T(8,128)(2,1)}, bf16[8,16,1024]{2,1,0:T(8,128)(2,1)}, bf16[8,16,1024]{2,1,0:T(8,128)(2,1)}, bf16[8,16,1024]{2,1,0:T(8,128)(...) custom-call(bf16[2048,256]{1,0:T(8,128)(2,1)} %get-tuple-element.156, ...), custom_call_target="tpu_custom_call" | custom-call | flops 8589934592 | bytes 29360128 | tf_op jit(solution)/shard_map/pallas_call | solution.py:466
  502.7 0.0 copy-start.2
  502.8 52.4 %shard_map.239 = (bf16[256,2048]{1,0:T(8,128)(2,1)}, f32[1,2048]{1,0:T(1,128)}, bf16[8,256,512]{2,1,0:T(8,128)(2,1)}, bf16[8,16,1024]{2,1,0:T(8,128)(2,1)}, bf16...) custom-call(bf16[2048,512]{1,0:T(8,128)(2,1)} %get-tuple-element.168, ...), custom_call_target="tpu_custom_call" | custom-call | flops 8589934592 | bytes 157286400 | tf_op jit(solution)/shard_map/pallas_call | solution.py:466
  555.1 0.0 copy-done.2
  555.1 0.7 maximum_bitcast_fusion
  555.9 0.6 pad.4.refs_1_
  556.5 151.3 %shard_map.240 = (bf16[256,8192]{1,0:T(8,128)(2,1)}, bf16[256,8192]{1,0:T(8,128)(2,1)}, bf16[2,8,32,2048]{3,2,1,0:T(8,128)(2,1)}, f32[8,256]{1,0:T(8,128)}, bf16...) custom-call(bf16[8,8,32,512]{3,2,1,0:T(8,128)(2,1)} %bitcast.44, ...), custom_call_target="tpu_custom_call" | custom-call | bytes 52428800 | tf_op jit(solution)/shard_map/pallas_call | solution.py:466
  707.8 1.3 fusion
  709.1 0.0 copy-start
  709.1 0.0 copy-start.1
  709.1 17.4 %shard_map.241 = (f32[8,32,2048]{2,1,0:T(8,128)}, f32[8,32,1024]{2,1,0:T(8,128)}, f32[8,32,1024]{2,1,0:T(8,128)}, f32[8,32,2048]{2,1,0:T(8,128)}, f32[8,32,8192]...) custom-call(bf16[8,16,1024]{2,1,0:T(8,128)(2,1)} %get-tuple-element.176.refs_0_, ...), custom_call_target="tpu_custom_call" | custom-call | bytes 47185920 | tf_op jit(solution)/shard_map/pallas_call | solution.py:1515
  726.5 0.0 copy-done
  726.5 1.0 copy.36
  727.5 0.0 copy-done.1
  727.5 1.0 copy.37
  (1 shorter events, 0.0 us)
Async XLA Ops:
  7.2 167.9 %all-gather.3.cloned.1.call-start = ((), (), s32[]{:S(2)}) async-start(), calls=%async_computation.1 | async-start | bytes 7864320 | tf_op jit(solution)/shard_map/all_gather | solution.py:1599
  29.7 65.6 %slice-start = ((bf16[256,8192]{1,0:T(8,128)(2,1)}), bf16[64,8192]{1,0:T(8,128)(2,1)S(1)}, s32[]{:S(2)}) async-start(bf16[256,8192]{1,0:T(8,128)(2,1)} %refs_0_.1), calls=%async_computation.2 | async-start | bytes 2097152 | tf_op jit(solution)/shard_map/slice | solution.py:1604
  29.7 65.6 %slice-start.1 = ((bf16[256,8192]{1,0:T(8,128)(2,1)}), bf16[64,8192]{1,0:T(8,128)(2,1)S(1)}, s32[]{:S(2)}) async-start(bf16[256,8192]{1,0:T(8,128)(2,1)} %refs_1_.4), calls=%async_computation.3 | async-start | bytes 2097152 | tf_op jit(solution)/shard_map/slice | solution.py:1604
  97.1 78.0 %all-to-all-start = ((bf16[64,8,2048]{2,0,1:T(8,128)(2,1)}), bf16[64,8,2048]{2,0,1:T(8,128)(2,1)}, u32[]{:S(2)}, u32[]{:S(2)}) async-start(bf16[64,8,2048]{2,0,1:T(8,128)(2,1)} %pad_maximum_fusion), calls=%async_computation | async-start | bytes 4194304 | tf_op jit(solution)/shard_map/all_to_all | solution.py:1582
  128.6 45.8 %copy-start.3 = (s32[1,16]{1,0:T(1,128)S(1)}, s32[1,16]{1,0:T(1,128)}, u32[]{:S(2)}) copy-start(s32[1,16]{1,0:T(1,128)} %order_ref.1) | copy-start | bytes 196
  502.7 52.4 %copy-start.2 = (f32[1,2048]{1,0:T(1,128)S(1)}, f32[1,2048]{1,0:T(1,128)}, u32[]{:S(2)}) copy-start(f32[1,2048]{1,0:T(1,128)} %get-tuple-element.194) | copy-start | bytes 24580
  709.1 17.4 %copy-start = (bf16[256,2048]{1,0:T(8,128)(2,1)S(1)}, bf16[256,2048]{1,0:T(8,128)(2,1)}, u32[]{:S(2)}) copy-start(bf16[256,2048]{1,0:T(8,128)(2,1)} %get-tuple-element.140) | copy-start | bytes 3145732
  709.1 18.4 %copy-start.1 = (bf16[256,2048]{1,0:T(8,128)(2,1)S(1)}, bf16[256,2048]{1,0:T(8,128)(2,1)}, u32[]{:S(2)}) copy-start(bf16[256,2048]{1,0:T(8,128)(2,1)} %get-tuple-element.175) | copy-start | bytes 3145732
Sparse Core Ops, SparseCore 0:
  29.9 116.5 all-gather.2

commit v11 on v10

--- a/solution.py
+++ b/solution.py
@@ -1106,34 +1106,58 @@
             self.store(number).wait()
 
 
-def scatter_kernel(turned, tile, extra, after, steps, ins, outs, scratch, line):
+UNITS = (
+    (ACROSS, 0), (ACROSS, 1), (ALONG_X, 0), (ALONG_Y, 1), (ALONG_X, 1), (ALONG_Y, 0),
+    (SIBLING, 0), (SIBLING, 1),
+)
+
+
+def scatter_kernel(turned, extra, after, steps, ins, outs, scratch, line):
     out_ref = outs[0] if after == "base" else scratch[-4]
     finals = ins[len(ins) - {"base": 1, "cast": 1, "back": 3}[after] :]
-    part, to_s, from_s, to_chip, held, relay, last, sends, recvs = scratch[:9]
-    a_ref, b_ref, loads = scratch[-3:]
-    loading = [
-        pltpu.make_async_copy(src, dst, loads.at[number])
-        for number, (src, dst) in enumerate(((ins[1], b_ref), (ins[0], a_ref)))
-    ]
-    for one in loading:
-        one.start()
+    part, to_s, from_s, to_link, relay, last, sends, recvs = scratch[:8]
+    a_ref, b_ref, load_sems = scratch[-3:]
     rows, width = out_ref.shape
-    half = rows // 2
+    half = width // 2
     _, _, core = place_in_group()
+    loading = {}
+
+    def load(name, src, dst):
+        loading[name] = pltpu.make_async_copy(src, dst, load_sems.at[len(loading)])
+        loading[name].start()
+
+    def load_weight(h):
+        where = (slice(h * half, (h + 1) * half), slice(None))
+        where = where if turned else where[::-1]
+        load(h, ins[1].at[where], b_ref.at[where])
+
+    def load_rows(chip):
+        where = chip_rows(*chip, rows)
+        load(chip, ins[0].at[where, :], a_ref.at[where, :])
+
+    load_weight(0)
+    load_rows(ACROSS)
+    load_weight(1)
+    for chip in (ALONG_X, ALONG_Y, SIBLING):
+        load_rows(chip)
     greet_group(line)
     line.start()
     if extra:
         columns_ref = a_ref
         if extra == "loaded":
-            columns_ref = scratch[13]
-            columns_copy = pltpu.make_async_copy(ins[3], columns_ref, scratch[14].at[0])
-            columns_copy.start()
-        term = WeightTerm(ins[2], columns_ref, outs[-1], scratch[9:13])
-    for one in loading:
-        one.wait()
+            columns_ref = scratch[12]
+            load("columns", ins[3], columns_ref)
+        term = WeightTerm(ins[2], columns_ref, outs[-1], scratch[8:12])
     own_at = pl.multiple_of(core * rows, rows)
     other_at = pl.multiple_of((1 - core) * rows, rows)
+    to_sib, to_x, to_y = (0, 0, 1), (0, 1, 0), (1, 0, 0)
     started = []
+
+    def ready(*names):
+        for name in names:
+            if name in loading:
+                loading.pop(name).wait()
+                loading[name, "done"] = None
 
     def send(number, src, dst, target):
         one = pltpu.make_async_remote_copy(
@@ -1142,7 +1166,6 @@
         )
         one.start()
         started.append(one)
-        return one
 
     def landed(number, where):
         pltpu.make_async_remote_copy(
@@ -1150,84 +1173,76 @@
             device_id={"grp": other(0, 0, 1)}, device_id_type=MESH,
         ).wait_recv()
 
-    to_sib, to_x, to_y = (0, 0, 1), (0, 1, 0), (1, 0, 0)
-
-    def make(number, chip):
-        where = chip_rows(*chip, rows)
-
-        def column(t, _):
-            cols = pl.ds(pl.multiple_of(t * tile, tile), tile)
-            lhs = a_ref[where, :]
-            if turned:
-                part[:, cols] = against_rows(lhs, b_ref[cols, :])
+    def make(n):
+        chip, h = UNITS[n]
+        ready(h, chip)
+        lhs = a_ref[chip_rows(*chip, rows), :]
+        cols = slice(h * half, (h + 1) * half)
+        if turned:
+            part[n % 2] = against_rows(lhs, b_ref[cols, :])
+        else:
+            part[n % 2] = matmul_f32(lhs, b_ref[:, cols])
+        to_s[n] = part[n % 2, pl.ds(other_at, rows), :].astype(bf16)
+        send(n, to_s.at[n], from_s.at[n], to_sib)
+
+    def own(n):
+        landed(n, from_s.at[n])
+        return part[n % 2, pl.ds(own_at, rows), :] + from_s[n].astype(f32)
+
+    def finish(n):
+        _, h = UNITS[n]
+        if n < 2:
+            to_link[n] = own(n).astype(bf16)
+            send(8 + n, to_link.at[n], relay.at[n], (to_x, to_y)[n])
+        elif n < 4:
+            to_link[n] = own(n).astype(bf16)
+            send(8 + n, to_link.at[n], last.at[(None, None, 0, 3)[n]], (to_x, to_y)[n - 2])
+        elif n < 6:
+            total = own(n)
+            landed(8 + h, relay.at[h])
+            to_link[n] = (total + relay[h].astype(f32)).astype(bf16)
+            send(8 + n, to_link.at[n], last.at[(1, 2)[n - 4]], (to_x, to_y)[n - 4])
+        else:
+            cols = slice(h * half, (h + 1) * half)
+            if after == "back":
+                out_ref[:, cols] = own(n)
             else:
-                part[:, cols] = matmul_f32(lhs, b_ref[:, cols])
-            return 0
-
-        lax.fori_loop(0, width // tile, column, 0)
-        to_s[number] = part[pl.ds(other_at, rows), :].astype(bf16)
-        send(number, to_s.at[number], from_s.at[number], to_sib)
-
-    def own(low, number):
-        at = pl.ds(pl.multiple_of(core * rows + low * half, half), half)
-        return part[at, :] + from_s[number, low * half : (low + 1) * half, :].astype(f32)
-
-    first, second = slice(0, half), slice(half, rows)
-    step = lambda point: line.step(steps.get(point, 0))
-    make(0, ACROSS)
-    landed(0, from_s.at[0])
-    to_chip[0, first, :] = own(0, 0).astype(bf16)
-    send(4, to_chip.at[0, first, :], relay.at[0], to_x)
-    to_chip[0, second, :] = own(1, 0).astype(bf16)
-    send(5, to_chip.at[0, second, :], relay.at[1], to_y)
-    step("across")
-    make(1, ALONG_X)
-    landed(1, from_s.at[1])
-    to_chip[1, first, :] = own(0, 1).astype(bf16)
-    send(6, to_chip.at[1, first, :], last.at[0, first, :], to_x)
-    held[0] = own(1, 1)
-    step("x")
-    make(2, ALONG_Y)
-    landed(2, from_s.at[2])
-    to_chip[2, second, :] = own(1, 2).astype(bf16)
-    send(7, to_chip.at[2, second, :], last.at[1, second, :], to_y)
-    held[1] = own(0, 2)
-    step("y")
-    if extra:
-        if extra == "loaded":
-            columns_copy.wait()
-        term.work((0, 1, 2))
-        step("work")
-    landed(5, relay.at[1])
-    to_chip[1, second, :] = (held[0] + relay[1].astype(f32)).astype(bf16)
-    send(8, to_chip.at[1, second, :], last.at[0, second, :], to_x)
-    landed(4, relay.at[0])
-    to_chip[2, first, :] = (held[1] + relay[0].astype(f32)).astype(bf16)
-    send(9, to_chip.at[2, first, :], last.at[1, first, :], to_y)
-    step("relayed")
-    make(3, SIBLING)
-    step("sibling")
-    if extra:
-        term.work((3, 4))
-        step("work2")
-        term.work((5, 6, 7))
-        step("work3")
-    landed(3, from_s.at[3])
-    for low in (0, 1):
-        at = slice(low * half, (low + 1) * half)
-        if after == "back":
-            out_ref[at, :] = own(low, 3)
-        else:
-            out_ref[at, :] = own(low, 3) + finals[0][at, :].astype(f32)
-    landed(6, last.at[0, first, :])
-    out_ref[first, :] += last[0, first, :].astype(f32)
-    landed(7, last.at[1, second, :])
-    out_ref[second, :] += last[1, second, :].astype(f32)
-    step("halves")
-    landed(8, last.at[0, second, :])
-    out_ref[second, :] += last[0, second, :].astype(f32)
-    landed(9, last.at[1, first, :])
-    out_ref[first, :] += last[1, first, :].astype(f32)
+                out_ref[:, cols] = own(n) + finals[0][:, cols].astype(f32)
+        line.step(steps.get(n, 0))
+
+    def work(numbers, point):
+        if extra:
+            ready("columns")
+            if columns_ref is a_ref:
+                ready(*(chip for chip, _ in UNITS))
+            term.work(numbers)
+        line.step(steps.get(point, 0))
+
+    make(0)
+    make(1)
+    finish(0)
+    make(2)
+    finish(1)
+    make(3)
+    finish(2)
+    make(4)
+    finish(3)
+    make(5)
+    work((0, 1), "early")
+    finish(4)
+    make(6)
+    finish(5)
+    make(7)
+    finish(6)
+    finish(7)
+    work((2, 3), "late")
+    work((4, 5), "later")
+    work((6, 7), "latest")
+    for number, slot, h in ((10, 0, 0), (11, 3, 1), (12, 1, 1), (13, 2, 0)):
+        cols = slice(h * half, (h + 1) * half)
+        landed(number, last.at[slot])
+        out_ref[:, cols] += last[slot].astype(f32)
+        line.step(steps.get(number, 0))
     if after == "cast":
         outs[0][...] = out_ref[...].astype(outs[0].dtype)
     if after == "back":
@@ -1238,11 +1253,11 @@
             at = pl.ds(pl.multiple_of(number * some, some), some)
             values, incoming = rows_ref[at, :].astype(f32), out_ref[at, :]
             inv = lax.rsqrt(jnp.mean(values * values, -1, keepdims=True) + EPS)
-            grad, term = norm_back(
+            grad, gain_part = norm_back(
                 upstream_ref[at, :].astype(f32), incoming, values * inv, inv, gain_ref[...]
             )
             outs[0][at, :] = grad.astype(outs[0].dtype)
-            return gain_term + term[None, :]
+            return gain_term + gain_part[None, :]
 
         outs[1][...] = lax.fori_loop(0, rows // some, norm_rows, jnp.zeros((1, width), f32))
     for one in started:
@@ -1258,22 +1273,21 @@
     length, depth = a.shape
     width = b.shape[0] if turned else b.shape[1]
     rows = length // 8
-    tile = min(256, width)
     ins = [(a, ANY), (b, ANY)]
     outs = [(jax.ShapeDtypeStruct((rows, width), dtype), VMEM)]
     after = "back" if back else "base" if dtype == f32 else "cast"
     if back:
         outs.append((jax.ShapeDtypeStruct((1, width), f32), VMEM))
+    piece = (rows, width // 2)
     scratch = [
-        pltpu.VMEM((2 * rows, width), f32),
-        pltpu.VMEM((4, rows, width), bf16),
-        pltpu.VMEM((4, rows, width), bf16),
-        pltpu.VMEM((3, rows, width), bf16),
-        pltpu.VMEM((2, rows // 2, width), f32),
-        pltpu.VMEM((2, rows // 2, width), bf16),
-        pltpu.VMEM((2, rows, width), bf16),
-        pltpu.SemaphoreType.DMA((10,)),
-        pltpu.SemaphoreType.DMA((10,)),
+        pltpu.VMEM((2, 2 * rows, width // 2), f32),
+        pltpu.VMEM((8,) + piece, bf16),
+        pltpu.VMEM((8,) + piece, bf16),
+        pltpu.VMEM((6,) + piece, bf16),
+        pltpu.VMEM((2,) + piece, bf16),
+        pltpu.VMEM((4,) + piece, bf16),
+        pltpu.SemaphoreType.DMA((14,)),
+        pltpu.SemaphoreType.DMA((14,)),
     ]
     flops, kind = 2 * length * depth * width, None
     if extra:
@@ -1291,16 +1305,16 @@
         ]
         if second is not None:
             ins.append((second, ANY))
-            scratch += [pltpu.VMEM(second.shape, bf16), pltpu.SemaphoreType.DMA((1,))]
+            scratch.append(pltpu.VMEM(second.shape, bf16))
         flops += 2 * length * first.shape[1] * columns.shape[1]
     ins += [(array, VMEM) for array in (back or (base,))]
     if after != "base":
         scratch.append(pltpu.VMEM((rows, width), f32))
     scratch += [
-        pltpu.VMEM(a.shape, bf16), pltpu.VMEM(b.shape, bf16), pltpu.SemaphoreType.DMA((2,))
+        pltpu.VMEM(a.shape, bf16), pltpu.VMEM(b.shape, bf16), pltpu.SemaphoreType.DMA((7,))
     ]
     return run(
-        functools.partial(scatter_kernel, turned, tile, kind, after, steps or {}), ins, outs, scratch,
+        functools.partial(scatter_kernel, turned, kind, after, steps or {}), ins, outs, scratch,
         line.pop("number"), (flops, 150 * rows * width * 2, 0), vmem=61, **line,
     )
 
@@ -1662,11 +1676,11 @@
 
         result, terms["gate_up"] = product_scattered(
             hidden, w_down, False, extra=(normed_two, grad_gate_up), base=mid, dtype=bf16,
-            steps={"x": 1, "y": 1, "work": 1, "relayed": 1, "sibling": 1, "work2": 1, "work3": 1}, **line(5, 10),
+            steps={1: 1, 3: 1, "early": 1, 7: 1, "late": 1, "later": 1, "latest": 1}, **line(5, 9),
         )
         grad_mid, gain_ffn_term = product_scattered(
             grad_gate_up, cols_gate_up, True, back=(grad_out, mid, ffn_gain),
-            steps={"across": 1, "x": 1, "y": 1, "relayed": 1, "sibling": 1, "halves": 1}, **line(6, 10),
+            steps={0: 1, 2: 1, 3: 1, 4: 1, 5: 1, 7: 1, 12: 1}, **line(6, 10),
         )
         grad_attended, out_term = attended_back(grad_mid, w_out, attended, **line(7, 8))
         terms["out"] = out_term.reshape(8, OUT // 2 * high, model_width)
@@ -1674,7 +1688,7 @@
         grad_x, gain_attn_term, qkv_term = product_scattered(
             grad_qkv, cols_qkv, True, extra=(normed_one, None), dtype=bf16,
             back=(grad_mid, x_rows, attn_gain),
-            steps={"y": 1, "work": 1, "relayed": 2, "work2": 1, "work3": 1}, **line(9, 8),
+            steps={3: 1, "early": 1, 5: 1, "late": 1, "latest": 1}, **line(9, 8),
         )
         gains = jnp.stack([gain_attn_term, gain_ffn_term]).reshape(2, groups, rows_here)
         gains = jnp.pad(jnp.moveaxis(gains, 0, 1), ((0, 0), (0, 6), (0, 0)))

time: 746 us -> 735 us (0.985)
  Pallas kernels: 710 us -> 699 us
    pallas_call x10, Pallas kernels: 665 us -> 654 us  [run(): pl.pallas_call(body, out_shape=tuple((shape for shape, _ in outs)), in_sp...]
where the time goes in v11:
time: 735 us; the launch traced here: 725 us
  Pallas kernels  699 us (95%)
  between operations  14.7 us (2%)
    pallas_call x10, Pallas kernels, run(): pl.pallas_call(body, out_shape=tuple((shape for shape, _ in outs)), in_sp...  654 us
    pallas_call x1, Pallas kernels, attend(): pl.pallas_call(functools.partial(attend_kernel, heads, order.shape[1], bl...  27.2 us
    pallas_call x1, Pallas kernels, finish(): pl.pallas_call(functools.partial(finish_kernel, heads), out_shape=tuple(s...  17.4 us
  transfers between devices with their start and end apart: 2, of which 0 were waited for; matrix products, arithmetic and copies ran while one was open for 0% of the time, Pallas kernels for 19%

profile of v11, /device:TPU:0, one launch (start us, length us, event | category | flops | bytes accessed | tf_op | source)
XLA Modules:
  0.0 725.1 jit_solution(16300532064158592103)
XLA Ops:
  7.2 0.0 all-gather.3.cloned.1.call-start
  7.2 22.5 %shard_map.230 = bf16[8,48,2048]{2,1,0:T(8,128)(2,1)} custom-call(bf16[256,8192]{1,0:T(8,128)(2,1)} %refs_0_.1, bf16[256,8192]{1,0:T(8,128)(2,1)} %refs_1_.4), custom_call_target="tpu_custom_call" | custom-call | bytes 39321600 | tf_op jit(solution)/shard_map/pallas_call | solution.py:466
  29.7 0.0 slice-start
  29.7 0.0 slice-start.1
  29.8 0.0 all-gather.3.cloned.1.call-update
  29.8 65.6 %shard_map.231 = (bf16[2048,2048]{1,0:T(8,128)(2,1)}, bf16[2048,512]{1,0:T(8,128)(2,1)}) custom-call(bf16[256,2048]{1,0:T(8,128)(2,1)} %bitcast.45, f32[1,2048]{1,0:T(1,128)} %bitcast.51, bf16[256,2048]{1,0:T(8,128)(2,1)} %refs_2_.1, bf16[256,1024]{1,0:T(8,128)(2,1)} %refs_3_.1, bf16[256,1024]{1,0:T(8,128)(2,1)} %refs_4_.1), custom_call_target="tpu_custom_call" | custom-call | bytes 157286400 | tf_op jit(solution)/shard_map/pallas_call | solution.py:466
  95.4 0.0 slice-done
  95.4 0.0 slice-done.1
  95.4 0.2 copy_bitcast_fusion
  95.6 1.5 pad_maximum_fusion
  97.1 4.4 all-to-all-start
  101.5 27.2 %shard_map.232 = (bf16[2048,256]{1,0:T(8,128)(2,1)}, bf16[2,2048,128]{2,1,0:T(8,128)(2,1)}, bf16[2048,128]{1,0:T(8,128)(2,1)}, bf16[2048,128]{1,0:T(8,128)(2,1)}...) custom-call(s32[1,16]{1,0:T(1,128)} %order_ref.1, bf16[2048,2048]{1,0:T(8,128)(2,1)} %get-tuple-element.129.rows_hbm.refs_2_, ...), custom_call_target="tpu_custom_call" | custom-call | flops 7516192768 | bytes 29360128 | tf_op jit(solution)/shard_map/pallas_call | solution.py:163
  128.6 0.0 copy-start.3
  128.6 44.3 %shard_map.233.refs_0_.refs_4_.refs_3_ = f32[256,2048]{1,0:T(8,128)} custom-call(bf16[2048,256]{1,0:T(8,128)(2,1)} %get-tuple-element.131.refs_0_.refs_2_, bf16[256,2048]{1,0:T(8,128)(2,1)} %refs_1_.7, bf16[256,2048]{1,0:T(8,128)(2,1)} %bitcast.46), custom_call_target="tpu_custom_call" | custom-call | flops 2147483648 | bytes 157286400 | tf_op jit(solution)/shard_map/pallas_call | solution.py:466
  173.0 0.0 copy-done.3
  173.0 0.7 iota_add_fusion
  173.7 0.0 all-to-all-done
  173.7 0.0 all-gather.3.cloned.1.call-done
  173.7 86.0 %shard_map.234 = (bf16[2048,2048]{1,0:T(8,128)(2,1)}, bf16[2048,1024]{1,0:T(8,128)(2,1)}, bf16[8,256,2048]{2,1,0:T(8,128)(2,1)}, bf16[2048,2048]{1,0:T(8,128)(2,1)}, bf16[4,256,2048]{2,1,0:T(8,128)(2,1)}) custom-call(f32[256,2048]{1,0:T(8,128)} %shard_map.233.refs_0_.refs_4_.refs_3_, f32[1,2048]{1,0:T(1,128)} %bitcast.68, bf16[256,2048]{1,0:T(8,128)(2,1)} %bitcast.64, ...), custom_call_target="tpu_custom_call" | custom-call | flops 34359738368 | bytes 314572800 | tf_op jit(solution)/shard_map/pallas_call | solution.py:466
  259.6 57.1 %shard_map.235 = (bf16[256,2048]{1,0:T(8,128)(2,1)}, bf16[8,256,2048]{2,1,0:T(8,128)(2,1)}, bf16[8,16,1024]{2,1,0:T(8,128)(2,1)}, bf16[8,16,1024]{2,1,0:T(8,128)...) custom-call(bf16[2048,1024]{1,0:T(8,128)(2,1)} %get-tuple-element.13, ...), custom_call_target="tpu_custom_call" | custom-call | flops 25769803776 | bytes 157286400 | tf_op jit(solution)/shard_map/pallas_call | solution.py:466
  316.7 68.2 %shard_map.236 = (f32[256,2048]{1,0:T(8,128)}, f32[1,2048]{1,0:T(1,128)}, bf16[8,16,1024]{2,1,0:T(8,128)(2,1)}, bf16[8,16,1024]{2,1,0:T(8,128)(2,1)}, bf16[8,16,...) custom-call(bf16[2048,2048]{1,0:T(8,128)(2,1)} %get-tuple-element.13, ...), custom_call_target="tpu_custom_call" | custom-call | flops 17179869184 | bytes 157286400 | tf_op jit(solution)/shard_map/pallas_call | solution.py:466
  385.0 54.7 %shard_map.237 = (bf16[2048,256]{1,0:T(8,128)(2,1)}, bf16[256,2048]{1,0:T(8,128)(2,1)}, bf16[8,16,1024]{2,1,0:T(8,128)(2,1)}, bf16[8,16,1024]{2,1,0:T(8,128)(2,1...) custom-call(f32[256,2048]{1,0:T(8,128)} %get-tuple-element.148.refs_, ...), custom_call_target="tpu_custom_call" | custom-call | flops 4294967296 | bytes 157286400 | tf_op jit(solution)/shard_map/pallas_call | solution.py:466
  439.7 47.1 %shard_map.238 = (bf16[2048,512]{1,0:T(8,128)(2,1)}, bf16[8,16,1024]{2,1,0:T(8,128)(2,1)}, bf16[8,16,1024]{2,1,0:T(8,128)(2,1)}, bf16[8,16,1024]{2,1,0:T(8,128)(...) custom-call(bf16[2048,256]{1,0:T(8,128)(2,1)} %get-tuple-element.155, ...), custom_call_target="tpu_custom_call" | custom-call | flops 8589934592 | bytes 29360128 | tf_op jit(solution)/shard_map/pallas_call | solution.py:466
  486.8 0.0 copy-start.2
  486.8 52.6 %shard_map.239 = (bf16[256,2048]{1,0:T(8,128)(2,1)}, f32[1,2048]{1,0:T(1,128)}, bf16[8,256,512]{2,1,0:T(8,128)(2,1)}, bf16[8,16,1024]{2,1,0:T(8,128)(2,1)}, bf16...) custom-call(bf16[2048,512]{1,0:T(8,128)(2,1)} %get-tuple-element.167, ...), custom_call_target="tpu_custom_call" | custom-call | flops 8589934592 | bytes 157286400 | tf_op jit(solution)/shard_map/pallas_call | solution.py:466
  539.4 0.0 copy-done.2
  539.4 0.7 maximum_bitcast_fusion
  540.1 0.6 pad.4.refs_1_
  540.7 156.4 %shard_map.240 = (bf16[256,8192]{1,0:T(8,128)(2,1)}, bf16[256,8192]{1,0:T(8,128)(2,1)}, bf16[2,8,32,2048]{3,2,1,0:T(8,128)(2,1)}, f32[8,256]{1,0:T(8,128)}, bf16...) custom-call(bf16[8,8,32,512]{3,2,1,0:T(8,128)(2,1)} %bitcast.44, ...), custom_call_target="tpu_custom_call" | custom-call | bytes 52428800 | tf_op jit(solution)/shard_map/pallas_call | solution.py:466
  697.1 1.3 fusion
  698.5 0.0 copy-start
  698.5 0.0 copy-start.1
  698.5 17.4 %shard_map.241 = (f32[8,32,2048]{2,1,0:T(8,128)}, f32[8,32,1024]{2,1,0:T(8,128)}, f32[8,32,1024]{2,1,0:T(8,128)}, f32[8,32,2048]{2,1,0:T(8,128)}, f32[8,32,8192]...) custom-call(bf16[8,16,1024]{2,1,0:T(8,128)(2,1)} %get-tuple-element.175.refs_0_, ...), custom_call_target="tpu_custom_call" | custom-call | bytes 47185920 | tf_op jit(solution)/shard_map/pallas_call | solution.py:1529
  715.8 0.0 copy-done
  715.8 1.0 copy.36
  716.8 0.0 copy-done.1
  716.8 1.0 copy.37
  (1 shorter events, 0.0 us)
Async XLA Ops:
  7.2 166.5 %all-gather.3.cloned.1.call-start = ((), (), s32[]{:S(2)}) async-start(), calls=%async_computation.1 | async-start | bytes 7864320 | tf_op jit(solution)/shard_map/all_gather | solution.py:1613
  29.7 65.6 %slice-start = ((bf16[256,8192]{1,0:T(8,128)(2,1)}), bf16[64,8192]{1,0:T(8,128)(2,1)S(1)}, s32[]{:S(2)}) async-start(bf16[256,8192]{1,0:T(8,128)(2,1)} %refs_0_.1), calls=%async_computation.2 | async-start | bytes 2097152 | tf_op jit(solution)/shard_map/slice | solution.py:1618
  29.7 65.6 %slice-start.1 = ((bf16[256,8192]{1,0:T(8,128)(2,1)}), bf16[64,8192]{1,0:T(8,128)(2,1)S(1)}, s32[]{:S(2)}) async-start(bf16[256,8192]{1,0:T(8,128)(2,1)} %refs_1_.4), calls=%async_computation.3 | async-start | bytes 2097152 | tf_op jit(solution)/shard_map/slice | solution.py:1618
  97.1 76.5 %all-to-all-start = ((bf16[64,8,2048]{2,0,1:T(8,128)(2,1)}), bf16[64,8,2048]{2,0,1:T(8,128)(2,1)}, u32[]{:S(2)}, u32[]{:S(2)}) async-start(bf16[64,8,2048]{2,0,1:T(8,128)(2,1)} %pad_maximum_fusion), calls=%async_computation | async-start | bytes 4194304 | tf_op jit(solution)/shard_map/all_to_all | solution.py:1596
  128.6 44.3 %copy-start.3 = (s32[1,16]{1,0:T(1,128)S(1)}, s32[1,16]{1,0:T(1,128)}, u32[]{:S(2)}) copy-start(s32[1,16]{1,0:T(1,128)} %order_ref.1) | copy-start | bytes 196
  486.8 52.6 %copy-start.2 = (f32[1,2048]{1,0:T(1,128)S(1)}, f32[1,2048]{1,0:T(1,128)}, u32[]{:S(2)}) copy-start(f32[1,2048]{1,0:T(1,128)} %get-tuple-element.193) | copy-start | bytes 24580
  698.5 17.4 %copy-start = (bf16[256,2048]{1,0:T(8,128)(2,1)S(1)}, bf16[256,2048]{1,0:T(8,128)(2,1)}, u32[]{:S(2)}) copy-start(bf16[256,2048]{1,0:T(8,128)(2,1)} %get-tuple-element.139) | copy-start | bytes 3145732
  698.5 18.4 %copy-start.1 = (bf16[256,2048]{1,0:T(8,128)(2,1)S(1)}, bf16[256,2048]{1,0:T(8,128)(2,1)}, u32[]{:S(2)}) copy-start(bf16[256,2048]{1,0:T(8,128)(2,1)} %get-tuple-element.174) | copy-start | bytes 3145732
Sparse Core Ops, SparseCore 0:
  29.9 116.5 all-gather.2

commit v12 on v11

--- a/solution.py
+++ b/solution.py
@@ -491,12 +491,12 @@
 
 
 def attend_back_kernel(
-    heads, block, ins, outs, scratch, line
+    heads, block, ins, outs, scratch, line, entered=False
 ):
     grad_ref, out_ref, q_ref, k_ref, v_ref, lse_ref, cos_ref, sin_ref, piece_ref, place_ref = ins
     (grad_qkv_ref,) = outs
     grads, centers, grad_q, placed = scratch
-    if line.ticks:
+    if line.ticks and not entered:
         line.signal(pltpu.get_barrier_semaphore())
         line.greet(pltpu.get_barrier_semaphore(), 0)
         line.start()
@@ -518,6 +518,7 @@
         return 0
 
     lax.fori_loop(0, blocks, take_block, 0)
+    line.step()
     grad_q[...] = jnp.zeros_like(grad_q)
 
     def key_block(j, _):
@@ -559,7 +560,7 @@
 
     for j in range(min(2, blocks - 1)):
         lax.fori_loop(j, j + 1, key_block, 0)
-        line.step(1 + j)
+        line.step(2 - j)
     lax.fori_loop(min(2, blocks - 1), blocks, key_block, 0)
 
     def turn_back(i, _):
@@ -585,27 +586,28 @@
     line.end()
 
 
-def attend_back(
-    order, grad, out, query, key, value, lse, cosine, sine, piece, heads, **line
-):
-    length = grad.shape[0]
-    block = min(512, length)
+def attend_back_operands(order, out, query, key, value, lse, cosine, sine, piece, heads):
+    length = out.shape[0]
     cut = length // order.shape[1]
     place = (order.reshape(-1, 1) * cut + jnp.arange(cut, dtype=order.dtype)).reshape(1, length)
-    tall = [grad, out, query, key, value, lse, cosine, sine, piece, place]
+    scratch = [
+        pltpu.VMEM((heads, length, HD), bf16),
+        pltpu.VMEM((heads, length, HD), f32),
+        pltpu.VMEM((heads, length, HD), f32),
+        pltpu.VMEM((length, (heads + 2) * HD), bf16),
+    ]
+    return [out, query, key, value, lse, cosine, sine, piece, place], scratch
+
+
+def attend_back(grad, operands, scratch, heads):
+    length = grad.shape[0]
     return run(
-        functools.partial(attend_back_kernel, heads, block),
-        [(array, VMEM) for array in tall],
+        functools.partial(attend_back_kernel, heads, min(512, length)),
+        [(array, VMEM) for array in [grad] + operands],
         [(jax.ShapeDtypeStruct((length, (heads + 2) * HD), bf16), VMEM)],
-        [
-            pltpu.VMEM((heads, length, HD), bf16),
-            pltpu.VMEM((heads, length, HD), f32),
-            pltpu.VMEM((heads, length, HD), f32),
-            pltpu.VMEM((length, (heads + 2) * HD), bf16),
-        ],
-        line.pop("number", None),
+        scratch,
+        None,
         (8 * heads * length * length * HD, 14 * length * HD * heads * 4, heads * length * length // 2),
-        **line,
     )[0]
 
 
@@ -717,7 +719,7 @@
             one.wait_send()
 
 
-def gather_rows(rows, all_ref, sends, recvs, on_chip, line, then=None):
+def gather_rows(rows, all_ref, sends, recvs, on_chip, line, then=None, final=True):
     rows_of = Gather(rows, all_ref, sends, recvs)
     rows_of.send_own()
     if then:
@@ -731,13 +733,16 @@
     rows_of.along_x()
     on_chip(*ALONG_X)
     rows_of.pass_across()
-    line.step()
+    line.step(2)
     rows_of.along_y()
     on_chip(*ALONG_Y)
     rows_of.across()
     on_chip(*ACROSS)
     rows_of.finish()
-    line.end()
+    if final:
+        line.end()
+    else:
+        line.step()
 
 
 GATHER_COPIES = 13
@@ -1019,10 +1024,10 @@
     )
 
 
-def attended_back_kernel(ins, outs, scratch, line):
-    grad_ref, w_ref, attended_ref = ins
-    grad_attended_ref, out_term_ref = outs
-    held, sends, recvs, sems, total = scratch
+def attention_back_kernel(heads, block, ins, outs, scratch, line):
+    grad_ref, w_ref, attended_ref = ins[:3]
+    grad_qkv_ref, out_term_ref = outs
+    held, sends, recvs, sems, total, grad_attended_ref = scratch[:6]
     rows = grad_ref.shape[0]
     moves = Moves(sems)
     greet_group(line)
@@ -1041,22 +1046,32 @@
         else:
             total[...] += term
 
-    gather_rows(rows, held, sends, recvs, on_chip, line)
+    gather_rows(rows, held, sends, recvs, on_chip, line, final=False)
     moves.finish()
-
-
-def attended_back(grad, w_out, attended, **line):
+    attend_back_kernel(
+        heads, block, (grad_attended_ref,) + tuple(ins[3:]), (grad_qkv_ref,), scratch[6:], line,
+        entered=True,
+    )
+
+
+def attention_back(grad, w_out, attended, back_ins, back_scratch, heads, **line):
     rows, width = grad.shape
+    length = 8 * rows
     return run(
-        attended_back_kernel,
-        [(array, VMEM) for array in (grad, w_out, attended)],
+        functools.partial(attention_back_kernel, heads, min(512, length)),
+        [(array, VMEM) for array in [grad, w_out, attended] + back_ins],
         [
-            (jax.ShapeDtypeStruct(attended.shape, bf16), VMEM),
+            (jax.ShapeDtypeStruct((length, (heads + 2) * HD), bf16), VMEM),
             (jax.ShapeDtypeStruct(w_out.shape, bf16), VMEM),
         ],
-        gather_scratch(rows, width, 1) + [pltpu.VMEM(w_out.shape, f32)],
+        gather_scratch(rows, width, 1)
+        + [pltpu.VMEM(w_out.shape, f32), pltpu.VMEM(attended.shape, bf16)]
+        + back_scratch,
         line.pop("number"),
-        (32 * rows * width * w_out.shape[0], 150 * rows * width * 2, 0),
+        (
+            32 * rows * width * w_out.shape[0] + 8 * heads * length * length * HD,
+            250 * rows * width * 2, heads * length * length // 2,
+        ),
         **line,
     )
 
@@ -1638,12 +1653,9 @@
         mid = x_flat + scatter(attended, w_out, False)
     grad_out = cotangent.reshape(local_rows, model_width)
 
-    def back_through_attention(grad_attended, **line):
-        return attend_back(
-            cut_order, grad_attended, attended_placed, query, key, value, lse, cosine, sine,
-            piece_ids, heads, **line,
-        )
-
+    back_ins, back_scratch = attend_back_operands(
+        cut_order, attended_placed, query, key, value, lse, cosine, sine, piece_ids, heads
+    )
     q_here = heads * HD
     if near:
         normed_two, hidden, cols_gate_up, grad_gate_up, down_term = feed_forward(
@@ -1682,9 +1694,10 @@
             grad_gate_up, cols_gate_up, True, back=(grad_out, mid, ffn_gain),
             steps={0: 1, 2: 1, 3: 1, 4: 1, 5: 1, 7: 1, 12: 1}, **line(6, 10),
         )
-        grad_attended, out_term = attended_back(grad_mid, w_out, attended, **line(7, 8))
+        grad_qkv, out_term = attention_back(
+            grad_mid, w_out, attended, back_ins, back_scratch, heads, **line(7, 15)
+        )
         terms["out"] = out_term.reshape(8, OUT // 2 * high, model_width)
-        grad_qkv = back_through_attention(grad_attended, **line(8, 7))
         grad_x, gain_attn_term, qkv_term = product_scattered(
             grad_qkv, cols_qkv, True, extra=(normed_one, None), dtype=bf16,
             back=(grad_mid, x_rows, attn_gain),
@@ -1720,7 +1733,8 @@
         grad_out.astype(f32), scatter(grad_gate_up, cols_gate_up, True), unit_two, inv_two, gain_ffn
     )
     grad_mid_low = gather(grad_mid.astype(bf16))
-    grad_qkv = back_through_attention(against_rows(grad_mid_low, w_out).astype(bf16))
+    grad_attended = against_rows(grad_mid_low, w_out).astype(bf16)
+    grad_qkv = attend_back(grad_attended, back_ins, back_scratch, heads)
     grad_x, gain_attn_term = norm_back(
         grad_mid, scatter(grad_qkv, cols_qkv, True), unit_one, inv_one, gain_attn
     )

time: 735 us -> 730 us (level)
    pallas_call x10 -> x9, Pallas kernels: 654 us -> 649 us  [run(): pl.pallas_call(body, out_shape=tuple((shape for shape, _ in outs)), in_sp...]
where the time goes in v12:
time: 730 us; the launch traced here: 720 us
  Pallas kernels  694 us (95%)
  between operations  14.7 us (2%)
    pallas_call x9, Pallas kernels, run(): pl.pallas_call(body, out_shape=tuple((shape for shape, _ in outs)), in_sp...  649 us
    pallas_call x1, Pallas kernels, attend(): pl.pallas_call(functools.partial(attend_kernel, heads, order.shape[1], bl...  27.2 us
    pallas_call x1, Pallas kernels, finish(): pl.pallas_call(functools.partial(finish_kernel, heads), out_shape=tuple(s...  17.4 us
  transfers between devices with their start and end apart: 2, of which 0 were waited for; matrix products, arithmetic and copies ran while one was open for 0% of the time, Pallas kernels for 19%

profile of v12, /device:TPU:0, one launch (start us, length us, event | category | flops | bytes accessed | tf_op | source)
XLA Modules:
  0.0 719.9 jit_solution(9619394447089252058)
XLA Ops:
  7.2 0.0 all-gather.3.cloned.1.call-start
  7.2 22.5 %shard_map.230 = bf16[8,48,2048]{2,1,0:T(8,128)(2,1)} custom-call(bf16[256,8192]{1,0:T(8,128)(2,1)} %refs_0_.1, bf16[256,8192]{1,0:T(8,128)(2,1)} %refs_1_.4), custom_call_target="tpu_custom_call" | custom-call | bytes 39321600 | tf_op jit(solution)/shard_map/pallas_call | solution.py:466
  29.7 0.0 slice-start
  29.7 0.0 slice-start.1
  29.8 0.0 all-gather.3.cloned.1.call-update
  29.8 65.6 %shard_map.231 = (bf16[2048,2048]{1,0:T(8,128)(2,1)}, bf16[2048,512]{1,0:T(8,128)(2,1)}) custom-call(bf16[256,2048]{1,0:T(8,128)(2,1)} %bitcast.45, f32[1,2048]{1,0:T(1,128)} %bitcast.51, bf16[256,2048]{1,0:T(8,128)(2,1)} %refs_2_.1, bf16[256,1024]{1,0:T(8,128)(2,1)} %refs_3_.1, bf16[256,1024]{1,0:T(8,128)(2,1)} %refs_4_.1), custom_call_target="tpu_custom_call" | custom-call | bytes 157286400 | tf_op jit(solution)/shard_map/pallas_call | solution.py:466
  95.4 0.0 slice-done
  95.4 0.0 slice-done.1
  95.4 0.2 copy_bitcast_fusion
  95.6 1.5 pad_maximum_fusion
  97.1 4.4 all-to-all-start
  101.5 27.2 %shard_map.232 = (bf16[2048,256]{1,0:T(8,128)(2,1)}, bf16[2,2048,128]{2,1,0:T(8,128)(2,1)}, bf16[2048,128]{1,0:T(8,128)(2,1)}, bf16[2048,128]{1,0:T(8,128)(2,1)}...) custom-call(s32[1,16]{1,0:T(1,128)} %order_ref.1, bf16[2048,2048]{1,0:T(8,128)(2,1)} %get-tuple-element.122.rows_hbm.refs_2_, ...), custom_call_target="tpu_custom_call" | custom-call | flops 7516192768 | bytes 29360128 | tf_op jit(solution)/shard_map/pallas_call | solution.py:163
  128.6 0.0 copy-start.3
  128.7 44.3 %shard_map.233.refs_0_.refs_4_.refs_3_ = f32[256,2048]{1,0:T(8,128)} custom-call(bf16[2048,256]{1,0:T(8,128)(2,1)} %get-tuple-element.124.refs_0_.refs_2_, bf16[256,2048]{1,0:T(8,128)(2,1)} %refs_1_.7, bf16[256,2048]{1,0:T(8,128)(2,1)} %bitcast.46), custom_call_target="tpu_custom_call" | custom-call | flops 2147483648 | bytes 157286400 | tf_op jit(solution)/shard_map/pallas_call | solution.py:466
  173.0 0.0 copy-done.3
  173.0 0.7 iota_add_fusion
  173.7 0.0 all-to-all-done
  173.7 0.0 all-gather.3.cloned.1.call-done
  173.7 86.0 %shard_map.234 = (bf16[2048,2048]{1,0:T(8,128)(2,1)}, bf16[2048,1024]{1,0:T(8,128)(2,1)}, bf16[8,256,2048]{2,1,0:T(8,128)(2,1)}, bf16[2048,2048]{1,0:T(8,128)(2,1)}, bf16[4,256,2048]{2,1,0:T(8,128)(2,1)}) custom-call(f32[256,2048]{1,0:T(8,128)} %shard_map.233.refs_0_.refs_4_.refs_3_, f32[1,2048]{1,0:T(1,128)} %bitcast.68, bf16[256,2048]{1,0:T(8,128)(2,1)} %bitcast.64, ...), custom_call_target="tpu_custom_call" | custom-call | flops 34359738368 | bytes 314572800 | tf_op jit(solution)/shard_map/pallas_call | solution.py:466
  259.7 57.1 %shard_map.235 = (bf16[256,2048]{1,0:T(8,128)(2,1)}, bf16[8,256,2048]{2,1,0:T(8,128)(2,1)}, bf16[8,16,1024]{2,1,0:T(8,128)(2,1)}, bf16[8,16,1024]{2,1,0:T(8,128)...) custom-call(bf16[2048,1024]{1,0:T(8,128)(2,1)} %get-tuple-element.12, ...), custom_call_target="tpu_custom_call" | custom-call | flops 25769803776 | bytes 157286400 | tf_op jit(solution)/shard_map/pallas_call | solution.py:466
  316.7 68.2 %shard_map.236 = (f32[256,2048]{1,0:T(8,128)}, f32[1,2048]{1,0:T(1,128)}, bf16[8,16,1024]{2,1,0:T(8,128)(2,1)}, bf16[8,16,1024]{2,1,0:T(8,128)(2,1)}, bf16[8,16,...) custom-call(bf16[2048,2048]{1,0:T(8,128)(2,1)} %get-tuple-element.13, ...), custom_call_target="tpu_custom_call" | custom-call | flops 17179869184 | bytes 157286400 | tf_op jit(solution)/shard_map/pallas_call | solution.py:466
  385.0 96.6 %shard_map.237 = (bf16[2048,512]{1,0:T(8,128)(2,1)}, bf16[256,2048]{1,0:T(8,128)(2,1)}, bf16[8,16,1024]{2,1,0:T(8,128)(2,1)}, bf16[8,16,1024]{2,1,0:T(8,128)(2,1...) custom-call(f32[256,2048]{1,0:T(8,128)} %get-tuple-element.141.refs_, ...), custom_call_target="tpu_custom_call" | custom-call | flops 12884901888 | bytes 262144000 | tf_op jit(solution)/shard_map/pallas_call | solution.py:466
  481.6 0.0 copy-start.2
  481.6 52.6 %shard_map.238 = (bf16[256,2048]{1,0:T(8,128)(2,1)}, f32[1,2048]{1,0:T(1,128)}, bf16[8,256,512]{2,1,0:T(8,128)(2,1)}, bf16[8,16,1024]{2,1,0:T(8,128)(2,1)}, bf16...) custom-call(bf16[2048,512]{1,0:T(8,128)(2,1)} %get-tuple-element.153, ...), custom_call_target="tpu_custom_call" | custom-call | flops 8589934592 | bytes 157286400 | tf_op jit(solution)/shard_map/pallas_call | solution.py:466
  534.2 0.0 copy-done.2
  534.2 0.7 maximum_bitcast_fusion
  534.9 0.6 pad.4.refs_1_
  535.5 156.4 %shard_map.239 = (bf16[256,8192]{1,0:T(8,128)(2,1)}, bf16[256,8192]{1,0:T(8,128)(2,1)}, bf16[2,8,32,2048]{3,2,1,0:T(8,128)(2,1)}, f32[8,256]{1,0:T(8,128)}, bf16...) custom-call(bf16[8,8,32,512]{3,2,1,0:T(8,128)(2,1)} %bitcast.44, ...), custom_call_target="tpu_custom_call" | custom-call | bytes 52428800 | tf_op jit(solution)/shard_map/pallas_call | solution.py:466
  691.9 1.3 fusion
  693.2 0.0 copy-start
  693.2 0.0 copy-start.1
  693.3 17.4 %shard_map.240 = (f32[8,32,2048]{2,1,0:T(8,128)}, f32[8,32,1024]{2,1,0:T(8,128)}, f32[8,32,1024]{2,1,0:T(8,128)}, f32[8,32,2048]{2,1,0:T(8,128)}, f32[8,32,8192]...) custom-call(bf16[8,16,1024]{2,1,0:T(8,128)(2,1)} %get-tuple-element.161.refs_0_, ...), custom_call_target="tpu_custom_call" | custom-call | bytes 47185920 | tf_op jit(solution)/shard_map/pallas_call | solution.py:1544
  710.6 0.0 copy-done
  710.6 1.0 copy.36
  711.6 0.0 copy-done.1
  711.6 1.0 copy.37
  (1 shorter events, 0.0 us)
Async XLA Ops:
  7.2 166.5 %all-gather.3.cloned.1.call-start = ((), (), s32[]{:S(2)}) async-start(), calls=%async_computation.1 | async-start | bytes 7864320 | tf_op jit(solution)/shard_map/all_gather | solution.py:1628
  29.7 65.6 %slice-start = ((bf16[256,8192]{1,0:T(8,128)(2,1)}), bf16[64,8192]{1,0:T(8,128)(2,1)S(1)}, s32[]{:S(2)}) async-start(bf16[256,8192]{1,0:T(8,128)(2,1)} %refs_0_.1), calls=%async_computation.2 | async-start | bytes 2097152 | tf_op jit(solution)/shard_map/slice | solution.py:1633
  29.7 65.6 %slice-start.1 = ((bf16[256,8192]{1,0:T(8,128)(2,1)}), bf16[64,8192]{1,0:T(8,128)(2,1)S(1)}, s32[]{:S(2)}) async-start(bf16[256,8192]{1,0:T(8,128)(2,1)} %refs_1_.4), calls=%async_computation.3 | async-start | bytes 2097152 | tf_op jit(solution)/shard_map/slice | solution.py:1633
  97.1 76.6 %all-to-all-start = ((bf16[64,8,2048]{2,0,1:T(8,128)(2,1)}), bf16[64,8,2048]{2,0,1:T(8,128)(2,1)}, u32[]{:S(2)}, u32[]{:S(2)}) async-start(bf16[64,8,2048]{2,0,1:T(8,128)(2,1)} %pad_maximum_fusion), calls=%async_computation | async-start | bytes 4194304 | tf_op jit(solution)/shard_map/all_to_all | solution.py:1611
  128.6 44.3 %copy-start.3 = (s32[1,16]{1,0:T(1,128)S(1)}, s32[1,16]{1,0:T(1,128)}, u32[]{:S(2)}) copy-start(s32[1,16]{1,0:T(1,128)} %order_ref.1) | copy-start | bytes 196
  481.6 52.6 %copy-start.2 = (f32[1,2048]{1,0:T(1,128)S(1)}, f32[1,2048]{1,0:T(1,128)}, u32[]{:S(2)}) copy-start(f32[1,2048]{1,0:T(1,128)} %get-tuple-element.179) | copy-start | bytes 24580
  693.2 17.4 %copy-start = (bf16[256,2048]{1,0:T(8,128)(2,1)S(1)}, bf16[256,2048]{1,0:T(8,128)(2,1)}, u32[]{:S(2)}) copy-start(bf16[256,2048]{1,0:T(8,128)(2,1)} %get-tuple-element.132) | copy-start | bytes 3145732
  693.2 18.4 %copy-start.1 = (bf16[256,2048]{1,0:T(8,128)(2,1)S(1)}, bf16[256,2048]{1,0:T(8,128)(2,1)}, u32[]{:S(2)}) copy-start(bf16[256,2048]{1,0:T(8,128)(2,1)} %get-tuple-element.160) | copy-start | bytes 3145732
Sparse Core Ops, SparseCore 0:
  29.9 116.5 all-gather.2

commit v13 on v12

--- a/solution.py
+++ b/solution.py
@@ -854,7 +854,7 @@
 
 
 def columns_kernel(rows_here, ins, outs, scratch, line):
-    (cols_ref,) = outs
+    cols_ref, packed_ref = outs
     sends, recvs, sems = scratch
     moves = Moves(sems)
     barrier = pltpu.get_barrier_semaphore()
@@ -870,21 +870,34 @@
             (weight.at[pl.ds(first, rows_here), :], width, cols_ref.at[me, :, low : low + width])
         )
         low += width
-    for one in send_columns(pieces, sends, recvs, moves):
+    copies = send_columns(pieces, sends, recvs, moves)
+    low = 0
+    for weight in ins:
+        width = weight.shape[1] // 8
+        for device in range(8):
+            moves.later(
+                weight.at[weight.shape[0] - packed_ref.shape[1] :, device * width : (device + 1) * width],
+                packed_ref.at[device, :, low : low + width],
+            )
+        low += width
+    for one in copies:
         one.wait()
     moves.finish()
 
 
-def columns_of_some(weights, rows_here, number):
+def columns_of_some(weights, rows_here, rest, number):
     deep = sum(weight.shape[1] for weight in weights) // 8
     return run(
         functools.partial(columns_kernel, rows_here),
         [(weight, ANY) for weight in weights],
-        [(jax.ShapeDtypeStruct((8, rows_here, deep), bf16), ANY)],
+        [
+            (jax.ShapeDtypeStruct((8, rows_here, deep), bf16), ANY),
+            (jax.ShapeDtypeStruct((8, rest, deep), bf16), ANY),
+        ],
         [pltpu.SemaphoreType.DMA((len(weights), 7))] * 2
-        + [pltpu.SemaphoreType.DMA((len(weights),))],
+        + [pltpu.SemaphoreType.DMA((9 * len(weights),))],
         number, (0, 50 * 8 * rows_here * deep, 0),
-    )[0]
+    )
 
 
 def feed_forward_kernel(tile, ins, outs, scratch, line):
@@ -1464,8 +1477,14 @@
 def finish_kernel(heads, *refs):
     chunks, rest = refs[: DOWN + OUT + QKV], refs[DOWN + OUT + QKV :]
     gate_rows, up_rows = rest[:2]
-    query, key, value, out, gate, up, down = rest[2:9]
-    low, wide, load_sems, store_sems = rest[9:]
+    kept = [
+        pltpu.make_async_copy(src, dst, rest[-1].at[number])
+        for number, (src, dst) in enumerate(zip(rest[2:4], rest[11:13]))
+    ]
+    for one in kept:
+        one.start()
+    query, key, value, out, gate, up, down = rest[4:11]
+    low, wide, load_sems, store_sems = rest[13:17]
     _, high, width = chunks[0].shape
     depth = low.shape[0]
 
@@ -1528,9 +1547,11 @@
     for number in range(len(jobs) - depth, len(jobs)):
         for one in stores(number):
             one.wait()
-
-
-def finish(chunks, gate_rows, up_rows, heads):
+    for one in kept:
+        one.wait()
+
+
+def finish(chunks, gate_rows, up_rows, others, heads):
     eight, high, width = chunks[0].shape
     width = 2 * width
     rows, wide = gate_rows.shape
@@ -1540,17 +1561,18 @@
 
     shapes = [split(columns) for columns in (8 * heads * HD, 8 * HD, 8 * HD, width, wide, wide)]
     shapes.append(jax.ShapeDtypeStruct((DOWN // 2, eight, high, width), f32))
-    depth = 6
+    depth = 12
     results = pl.pallas_call(
         functools.partial(finish_kernel, heads),
-        out_shape=tuple(shapes),
-        in_specs=[pl.BlockSpec(memory_space=pl.ANY)] * (len(chunks) + 2),
-        out_specs=tuple([pl.BlockSpec(memory_space=pl.ANY)] * 7),
+        out_shape=tuple(shapes) + tuple(jax.ShapeDtypeStruct(x.shape, x.dtype) for x in others),
+        in_specs=[pl.BlockSpec(memory_space=pl.ANY)] * (len(chunks) + 4),
+        out_specs=tuple([pl.BlockSpec(memory_space=pl.ANY)] * 9),
         scratch_shapes=[
             pltpu.VMEM((depth, eight, high, width), bf16),
             pltpu.VMEM((depth, eight, high, width), f32),
             pltpu.SemaphoreType.DMA((depth,)),
             pltpu.SemaphoreType.DMA((depth, 12)),
+            pltpu.SemaphoreType.DMA((2,)),
         ],
         compiler_params=pltpu.CompilerParams(vmem_limit_bytes=60 * 2**20),
         cost_estimate=pl.CostEstimate(
@@ -1558,10 +1580,10 @@
         ),
     )(
         *chunks, gate_rows.reshape(eight, rows // eight, wide),
-        up_rows.reshape(eight, rows // eight, wide),
+        up_rows.reshape(eight, rows // eight, wide), *others,
     )
     flat = [result.reshape(rows, -1) for result in results[:6]]
-    return flat + [results[6].reshape(-1, width)]
+    return flat + [results[6].reshape(-1, width)], results[7:]
 
 
 def sum_over_sequences(term):
@@ -1623,21 +1645,14 @@
     attn_gain, ffn_gain = gain_attn.reshape(1, -1), gain_ffn.reshape(1, -1)
     if near:
         share = rows_here // (4 * reps) * 3
-        spread = columns_of_some((w_gate, w_up), share, 11)
-        x_first, spread = lax.optimization_barrier((x_rows, spread))
+        spread, rest = columns_of_some((w_gate, w_up), share, rows_here - reps * share, 11)
+        x_first, spread, rest = lax.optimization_barrier((x_rows, spread, rest))
         spread = lax.all_gather(spread, "rep", axis=0)
         normed_one, cols_qkv = gather_normed(
             x_first, attn_gain, (w_query, w_key, w_value), number=1
         )
-        last_gate, last_up, normed_one = lax.optimization_barrier(
-            (w_gate[reps * share :], w_up[reps * share :], normed_one)
-        )
-        rest = to_columns(
-            jnp.concatenate(
-                [part.reshape(rows_here - reps * share, groups, -1) for part in (last_gate, last_up)],
-                -1,
-            )
-        ).reshape(groups, rows_here - reps * share, -1)
+        rest, normed_one = lax.optimization_barrier((rest, normed_one))
+        rest = lax.all_to_all(rest, "grp", 0, 0, tiled=True)
     else:
         normed_one = gather(rms_normed(x_flat, attn_gain).astype(bf16))
         cols_qkv = to_columns(
@@ -1711,8 +1726,10 @@
             {c: sums.done[c] for c in sums.done if c >= DOWN}, hidden_here, **rest,
         )
         straight = [n for n in range(CHUNKS) if n < DOWN or n >= DOWN + GATE_UP]
-        weight_grads = finish([sums.done[n] for n in straight], gate_rows, up_rows, heads)
-        shaped = tuple(rows.reshape(layer_input.shape) for rows in (result, grad_x))
+        weight_grads, shaped = finish(
+            [sums.done[n] for n in straight], gate_rows, up_rows, (result, grad_x), heads
+        )
+        shaped = tuple(rows.reshape(layer_input.shape) for rows in shaped)
         return shaped + tuple(weight_grads) + (own_gains[0], own_gains[1])
 
     unit_one = x_flat * inv_one

time: 730 us -> 826 us (1.13)
  Pallas kernels: 694 us -> 794 us
    pallas_call x9, Pallas kernels: 649 us -> 700 us  [run(): pl.pallas_call(body, out_shape=tuple((shape for shape, _ in outs)), in_sp...]
    pallas_call x1, Pallas kernels: 17.4 us -> 66 us  [finish(): pl.pallas_call(functools.partial(finish_kernel, heads), out_shape=tuple(s...]
  transfers between devices with their start and end apart: 2 -> 2, of which waited for: 0 -> 0; matrix products, arithmetic and copies ran while one was open for 0% -> 0% of each run, Pallas kernels for 19% -> 17%
where the time goes in v13:
time: 826 us; the launch traced here: 816 us
  Pallas kernels  794 us (96%)
  between operations  14.6 us (2%)
    pallas_call x9, Pallas kernels, run(): pl.pallas_call(body, out_shape=tuple((shape for shape, _ in outs)), in_sp...  700 us
    pallas_call x1, Pallas kernels, finish(): pl.pallas_call(functools.partial(finish_kernel, heads), out_shape=tuple(s...  66 us
    pallas_call x1, Pallas kernels, attend(): pl.pallas_call(functools.partial(attend_kernel, heads, order.shape[1], bl...  27.2 us
  transfers between devices with their start and end apart: 2, of which 0 were waited for; matrix products, arithmetic and copies ran while one was open for 0% of the time, Pallas kernels for 17%

profile of v13, /device:TPU:0, one launch (start us, length us, event | category | flops | bytes accessed | tf_op | source)
XLA Modules:
  0.0 816.1 jit_solution(860751950463144942)
XLA Ops:
  7.2 0.0 all-gather.3.cloned.1.call-start
  7.2 75.0 %shard_map.230 = (bf16[8,48,2048]{2,1,0:T(8,128)(2,1)}, bf16[8,64,2048]{2,1,0:T(8,128)(2,1)}) custom-call(bf16[256,8192]{1,0:T(8,128)(2,1)} %refs_0_.1, bf16[256,8192]{1,0:T(8,128)(2,1)} %refs_1_.4), custom_call_target="tpu_custom_call" | custom-call | bytes 39321600 | tf_op jit(solution)/shard_map/pallas_call | solution.py:466
  82.2 0.0 all-gather.3.cloned.1.call-update
  82.3 64.4 %shard_map.231 = (bf16[2048,2048]{1,0:T(8,128)(2,1)}, bf16[2048,512]{1,0:T(8,128)(2,1)}) custom-call(bf16[256,2048]{1,0:T(8,128)(2,1)} %bitcast.32, f32[1,2048]{1,0:T(1,128)} %bitcast.36, bf16[256,2048]{1,0:T(8,128)(2,1)} %refs_2_.1, bf16[256,1024]{1,0:T(8,128)(2,1)} %refs_3_.1, bf16[256,1024]{1,0:T(8,128)(2,1)} %refs_4_.1), custom_call_target="tpu_custom_call" | custom-call | bytes 157286400 | tf_op jit(solution)/shard_map/pallas_call | solution.py:466
  146.7 4.4 all-to-all-start
  151.1 27.2 %shard_map.232 = (bf16[2048,256]{1,0:T(8,128)(2,1)}, bf16[2,2048,128]{2,1,0:T(8,128)(2,1)}, bf16[2048,128]{1,0:T(8,128)(2,1)}, bf16[2048,128]{1,0:T(8,128)(2,1)}...) custom-call(s32[1,16]{1,0:T(1,128)} %order_ref.1, bf16[2048,2048]{1,0:T(8,128)(2,1)} %get-tuple-element.129.rows_hbm.refs_2_, ...), custom_call_target="tpu_custom_call" | custom-call | flops 7516192768 | bytes 29360128 | tf_op jit(solution)/shard_map/pallas_call | solution.py:163
  178.2 0.0 copy-start.1
  178.3 44.3 %shard_map.233.refs_0_.refs_4_.refs_3_ = f32[256,2048]{1,0:T(8,128)} custom-call(bf16[2048,256]{1,0:T(8,128)(2,1)} %get-tuple-element.131.refs_0_.refs_2_, bf16[256,2048]{1,0:T(8,128)(2,1)} %refs_1_.7, bf16[256,2048]{1,0:T(8,128)(2,1)} %bitcast.33), custom_call_target="tpu_custom_call" | custom-call | flops 2147483648 | bytes 157286400 | tf_op jit(solution)/shard_map/pallas_call | solution.py:466
  222.6 0.0 copy-done.1
  222.6 0.7 iota_add_fusion
  223.3 0.0 all-to-all-done.refs_4_
  223.3 0.0 all-gather.3.cloned.1.call-done
  223.3 85.9 %shard_map.234 = (bf16[2048,2048]{1,0:T(8,128)(2,1)}, bf16[2048,1024]{1,0:T(8,128)(2,1)}, bf16[8,256,2048]{2,1,0:T(8,128)(2,1)}, bf16[2048,2048]{1,0:T(8,128)(2,1)}, bf16[4,256,2048]{2,1,0:T(8,128)(2,1)}) custom-call(f32[256,2048]{1,0:T(8,128)} %shard_map.233.refs_0_.refs_4_.refs_3_, f32[1,2048]{1,0:T(1,128)} %bitcast.55, bf16[256,2048]{1,0:T(8,128)(2,1)} %bitcast.49, ...), custom_call_target="tpu_custom_call" | custom-call | flops 34359738368 | bytes 314572800 | tf_op jit(solution)/shard_map/pallas_call | solution.py:466
  309.2 57.1 %shard_map.235 = (bf16[256,2048]{1,0:T(8,128)(2,1)}, bf16[8,256,2048]{2,1,0:T(8,128)(2,1)}, bf16[8,16,1024]{2,1,0:T(8,128)(2,1)}, bf16[8,16,1024]{2,1,0:T(8,128)...) custom-call(bf16[2048,1024]{1,0:T(8,128)(2,1)} %get-tuple-element.13, ...), custom_call_target="tpu_custom_call" | custom-call | flops 25769803776 | bytes 157286400 | tf_op jit(solution)/shard_map/pallas_call | solution.py:466
  366.3 68.2 %shard_map.236 = (f32[256,2048]{1,0:T(8,128)}, f32[1,2048]{1,0:T(1,128)}, bf16[8,16,1024]{2,1,0:T(8,128)(2,1)}, bf16[8,16,1024]{2,1,0:T(8,128)(2,1)}, bf16[8,16,...) custom-call(bf16[2048,2048]{1,0:T(8,128)(2,1)} %get-tuple-element.13, ...), custom_call_target="tpu_custom_call" | custom-call | flops 17179869184 | bytes 157286400 | tf_op jit(solution)/shard_map/pallas_call | solution.py:466
  434.6 96.4 %shard_map.237 = (bf16[2048,512]{1,0:T(8,128)(2,1)}, bf16[256,2048]{1,0:T(8,128)(2,1)}, bf16[8,16,1024]{2,1,0:T(8,128)(2,1)}, bf16[8,16,1024]{2,1,0:T(8,128)(2,1...) custom-call(f32[256,2048]{1,0:T(8,128)} %get-tuple-element.159.refs_, ...), custom_call_target="tpu_custom_call" | custom-call | flops 12884901888 | bytes 262144000 | tf_op jit(solution)/shard_map/pallas_call | solution.py:466
  531.0 0.0 copy-start
  531.0 52.7 %shard_map.238 = (bf16[256,2048]{1,0:T(8,128)(2,1)}, f32[1,2048]{1,0:T(1,128)}, bf16[8,256,512]{2,1,0:T(8,128)(2,1)}, bf16[8,16,1024]{2,1,0:T(8,128)(2,1)}, bf16...) custom-call(bf16[2048,512]{1,0:T(8,128)(2,1)} %get-tuple-element.174, ...), custom_call_target="tpu_custom_call" | custom-call | flops 8589934592 | bytes 157286400 | tf_op jit(solution)/shard_map/pallas_call | solution.py:466
  583.7 0.0 copy-done
  583.7 0.7 maximum_bitcast_fusion
  584.4 0.6 pad.4.refs_1_
  585.0 156.4 %shard_map.239 = (bf16[256,8192]{1,0:T(8,128)(2,1)}, bf16[256,8192]{1,0:T(8,128)(2,1)}, bf16[2,8,32,2048]{3,2,1,0:T(8,128)(2,1)}, f32[8,256]{1,0:T(8,128)}, bf16...) custom-call(bf16[8,8,32,512]{3,2,1,0:T(8,128)(2,1)} %bitcast.31, ...), custom_call_target="tpu_custom_call" | custom-call | bytes 52428800 | tf_op jit(solution)/shard_map/pallas_call | solution.py:466
  741.4 1.3 fusion
  742.8 66.0 %shard_map.240 = (f32[8,32,2048]{2,1,0:T(8,128)}, f32[8,32,1024]{2,1,0:T(8,128)}, f32[8,32,1024]{2,1,0:T(8,128)}, f32[8,32,2048]{2,1,0:T(8,128)}, f32[8,32,8192]...) custom-call(bf16[8,16,1024]{2,1,0:T(8,128)(2,1)} %get-tuple-element., ...), custom_call_target="tpu_custom_call" | custom-call | bytes 47185920 | tf_op jit(solution)/shard_map/pallas_call | solution.py:1565
  (1 shorter events, 0.0 us)
Async XLA Ops:
  7.2 216.1 %all-gather.3.cloned.1.call-start = ((), (), s32[]{:S(2)}) async-start(), calls=%async_computation.1 | async-start | bytes 7864320 | tf_op jit(solution)/shard_map/all_gather | solution.py:1650
  146.7 76.6 %all-to-all-start = ((bf16[8,64,2048]{2,1,0:T(8,128)(2,1)}), bf16[8,64,2048]{2,1,0:T(8,128)(2,1)}, u32[]{:S(2)}, u32[]{:S(2)}) async-start(bf16[8,64,2048]{2,1,0:T(8,128)(2,1)} %get-tuple-element.133), calls=%async_computation | async-start | bytes 4194304 | tf_op jit(solution)/shard_map/all_to_all | solution.py:1655
  178.2 44.3 %copy-start.1 = (s32[1,16]{1,0:T(1,128)S(1)}, s32[1,16]{1,0:T(1,128)}, u32[]{:S(2)}) copy-start(s32[1,16]{1,0:T(1,128)} %order_ref.1) | copy-start | bytes 196
  531.0 52.7 %copy-start = (f32[1,2048]{1,0:T(1,128)S(1)}, f32[1,2048]{1,0:T(1,128)}, u32[]{:S(2)}) copy-start(f32[1,2048]{1,0:T(1,128)} %get-tuple-element.183) | copy-start | bytes 24580
Sparse Core Ops, SparseCore 0:
  82.4 114.7 all-gather.2

commit v14 on v12

--- a/solution.py
+++ b/solution.py
@@ -290,7 +290,8 @@
             slot = self.outs[tick - 2 * LAG]
             total = (
                 lambda: self.remote(2, number, done, slot, self.partner),
-                lambda: pltpu.make_async_copy(done, slot, self.local.at[1, number]),
+                lambda: pltpu.make_async_copy(held_total, slot, self.local.at[1, number]),
+                lambda: pltpu.make_async_copy(done, held_total, self.carries.at[3, number]),
             )
         return term, pair, total
 
@@ -311,7 +312,7 @@
             if term:
                 term[1]().start()
             if total:
-                total[1]().start()
+                total[2 if number < LAG else 1]().start()
             if pair and number < LAG:
                 pair[1]().start()
 
@@ -329,7 +330,8 @@
         def _():
             if total:
                 total[0]().wait_send()
-                total[1]().wait()
+                if number >= LAG:
+                    total[1]().wait()
             if pair:
                 pair[0]().wait_send()
                 pair[0]().wait_recv()
@@ -337,7 +339,7 @@
                 term[0]().wait_recv()
 
     def add(self, number):
-        term, pair, _ = self.hops(number)
+        term, pair, total = self.hops(number)
         tick = self.first + number
 
         def sum_of(into, first, second):
@@ -349,6 +351,9 @@
 
         @pl.when(is_middle())
         def _():
+            if total and number < LAG:
+                total[2]().wait()
+                total[1]().start()
             if pair:
                 if number < LAG:
                     pair[1]().wait()
@@ -360,6 +365,8 @@
             if term:
                 term[1]().wait()
                 sum_of(self.pair.at[tick % (LAG + 1)], self.own.at[tick % LAG], self.inward.at[number])
+            if total and number < LAG:
+                total[1]().wait()
 
     def keep(self, number):
         tick = self.first + number
@@ -449,7 +456,7 @@
             pltpu.VMEM((LAG + 1,) + sums.shape, bf16),
             pltpu.SemaphoreType.DMA((2, 3, ticks)),
             pltpu.SemaphoreType.DMA((2, ticks)),
-            pltpu.SemaphoreType.DMA((3, LAG)),
+            pltpu.SemaphoreType.DMA((4, LAG)),
         ]
 
     def body(*refs):
@@ -1540,7 +1547,7 @@
 
     shapes = [split(columns) for columns in (8 * heads * HD, 8 * HD, 8 * HD, width, wide, wide)]
     shapes.append(jax.ShapeDtypeStruct((DOWN // 2, eight, high, width), f32))
-    depth = 6
+    depth = 12
     results = pl.pallas_call(
         functools.partial(finish_kernel, heads),
         out_shape=tuple(shapes),

time: 730 us -> 731 us (level)
  no operation moved by 1% of the time
where the time goes in v14:
time: 731 us; the launch traced here: 721 us
  Pallas kernels  695 us (95%)
  between operations  14.7 us (2%)
    pallas_call x9, Pallas kernels, run(): pl.pallas_call(body, out_shape=tuple((shape for shape, _ in outs)), in_sp...  650 us
    pallas_call x1, Pallas kernels, attend(): pl.pallas_call(functools.partial(attend_kernel, heads, order.shape[1], bl...  27.2 us
    pallas_call x1, Pallas kernels, finish(): pl.pallas_call(functools.partial(finish_kernel, heads), out_shape=tuple(s...  18 us
  transfers between devices with their start and end apart: 2, of which 0 were waited for; matrix products, arithmetic and copies ran while one was open for 0% of the time, Pallas kernels for 19%

profile of v14, /device:TPU:0, one launch (start us, length us, event | category | flops | bytes accessed | tf_op | source)
XLA Modules:
  0.0 721.1 jit_solution(6792946008765880569)
XLA Ops:
  7.2 0.0 all-gather.3.cloned.1.call-start
  7.2 22.5 %shard_map.230 = bf16[8,48,2048]{2,1,0:T(8,128)(2,1)} custom-call(bf16[256,8192]{1,0:T(8,128)(2,1)} %refs_0_.1, bf16[256,8192]{1,0:T(8,128)(2,1)} %refs_1_.4), custom_call_target="tpu_custom_call" | custom-call | bytes 39321600 | tf_op jit(solution)/shard_map/pallas_call | solution.py:473
  29.7 0.0 slice-start
  29.7 0.0 slice-start.1
  29.8 0.0 all-gather.3.cloned.1.call-update
  29.8 65.6 %shard_map.231 = (bf16[2048,2048]{1,0:T(8,128)(2,1)}, bf16[2048,512]{1,0:T(8,128)(2,1)}) custom-call(bf16[256,2048]{1,0:T(8,128)(2,1)} %bitcast.45, f32[1,2048]{1,0:T(1,128)} %bitcast.51, bf16[256,2048]{1,0:T(8,128)(2,1)} %refs_2_.1, bf16[256,1024]{1,0:T(8,128)(2,1)} %refs_3_.1, bf16[256,1024]{1,0:T(8,128)(2,1)} %refs_4_.1), custom_call_target="tpu_custom_call" | custom-call | bytes 157286400 | tf_op jit(solution)/shard_map/pallas_call | solution.py:473
  95.4 0.0 slice-done
  95.4 0.0 slice-done.1
  95.4 0.2 copy_bitcast_fusion
  95.6 1.5 pad_maximum_fusion
  97.1 4.4 all-to-all-start
  101.5 27.2 %shard_map.232 = (bf16[2048,256]{1,0:T(8,128)(2,1)}, bf16[2,2048,128]{2,1,0:T(8,128)(2,1)}, bf16[2048,128]{1,0:T(8,128)(2,1)}, bf16[2048,128]{1,0:T(8,128)(2,1)}...) custom-call(s32[1,16]{1,0:T(1,128)} %order_ref.1, bf16[2048,2048]{1,0:T(8,128)(2,1)} %get-tuple-element.122.rows_hbm.refs_2_, ...), custom_call_target="tpu_custom_call" | custom-call | flops 7516192768 | bytes 29360128 | tf_op jit(solution)/shard_map/pallas_call | solution.py:163
  128.6 0.0 copy-start.3
  128.7 44.3 %shard_map.233.refs_0_.refs_4_.refs_3_ = f32[256,2048]{1,0:T(8,128)} custom-call(bf16[2048,256]{1,0:T(8,128)(2,1)} %get-tuple-element.124.refs_0_.refs_2_, bf16[256,2048]{1,0:T(8,128)(2,1)} %refs_1_.7, bf16[256,2048]{1,0:T(8,128)(2,1)} %bitcast.46), custom_call_target="tpu_custom_call" | custom-call | flops 2147483648 | bytes 157286400 | tf_op jit(solution)/shard_map/pallas_call | solution.py:473
  173.0 0.0 copy-done.3
  173.0 0.7 iota_add_fusion
  173.7 0.0 all-to-all-done
  173.7 0.0 all-gather.3.cloned.1.call-done
  173.7 86.0 %shard_map.234 = (bf16[2048,2048]{1,0:T(8,128)(2,1)}, bf16[2048,1024]{1,0:T(8,128)(2,1)}, bf16[8,256,2048]{2,1,0:T(8,128)(2,1)}, bf16[2048,2048]{1,0:T(8,128)(2,1)}, bf16[4,256,2048]{2,1,0:T(8,128)(2,1)}) custom-call(f32[256,2048]{1,0:T(8,128)} %shard_map.233.refs_0_.refs_4_.refs_3_, f32[1,2048]{1,0:T(1,128)} %bitcast.68, bf16[256,2048]{1,0:T(8,128)(2,1)} %bitcast.64, ...), custom_call_target="tpu_custom_call" | custom-call | flops 34359738368 | bytes 314572800 | tf_op jit(solution)/shard_map/pallas_call | solution.py:473
  259.7 57.1 %shard_map.235 = (bf16[256,2048]{1,0:T(8,128)(2,1)}, bf16[8,256,2048]{2,1,0:T(8,128)(2,1)}, bf16[8,16,1024]{2,1,0:T(8,128)(2,1)}, bf16[8,16,1024]{2,1,0:T(8,128)...) custom-call(bf16[2048,1024]{1,0:T(8,128)(2,1)} %get-tuple-element.12, ...), custom_call_target="tpu_custom_call" | custom-call | flops 25769803776 | bytes 157286400 | tf_op jit(solution)/shard_map/pallas_call | solution.py:473
  316.8 68.3 %shard_map.236 = (f32[256,2048]{1,0:T(8,128)}, f32[1,2048]{1,0:T(1,128)}, bf16[8,16,1024]{2,1,0:T(8,128)(2,1)}, bf16[8,16,1024]{2,1,0:T(8,128)(2,1)}, bf16[8,16,...) custom-call(bf16[2048,2048]{1,0:T(8,128)(2,1)} %get-tuple-element.13, ...), custom_call_target="tpu_custom_call" | custom-call | flops 17179869184 | bytes 157286400 | tf_op jit(solution)/shard_map/pallas_call | solution.py:473
  385.0 96.6 %shard_map.237 = (bf16[2048,512]{1,0:T(8,128)(2,1)}, bf16[256,2048]{1,0:T(8,128)(2,1)}, bf16[8,16,1024]{2,1,0:T(8,128)(2,1)}, bf16[8,16,1024]{2,1,0:T(8,128)(2,1...) custom-call(f32[256,2048]{1,0:T(8,128)} %get-tuple-element.141.refs_, ...), custom_call_target="tpu_custom_call" | custom-call | flops 12884901888 | bytes 262144000 | tf_op jit(solution)/shard_map/pallas_call | solution.py:473
  481.6 0.0 copy-start.2
  481.6 52.6 %shard_map.238 = (bf16[256,2048]{1,0:T(8,128)(2,1)}, f32[1,2048]{1,0:T(1,128)}, bf16[8,256,512]{2,1,0:T(8,128)(2,1)}, bf16[8,16,1024]{2,1,0:T(8,128)(2,1)}, bf16...) custom-call(bf16[2048,512]{1,0:T(8,128)(2,1)} %get-tuple-element.153, ...), custom_call_target="tpu_custom_call" | custom-call | flops 8589934592 | bytes 157286400 | tf_op jit(solution)/shard_map/pallas_call | solution.py:473
  534.3 0.0 copy-done.2
  534.3 0.7 maximum_bitcast_fusion
  535.0 0.6 pad.4.refs_1_
  535.6 156.9 %shard_map.239 = (bf16[256,8192]{1,0:T(8,128)(2,1)}, bf16[256,8192]{1,0:T(8,128)(2,1)}, bf16[2,8,32,2048]{3,2,1,0:T(8,128)(2,1)}, f32[8,256]{1,0:T(8,128)}, bf16...) custom-call(bf16[8,8,32,512]{3,2,1,0:T(8,128)(2,1)} %bitcast.44, ...), custom_call_target="tpu_custom_call" | custom-call | bytes 52428800 | tf_op jit(solution)/shard_map/pallas_call | solution.py:473
  692.5 1.3 fusion
  693.9 0.0 copy-start
  693.9 0.0 copy-start.1
  693.9 18.0 %shard_map.240 = (f32[8,32,2048]{2,1,0:T(8,128)}, f32[8,32,1024]{2,1,0:T(8,128)}, f32[8,32,1024]{2,1,0:T(8,128)}, f32[8,32,2048]{2,1,0:T(8,128)}, f32[8,32,8192]...) custom-call(bf16[8,16,1024]{2,1,0:T(8,128)(2,1)} %get-tuple-element.161.refs_0_, ...), custom_call_target="tpu_custom_call" | custom-call | bytes 47185920 | tf_op jit(solution)/shard_map/pallas_call | solution.py:1551
  711.9 0.0 copy-done
  711.9 1.0 copy.36
  712.9 0.0 copy-done.1
  712.9 1.0 copy.37
  (1 shorter events, 0.0 us)
Async XLA Ops:
  7.2 166.5 %all-gather.3.cloned.1.call-start = ((), (), s32[]{:S(2)}) async-start(), calls=%async_computation.1 | async-start | bytes 7864320 | tf_op jit(solution)/shard_map/all_gather | solution.py:1635
  29.7 65.6 %slice-start = ((bf16[256,8192]{1,0:T(8,128)(2,1)}), bf16[64,8192]{1,0:T(8,128)(2,1)S(1)}, s32[]{:S(2)}) async-start(bf16[256,8192]{1,0:T(8,128)(2,1)} %refs_0_.1), calls=%async_computation.2 | async-start | bytes 2097152 | tf_op jit(solution)/shard_map/slice | solution.py:1640
  29.7 65.6 %slice-start.1 = ((bf16[256,8192]{1,0:T(8,128)(2,1)}), bf16[64,8192]{1,0:T(8,128)(2,1)S(1)}, s32[]{:S(2)}) async-start(bf16[256,8192]{1,0:T(8,128)(2,1)} %refs_1_.4), calls=%async_computation.3 | async-start | bytes 2097152 | tf_op jit(solution)/shard_map/slice | solution.py:1640
  97.1 76.6 %all-to-all-start = ((bf16[64,8,2048]{2,0,1:T(8,128)(2,1)}), bf16[64,8,2048]{2,0,1:T(8,128)(2,1)}, u32[]{:S(2)}, u32[]{:S(2)}) async-start(bf16[64,8,2048]{2,0,1:T(8,128)(2,1)} %pad_maximum_fusion), calls=%async_computation | async-start | bytes 4194304 | tf_op jit(solution)/shard_map/all_to_all | solution.py:1618
  128.6 44.3 %copy-start.3 = (s32[1,16]{1,0:T(1,128)S(1)}, s32[1,16]{1,0:T(1,128)}, u32[]{:S(2)}) copy-start(s32[1,16]{1,0:T(1,128)} %order_ref.1) | copy-start | bytes 196
  481.6 52.6 %copy-start.2 = (f32[1,2048]{1,0:T(1,128)S(1)}, f32[1,2048]{1,0:T(1,128)}, u32[]{:S(2)}) copy-start(f32[1,2048]{1,0:T(1,128)} %get-tuple-element.179) | copy-start | bytes 24580
  693.9 18.0 %copy-start = (bf16[256,2048]{1,0:T(8,128)(2,1)S(1)}, bf16[256,2048]{1,0:T(8,128)(2,1)}, u32[]{:S(2)}) copy-start(bf16[256,2048]{1,0:T(8,128)(2,1)} %get-tuple-element.132) | copy-start | bytes 3145732
  693.9 19.0 %copy-start.1 = (bf16[256,2048]{1,0:T(8,128)(2,1)S(1)}, bf16[256,2048]{1,0:T(8,128)(2,1)}, u32[]{:S(2)}) copy-start(bf16[256,2048]{1,0:T(8,128)(2,1)} %get-tuple-element.160) | copy-start | bytes 3145732
Sparse Core Ops, SparseCore 0:
  29.9 116.5 all-gather.2

commit v15 on v14

--- a/solution.py
+++ b/solution.py
@@ -978,9 +978,9 @@
     first.pass_across()
     first.along_y()
     forward(*ALONG_Y)
-    second.relay()
     first.across()
     forward(*ACROSS)
+    second.relay()
     down_load.wait()
     second.sibling()
     backward(*SIBLING)

time: 731 us -> 731 us (level)
  no operation moved by 1% of the time
where the time goes in v15:
time: 731 us; the launch traced here: 721 us
  Pallas kernels  695 us (95%)
  between operations  14.7 us (2%)
    pallas_call x9, Pallas kernels, run(): pl.pallas_call(body, out_shape=tuple((shape for shape, _ in outs)), in_sp...  650 us
    pallas_call x1, Pallas kernels, attend(): pl.pallas_call(functools.partial(attend_kernel, heads, order.shape[1], bl...  27.2 us
    pallas_call x1, Pallas kernels, finish(): pl.pallas_call(functools.partial(finish_kernel, heads), out_shape=tuple(s...  18 us
  transfers between devices with their start and end apart: 2, of which 0 were waited for; matrix products, arithmetic and copies ran while one was open for 0% of the time, Pallas kernels for 19%

profile of v15, /device:TPU:0, one launch (start us, length us, event | category | flops | bytes accessed | tf_op | source)
XLA Modules:
  0.0 721.1 jit_solution(17000047255225783942)
XLA Ops:
  7.2 0.0 all-gather.3.cloned.1.call-start
  7.2 22.5 %shard_map.230 = bf16[8,48,2048]{2,1,0:T(8,128)(2,1)} custom-call(bf16[256,8192]{1,0:T(8,128)(2,1)} %refs_0_.1, bf16[256,8192]{1,0:T(8,128)(2,1)} %refs_1_.4), custom_call_target="tpu_custom_call" | custom-call | bytes 39321600 | tf_op jit(solution)/shard_map/pallas_call | solution.py:473
  29.7 0.0 slice-start
  29.7 0.0 slice-start.1
  29.8 0.0 all-gather.3.cloned.1.call-update
  29.8 65.6 %shard_map.231 = (bf16[2048,2048]{1,0:T(8,128)(2,1)}, bf16[2048,512]{1,0:T(8,128)(2,1)}) custom-call(bf16[256,2048]{1,0:T(8,128)(2,1)} %bitcast.45, f32[1,2048]{1,0:T(1,128)} %bitcast.51, bf16[256,2048]{1,0:T(8,128)(2,1)} %refs_2_.1, bf16[256,1024]{1,0:T(8,128)(2,1)} %refs_3_.1, bf16[256,1024]{1,0:T(8,128)(2,1)} %refs_4_.1), custom_call_target="tpu_custom_call" | custom-call | bytes 157286400 | tf_op jit(solution)/shard_map/pallas_call | solution.py:473
  95.4 0.0 slice-done
  95.4 0.0 slice-done.1
  95.4 0.2 copy_bitcast_fusion
  95.6 1.5 pad_maximum_fusion
  97.1 4.4 all-to-all-start
  101.5 27.2 %shard_map.232 = (bf16[2048,256]{1,0:T(8,128)(2,1)}, bf16[2,2048,128]{2,1,0:T(8,128)(2,1)}, bf16[2048,128]{1,0:T(8,128)(2,1)}, bf16[2048,128]{1,0:T(8,128)(2,1)}...) custom-call(s32[1,16]{1,0:T(1,128)} %order_ref.1, bf16[2048,2048]{1,0:T(8,128)(2,1)} %get-tuple-element.122.rows_hbm.refs_2_, ...), custom_call_target="tpu_custom_call" | custom-call | flops 7516192768 | bytes 29360128 | tf_op jit(solution)/shard_map/pallas_call | solution.py:163
  128.6 0.0 copy-start.3
  128.7 44.3 %shard_map.233.refs_0_.refs_4_.refs_3_ = f32[256,2048]{1,0:T(8,128)} custom-call(bf16[2048,256]{1,0:T(8,128)(2,1)} %get-tuple-element.124.refs_0_.refs_2_, bf16[256,2048]{1,0:T(8,128)(2,1)} %refs_1_.7, bf16[256,2048]{1,0:T(8,128)(2,1)} %bitcast.46), custom_call_target="tpu_custom_call" | custom-call | flops 2147483648 | bytes 157286400 | tf_op jit(solution)/shard_map/pallas_call | solution.py:473
  173.0 0.0 copy-done.3
  173.0 0.7 iota_add_fusion
  173.7 0.0 all-to-all-done
  173.7 0.0 all-gather.3.cloned.1.call-done
  173.7 86.0 %shard_map.234 = (bf16[2048,2048]{1,0:T(8,128)(2,1)}, bf16[2048,1024]{1,0:T(8,128)(2,1)}, bf16[8,256,2048]{2,1,0:T(8,128)(2,1)}, bf16[2048,2048]{1,0:T(8,128)(2,1)}, bf16[4,256,2048]{2,1,0:T(8,128)(2,1)}) custom-call(f32[256,2048]{1,0:T(8,128)} %shard_map.233.refs_0_.refs_4_.refs_3_, f32[1,2048]{1,0:T(1,128)} %bitcast.68, bf16[256,2048]{1,0:T(8,128)(2,1)} %bitcast.64, ...), custom_call_target="tpu_custom_call" | custom-call | flops 34359738368 | bytes 314572800 | tf_op jit(solution)/shard_map/pallas_call | solution.py:473
  259.7 57.1 %shard_map.235 = (bf16[256,2048]{1,0:T(8,128)(2,1)}, bf16[8,256,2048]{2,1,0:T(8,128)(2,1)}, bf16[8,16,1024]{2,1,0:T(8,128)(2,1)}, bf16[8,16,1024]{2,1,0:T(8,128)...) custom-call(bf16[2048,1024]{1,0:T(8,128)(2,1)} %get-tuple-element.12, ...), custom_call_target="tpu_custom_call" | custom-call | flops 25769803776 | bytes 157286400 | tf_op jit(solution)/shard_map/pallas_call | solution.py:473
  316.8 68.3 %shard_map.236 = (f32[256,2048]{1,0:T(8,128)}, f32[1,2048]{1,0:T(1,128)}, bf16[8,16,1024]{2,1,0:T(8,128)(2,1)}, bf16[8,16,1024]{2,1,0:T(8,128)(2,1)}, bf16[8,16,...) custom-call(bf16[2048,2048]{1,0:T(8,128)(2,1)} %get-tuple-element.13, ...), custom_call_target="tpu_custom_call" | custom-call | flops 17179869184 | bytes 157286400 | tf_op jit(solution)/shard_map/pallas_call | solution.py:473
  385.0 96.6 %shard_map.237 = (bf16[2048,512]{1,0:T(8,128)(2,1)}, bf16[256,2048]{1,0:T(8,128)(2,1)}, bf16[8,16,1024]{2,1,0:T(8,128)(2,1)}, bf16[8,16,1024]{2,1,0:T(8,128)(2,1...) custom-call(f32[256,2048]{1,0:T(8,128)} %get-tuple-element.141.refs_, ...), custom_call_target="tpu_custom_call" | custom-call | flops 12884901888 | bytes 262144000 | tf_op jit(solution)/shard_map/pallas_call | solution.py:473
  481.6 0.0 copy-start.2
  481.6 52.6 %shard_map.238 = (bf16[256,2048]{1,0:T(8,128)(2,1)}, f32[1,2048]{1,0:T(1,128)}, bf16[8,256,512]{2,1,0:T(8,128)(2,1)}, bf16[8,16,1024]{2,1,0:T(8,128)(2,1)}, bf16...) custom-call(bf16[2048,512]{1,0:T(8,128)(2,1)} %get-tuple-element.153, ...), custom_call_target="tpu_custom_call" | custom-call | flops 8589934592 | bytes 157286400 | tf_op jit(solution)/shard_map/pallas_call | solution.py:473
  534.3 0.0 copy-done.2
  534.3 0.7 maximum_bitcast_fusion
  535.0 0.6 pad.4.refs_1_
  535.6 156.9 %shard_map.239 = (bf16[256,8192]{1,0:T(8,128)(2,1)}, bf16[256,8192]{1,0:T(8,128)(2,1)}, bf16[2,8,32,2048]{3,2,1,0:T(8,128)(2,1)}, f32[8,256]{1,0:T(8,128)}, bf16...) custom-call(bf16[8,8,32,512]{3,2,1,0:T(8,128)(2,1)} %bitcast.44, ...), custom_call_target="tpu_custom_call" | custom-call | bytes 52428800 | tf_op jit(solution)/shard_map/pallas_call | solution.py:473
  692.5 1.3 fusion
  693.9 0.0 copy-start
  693.9 0.0 copy-start.1
  693.9 18.0 %shard_map.240 = (f32[8,32,2048]{2,1,0:T(8,128)}, f32[8,32,1024]{2,1,0:T(8,128)}, f32[8,32,1024]{2,1,0:T(8,128)}, f32[8,32,2048]{2,1,0:T(8,128)}, f32[8,32,8192]...) custom-call(bf16[8,16,1024]{2,1,0:T(8,128)(2,1)} %get-tuple-element.161.refs_0_, ...), custom_call_target="tpu_custom_call" | custom-call | bytes 47185920 | tf_op jit(solution)/shard_map/pallas_call | solution.py:1551
  711.9 0.0 copy-done
  711.9 1.0 copy.36
  712.9 0.0 copy-done.1
  712.9 1.0 copy.37
  (1 shorter events, 0.0 us)
Async XLA Ops:
  7.2 166.5 %all-gather.3.cloned.1.call-start = ((), (), s32[]{:S(2)}) async-start(), calls=%async_computation.1 | async-start | bytes 7864320 | tf_op jit(solution)/shard_map/all_gather | solution.py:1635
  29.7 65.6 %slice-start = ((bf16[256,8192]{1,0:T(8,128)(2,1)}), bf16[64,8192]{1,0:T(8,128)(2,1)S(1)}, s32[]{:S(2)}) async-start(bf16[256,8192]{1,0:T(8,128)(2,1)} %refs_0_.1), calls=%async_computation.2 | async-start | bytes 2097152 | tf_op jit(solution)/shard_map/slice | solution.py:1640
  29.7 65.6 %slice-start.1 = ((bf16[256,8192]{1,0:T(8,128)(2,1)}), bf16[64,8192]{1,0:T(8,128)(2,1)S(1)}, s32[]{:S(2)}) async-start(bf16[256,8192]{1,0:T(8,128)(2,1)} %refs_1_.4), calls=%async_computation.3 | async-start | bytes 2097152 | tf_op jit(solution)/shard_map/slice | solution.py:1640
  97.1 76.6 %all-to-all-start = ((bf16[64,8,2048]{2,0,1:T(8,128)(2,1)}), bf16[64,8,2048]{2,0,1:T(8,128)(2,1)}, u32[]{:S(2)}, u32[]{:S(2)}) async-start(bf16[64,8,2048]{2,0,1:T(8,128)(2,1)} %pad_maximum_fusion), calls=%async_computation | async-start | bytes 4194304 | tf_op jit(solution)/shard_map/all_to_all | solution.py:1618
  128.6 44.3 %copy-start.3 = (s32[1,16]{1,0:T(1,128)S(1)}, s32[1,16]{1,0:T(1,128)}, u32[]{:S(2)}) copy-start(s32[1,16]{1,0:T(1,128)} %order_ref.1) | copy-start | bytes 196
  481.6 52.6 %copy-start.2 = (f32[1,2048]{1,0:T(1,128)S(1)}, f32[1,2048]{1,0:T(1,128)}, u32[]{:S(2)}) copy-start(f32[1,2048]{1,0:T(1,128)} %get-tuple-element.179) | copy-start | bytes 24580
  693.9 18.0 %copy-start = (bf16[256,2048]{1,0:T(8,128)(2,1)S(1)}, bf16[256,2048]{1,0:T(8,128)(2,1)}, u32[]{:S(2)}) copy-start(bf16[256,2048]{1,0:T(8,128)(2,1)} %get-tuple-element.132) | copy-start | bytes 3145732
  693.9 19.0 %copy-start.1 = (bf16[256,2048]{1,0:T(8,128)(2,1)S(1)}, bf16[256,2048]{1,0:T(8,128)(2,1)}, u32[]{:S(2)}) copy-start(bf16[256,2048]{1,0:T(8,128)(2,1)} %get-tuple-element.160) | copy-start | bytes 3145732
Sparse Core Ops, SparseCore 0:
  29.9 116.5 all-gather.2
